TPU v7x, 512 devices: a whole 4x8x8 slice. The times are simulated.
512 devices in a mesh: ctx: 64 (over y, z_lo, core), fsdp: 8 (over z_hi, x).
Axes of the slice: x: 4, y: 8, z: 8 (z_hi: 2, z_lo: 4; z = z_hi * 4 + z_lo), core: 2. Of those that a mesh axis runs over, the one named last changes fastest.
Arguments:
- tokens: bfloat16 [16384, 8192], P('ctx'), may hold values from -6 to 6
- query_weight: bfloat16 [8192, 4096], P('ctx', 'fsdp'), may hold values from -0.0625 to 0.0625
- key_weight: bfloat16 [8192, 1024], P('ctx', 'fsdp'), may hold values from -0.0625 to 0.0625
- value_weight: bfloat16 [8192, 1024], P('ctx', 'fsdp'), may hold values from -0.0625 to 0.0625
- adapter_down_weight: bfloat16 [8192, 32], P('ctx'), may hold values from -0.0625 to 0.0625
- query_up_weight: bfloat16 [16, 4096], P(None, 'fsdp'), may hold values from -1.5 to 1.5
- value_up_weight: bfloat16 [16, 1024], P(None, 'fsdp'), may hold values from -1.5 to 1.5
- head_shifts: int32 [32], P('fsdp'), may hold values from 0 to 1024, as said below
- output_gradient: bfloat16 [16384, 4096], P('ctx', 'fsdp'), may hold values from -6 to 6
Outputs:
- attention: bfloat16 [16384, 4096], P('ctx', 'fsdp')
- value_gradient: bfloat16 [16384, 1024], P('ctx', 'fsdp')
- grad_down: float32 [8192, 32], P('ctx')
- query_up_gradient: float32 [16, 4096], P(None, 'fsdp')
- value_up_gradient: float32 [16, 1024], P(None, 'fsdp')
Inputs may be any that keep to these rules, and one draw needn't show every extreme that they name: `head_shifts`: exactly half of the 32 heads have offset 2048 // 2, the others 0.
All inputs are finite; a program needn't handle non-finite values.
Results may differ from a plain program's by a relative error of at most 0.025.
The roundings to bfloat16 on the way count: a program that leaves them out, or rounds other values in their place, can miss the bound.
Values may be sent and summed in bfloat16 or wider, within the bound.
No kernel may reach another device: no remote copies, remote signals or barrier semaphores. Data moves between devices by JAX's collectives and lax.ppermute only.
A program may use at most 64 MiB of HBM per device.

v0:
```python
import jax
import jax.numpy as jnp
from jax import lax
from jax.sharding import PartitionSpec as P

GROUP = 2048


adapter_scale = 1.0


def from_behind(value, axis, steps):
    count = lax.axis_size(axis)
    pairs = [(source, (source + steps) % count) for source in range(count)]
    return lax.ppermute(value, axis, pairs)


def masked_softmax(logits, allowed):
    shifted = jnp.where(allowed, logits, -1e30)
    highest = jnp.max(shifted, axis=-1, keepdims=True)
    weights = jnp.where(allowed, jnp.exp(shifted - highest), 0.0)
    return weights / jnp.sum(weights, axis=-1, keepdims=True)


def on_device(
    tokens,
    query_weight,
    key_weight,
    value_weight,
    adapter_down_weight,
    query_up_weight,
    value_up_weight,
    head_shifts,
    output_gradient,
):
    rows_here = tokens.shape[0]
    heads_here = head_shifts.shape[0]
    width_query = query_weight.shape[1]
    head_width = width_query // heads_here
    width_value = key_weight.shape[1]
    pairs_here = width_value // head_width
    repeat = heads_here // pairs_here
    adapter_rank_count = adapter_down_weight.shape[1] // 2
    devices = lax.axis_size("ctx")
    seq_length = rows_here * devices
    back_steps = GROUP // rows_here - 1
    blocks_count = back_steps + 1
    key_count = blocks_count * rows_here
    score_scale = head_width ** (-0.5)
    position = lax.axis_index("ctx")
    gathered = (
        lax.all_gather(query_weight, "ctx", axis=0, tiled=True),
        lax.all_gather(key_weight, "ctx", axis=0, tiled=True),
        lax.all_gather(value_weight, "ctx", axis=0, tiled=True),
        lax.all_gather(adapter_down_weight, "ctx", axis=0, tiled=True),
    )
    projected_query, proj_key, projected_value, proj_low = (
        jnp.dot(tokens, weight_rows, preferred_element_type=jnp.float32) for weight_rows in gathered
    )
    reduced_activations = proj_low.astype(jnp.bfloat16)
    query_reduced = reduced_activations[:, :adapter_rank_count]
    value_reduced = reduced_activations[:, adapter_rank_count:]
    query_matrix = (
        projected_query
        + adapter_scale
        * jnp.dot(query_reduced, query_up_weight, preferred_element_type=jnp.float32)
    ).astype(jnp.bfloat16)
    keys_here = proj_key.astype(jnp.bfloat16)
    values_here = (
        projected_value
        + adapter_scale
        * jnp.dot(value_reduced, value_up_weight, preferred_element_type=jnp.float32)
    ).astype(jnp.bfloat16)
    kv_pair = jnp.stack([keys_here, values_here])

    def pass_along(carried, unused_item):
        arrived = from_behind(carried, "ctx", 1)
        return (arrived, arrived)

    _, remote = lax.scan(pass_along, kv_pair, None, length=back_steps)
    blocks = jnp.concatenate([kv_pair[None], remote], axis=0)
    key_all = blocks[:, 0].reshape(key_count, pairs_here, head_width)
    value_all = blocks[:, 1].reshape(key_count, pairs_here, head_width)
    local_rows = jnp.arange(rows_here, dtype=jnp.int32)
    query_pos = position * rows_here + local_rows
    owners = jnp.mod(position - jnp.arange(blocks_count, dtype=jnp.int32), devices)
    key_pos = (owners[:, None] * rows_here + local_rows[None, :]).reshape(key_count)
    offsets = head_shifts.reshape(pairs_here, repeat, 1)
    query_roll = jnp.mod(query_pos[None, None, :] - offsets, seq_length)
    key_roll = jnp.mod(key_pos[None, None, :] - offsets, seq_length)
    same_group = query_roll[..., :, None] // GROUP == key_roll[..., None, :] // GROUP
    allowed = same_group & (key_roll[..., None, :] <= query_roll[..., :, None])
    query_heads = query_matrix.reshape(rows_here, pairs_here, repeat, head_width)
    scores = jnp.einsum("tgrd,lgd->grtl", query_heads, key_all, preferred_element_type=jnp.float32)
    attn_weights = masked_softmax(scores * score_scale, allowed)
    weights_low = attn_weights.astype(jnp.bfloat16)
    output_heads = jnp.einsum(
        "grtl,lgd->tgrd", weights_low, value_all, preferred_element_type=jnp.float32
    ).astype(jnp.bfloat16)
    attention = output_heads.reshape(rows_here, width_query)
    grad_heads = output_gradient.reshape(rows_here, pairs_here, repeat, head_width)
    grad_weights = jnp.einsum(
        "tgrd,lgd->grtl", grad_heads, value_all, preferred_element_type=jnp.float32
    )
    correction = jnp.sum(
        grad_heads.astype(jnp.float32) * output_heads.astype(jnp.float32), axis=-1
    ).transpose(1, 2, 0)
    grad_scores = (attn_weights * (grad_weights - correction[..., None])).astype(jnp.bfloat16)
    query_gradient = (
        jnp.einsum("grtl,lgd->tgrd", grad_scores, key_all, preferred_element_type=jnp.float32)
        * score_scale
    ).astype(jnp.bfloat16)
    query_gradient = query_gradient.reshape(rows_here, width_query)
    value_terms = jnp.einsum(
        "grtl,tgrd->lgd", weights_low, grad_heads, preferred_element_type=jnp.float32
    )
    value_terms = value_terms.reshape(blocks_count, rows_here, width_value)

    def carry_forward(running, block_term):
        return (from_behind(running, "ctx", 1) + block_term, None)

    running_sum, _ = lax.scan(carry_forward, value_terms[0], value_terms[1:])
    summed = from_behind(running_sum, "ctx", -back_steps)
    value_gradient = summed.astype(jnp.bfloat16)
    rank_terms = jnp.concatenate(
        [
            adapter_scale
            * jnp.dot(query_gradient, query_up_weight.T, preferred_element_type=jnp.float32),
            adapter_scale
            * jnp.dot(value_gradient, value_up_weight.T, preferred_element_type=jnp.float32),
        ],
        axis=1,
    )
    rank_grad = lax.psum(rank_terms, "fsdp").astype(jnp.bfloat16)
    grad_down = lax.psum_scatter(
        lax.dot_general(
            tokens, rank_grad, (((0,), (0,)), ((), ())), preferred_element_type=jnp.float32
        ),
        "ctx",
        scatter_dimension=0,
        tiled=True,
    )
    query_portion = adapter_scale * lax.dot_general(
        query_reduced, query_gradient, (((0,), (0,)), ((), ())), preferred_element_type=jnp.float32
    )
    value_portion = adapter_scale * lax.dot_general(
        value_reduced, value_gradient, (((0,), (0,)), ((), ())), preferred_element_type=jnp.float32
    )
    query_up_gradient, value_up_gradient = lax.psum((query_portion, value_portion), "ctx")
    return (attention, value_gradient, grad_down, query_up_gradient, value_up_gradient)


def solution(mesh):
    in_specs = (
        P("ctx", None),
        P("ctx", "fsdp"),
        P("ctx", "fsdp"),
        P("ctx", "fsdp"),
        P("ctx", None),
        P(None, "fsdp"),
        P(None, "fsdp"),
        P("fsdp"),
        P("ctx", "fsdp"),
    )
    out_specs = (
        P("ctx", "fsdp"),
        P("ctx", "fsdp"),
        P("ctx", None),
        P(None, "fsdp"),
        P(None, "fsdp"),
    )
    return jax.shard_map(
        on_device, mesh=mesh, in_specs=in_specs, out_specs=out_specs, check_vma=False
    )
```

profile of v0, /device:TPU:1, one launch (start us, length us, event | category | flops | bytes accessed | tf_op | source)
XLA Modules:
  0.0 814.9 jit_solution(8477409543605219956)
XLA Ops:
  11.4 85.5 %all_gather.14 = bf16[8192,32]{0,1:T(8,128)(2,1)S(1)} all-gather(bf16[128,32]{0,1:T(8,128)(2,1)} %param.17), channel_id=1, replica_groups=mesh['ctx'=64,'fsdp'=8] {'ctx'}, dimensions={0}, use_global_device_ids=true | all-gather | bytes 532480 | tf_op jit(solution)/shard_map/all_gather | solution.py:55
  102.2 32.4 %all-gather.4.cloned.1.call-done = bf16[8192,128]{1,0:T(8,128)(2,1)} async-done(((bf16[128,128]{1,0:T(8,128)(2,1)}), bf16[8192,128]{1,0:T(8,128)(2,1)}) %all-gather.4.cloned.1.call-update) | async-done | bytes 2097168 | tf_op jit(solution)/shard_map/all_gather | solution.py:53
  138.7 114.1 %all-gather.6.cloned.1.call-done = bf16[8192,128]{1,0:T(8,128)(2,1)} async-done(((bf16[128,128]{1,0:T(8,128)(2,1)}), bf16[8192,128]{1,0:T(8,128)(2,1)}) %all-gather.6.cloned.1.call-update) | async-done | bytes 2097168 | tf_op jit(solution)/shard_map/all_gather | solution.py:54
  257.0 65.9 %while.22 = (s32[]{:T(128)}, bf16[2,256,128]{2,1,0:T(8,128)(2,1)S(1)}, bf16[7,2,256,128]{3,2,1,0:T(8,128)(2,1)S(1)}, s32[]{:T(128)}) while((s32[]{:T(128)}, bf16[2,256,128]{2,1,0:T(8,128)(2,1)S(1)}, bf16[7,2,256,128]{3,2,1,0:T(8,128)(2,1)S(1)}, s32[]{:T(128)}) %tuple.43), condition=%wide.region_1.2_spmd, body=%wide.region_0.1_spmd.sunk | while | flops 2 | bytes 1048681 | solution.py:80
  261.4 4.4 collective-permute-start
  265.8 4.6 collective-permute-done
  272.9 8.0 collective-permute-done
  282.9 8.5 %collective-permute-done = bf16[2,256,128]{2,1,0:T(8,128)(2,1)S(1)} collective-permute-done((bf16[2,256,128]{2,1,0:T(8,128)(2,1)S(1)}, bf16[2,256,128]{2,1,0:T(8,128)(2,1)S(1)}, u32[]{:S(2)}, u32[]{:S(2)}) %collective-permute-start) | collective-permute-done | bytes 131104 | tf_op jit(solution)/shard_map/while/body/eval_jaxpr/ppermute | solution.py:15
  293.4 8.5 %collective-permute-done = bf16[2,256,128]{2,1,0:T(8,128)(2,1)S(1)} collective-permute-done((bf16[2,256,128]{2,1,0:T(8,128)(2,1)S(1)}, bf16[2,256,128]{2,1,0:T(8,128)(2,1)S(1)}, u32[]{:S(2)}, u32[]{:S(2)}) %collective-permute-start) | collective-permute-done | bytes 131104 | tf_op jit(solution)/shard_map/while/body/eval_jaxpr/ppermute | solution.py:15
  303.9 8.5 %collective-permute-done = bf16[2,256,128]{2,1,0:T(8,128)(2,1)S(1)} collective-permute-done((bf16[2,256,128]{2,1,0:T(8,128)(2,1)S(1)}, bf16[2,256,128]{2,1,0:T(8,128)(2,1)S(1)}, u32[]{:S(2)}, u32[]{:S(2)}) %collective-permute-start) | collective-permute-done | bytes 131104 | tf_op jit(solution)/shard_map/while/body/eval_jaxpr/ppermute | solution.py:15
  314.3 8.5 %collective-permute-done = bf16[2,256,128]{2,1,0:T(8,128)(2,1)S(1)} collective-permute-done((bf16[2,256,128]{2,1,0:T(8,128)(2,1)S(1)}, bf16[2,256,128]{2,1,0:T(8,128)(2,1)S(1)}, u32[]{:S(2)}, u32[]{:S(2)}) %collective-permute-start) | collective-permute-done | bytes 131104 | tf_op jit(solution)/shard_map/while/body/eval_jaxpr/ppermute | solution.py:15
  322.9 54.9 %all-gather.8.cloned.1.call-done = bf16[8192,512]{1,0:T(8,128)(2,1)} async-done(((bf16[128,512]{1,0:T(8,128)(2,1)}), bf16[8192,512]{1,0:T(8,128)(2,1)}) %all-gather.8.cloned.1.call-update) | async-done | bytes 8388624 | tf_op jit(solution)/shard_map/all_gather | solution.py:52
  377.8 7.0 fusion.59
  396.2 7.2 fusion.22
  403.5 64.4 %while.23 = (s32[]{:T(128)}, f32[256,128]{1,0:T(8,128)S(1)}, f32[7,256,128]{2,1,0:T(8,128)S(1)}, s32[]{:T(128)}) while((s32[]{:T(128)}, f32[256,128]{1,0:T(8,128)S(1)}, f32[7,256,128]{2,1,0:T(8,128)S(1)}, s32[]{:T(128)}) %tuple.59), condition=%wide.region_5.6_spmd, body=%wide.region_4.5_spmd.sunk | while | flops 32770 | bytes 917609 | solution.py:122
  408.0 4.4 collective-permute-start.1
  418.7 8.2 %collective-permute-done.1 = f32[256,128]{1,0:T(8,128)S(1)} collective-permute-done((f32[256,128]{1,0:T(8,128)S(1)}, f32[256,128]{1,0:T(8,128)S(1)}, u32[]{:S(2)}, u32[]{:S(2)}) %collective-permute-start.1) | collective-permute-done | bytes 131104 | tf_op jit(solution)/shard_map/while/body/eval_jaxpr/ppermute | solution.py:15
  428.9 8.3 %collective-permute-done.1 = f32[256,128]{1,0:T(8,128)S(1)} collective-permute-done((f32[256,128]{1,0:T(8,128)S(1)}, f32[256,128]{1,0:T(8,128)S(1)}, u32[]{:S(2)}, u32[]{:S(2)}) %collective-permute-start.1) | collective-permute-done | bytes 131104 | tf_op jit(solution)/shard_map/while/body/eval_jaxpr/ppermute | solution.py:15
  439.1 8.3 %collective-permute-done.1 = f32[256,128]{1,0:T(8,128)S(1)} collective-permute-done((f32[256,128]{1,0:T(8,128)S(1)}, f32[256,128]{1,0:T(8,128)S(1)}, u32[]{:S(2)}, u32[]{:S(2)}) %collective-permute-start.1) | collective-permute-done | bytes 131104 | tf_op jit(solution)/shard_map/while/body/eval_jaxpr/ppermute | solution.py:15
  449.4 8.3 %collective-permute-done.1 = f32[256,128]{1,0:T(8,128)S(1)} collective-permute-done((f32[256,128]{1,0:T(8,128)S(1)}, f32[256,128]{1,0:T(8,128)S(1)}, u32[]{:S(2)}, u32[]{:S(2)}) %collective-permute-start.1) | collective-permute-done | bytes 131104 | tf_op jit(solution)/shard_map/while/body/eval_jaxpr/ppermute | solution.py:15
  459.6 8.3 %collective-permute-done.1 = f32[256,128]{1,0:T(8,128)S(1)} collective-permute-done((f32[256,128]{1,0:T(8,128)S(1)}, f32[256,128]{1,0:T(8,128)S(1)}, u32[]{:S(2)}, u32[]{:S(2)}) %collective-permute-start.1) | collective-permute-done | bytes 131104 | tf_op jit(solution)/shard_map/while/body/eval_jaxpr/ppermute | solution.py:15
  473.9 45.7 %psum.21 = bf16[256,32]{0,1:T(8,128)(2,1)S(1)} all-reduce(f32[256,32]{0,1:T(8,128)S(1)} %pad_maximum_fusion.2), channel_id=1, replica_groups=mesh['ctx'=64,'fsdp'=8] {'fsdp'}, use_global_device_ids=true, to_apply=%region_7.8 | all-reduce | flops 8192 | bytes 49152 | tf_op jit(solution)/shard_map/psum | solution.py:134
  524.8 274.8 %all-reduce = (f32[16,512]{1,0:T(8,128)}, f32[16,128]{1,0:T(8,128)}) all-reduce(f32[16,512]{1,0:T(8,128)S(1)} %fusion.43, f32[16,128]{1,0:T(8,128)S(1)} %fusion.46), channel_id=1, replica_groups=mesh['ctx'=64,'fsdp'=8] {'ctx'}, use_global_device_ids=true, to_apply=%region_9.10 | all-reduce | flops 10240 | bytes 81920 | tf_op jit(solution)/shard_map/psum | solution.py:149
  799.5 8.2 %reduce-scatter.2.cloned.1.call-done = f32[128,32]{0,1:T(8,128)} async-done(((f32[8192,32]{0,1:T(8,128)}), f32[128,32]{0,1:T(8,128)}) %reduce-scatter.2.cloned.1.call-update) | async-done | bytes 16400 | tf_op jit(solution)/shard_map/reduce_scatter | solution.py:135
  (85 shorter events, 74.0 us)
Async XLA Ops:
  7.2 377.7 %copy-start = (bf16[16,512]{1,0:T(8,128)(2,1)S(1)}, bf16[16,512]{1,0:T(8,128)(2,1)}, u32[]{:S(2)}) copy-start(bf16[16,512]{1,0:T(8,128)(2,1)} %param.18) | copy-start | bytes 49156
  7.2 127.4 %all-gather.4.cloned.1.call-start = ((), (), s32[]{:S(2)}) async-start(), calls=%async_computation.1 | async-start | bytes 2129920 | tf_op jit(solution)/shard_map/all_gather | solution.py:53
  7.9 244.9 %all-gather.6.cloned.1.call-start = ((), (), s32[]{:S(2)}) async-start(), calls=%async_computation.2 | async-start | bytes 2129920 | tf_op jit(solution)/shard_map/all_gather | solution.py:54
  8.7 369.2 %all-gather.8.cloned.1.call-start = ((), (), s32[]{:S(2)}) async-start(), calls=%async_computation.3 | async-start | bytes 8519680 | tf_op jit(solution)/shard_map/all_gather | solution.py:52
  9.4 798.3 %reduce-scatter.2.cloned.1.call-start = ((), (), s32[]{:S(2)}) async-start(), calls=%async_computation.4 | async-start | bytes 1064960 | tf_op jit(solution)/shard_map/reduce_scatter | solution.py:135
  257.2 4.2 collective-permute-start
  261.4 9.0 %collective-permute-start = (bf16[2,256,128]{2,1,0:T(8,128)(2,1)S(1)}, bf16[2,256,128]{2,1,0:T(8,128)(2,1)S(1)}, u32[]{:S(2)}, u32[]{:S(2)}) collective-permute-start(bf16[2,256,128]{2,1,0:T(8,128)(2,1)S(1)} %get-tuple-element.120), channel_id=1, source_target_pairs={{0,8},{8,16},{16,24},{24,32},{32,40},{40,48},{48,56},{56,64},{64,7... | collective-permute-start | bytes 393224 | tf_op jit(solution)/shard_map/while/body/eval_jaxpr/ppermute | solution.py:15
  270.5 10.4 %collective-permute-start = (bf16[2,256,128]{2,1,0:T(8,128)(2,1)S(1)}, bf16[2,256,128]{2,1,0:T(8,128)(2,1)S(1)}, u32[]{:S(2)}, u32[]{:S(2)}) collective-permute-start(bf16[2,256,128]{2,1,0:T(8,128)(2,1)S(1)} %get-tuple-element.120), channel_id=1, source_target_pairs={{0,8},{8,16},{16,24},{24,32},{32,40},{40,48},{48,56},{56,64},{64,7... | collective-permute-start | bytes 393224 | tf_op jit(solution)/shard_map/while/body/eval_jaxpr/ppermute | solution.py:15
  280.9 10.4 %collective-permute-start = (bf16[2,256,128]{2,1,0:T(8,128)(2,1)S(1)}, bf16[2,256,128]{2,1,0:T(8,128)(2,1)S(1)}, u32[]{:S(2)}, u32[]{:S(2)}) collective-permute-start(bf16[2,256,128]{2,1,0:T(8,128)(2,1)S(1)} %get-tuple-element.120), channel_id=1, source_target_pairs={{0,8},{8,16},{16,24},{24,32},{32,40},{40,48},{48,56},{56,64},{64,7... | collective-permute-start | bytes 393224 | tf_op jit(solution)/shard_map/while/body/eval_jaxpr/ppermute | solution.py:15
  291.4 10.4 %collective-permute-start = (bf16[2,256,128]{2,1,0:T(8,128)(2,1)S(1)}, bf16[2,256,128]{2,1,0:T(8,128)(2,1)S(1)}, u32[]{:S(2)}, u32[]{:S(2)}) collective-permute-start(bf16[2,256,128]{2,1,0:T(8,128)(2,1)S(1)} %get-tuple-element.120), channel_id=1, source_target_pairs={{0,8},{8,16},{16,24},{24,32},{32,40},{40,48},{48,56},{56,64},{64,7... | collective-permute-start | bytes 393224 | tf_op jit(solution)/shard_map/while/body/eval_jaxpr/ppermute | solution.py:15
  301.9 10.4 %collective-permute-start = (bf16[2,256,128]{2,1,0:T(8,128)(2,1)S(1)}, bf16[2,256,128]{2,1,0:T(8,128)(2,1)S(1)}, u32[]{:S(2)}, u32[]{:S(2)}) collective-permute-start(bf16[2,256,128]{2,1,0:T(8,128)(2,1)S(1)} %get-tuple-element.120), channel_id=1, source_target_pairs={{0,8},{8,16},{16,24},{24,32},{32,40},{40,48},{48,56},{56,64},{64,7... | collective-permute-start | bytes 393224 | tf_op jit(solution)/shard_map/while/body/eval_jaxpr/ppermute | solution.py:15
  312.4 10.4 %collective-permute-start = (bf16[2,256,128]{2,1,0:T(8,128)(2,1)S(1)}, bf16[2,256,128]{2,1,0:T(8,128)(2,1)S(1)}, u32[]{:S(2)}, u32[]{:S(2)}) collective-permute-start(bf16[2,256,128]{2,1,0:T(8,128)(2,1)S(1)} %get-tuple-element.120), channel_id=1, source_target_pairs={{0,8},{8,16},{16,24},{24,32},{32,40},{40,48},{48,56},{56,64},{64,7... | collective-permute-start | bytes 393224 | tf_op jit(solution)/shard_map/while/body/eval_jaxpr/ppermute | solution.py:15
  387.6 6.5 copy-start.1
  390.8 3.3 copy-start.2
  396.2 77.6 %copy-start.3 = (bf16[16,128]{1,0:T(8,128)(2,1)S(1)}, bf16[16,128]{1,0:T(8,128)(2,1)}, u32[]{:S(2)}) copy-start(bf16[16,128]{1,0:T(8,128)(2,1)} %param.19) | copy-start | bytes 12292
  403.5 4.5 collective-permute-start.1
  408.0 8.7 %collective-permute-start.1 = (f32[256,128]{1,0:T(8,128)S(1)}, f32[256,128]{1,0:T(8,128)S(1)}, u32[]{:S(2)}, u32[]{:S(2)}) collective-permute-start(f32[256,128]{1,0:T(8,128)S(1)} %get-tuple-element.132), channel_id=1, source_target_pairs={{0,8},{8,16},{16,24},{24,32},{32,40},{40,48},{48,56},{56,64},{64,7... | collective-permute-start | bytes 393224 | tf_op jit(solution)/shard_map/while/body/eval_jaxpr/ppermute | solution.py:15
  416.8 10.2 %collective-permute-start.1 = (f32[256,128]{1,0:T(8,128)S(1)}, f32[256,128]{1,0:T(8,128)S(1)}, u32[]{:S(2)}, u32[]{:S(2)}) collective-permute-start(f32[256,128]{1,0:T(8,128)S(1)} %get-tuple-element.132), channel_id=1, source_target_pairs={{0,8},{8,16},{16,24},{24,32},{32,40},{40,48},{48,56},{56,64},{64,7... | collective-permute-start | bytes 393224 | tf_op jit(solution)/shard_map/while/body/eval_jaxpr/ppermute | solution.py:15
  427.0 10.2 %collective-permute-start.1 = (f32[256,128]{1,0:T(8,128)S(1)}, f32[256,128]{1,0:T(8,128)S(1)}, u32[]{:S(2)}, u32[]{:S(2)}) collective-permute-start(f32[256,128]{1,0:T(8,128)S(1)} %get-tuple-element.132), channel_id=1, source_target_pairs={{0,8},{8,16},{16,24},{24,32},{32,40},{40,48},{48,56},{56,64},{64,7... | collective-permute-start | bytes 393224 | tf_op jit(solution)/shard_map/while/body/eval_jaxpr/ppermute | solution.py:15
  437.2 10.2 %collective-permute-start.1 = (f32[256,128]{1,0:T(8,128)S(1)}, f32[256,128]{1,0:T(8,128)S(1)}, u32[]{:S(2)}, u32[]{:S(2)}) collective-permute-start(f32[256,128]{1,0:T(8,128)S(1)} %get-tuple-element.132), channel_id=1, source_target_pairs={{0,8},{8,16},{16,24},{24,32},{32,40},{40,48},{48,56},{56,64},{64,7... | collective-permute-start | bytes 393224 | tf_op jit(solution)/shard_map/while/body/eval_jaxpr/ppermute | solution.py:15
  447.4 10.2 %collective-permute-start.1 = (f32[256,128]{1,0:T(8,128)S(1)}, f32[256,128]{1,0:T(8,128)S(1)}, u32[]{:S(2)}, u32[]{:S(2)}) collective-permute-start(f32[256,128]{1,0:T(8,128)S(1)} %get-tuple-element.132), channel_id=1, source_target_pairs={{0,8},{8,16},{16,24},{24,32},{32,40},{40,48},{48,56},{56,64},{64,7... | collective-permute-start | bytes 393224 | tf_op jit(solution)/shard_map/while/body/eval_jaxpr/ppermute | solution.py:15
  457.7 10.2 %collective-permute-start.1 = (f32[256,128]{1,0:T(8,128)S(1)}, f32[256,128]{1,0:T(8,128)S(1)}, u32[]{:S(2)}, u32[]{:S(2)}) collective-permute-start(f32[256,128]{1,0:T(8,128)S(1)} %get-tuple-element.132), channel_id=1, source_target_pairs={{0,8},{8,16},{16,24},{24,32},{32,40},{40,48},{48,56},{56,64},{64,7... | collective-permute-start | bytes 393224 | tf_op jit(solution)/shard_map/while/body/eval_jaxpr/ppermute | solution.py:15
  467.9 5.9 collective-permute-start.2
Sparse Core Ops, SparseCore 0:
  10.2 124.3 all-gather.3
  136.7 116.0 all-gather.5
  255.0 122.8 all-gather.7
  523.8 283.9 reduce-scatter.1
where the time goes:
time: 820 us; the launch traced here: 815 us
  blocking collectives  406 us (50%)
  waiting for transfers between devices  311 us (38%)
  matrix products  36.2 us (4%)
  starting transfers between devices  35.4 us (4%)
  between operations  14 us (2%)
  other arithmetic  8.31 us (1%)
    psum x1, blocking collectives, on_device(): lax.psum((query_portion, value_portion), 'ctx')  275 us
    all_gather x1, waiting for transfers between devices, on_device(): lax.all_gather(value_weight, 'ctx', axis=0, tiled=True)  114 us
    ppermute x15, waiting for transfers between devices, from_behind(): return lax.ppermute(value, axis, pairs)  99.8 us
    all_gather x1, blocking collectives, on_device(): lax.all_gather(adapter_down_weight, 'ctx', axis=0, tiled=True)  85.5 us
    all_gather x1, waiting for transfers between devices, on_device(): lax.all_gather(query_weight, 'ctx', axis=0, tiled=True)  54.9 us
    psum x1, blocking collectives, on_device(): rank_grad = lax.psum(rank_terms, 'fsdp').astype(jnp.bfloat16)  45.7 us
    ppermute x15, starting transfers between devices, from_behind(): return lax.ppermute(value, axis, pairs)  35.3 us
    all_gather x1, waiting for transfers between devices, on_device(): lax.all_gather(key_weight, 'ctx', axis=0, tiled=True)  32.4 us
  transfers between devices with their start and end apart: 19, of which 19 were waited for; matrix products, arithmetic and copies ran while one was open for 2% of the time, Pallas kernels for 0%

commit v1 on v0

v1 whole, which is shorter than its diff:
```python
import jax
import jax.numpy as jnp
from jax import lax
from jax.sharding import PartitionSpec as P

GROUP = 2048
bf16 = jnp.bfloat16
f32 = jnp.float32


def groups_of(devices, members):
    half = members // 2
    plain = [[start + i for i in range(members)] for start in range(0, devices, members)]
    shifted = [
        [(start + half + i) % devices for i in range(members)]
        for start in range(0, devices, members)
    ]
    return plain, shifted


def spread(value, axis, groups=None):
    count = len(groups[0]) if groups else lax.axis_size(axis)
    copies = jnp.broadcast_to(value[None], (count, *value.shape))
    return lax.all_to_all(copies, axis, 0, 0, tiled=True, axis_index_groups=groups)


def on_device(
    tokens,
    query_weight,
    key_weight,
    value_weight,
    adapter_down_weight,
    query_up_weight,
    value_up_weight,
    head_shifts,
    output_gradient,
):
    rows = tokens.shape[0]
    heads = head_shifts.shape[0]
    width = query_weight.shape[1]
    size = width // heads
    rank = adapter_down_weight.shape[1] // 2
    devices = lax.axis_size("ctx")
    members = GROUP // rows
    scale = size ** (-0.5)
    position = lax.axis_index("ctx")
    plain, shifted = groups_of(devices, members)
    across = [[g[i] for g in plain] for i in range(members)]

    packed = jnp.concatenate(
        [query_weight, key_weight, value_weight, adapter_down_weight], axis=1
    )
    gathered = lax.all_gather(packed, "ctx", axis=0, tiled=True)
    projected = jnp.dot(tokens, gathered, preferred_element_type=f32)
    low = projected[:, width + 2 * size :].astype(bf16)
    low_q, low_v = low[:, :rank], low[:, rank:]
    query = (
        projected[:, :width] + jnp.dot(low_q, query_up_weight, preferred_element_type=f32)
    ).astype(bf16)
    keys = projected[:, width : width + size].astype(bf16)
    values = (
        projected[:, width + size : width + 2 * size]
        + jnp.dot(low_v, value_up_weight, preferred_element_type=f32)
    ).astype(bf16)
    pair = jnp.stack([keys, values])
    kv = jnp.stack([spread(pair, "ctx", plain), spread(pair, "ctx", shifted)])
    kv = kv.transpose(0, 2, 1, 3, 4).reshape(2, 2, GROUP, size)

    moved = head_shifts != 0
    key_heads = jnp.where(moved[:, None, None], kv[1, 0], kv[0, 0])
    value_heads = jnp.where(moved[:, None, None], kv[1, 1], kv[0, 1])
    place = jnp.where(moved, (position + members // 2) % members, position % members)
    row = place[:, None] * rows + jnp.arange(rows, dtype=jnp.int32)
    allowed = jnp.arange(GROUP, dtype=jnp.int32)[None, None, :] <= row[:, :, None]
    query_heads = query.reshape(rows, heads, size)
    grad_heads = output_gradient.reshape(rows, heads, size)
    scores = jnp.einsum("thd,hld->htl", query_heads, key_heads, preferred_element_type=f32)
    scores = jnp.where(allowed, scores * scale, -1e30)
    weights = jnp.exp(scores - jnp.max(scores, axis=-1, keepdims=True))
    weights = jnp.where(allowed, weights, 0.0)
    weights = weights / jnp.sum(weights, axis=-1, keepdims=True)
    weights_low = weights.astype(bf16)
    output = jnp.einsum(
        "htl,hld->thd", weights_low, value_heads, preferred_element_type=f32
    ).astype(bf16)
    grad_weights = jnp.einsum(
        "thd,hld->htl", grad_heads, value_heads, preferred_element_type=f32
    )
    correction = jnp.sum(grad_heads.astype(f32) * output.astype(f32), axis=-1).T
    grad_scores = (weights * (grad_weights - correction[..., None])).astype(bf16)
    grad_query = (
        jnp.einsum("htl,hld->thd", grad_scores, key_heads, preferred_element_type=f32) * scale
    ).astype(bf16)
    grad_query = grad_query.reshape(rows, width)
    value_parts = jnp.einsum(
        "htl,thd->hld", weights_low, grad_heads, preferred_element_type=f32
    )

    query_up_part = lax.dot_general(
        low_q, grad_query, (((0,), (0,)), ((), ())), preferred_element_type=f32
    ).astype(bf16)
    query_up_part = jnp.sum(spread(query_up_part, "ctx", across).astype(f32), axis=0).astype(bf16)
    query_up_gradient = jnp.sum(spread(query_up_part, "ctx", plain).astype(f32), axis=0)

    value_gradient = 0.0
    for groups, mine in ((plain, ~moved), (shifted, moved)):
        part = jnp.sum(jnp.where(mine[:, None, None], value_parts, 0.0), axis=0)
        part = part.astype(bf16).reshape(members, rows, size)
        arrived = lax.all_to_all(part, "ctx", 0, 0, tiled=True, axis_index_groups=groups)
        value_gradient = value_gradient + jnp.sum(arrived.astype(f32), axis=0)
    value_gradient = value_gradient.astype(bf16)

    rank_terms = jnp.concatenate(
        [
            jnp.dot(grad_query, query_up_weight.T, preferred_element_type=f32),
            jnp.dot(value_gradient, value_up_weight.T, preferred_element_type=f32),
        ],
        axis=1,
    ).astype(bf16)
    rank_grad = jnp.sum(spread(rank_terms, "fsdp").astype(f32), axis=0).astype(bf16)
    grad_down = lax.dot_general(
        rank_grad, tokens, (((0,), (0,)), ((), ())), preferred_element_type=f32
    ).astype(bf16)
    grad_down = grad_down.reshape(2 * rank, devices, -1).transpose(1, 0, 2)
    value_up_part = lax.dot_general(
        low_v, value_gradient, (((0,), (0,)), ((), ())), preferred_element_type=f32
    ).astype(bf16)
    payload = jnp.concatenate(
        [grad_down, jnp.broadcast_to(value_up_part[None], (devices, rank, size))], axis=1
    )
    payload = lax.all_to_all(payload, "ctx", 0, 0, tiled=True)
    payload = jnp.sum(payload.astype(f32), axis=0)
    return (
        output.reshape(rows, width),
        value_gradient,
        payload[: 2 * rank].T,
        query_up_gradient,
        payload[2 * rank :],
    )


def solution(mesh):
    in_specs = (
        P("ctx", None),
        P("ctx", "fsdp"),
        P("ctx", "fsdp"),
        P("ctx", "fsdp"),
        P("ctx", None),
        P(None, "fsdp"),
        P(None, "fsdp"),
        P("fsdp"),
        P("ctx", "fsdp"),
    )
    out_specs = (
        P("ctx", "fsdp"),
        P("ctx", "fsdp"),
        P("ctx", None),
        P(None, "fsdp"),
        P(None, "fsdp"),
    )
    return jax.shard_map(
        on_device, mesh=mesh, in_specs=in_specs, out_specs=out_specs, check_vma=False
    )
```

time: 820 us -> 356 us (0.43)
  blocking collectives: 406 us -> 28.2 us
  waiting for transfers between devices: 311 us -> 217 us
    psum x2 -> x0, blocking collectives: 320 us -> none  [the longest x1 275 us: on_device(): lax.psum((query_portion, value_portion), 'ctx')]
    ppermute x15 -> x0, waiting for transfers between devices: 99.8 us -> none  [from_behind(): return lax.ppermute(value, axis, pairs)]
    all_gather x1 -> x0, blocking collectives: 85.5 us -> none  [on_device(): lax.all_gather(adapter_down_weight, 'ctx', axis=0, tiled=True)]
    all_to_all x0 -> x7, waiting for transfers between devices: none -> 76.7 us  [the longest x4 41.6 us: spread(): lax.all_to_all(copies, axis, 0, 0, tiled=True, axis_index_groups=groups)]
    all_gather x3 -> x1, waiting for transfers between devices: 201 us -> 140 us  [on_device(): gathered = lax.all_gather(packed, 'ctx', axis=0, tiled=True)]
    all_to_all x0 -> x7, starting transfers between devices: none -> 42.6 us  [the longest x4 25.4 us: spread(): lax.all_to_all(copies, axis, 0, 0, tiled=True, axis_index_groups=groups)]
    ppermute x15 -> x0, starting transfers between devices: 35.3 us -> none  [from_behind(): return lax.ppermute(value, axis, pairs)]
    all_to_all x0 -> x1, blocking collectives: none -> 28.2 us  [spread(): lax.all_to_all(copies, axis, 0, 0, tiled=True, axis_index_groups=groups)]
  transfers between devices with their start and end apart: 19 -> 8, of which waited for: 19 -> 8; matrix products, arithmetic and copies ran while one was open for 2% -> 6% of each run, Pallas kernels for 0% -> 0%
where the time goes in v1:
time: 356 us; the launch traced here: 355 us
  waiting for transfers between devices  217 us (61%)
  starting transfers between devices  42.7 us (12%)
  matrix products  31.6 us (9%)
  blocking collectives  28.2 us (8%)
  between operations  14.3 us (4%)
  other arithmetic  11.4 us (3%)
  local copies, waits for them, and re-layouts  9.33 us (3%)
    all_gather x1, waiting for transfers between devices, on_device(): gathered = lax.all_gather(packed, 'ctx', axis=0, tiled=True)  140 us
    all_to_all x4, waiting for transfers between devices, spread(): lax.all_to_all(copies, axis, 0, 0, tiled=True, axis_index_groups=groups)  41.6 us
    all_to_all x1, blocking collectives, spread(): lax.all_to_all(copies, axis, 0, 0, tiled=True, axis_index_groups=groups)  28.2 us
    all_to_all x4, starting transfers between devices, spread(): lax.all_to_all(copies, axis, 0, 0, tiled=True, axis_index_groups=groups)  25.4 us
    all_to_all x1, waiting for transfers between devices, on_device(): payload = lax.all_to_all(payload, 'ctx', 0, 0, tiled=True)  21.7 us
    all_to_all x2, waiting for transfers between devices, on_device(): lax.all_to_all(part, 'ctx', 0, 0, tiled=True, axis_index_groups=groups)  13.5 us
    all_to_all x2, starting transfers between devices, on_device(): lax.all_to_all(part, 'ctx', 0, 0, tiled=True, axis_index_groups=groups)  12.1 us
    dot_general x1, matrix products, on_device(): projected = jnp.dot(tokens, gathered, preferred_element_type=f32)  10.4 us
  transfers between devices with their start and end apart: 8, of which 8 were waited for; matrix products, arithmetic and copies ran while one was open for 6% of the time, Pallas kernels for 0%

profile of v1, /device:TPU:1, one launch (start us, length us, event | category | flops | bytes accessed | tf_op | source)
XLA Modules:
  0.0 354.5 jit_solution(10953744883600425402)
XLA Ops:
  8.0 1.7 pad_maximum_fusion.2
  9.7 140.3 %all-gather.2.cloned.1.call-done = bf16[8192,800]{1,0:T(8,128)(2,1)} async-done(((bf16[128,800]{1,0:T(8,128)(2,1)}), bf16[8192,800]{1,0:T(8,128)(2,1)}) %all-gather.2.cloned.1.call-update) | async-done | bytes 13107216 | tf_op jit(solution)/shard_map/all_gather | solution.py:53
  150.0 10.4 %fusion.50 = (bf16[256,800]{0,1:T(8,128)(2,1)S(1)}, f32[256,800]{0,1:T(8,128)S(1)}) fusion(bf16[8192,800]{1,0:T(8,128)(2,1)} %all-gather.2.cloned.1.call-done, bf16[256,8192]{1,0:T(8,128)(2,1)} %param.9), kind=kOutput, calls=%fused_computation.78 | convolution fusion | flops 3355648000 | bytes 18530304 | tf_op jit(solution)/shard_map/dot_general | solution.py:54
  162.0 28.2 %all_to_all.40 = bf16[8,2,256,128]{3,2,1,0:T(8,128)(2,1)S(1)} all-to-all(bf16[8,2,256,128]{3,2,1,0:T(8,128)(2,1)} %broadcast_in_dim.102), channel_id=1, replica_groups={{32,40,48,56,64,72,80,88},{96,104,112,120,128,136,144,152},{160,168,176..., dimensions={0} | all-to-all | bytes 2097152 | tf_op jit(solution)/shard_map/all_to_all | solution.py:24
  190.2 5.8 %all-to-all-start = ((bf16[8,2,256,128]{3,2,1,0:T(8,128)(2,1)}), bf16[8,2,256,128]{3,2,1,0:T(8,128)(2,1)S(1)}, u32[]{:S(2)}, u32[]{:S(2)}) async-start(bf16[8,2,256,128]{3,2,1,0:T(8,128)(2,1)} %broadcast_in_dim.102), calls=%async_computation | async-start | bytes 2097152 | tf_op jit(solution)/shard_map/all_to_all | solution.py:24
  198.0 23.7 %all-to-all-done = bf16[8,2,256,128]{3,2,1,0:T(8,128)(2,1)S(1)} async-done(((bf16[8,2,256,128]{3,2,1,0:T(8,128)(2,1)}), bf16[8,2,256,128]{3,2,1,0:T(8,128)(2,1)S(1)}, u32[]{:S(2)}, u32[]{:S(2)}) %all-to-all-start) | async-done | bytes 1048608 | tf_op jit(solution)/shard_map/all_to_all | solution.py:24
  223.5 6.1 %fusion.51 = (f32[4,256]{1,0:T(4,128)S(1)}, f32[4,256,2048]{2,1,0:T(8,128)S(1)}) fusion(f32[4,256,2048]{2,1,0:T(8,128)S(1)} %fusion.9, s32[4,256]{1,0:T(4,128)S(1)} %iota_add_fusion), kind=kOutput, calls=%fused_computation.79 | output fusion | flops 18876416 | bytes 16785408 | tf_op jit(solution)/shard_map/sub | solution.py:79
  231.1 1.8 copy-done.1
  232.9 3.3 select_reduce_fusion
  236.1 6.8 %all-to-all-start.3 = ((bf16[8,256,128]{2,1,0:T(8,128)(2,1)}), bf16[8,256,128]{2,1,0:T(8,128)(2,1)S(1)}, u32[]{:S(2)}, u32[]{:S(2)}) async-start(bf16[8,256,128]{2,1,0:T(8,128)(2,1)} %bitcast.17), calls=%async_computation.3 | async-start | bytes 1048576 | tf_op jit(solution)/shard_map/all_to_all | solution.py:109
  243.0 3.8 %multiply_reduce_fusion = (f32[256,4]{0,1:T(4,128)S(1)}, bf16[4,128,256]{2,1,0:T(8,128)(2,1)S(1)}) fusion(bf16[256,512]{0,1:T(8,128)(2,1)S(1)} %copy-done.6, bf16[4,256,2048]{2,1,0:T(8,128)(2,1)} %copy-done.2, pred[4]{0:T(512)(128)(4,1)S(1)} %get-tuple-element.37, bf16[2048,128]{1,0:T(8,128)(2,1)S(1)} %get-tuple-element.35, ...), kind=kOutput, calls=%fused_computation.60 | convolution fusion | flops 538573824 | bytes 5771268 | tf_op jit(solution)/shard_map/htl,hld->thd/dot_general | solution.py:83
  246.7 6.9 %all-to-all-done.3 = bf16[8,256,128]{2,1,0:T(8,128)(2,1)S(1)} async-done(((bf16[8,256,128]{2,1,0:T(8,128)(2,1)}), bf16[8,256,128]{2,1,0:T(8,128)(2,1)S(1)}, u32[]{:S(2)}, u32[]{:S(2)}) %all-to-all-start.3) | async-done | bytes 524320 | tf_op jit(solution)/shard_map/all_to_all | solution.py:109
  253.6 5.3 %all-to-all-start.2 = ((bf16[8,256,128]{2,1,0:T(8,128)(2,1)}), bf16[8,256,128]{2,1,0:T(8,128)(2,1)S(1)}, u32[]{:S(2)}, u32[]{:S(2)}) async-start(bf16[8,256,128]{2,1,0:T(8,128)(2,1)} %bitcast.16), calls=%async_computation.2 | async-start | bytes 1048576 | tf_op jit(solution)/shard_map/all_to_all | solution.py:109
  258.9 6.8 %fusion.22 = bf16[4,128,256]{2,1,0:T(8,128)(2,1)S(1)} fusion(pred[4]{0:T(512)(128)(4,1)S(1)} %get-tuple-element.37, bf16[256,4,128]{0,2,1:T(8,128)(2,1)S(1)} %bitcast.78, f32[4,256]{1,0:T(4,128)S(1)} %bitcast.79, f32[4,256,2048]{2,1,0:T(8,128)} %copy-done.1, f32[4,256]{1,0:T(4,128)S(1)} %get-tuple-element.40, bf16[2048,128]{1,0:T(8,128)(2,1)S(1)} %get-tuple-element.33, ...), kind=kOutput, calls=%fused_computation.32 | convolution fusion | flops 1084489728 | bytes 11018244 | tf_op jit(solution)/shard_map/htl,hld->thd/dot_general | solution.py:92
  266.8 6.6 %all-to-all-done.2 = bf16[8,256,128]{2,1,0:T(8,128)(2,1)S(1)} async-done(((bf16[8,256,128]{2,1,0:T(8,128)(2,1)}), bf16[8,256,128]{2,1,0:T(8,128)(2,1)S(1)}, u32[]{:S(2)}, u32[]{:S(2)}) %all-to-all-start.2) | async-done | bytes 524320 | tf_op jit(solution)/shard_map/all_to_all | solution.py:109
  274.1 4.5 %all-to-all-start.6 = ((bf16[8,16,512]{2,1,0:T(8,128)(2,1)}), bf16[8,16,512]{2,1,0:T(8,128)(2,1)S(1)}, u32[]{:S(2)}, u32[]{:S(2)}) async-start(bf16[8,16,512]{2,1,0:T(8,128)(2,1)} %broadcast_in_dim.115), calls=%async_computation.6 | async-start | bytes 262144 | tf_op jit(solution)/shard_map/all_to_all | solution.py:24
  278.9 7.6 %all-to-all-done.6 = bf16[8,16,512]{2,1,0:T(8,128)(2,1)S(1)} async-done(((bf16[8,16,512]{2,1,0:T(8,128)(2,1)}), bf16[8,16,512]{2,1,0:T(8,128)(2,1)S(1)}, u32[]{:S(2)}, u32[]{:S(2)}) %all-to-all-start.6) | async-done | bytes 131104 | tf_op jit(solution)/shard_map/all_to_all | solution.py:24
  287.2 8.0 %all-to-all-start.4 = ((bf16[8,256,32]{1,2,0:T(8,128)(2,1)}), bf16[8,256,32]{1,2,0:T(8,128)(2,1)S(1)}, u32[]{:S(2)}, u32[]{:S(2)}) async-start(bf16[8,256,32]{1,2,0:T(8,128)(2,1)} %broadcast_in_dim.113), calls=%async_computation.4 | async-start | bytes 262144 | tf_op jit(solution)/shard_map/all_to_all | solution.py:24
  296.0 8.5 %all-to-all-done.4 = bf16[8,256,32]{1,2,0:T(8,128)(2,1)S(1)} async-done(((bf16[8,256,32]{1,2,0:T(8,128)(2,1)}), bf16[8,256,32]{1,2,0:T(8,128)(2,1)S(1)}, u32[]{:S(2)}, u32[]{:S(2)}) %all-to-all-start.4) | async-done | bytes 131104 | tf_op jit(solution)/shard_map/all_to_all | solution.py:24
  305.2 7.1 %all-to-all-start.7 = ((bf16[8,16,512]{2,1,0:T(8,128)(2,1)}), bf16[8,16,512]{2,1,0:T(8,128)(2,1)S(1)}, u32[]{:S(2)}, u32[]{:S(2)}) async-start(bf16[8,16,512]{2,1,0:T(8,128)(2,1)} %broadcast_in_dim.116), calls=%async_computation.7 | async-start | bytes 262144 | tf_op jit(solution)/shard_map/all_to_all | solution.py:24
  312.3 3.0 fusion.18
  316.4 1.7 all-to-all-done.7
  318.1 5.1 %all-to-all-start.5 = ((bf16[64,48,128]{2,1,0:T(8,128)(2,1)}), bf16[64,48,128]{2,1,0:T(8,128)(2,1)S(1)}, u32[]{:S(2)}, u32[]{:S(2)}) async-start(bf16[64,48,128]{2,1,0:T(8,128)(2,1)} %pad_maximum_fusion.1), calls=%async_computation.5 | async-start | bytes 1572864 | tf_op jit(solution)/shard_map/all_to_all | solution.py:131
  324.7 21.7 %all-to-all-done.5 = bf16[64,48,128]{2,1,0:T(8,128)(2,1)S(1)} async-done(((bf16[64,48,128]{2,1,0:T(8,128)(2,1)}), bf16[64,48,128]{2,1,0:T(8,128)(2,1)S(1)}, u32[]{:S(2)}, u32[]{:S(2)}) %all-to-all-start.5) | async-done | bytes 786464 | tf_op jit(solution)/shard_map/all_to_all | solution.py:131
  (59 shorter events, 15.6 us)
Async XLA Ops:
  7.2 189.8 %copy-start = (bf16[16,512]{1,0:T(8,128)(2,1)S(1)}, bf16[16,512]{1,0:T(8,128)(2,1)}, u32[]{:S(2)}) copy-start(bf16[16,512]{1,0:T(8,128)(2,1)} %param.14) | copy-start | bytes 49156
  7.2 142.8 %all-gather.2.cloned.1.call-start = ((), (), s32[]{:S(2)}) async-start(), calls=%async_computation.8 | async-start | bytes 14909440 | tf_op jit(solution)/shard_map/all_gather | solution.py:53
  9.7 150.7 %copy-start.8 = (bf16[16,128]{1,0:T(8,128)(2,1)S(1)}, bf16[16,128]{1,0:T(8,128)(2,1)}, u32[]{:S(2)}) copy-start(bf16[16,128]{1,0:T(8,128)(2,1)} %param.15) | copy-start | bytes 12292
  160.4 29.8 %copy-start.7 = (bf16[256,800]{0,1:T(8,128)(2,1)}, bf16[256,800]{0,1:T(8,128)(2,1)S(1)}, u32[]{:S(2)}) copy-start(bf16[256,800]{0,1:T(8,128)(2,1)S(1)} %get-tuple-element.38) | copy-start | bytes 1228804
  160.4 35.6 %copy-start.5 = (bf16[256,512]{1,0:T(8,128)(2,1)S(1)}, bf16[256,512]{1,0:T(8,128)(2,1)}, u32[]{:S(2)}) copy-start(bf16[256,512]{1,0:T(8,128)(2,1)} %param.17) | copy-start | bytes 786436
  160.4 36.4 %copy-start.9 = (s32[4]{0:T(128)S(1)}, s32[4]{0:T(128)}, u32[]{:S(2)}) copy-start(s32[4]{0:T(128)} %param.16) | copy-start | bytes 52
  190.2 31.5 %all-to-all-start = ((bf16[8,2,256,128]{3,2,1,0:T(8,128)(2,1)}), bf16[8,2,256,128]{3,2,1,0:T(8,128)(2,1)S(1)}, u32[]{:S(2)}, u32[]{:S(2)}) async-start(bf16[8,2,256,128]{3,2,1,0:T(8,128)(2,1)} %broadcast_in_dim.102), calls=%async_computation | async-start | bytes 2097152 | tf_op jit(solution)/shard_map/all_to_all | solution.py:24
  222.2 20.8 %copy-start.4 = (bf16[2048,128]{1,0:T(8,128)(2,1)}, bf16[2048,128]{1,0:T(8,128)(2,1)S(1)}, u32[]{:S(2)}) copy-start(bf16[2048,128]{1,0:T(8,128)(2,1)S(1)} %get-tuple-element.35) | copy-start | bytes 1572868
  229.7 3.2 copy-start.1
  229.7 3.2 copy-start.6
  232.9 3.3 copy-start.2
  236.1 17.5 %all-to-all-start.3 = ((bf16[8,256,128]{2,1,0:T(8,128)(2,1)}), bf16[8,256,128]{2,1,0:T(8,128)(2,1)S(1)}, u32[]{:S(2)}, u32[]{:S(2)}) async-start(bf16[8,256,128]{2,1,0:T(8,128)(2,1)} %bitcast.17), calls=%async_computation.3 | async-start | bytes 1048576 | tf_op jit(solution)/shard_map/all_to_all | solution.py:109
  253.6 19.8 %all-to-all-start.2 = ((bf16[8,256,128]{2,1,0:T(8,128)(2,1)}), bf16[8,256,128]{2,1,0:T(8,128)(2,1)S(1)}, u32[]{:S(2)}, u32[]{:S(2)}) async-start(bf16[8,256,128]{2,1,0:T(8,128)(2,1)} %bitcast.16), calls=%async_computation.2 | async-start | bytes 1048576 | tf_op jit(solution)/shard_map/all_to_all | solution.py:109
  274.1 12.4 %all-to-all-start.6 = ((bf16[8,16,512]{2,1,0:T(8,128)(2,1)}), bf16[8,16,512]{2,1,0:T(8,128)(2,1)S(1)}, u32[]{:S(2)}, u32[]{:S(2)}) async-start(bf16[8,16,512]{2,1,0:T(8,128)(2,1)} %broadcast_in_dim.115), calls=%async_computation.6 | async-start | bytes 262144 | tf_op jit(solution)/shard_map/all_to_all | solution.py:24
  278.8 37.7 %copy-start.3 = (bf16[256,128]{1,0:T(8,128)(2,1)}, bf16[256,128]{1,0:T(8,128)(2,1)S(1)}, u32[]{:S(2)}) copy-start(bf16[256,128]{1,0:T(8,128)(2,1)S(1)} %add_convert_fusion) | copy-start | bytes 196612
  287.2 17.4 %all-to-all-start.4 = ((bf16[8,256,32]{1,2,0:T(8,128)(2,1)}), bf16[8,256,32]{1,2,0:T(8,128)(2,1)S(1)}, u32[]{:S(2)}, u32[]{:S(2)}) async-start(bf16[8,256,32]{1,2,0:T(8,128)(2,1)} %broadcast_in_dim.113), calls=%async_computation.4 | async-start | bytes 262144 | tf_op jit(solution)/shard_map/all_to_all | solution.py:24
  305.2 12.9 %all-to-all-start.7 = ((bf16[8,16,512]{2,1,0:T(8,128)(2,1)}), bf16[8,16,512]{2,1,0:T(8,128)(2,1)S(1)}, u32[]{:S(2)}, u32[]{:S(2)}) async-start(bf16[8,16,512]{2,1,0:T(8,128)(2,1)} %broadcast_in_dim.116), calls=%async_computation.7 | async-start | bytes 262144 | tf_op jit(solution)/shard_map/all_to_all | solution.py:24
  318.1 28.2 %all-to-all-start.5 = ((bf16[64,48,128]{2,1,0:T(8,128)(2,1)}), bf16[64,48,128]{2,1,0:T(8,128)(2,1)S(1)}, u32[]{:S(2)}, u32[]{:S(2)}) async-start(bf16[64,48,128]{2,1,0:T(8,128)(2,1)} %pad_maximum_fusion.1), calls=%async_computation.5 | async-start | bytes 1572864 | tf_op jit(solution)/shard_map/all_to_all | solution.py:131
Sparse Core Ops, SparseCore 0:
  10.7 139.2 all-gather.1

commit v2 on v1

v2 whole, which is shorter than its diff:
```python
import functools

import jax
import jax.numpy as jnp
from jax import lax
from jax.experimental import pallas as pl
from jax.experimental.pallas import tpu as pltpu
from jax.sharding import PartitionSpec as P

GROUP = 2048
bf16 = jnp.bfloat16
f32 = jnp.float32
NT = (((1,), (1,)), ((), ()))
TN = (((0,), (0,)), ((), ()))


def spread(value, axis, groups=None):
    count = len(groups[0]) if groups else lax.axis_size(axis)
    copies = jnp.broadcast_to(value[None], (count, *value.shape))
    return lax.all_to_all(copies, axis, 0, 0, tiled=True, axis_index_groups=groups)


def to_chip(value, chips, other_core):
    count = lax.axis_size("ctx")
    pairs = []
    for source in range(count):
        core = source % 2
        target = (source - core + 2 * chips) % count + (1 - core if other_core else core)
        pairs.append((source, target))
    return lax.ppermute(value, "ctx", pairs)


def attention_kernel(
    scale, tile, info, query, grad_out, kv, out, grad_query, grad_value, probs, acc, stat
):
    rows, size = query.shape[0], kv.shape[-1]
    heads = query.shape[1] // size
    block = kv.shape[2]
    key_slot = info[heads]
    value_slot = 1 - key_slot
    lanes = 128
    grad_value[...] = jnp.zeros_like(grad_value)

    def fold(values, op):
        total = values[:, :lanes]
        for start in range(lanes, values.shape[1], lanes):
            total = op(total, values[:, start : start + lanes])
        return total

    for head in range(heads):
        columns = slice(head * size, (head + 1) * size)
        seen = info[head] + 1

        def one_tile(index, carry, columns=columns, seen=seen):
            here = pl.ds(pl.multiple_of(index * tile, tile), tile)
            q = query[here, columns]
            do = grad_out[here, columns]

            def score(d):
                return lax.dot_general(
                    q, kv[key_slot, d], NT, preferred_element_type=f32
                ) * scale

            row = index * tile + lax.broadcasted_iota(jnp.int32, (tile, block), 0)
            column = lax.broadcasted_iota(jnp.int32, (tile, block), 1)
            own = jnp.where(column <= row, score(0), -1e30)
            probs[0] = own
            stat[...] = fold(own, jnp.maximum)

            def first(d, carry):
                s = score(d)
                probs[d] = s
                stat[...] = jnp.maximum(stat[...], fold(s, jnp.maximum))
                return carry

            lax.fori_loop(1, seen, first, 0)
            highest = jnp.max(stat[...], axis=1, keepdims=True)
            stat[...] = jnp.zeros_like(stat)

            def second(d, carry):
                e = jnp.exp(probs[d] - highest)
                probs[d] = e
                stat[...] += fold(e, jnp.add)
                return carry

            lax.fori_loop(0, seen, second, 0)
            inverse = 1.0 / jnp.sum(stat[...], axis=1, keepdims=True)
            acc[...] = jnp.zeros_like(acc)

            def third(d, carry):
                p = probs[d] * inverse
                probs[d] = p
                low = p.astype(bf16)
                acc[...] += jnp.dot(low, kv[value_slot, d], preferred_element_type=f32)
                grad_value[d] += lax.dot_general(low, do, TN, preferred_element_type=f32)
                return carry

            lax.fori_loop(0, seen, third, 0)
            result = acc[...].astype(bf16)
            out[here, columns] = result
            correction = jnp.sum(do.astype(f32) * result.astype(f32), axis=1, keepdims=True)
            acc[...] = jnp.zeros_like(acc)

            def fourth(d, carry):
                dp = lax.dot_general(do, kv[value_slot, d], NT, preferred_element_type=f32)
                ds = (probs[d] * (dp - correction)).astype(bf16)
                acc[...] += jnp.dot(ds, kv[key_slot, d], preferred_element_type=f32)
                return carry

            lax.fori_loop(0, seen, fourth, 0)
            grad_query[here, columns] = (acc[...] * scale).astype(bf16)
            return carry

        lax.fori_loop(0, rows // tile, one_tile, 0)


def attend(info, query, grad_out, kv, tile=256):
    rows, width = query.shape
    size = kv.shape[-1]
    blocks, block = kv.shape[1:3]
    vmem = pl.BlockSpec(memory_space=pltpu.VMEM)
    return pl.pallas_call(
        functools.partial(attention_kernel, size ** (-0.5), tile),
        out_shape=(
            jax.ShapeDtypeStruct((rows, width), bf16),
            jax.ShapeDtypeStruct((rows, width), bf16),
            jax.ShapeDtypeStruct((blocks, block, size), f32),
        ),
        in_specs=[pl.BlockSpec(memory_space=pltpu.SMEM), vmem, vmem, vmem],
        out_specs=(vmem, vmem, vmem),
        scratch_shapes=[
            pltpu.VMEM((blocks, tile, block), f32),
            pltpu.VMEM((tile, size), f32),
            pltpu.VMEM((tile, 128), f32),
        ],
        compiler_params=pltpu.CompilerParams(vmem_limit_bytes=40 * 1024 * 1024),
        cost_estimate=pl.CostEstimate(
            flops=10 * rows * width * blocks * block,
            bytes_accessed=4 * 1024 * 1024,
            transcendentals=rows * width // size * blocks * block,
        ),
        name="attention",
    )(info, query, grad_out, kv)


def on_device(
    tokens,
    query_weight,
    key_weight,
    value_weight,
    adapter_down_weight,
    query_up_weight,
    value_up_weight,
    head_shifts,
    output_gradient,
):
    rows, model = tokens.shape
    heads = head_shifts.shape[0]
    width = query_weight.shape[1]
    size = width // heads
    half = width // 2
    depth = query_weight.shape[0]
    rank = adapter_down_weight.shape[1] // 2
    devices = lax.axis_size("ctx")
    chips = GROUP // (2 * rows)
    members = 2 * chips
    position = lax.axis_index("ctx")
    core = position % 2
    chip = position // 2 % chips
    plain = [[start + i for i in range(members)] for start in range(0, devices, members)]
    across = [[g[i] for g in plain] for i in range(members)]
    planes = devices // members

    def both(mine, theirs):
        return jnp.concatenate(
            [jnp.where(core == 0, mine, theirs), jnp.where(core == 0, theirs, mine)], axis=0
        )

    def half_of(array, which):
        return lax.dynamic_slice_in_dim(array, which * (array.shape[0] // 2), array.shape[0] // 2)

    down = adapter_down_weight.T
    kv_rows = jnp.stack(
        [jnp.concatenate([key_weight, down]), jnp.concatenate([value_weight, down])]
    )
    kv_rows = jnp.broadcast_to(kv_rows[None], (chips, *kv_rows.shape))
    kv_rows = lax.all_to_all(
        kv_rows.reshape(members, depth + 2 * rank, size),
        "ctx", 0, 0, tiled=True, axis_index_groups=plain,
    )
    kv_rows = lax.all_gather(kv_rows, "ctx", axis=0, tiled=True, axis_index_groups=across)
    q_rows = jnp.stack([query_weight[:, :half], query_weight[:, half:]])
    q_rows = jnp.broadcast_to(q_rows[None], (chips, *q_rows.shape))
    q_rows = lax.all_to_all(
        q_rows.reshape(members, depth, half),
        "ctx", 0, 0, tiled=True, axis_index_groups=plain,
    )
    q_rows = lax.all_gather(
        q_rows.reshape(members * depth, half),
        "ctx", axis=0, tiled=True, axis_index_groups=across,
    )

    chip_tokens = both(tokens, to_chip(tokens, 0, True))
    grad_halves = output_gradient.reshape(rows, 2, half).transpose(1, 0, 2)
    grad_mine = lax.dynamic_index_in_dim(grad_halves, core, 0, keepdims=False)
    grad_away = lax.dynamic_index_in_dim(grad_halves, 1 - core, 0, keepdims=False)
    grad_out = both(grad_mine, to_chip(grad_away, 0, True))

    low_weight = kv_rows[:, depth:].transpose(1, 0, 2).reshape(2 * rank, model)
    low = lax.dot_general(chip_tokens, low_weight, NT, preferred_element_type=f32).astype(bf16)
    low_q, low_v = low[:, :rank], low[:, rank:]
    mine = jnp.dot(
        chip_tokens, kv_rows[:, :depth].reshape(model, size), preferred_element_type=f32
    )
    extra = jnp.dot(low_v, value_up_weight, preferred_element_type=f32)
    mine = (mine + jnp.where(core == 1, extra, 0.0)).astype(bf16)
    kv = jnp.stack(
        [
            jnp.stack([mine] + [to_chip(mine, d, False) for d in range(1, chips)]),
            jnp.stack([to_chip(mine, d, True) for d in range(chips)]),
        ]
    )

    up_mine = lax.dynamic_slice_in_dim(query_up_weight, core * half, half, axis=1)
    query = (
        jnp.dot(chip_tokens, q_rows, preferred_element_type=f32)
        + jnp.dot(low_q, up_mine, preferred_element_type=f32)
    ).astype(bf16)

    shifts = lax.dynamic_slice_in_dim(head_shifts, core * (heads // 2), heads // 2)
    seen = jnp.where(shifts != 0, (chip + chips // 2) % chips, chip)
    info = jnp.concatenate([seen, core[None]]).astype(jnp.int32)
    output, grad_query, value_parts = attend(info, query, grad_out, kv)

    attention_mine = half_of(output, core)
    attention_other = to_chip(half_of(output, 1 - core), 0, True)
    attention = jnp.concatenate(
        [
            jnp.where(core == 0, attention_mine, attention_other),
            jnp.where(core == 0, attention_other, attention_mine),
        ],
        axis=1,
    )

    value_parts = value_parts.reshape(chips, 2, rows, size).astype(bf16)
    same = lax.dynamic_index_in_dim(value_parts, core, 1, keepdims=False)
    cross = lax.dynamic_index_in_dim(value_parts, 1 - core, 1, keepdims=False)
    arrived = [same[0]]
    arrived += [to_chip(cross[d], -d, True) for d in range(chips)]
    arrived += [to_chip(same[d], -d, False) for d in range(1, chips)]
    value_gradient = functools.reduce(jnp.add, [a.astype(f32) for a in arrived]).astype(bf16)

    query_up_part = lax.dot_general(low_q, grad_query, TN, preferred_element_type=f32)
    query_up_part = query_up_part.astype(bf16).reshape(planes, rank // planes, half)
    query_up_part = lax.all_to_all(
        query_up_part, "ctx", 0, 0, tiled=True, axis_index_groups=across
    )
    query_up_part = jnp.sum(
        query_up_part.reshape(planes, rank // planes, half).astype(f32), axis=0
    ).astype(bf16)

    rank_q = lax.dot_general(grad_query, up_mine, NT, preferred_element_type=f32)
    rank_q = half_of(rank_q, core) + to_chip(half_of(rank_q, 1 - core), 0, True)
    rank_v = lax.dot_general(value_gradient, value_up_weight, NT, preferred_element_type=f32)
    rank_terms = jnp.concatenate([rank_q, rank_v], axis=1).astype(bf16)
    rank_grad = jnp.sum(spread(rank_terms, "fsdp").astype(f32), axis=0).astype(bf16)
    grad_down = lax.dot_general(rank_grad, tokens, TN, preferred_element_type=f32)
    grad_down = grad_down.astype(bf16).reshape(2 * rank, devices, depth).transpose(1, 0, 2)
    value_up_part = lax.dot_general(
        half_of(low_v, core), value_gradient, TN, preferred_element_type=f32
    ).astype(bf16)
    shared = jnp.concatenate(
        [value_up_part, query_up_part.reshape(-1, size)], axis=0
    )
    payload = jnp.concatenate(
        [grad_down, jnp.broadcast_to(shared[None], (devices, *shared.shape))], axis=1
    )
    payload = lax.all_to_all(payload, "ctx", 0, 0, tiled=True)
    summed = jnp.sum(payload[:, : 3 * rank].astype(f32), axis=0)
    query_up = payload[:, 3 * rank :].astype(f32)
    query_up = query_up.reshape(planes, chips, 2, rank // planes, half).sum(axis=1)
    query_up_gradient = query_up.transpose(0, 2, 1, 3).reshape(rank, width)
    return (
        attention,
        value_gradient,
        summed[: 2 * rank].T,
        query_up_gradient,
        summed[2 * rank :],
    )


def solution(mesh):
    in_specs = (
        P("ctx", None),
        P("ctx", "fsdp"),
        P("ctx", "fsdp"),
        P("ctx", "fsdp"),
        P("ctx", None),
        P(None, "fsdp"),
        P(None, "fsdp"),
        P("fsdp"),
        P("ctx", "fsdp"),
    )
    out_specs = (
        P("ctx", "fsdp"),
        P("ctx", "fsdp"),
        P("ctx", None),
        P(None, "fsdp"),
        P(None, "fsdp"),
    )
    return jax.shard_map(
        on_device, mesh=mesh, in_specs=in_specs, out_specs=out_specs, check_vma=False
    )
```

time: 356 us -> 273 us (0.77)
  waiting for transfers between devices: 217 us -> 71.8 us
  starting transfers between devices: 42.7 us -> 102 us
  matrix products: 31.6 us -> 18.5 us
  Pallas kernels: 0 us -> 10.1 us
  blocking collectives: 28.2 us -> 38 us
    all_gather x1 -> x2, waiting for transfers between devices: 140 us -> 26.7 us  [the longest x1 14.5 us: on_device(): lax.all_gather(q_rows.reshape(members * depth, half), 'ctx', axis=0, tile...]
    ppermute x0 -> x18, starting transfers between devices: none -> 79.7 us  [to_chip(): return lax.ppermute(value, 'ctx', pairs)]
    all_to_all x4 -> x1, waiting for transfers between devices: 41.6 us -> 9.2 us  [spread(): lax.all_to_all(copies, axis, 0, 0, tiled=True, axis_index_groups=groups)]
    all_to_all x4 -> x1, starting transfers between devices: 25.4 us -> 10.1 us  [spread(): lax.all_to_all(copies, axis, 0, 0, tiled=True, axis_index_groups=groups)]
    ppermute x0 -> x18, waiting for transfers between devices: none -> 14.2 us  [to_chip(): return lax.ppermute(value, 'ctx', pairs)]
    all_to_all x2 -> x1, waiting for transfers between devices: 13.5 us -> 0.1 us  [on_device(): lax.all_to_all(query_up_part, 'ctx', 0, 0, tiled=True, axis_index_groups=...]
    dot_general x12 -> x10, matrix products: 31.6 us -> 18.5 us  [the longest x1 6.99 us: on_device(): jnp.dot(chip_tokens, q_rows, preferred_element_type=f32)]
    pallas_call x0 -> x1, Pallas kernels: none -> 10.1 us  [attend(): pl.pallas_call(functools.partial(attention_kernel, size ** (-0.5), tile),...]
  transfers between devices with their start and end apart: 8 -> 23, of which waited for: 8 -> 11; matrix products, arithmetic and copies ran while one was open for 6% -> 7% of each run, Pallas kernels for 0% -> 0%
where the time goes in v2:
time: 273 us; the launch traced here: 272 us
  starting transfers between devices  102 us (37%)
  waiting for transfers between devices  71.8 us (26%)
  blocking collectives  38 us (14%)
  matrix products  18.5 us (7%)
  between operations  14.7 us (5%)
  Pallas kernels  10.1 us (4%)
  other arithmetic  9.46 us (3%)
  local copies, waits for them, and re-layouts  7.33 us (3%)
    ppermute x18, starting transfers between devices, to_chip(): return lax.ppermute(value, 'ctx', pairs)  79.7 us
    all_to_all x1, waiting for transfers between devices, on_device(): payload = lax.all_to_all(payload, 'ctx', 0, 0, tiled=True)  21.5 us
    all_to_all x1, blocking collectives, on_device(): lax.all_to_all(kv_rows.reshape(members, depth + 2 * rank, size), 'ctx', 0...  20.3 us
    all_to_all x1, blocking collectives, on_device(): lax.all_to_all(q_rows.reshape(members, depth, half), 'ctx', 0, 0, tiled=T...  17.7 us
    all_gather x1, waiting for transfers between devices, on_device(): lax.all_gather(q_rows.reshape(members * depth, half), 'ctx', axis=0, tile...  14.5 us
    ppermute x18, waiting for transfers between devices, to_chip(): return lax.ppermute(value, 'ctx', pairs)  14.2 us
    all_gather x1, waiting for transfers between devices, on_device(): lax.all_gather(kv_rows, 'ctx', axis=0, tiled=True, axis_index_groups=across)  12.2 us
    pallas_call x1, Pallas kernels, attend(): pl.pallas_call(functools.partial(attention_kernel, size ** (-0.5), tile),...  10.1 us
  transfers between devices with their start and end apart: 23, of which 11 were waited for; matrix products, arithmetic and copies ran while one was open for 7% of the time, Pallas kernels for 0%

profile of v2, /device:TPU:1, one launch (start us, length us, event | category | flops | bytes accessed | tf_op | source)
XLA Modules:
  0.0 271.9 jit_solution(7623877793846583358)
XLA Ops:
  8.1 20.3 %all_to_all.25 = bf16[8,160,128]{2,1,0:T(8,128)(2,1)} all-to-all(bf16[8,160,128]{2,1,0:T(8,128)(2,1)S(1)} %bitcast.93), channel_id=1, replica_groups={{0,8,16,24,32,40,48,56},{64,72,80,88,96,104,112,120},{128,136,144,152,1..., dimensions={0} | all-to-all | bytes 655360 | tf_op jit(solution)/shard_map/all_to_all | solution.py:187
  32.2 17.7 %all_to_all.26 = bf16[8,128,256]{2,1,0:T(8,128)(2,1)} all-to-all(bf16[8,128,256]{2,1,0:T(8,128)(2,1)S(1)} %bitcast.90), channel_id=1, replica_groups={{0,8,16,24,32,40,48,56},{64,72,80,88,96,104,112,120},{128,136,144,152,1..., dimensions={0} | all-to-all | bytes 1048576 | tf_op jit(solution)/shard_map/all_to_all | solution.py:194
  53.5 5.9 %broadcast_select_fusion.1 = (bf16[256,8192]{1,0:T(8,128)(2,1)}, bf16[256,8192]{1,0:T(8,128)(2,1)}) fusion(bf16[256,8192]{1,0:T(8,128)(2,1)} %param.9, bf16[256,8192]{1,0:T(8,128)(2,1)} %collective-permute-done, pred[]{:T(512)S(6)} %eq.8), kind=kLoop, calls=%fused_computation.3 | loop fusion | flops 4194304 | bytes 16777216 | tf_op jit(solution)/shard_map/jit(_where)/select_n | solution.py:176
  59.4 12.2 %all-gather.5.cloned.1.call-done = bf16[64,160,128]{2,1,0:T(8,128)(2,1)} async-done(((bf16[8,160,128]{2,1,0:T(8,128)(2,1)}), bf16[64,160,128]{2,1,0:T(8,128)(2,1)}) %all-gather.5.cloned.1.call-update) | async-done | bytes 2621456 | tf_op jit(solution)/shard_map/all_gather | solution.py:191
  73.8 5.1 %fusion.8 = bf16[512,32]{0,1:T(8,128)(2,1)S(1)} fusion(bf16[256,8192]{1,0:T(8,128)(2,1)} %get-tuple-element.12, bf16[256,8192]{1,0:T(8,128)(2,1)S(1)} %copy-done.1, bf16[64,160,128]{2,1,0:T(8,128)(2,1)} %all-gather.5.cloned.1.call-done), kind=kOutput, calls=%fused_computation.14 | convolution fusion | flops 285229056 | bytes 8945664 | tf_op jit(solution)/shard_map/dot_general | solution.py:210
  81.5 3.4 %collective-permute-start.2 = (bf16[512,128]{1,0:T(8,128)(2,1)S(1)}, bf16[512,128]{1,0:T(8,128)(2,1)S(1)}, u32[]{:S(2)}, u32[]{:S(2)}) collective-permute-start(bf16[512,128]{1,0:T(8,128)(2,1)S(1)} %fusion.7), channel_id=1, source_target_pairs={{0,16},{8,24},{16,32},{24,40},{32,48},{40,56},{48,64},{56,72},{64,... | collective-permute-start | bytes 393224 | tf_op jit(solution)/shard_map/ppermute | solution.py:30
  84.9 3.9 %collective-permute-start.3 = (bf16[512,128]{1,0:T(8,128)(2,1)S(1)}, bf16[512,128]{1,0:T(8,128)(2,1)S(1)}, u32[]{:S(2)}, u32[]{:S(2)}) collective-permute-start(bf16[512,128]{1,0:T(8,128)(2,1)S(1)} %fusion.7), channel_id=1, source_target_pairs={{0,32},{8,40},{16,48},{24,56},{32,64},{40,72},{48,80},{56,88},{64,... | collective-permute-start | bytes 393224 | tf_op jit(solution)/shard_map/ppermute | solution.py:30
  88.9 3.9 %collective-permute-start.4 = (bf16[512,128]{1,0:T(8,128)(2,1)S(1)}, bf16[512,128]{1,0:T(8,128)(2,1)S(1)}, u32[]{:S(2)}, u32[]{:S(2)}) collective-permute-start(bf16[512,128]{1,0:T(8,128)(2,1)S(1)} %fusion.7), channel_id=1, source_target_pairs={{0,48},{8,56},{16,64},{24,72},{32,80},{40,88},{48,96},{56,104},{64... | collective-permute-start | bytes 393224 | tf_op jit(solution)/shard_map/ppermute | solution.py:30
  92.9 6.2 %collective-permute-start.5 = (bf16[512,128]{1,0:T(8,128)(2,1)S(1)}, bf16[512,128]{1,0:T(8,128)(2,1)S(1)}, u32[]{:S(2)}, u32[]{:S(2)}) collective-permute-start(bf16[512,128]{1,0:T(8,128)(2,1)S(1)} %fusion.7), channel_id=1, source_target_pairs={{0,8},{8,0},{16,24},{24,16},{32,40},{40,32},{48,56},{56,48},{64,72... | collective-permute-start | bytes 393224 | tf_op jit(solution)/shard_map/ppermute | solution.py:30
  104.1 4.4 %collective-permute-start.8 = (bf16[512,128]{1,0:T(8,128)(2,1)S(1)}, bf16[512,128]{1,0:T(8,128)(2,1)S(1)}, u32[]{:S(2)}, u32[]{:S(2)}) collective-permute-start(bf16[512,128]{1,0:T(8,128)(2,1)S(1)} %fusion.7), channel_id=1, source_target_pairs={{0,56},{8,48},{16,72},{24,64},{32,88},{40,80},{48,104},{56,96},{64... | collective-permute-start | bytes 393224 | tf_op jit(solution)/shard_map/ppermute | solution.py:30
  108.9 5.2 %collective-permute-done.6 = bf16[512,128]{1,0:T(8,128)(2,1)S(1)} collective-permute-done((bf16[512,128]{1,0:T(8,128)(2,1)S(1)}, bf16[512,128]{1,0:T(8,128)(2,1)S(1)}, u32[]{:S(2)}, u32[]{:S(2)}) %collective-permute-start.6) | collective-permute-done | bytes 131104 | tf_op jit(solution)/shard_map/ppermute | solution.py:30
  117.7 14.5 %all-gather.3.cloned.1.call-done = bf16[8192,256]{1,0:T(8,128)(2,1)} async-done(((bf16[1024,256]{1,0:T(8,128)(2,1)}), bf16[8192,256]{1,0:T(8,128)(2,1)}) %all-gather.3.cloned.1.call-update) | async-done | bytes 4194320 | tf_op jit(solution)/shard_map/all_gather | solution.py:198
  132.2 7.0 %fusion.5.query = bf16[512,256]{1,0:T(8,128)(2,1)S(1)} fusion(f32[512,256]{1,0:T(8,128)S(1)} %fusion.21, bf16[8192,256]{1,0:T(8,128)(2,1)} %all-gather.3.cloned.1.call-done, bf16[256,8192]{1,0:T(8,128)(2,1)} %get-tuple-element.12, bf16[256,8192]{1,0:T(8,128)(2,1)} %get-tuple-element.11), kind=kOutput, calls=%fused_computation.10 | convolution fusion | flops 2164523008 | bytes 13369344 | tf_op jit(solution)/shard_map/dot_general | solution.py:226
  139.2 10.1 %attention.1 = (bf16[512,256]{1,0:T(8,128)(2,1)S(1)}, bf16[512,256]{1,0:T(8,128)(2,1)S(1)}, f32[4,512,128]{2,1,0:T(8,128)S(1)}) custom-call(s32[3]{0:T(128)S(1)} %pad_add_fusion.info, bf16[512,256]{1,0:T(8,128)(2,1)S(1)} %fusion.5.query, bf16[512,256]{1,0:T(8,128)(2,1)S(1)} %pad_maximum_fusion.16.grad_out, bf16[2,4,512,128]{3,2,1,0:T(8,128)(2,1)S(1)} %pad_maximum_fusion.14.kv), custom_call_target="tpu_custom_call" | custom-call | flops 2684354560 | bytes 4194304 | tf_op jit(solution)/shard_map/attention/pallas_call | solution.py:122
  154.2 23.6 %collective-permute-start.11 = (bf16[256,128]{1,0:T(8,128)(2,1)S(1)}, bf16[256,128]{1,0:T(8,128)(2,1)S(1)}, u32[]{:S(2)}, u32[]{:S(2)}) collective-permute-start(bf16[256,128]{1,0:T(8,128)(2,1)S(1)} %get-tuple-element.17), channel_id=1, source_target_pairs={{0,504},{8,496},{16,8},{24,0},{32,24},{40,16},{48,40},{56,32},{64,... | collective-permute-start | bytes 196616 | tf_op jit(solution)/shard_map/ppermute | solution.py:30
  178.5 4.1 %all-to-all-start.3 = ((bf16[8,2,256]{2,1,0:T(2,128)(2,1)}), bf16[8,2,256]{2,1,0:T(2,128)(2,1)S(1)}, u32[]{:S(2)}, u32[]{:S(2)}) async-start(bf16[8,2,256]{2,1,0:T(2,128)(2,1)} %reshape.95), calls=%async_computation.3 | async-start | bytes 16384 | tf_op jit(solution)/shard_map/all_to_all | solution.py:255
  184.5 4.5 %collective-permute-start.13 = (bf16[256,128]{1,0:T(8,128)(2,1)S(1)}, bf16[256,128]{1,0:T(8,128)(2,1)S(1)}, u32[]{:S(2)}, u32[]{:S(2)}) collective-permute-start(bf16[256,128]{1,0:T(8,128)(2,1)S(1)} %get-tuple-element.18), channel_id=1, source_target_pairs={{0,472},{8,464},{16,488},{24,480},{32,504},{40,496},{48,8},{56,0},... | collective-permute-start | bytes 196616 | tf_op jit(solution)/shard_map/ppermute | solution.py:30
  189.2 5.3 %collective-permute-start.14 = (bf16[256,128]{1,0:T(8,128)(2,1)S(1)}, bf16[256,128]{1,0:T(8,128)(2,1)S(1)}, u32[]{:S(2)}, u32[]{:S(2)}) collective-permute-start(bf16[256,128]{1,0:T(8,128)(2,1)S(1)} %get-tuple-element.15), channel_id=1, source_target_pairs={{0,496},{8,504},{16,0},{24,8},{32,16},{40,24},{48,32},{56,40},{64,... | collective-permute-start | bytes 196616 | tf_op jit(solution)/shard_map/ppermute | solution.py:30
  194.5 3.1 %collective-permute-start.15 = (bf16[256,128]{1,0:T(8,128)(2,1)S(1)}, bf16[256,128]{1,0:T(8,128)(2,1)S(1)}, u32[]{:S(2)}, u32[]{:S(2)}) collective-permute-start(bf16[256,128]{1,0:T(8,128)(2,1)S(1)} %get-tuple-element.14), channel_id=1, source_target_pairs={{0,480},{8,488},{16,496},{24,504},{32,0},{40,8},{48,16},{56,24},{6... | collective-permute-start | bytes 196616 | tf_op jit(solution)/shard_map/ppermute | solution.py:30
  205.4 10.1 %all-to-all-start.2 = ((bf16[8,256,32]{1,2,0:T(8,128)(2,1)}), bf16[8,256,32]{1,2,0:T(8,128)(2,1)S(1)}, u32[]{:S(2)}, u32[]{:S(2)}) async-start(bf16[8,256,32]{1,2,0:T(8,128)(2,1)} %broadcast_in_dim.45), calls=%async_computation.2 | async-start | bytes 262144 | tf_op jit(solution)/shard_map/all_to_all | solution.py:20
  215.7 9.2 %all-to-all-done.2 = bf16[8,256,32]{1,2,0:T(8,128)(2,1)S(1)} async-done(((bf16[8,256,32]{1,2,0:T(8,128)(2,1)}), bf16[8,256,32]{1,2,0:T(8,128)(2,1)S(1)}, u32[]{:S(2)}, u32[]{:S(2)}) %all-to-all-start.2) | async-done | bytes 131104 | tf_op jit(solution)/shard_map/all_to_all | solution.py:20
  224.9 3.0 %fusion.3 = bf16[4,64,8,128]{3,2,1,0:T(8,128)(2,1)S(1)} fusion(bf16[256,32]{0,1:T(8,128)(2,1)S(1)} %reduce_sum.42, bf16[256,8192]{1,0:T(8,128)(2,1)} %param.9), kind=kOutput, calls=%fused_computation.8 | convolution fusion | flops 134479872 | bytes 4734976 | tf_op jit(solution)/shard_map/dot_general | solution.py:267
  229.1 8.1 %all-to-all-start.4 = ((bf16[64,52,128]{2,1,0:T(8,128)(2,1)}), bf16[64,52,128]{2,1,0:T(8,128)(2,1)S(1)}, u32[]{:S(2)}, u32[]{:S(2)}) async-start(bf16[64,52,128]{2,1,0:T(8,128)(2,1)} %pad_maximum_fusion.15), calls=%async_computation.4 | async-start | bytes 1835008 | tf_op jit(solution)/shard_map/all_to_all | solution.py:278
  241.3 21.5 %all-to-all-done.4 = bf16[64,52,128]{2,1,0:T(8,128)(2,1)S(1)} async-done(((bf16[64,52,128]{2,1,0:T(8,128)(2,1)}), bf16[64,52,128]{2,1,0:T(8,128)(2,1)S(1)}, u32[]{:S(2)}, u32[]{:S(2)}) %all-to-all-start.4) | async-done | bytes 852000 | tf_op jit(solution)/shard_map/all_to_all | solution.py:278
  (97 shorter events, 44.9 us)
Async XLA Ops:
  7.2 101.3 %copy-start = (bf16[16,512]{1,0:T(8,128)(2,1)S(1)}, bf16[16,512]{1,0:T(8,128)(2,1)}, u32[]{:S(2)}) copy-start(bf16[16,512]{1,0:T(8,128)(2,1)} %param.14) | copy-start | bytes 49156
  7.2 64.4 %all-gather.5.cloned.1.call-start = ((), (), s32[]{:S(2)}) async-start(), calls=%async_computation.6 | async-start | bytes 2949120 | tf_op jit(solution)/shard_map/all_gather | solution.py:191
  28.5 103.7 %all-gather.3.cloned.1.call-start = ((), (), s32[]{:S(2)}) async-start(), calls=%async_computation.5 | async-start | bytes 4718592 | tf_op jit(solution)/shard_map/all_gather | solution.py:198
  28.6 24.9 %collective-permute-start = (bf16[256,8192]{1,0:T(8,128)(2,1)}, bf16[256,8192]{1,0:T(8,128)(2,1)}, u32[]{:S(2)}, u32[]{:S(2)}) collective-permute-start(bf16[256,8192]{1,0:T(8,128)(2,1)} %param.9), channel_id=1, source_target_pairs={{0,8},{8,0},{16,24},{24,16},{32,40},{40,32},{48,56},{56,48},{64,72... | collective-permute-start | bytes 12582920 | tf_op jit(solution)/shard_map/ppermute | solution.py:30
  50.6 38.2 %collective-permute-start.1 = (bf16[256,256]{1,0:T(8,128)(2,1)S(1)}, bf16[256,256]{1,0:T(8,128)(2,1)S(1)}, u32[]{:S(2)}, u32[]{:S(2)}) collective-permute-start(bf16[256,256]{1,0:T(8,128)(2,1)S(1)} %bitcast.94), channel_id=1, source_target_pairs={{0,8},{8,0},{16,24},{24,16},{32,40},{40,32},{48,56},{56,48},{64,72... | collective-permute-start | bytes 393224 | tf_op jit(solution)/shard_map/ppermute | solution.py:30
  81.5 19.9 %collective-permute-start.2 = (bf16[512,128]{1,0:T(8,128)(2,1)S(1)}, bf16[512,128]{1,0:T(8,128)(2,1)S(1)}, u32[]{:S(2)}, u32[]{:S(2)}) collective-permute-start(bf16[512,128]{1,0:T(8,128)(2,1)S(1)} %fusion.7), channel_id=1, source_target_pairs={{0,16},{8,24},{16,32},{24,40},{32,48},{40,56},{48,64},{56,72},{64,... | collective-permute-start | bytes 393224 | tf_op jit(solution)/shard_map/ppermute | solution.py:30
  84.9 19.2 %collective-permute-start.3 = (bf16[512,128]{1,0:T(8,128)(2,1)S(1)}, bf16[512,128]{1,0:T(8,128)(2,1)S(1)}, u32[]{:S(2)}, u32[]{:S(2)}) collective-permute-start(bf16[512,128]{1,0:T(8,128)(2,1)S(1)} %fusion.7), channel_id=1, source_target_pairs={{0,32},{8,40},{16,48},{24,56},{32,64},{40,72},{48,80},{56,88},{64,... | collective-permute-start | bytes 393224 | tf_op jit(solution)/shard_map/ppermute | solution.py:30
  88.9 19.9 %collective-permute-start.4 = (bf16[512,128]{1,0:T(8,128)(2,1)S(1)}, bf16[512,128]{1,0:T(8,128)(2,1)S(1)}, u32[]{:S(2)}, u32[]{:S(2)}) collective-permute-start(bf16[512,128]{1,0:T(8,128)(2,1)S(1)} %fusion.7), channel_id=1, source_target_pairs={{0,48},{8,56},{16,64},{24,72},{32,80},{40,88},{48,96},{56,104},{64... | collective-permute-start | bytes 393224 | tf_op jit(solution)/shard_map/ppermute | solution.py:30
  92.9 16.0 %collective-permute-start.5 = (bf16[512,128]{1,0:T(8,128)(2,1)S(1)}, bf16[512,128]{1,0:T(8,128)(2,1)S(1)}, u32[]{:S(2)}, u32[]{:S(2)}) collective-permute-start(bf16[512,128]{1,0:T(8,128)(2,1)S(1)} %fusion.7), channel_id=1, source_target_pairs={{0,8},{8,0},{16,24},{24,16},{32,40},{40,32},{48,56},{56,48},{64,72... | collective-permute-start | bytes 393224 | tf_op jit(solution)/shard_map/ppermute | solution.py:30
  99.1 15.0 %collective-permute-start.6 = (bf16[512,128]{1,0:T(8,128)(2,1)S(1)}, bf16[512,128]{1,0:T(8,128)(2,1)S(1)}, u32[]{:S(2)}, u32[]{:S(2)}) collective-permute-start(bf16[512,128]{1,0:T(8,128)(2,1)S(1)} %fusion.7), channel_id=1, source_target_pairs={{0,24},{8,16},{16,40},{24,32},{32,56},{40,48},{48,72},{56,64},{64,... | collective-permute-start | bytes 393224 | tf_op jit(solution)/shard_map/ppermute | solution.py:30
  101.4 14.0 %collective-permute-start.7 = (bf16[512,128]{1,0:T(8,128)(2,1)S(1)}, bf16[512,128]{1,0:T(8,128)(2,1)S(1)}, u32[]{:S(2)}, u32[]{:S(2)}) collective-permute-start(bf16[512,128]{1,0:T(8,128)(2,1)S(1)} %fusion.7), channel_id=1, source_target_pairs={{0,40},{8,32},{16,56},{24,48},{32,72},{40,64},{48,88},{56,80},{64,... | collective-permute-start | bytes 393224 | tf_op jit(solution)/shard_map/ppermute | solution.py:30
  104.1 13.4 %collective-permute-start.8 = (bf16[512,128]{1,0:T(8,128)(2,1)S(1)}, bf16[512,128]{1,0:T(8,128)(2,1)S(1)}, u32[]{:S(2)}, u32[]{:S(2)}) collective-permute-start(bf16[512,128]{1,0:T(8,128)(2,1)S(1)} %fusion.7), channel_id=1, source_target_pairs={{0,56},{8,48},{16,72},{24,64},{32,88},{40,80},{48,104},{56,96},{64... | collective-permute-start | bytes 393224 | tf_op jit(solution)/shard_map/ppermute | solution.py:30
  149.5 39.7 %collective-permute-start.17 = (f32[256,16]{0,1:T(8,128)S(1)}, f32[256,16]{0,1:T(8,128)S(1)}, u32[]{:S(2)}, u32[]{:S(2)}) collective-permute-start(f32[256,16]{0,1:T(8,128)S(1)} %constant_dynamic-slice_fusion), channel_id=1, source_target_pairs={{0,8},{8,0},{16,24},{24,16},{32,40},{40,32},{48,56},{56,48},{64,72... | collective-permute-start | bytes 49160 | tf_op jit(solution)/shard_map/ppermute | solution.py:30
  152.2 42.3 %collective-permute-start.10 = (bf16[256,128]{1,0:T(8,128)(2,1)S(1)}, bf16[256,128]{1,0:T(8,128)(2,1)S(1)}, u32[]{:S(2)}, u32[]{:S(2)}) collective-permute-start(bf16[256,128]{1,0:T(8,128)(2,1)S(1)} %get-tuple-element.13), channel_id=1, source_target_pairs={{0,8},{8,0},{16,24},{24,16},{32,40},{40,32},{48,56},{56,48},{64,72... | collective-permute-start | bytes 196616 | tf_op jit(solution)/shard_map/ppermute | solution.py:30
  154.2 43.5 %collective-permute-start.11 = (bf16[256,128]{1,0:T(8,128)(2,1)S(1)}, bf16[256,128]{1,0:T(8,128)(2,1)S(1)}, u32[]{:S(2)}, u32[]{:S(2)}) collective-permute-start(bf16[256,128]{1,0:T(8,128)(2,1)S(1)} %get-tuple-element.17), channel_id=1, source_target_pairs={{0,504},{8,496},{16,8},{24,0},{32,24},{40,16},{48,40},{56,32},{64,... | collective-permute-start | bytes 196616 | tf_op jit(solution)/shard_map/ppermute | solution.py:30
  178.5 10.6 %all-to-all-start.3 = ((bf16[8,2,256]{2,1,0:T(2,128)(2,1)}), bf16[8,2,256]{2,1,0:T(2,128)(2,1)S(1)}, u32[]{:S(2)}, u32[]{:S(2)}) async-start(bf16[8,2,256]{2,1,0:T(2,128)(2,1)} %reshape.95), calls=%async_computation.3 | async-start | bytes 16384 | tf_op jit(solution)/shard_map/all_to_all | solution.py:255
  182.6 17.3 %collective-permute-start.12 = (bf16[256,128]{1,0:T(8,128)(2,1)S(1)}, bf16[256,128]{1,0:T(8,128)(2,1)S(1)}, u32[]{:S(2)}, u32[]{:S(2)}) collective-permute-start(bf16[256,128]{1,0:T(8,128)(2,1)S(1)} %get-tuple-element.16), channel_id=1, source_target_pairs={{0,488},{8,480},{16,504},{24,496},{32,8},{40,0},{48,24},{56,16},{6... | collective-permute-start | bytes 196616 | tf_op jit(solution)/shard_map/ppermute | solution.py:30
  184.5 15.4 %collective-permute-start.13 = (bf16[256,128]{1,0:T(8,128)(2,1)S(1)}, bf16[256,128]{1,0:T(8,128)(2,1)S(1)}, u32[]{:S(2)}, u32[]{:S(2)}) collective-permute-start(bf16[256,128]{1,0:T(8,128)(2,1)S(1)} %get-tuple-element.18), channel_id=1, source_target_pairs={{0,472},{8,464},{16,488},{24,480},{32,504},{40,496},{48,8},{56,0},... | collective-permute-start | bytes 196616 | tf_op jit(solution)/shard_map/ppermute | solution.py:30
  189.2 10.7 %collective-permute-start.14 = (bf16[256,128]{1,0:T(8,128)(2,1)S(1)}, bf16[256,128]{1,0:T(8,128)(2,1)S(1)}, u32[]{:S(2)}, u32[]{:S(2)}) collective-permute-start(bf16[256,128]{1,0:T(8,128)(2,1)S(1)} %get-tuple-element.15), channel_id=1, source_target_pairs={{0,496},{8,504},{16,0},{24,8},{32,16},{40,24},{48,32},{56,40},{64,... | collective-permute-start | bytes 196616 | tf_op jit(solution)/shard_map/ppermute | solution.py:30
  194.5 7.5 %collective-permute-start.15 = (bf16[256,128]{1,0:T(8,128)(2,1)S(1)}, bf16[256,128]{1,0:T(8,128)(2,1)S(1)}, u32[]{:S(2)}, u32[]{:S(2)}) collective-permute-start(bf16[256,128]{1,0:T(8,128)(2,1)S(1)} %get-tuple-element.14), channel_id=1, source_target_pairs={{0,480},{8,488},{16,496},{24,504},{32,0},{40,8},{48,16},{56,24},{6... | collective-permute-start | bytes 196616 | tf_op jit(solution)/shard_map/ppermute | solution.py:30
  197.7 6.8 %collective-permute-start.16 = (bf16[256,128]{1,0:T(8,128)(2,1)S(1)}, bf16[256,128]{1,0:T(8,128)(2,1)S(1)}, u32[]{:S(2)}, u32[]{:S(2)}) collective-permute-start(bf16[256,128]{1,0:T(8,128)(2,1)S(1)} %get-tuple-element.19), channel_id=1, source_target_pairs={{0,464},{8,472},{16,480},{24,488},{32,496},{40,504},{48,0},{56,8},... | collective-permute-start | bytes 196616 | tf_op jit(solution)/shard_map/ppermute | solution.py:30
  205.4 19.4 %all-to-all-start.2 = ((bf16[8,256,32]{1,2,0:T(8,128)(2,1)}), bf16[8,256,32]{1,2,0:T(8,128)(2,1)S(1)}, u32[]{:S(2)}, u32[]{:S(2)}) async-start(bf16[8,256,32]{1,2,0:T(8,128)(2,1)} %broadcast_in_dim.45), calls=%async_computation.2 | async-start | bytes 262144 | tf_op jit(solution)/shard_map/all_to_all | solution.py:20
  229.1 33.7 %all-to-all-start.4 = ((bf16[64,52,128]{2,1,0:T(8,128)(2,1)}), bf16[64,52,128]{2,1,0:T(8,128)(2,1)S(1)}, u32[]{:S(2)}, u32[]{:S(2)}) async-start(bf16[64,52,128]{2,1,0:T(8,128)(2,1)} %pad_maximum_fusion.15), calls=%async_computation.4 | async-start | bytes 1835008 | tf_op jit(solution)/shard_map/all_to_all | solution.py:278
  237.2 3.3 %collective-permute-start.9 = (bf16[256,256]{1,0:T(8,128)(2,1)S(1)}, bf16[256,256]{1,0:T(8,128)(2,1)S(1)}, u32[]{:S(2)}, u32[]{:S(2)}) collective-permute-start(bf16[256,256]{1,0:T(8,128)(2,1)S(1)} %constant_dynamic-slice_fusion.1), channel_id=1, source_target_pairs={{0,8},{8,0},{16,24},{24,16},{32,40},{40,32},{48,56},{56,48},{64,72... | collective-permute-start | bytes 393224 | tf_op jit(solution)/shard_map/ppermute | solution.py:30
  (7 other events, 131.3 us)
Sparse Core Ops, SparseCore 0:
  28.6 42.8 all-gather.4
  73.6 58.5 all-gather.2

commit v3 on v2

--- a/solution.py
+++ b/solution.py
@@ -195,9 +195,14 @@
         q_rows.reshape(members, depth, half),
         "ctx", 0, 0, tiled=True, axis_index_groups=plain,
     )
-    q_rows = lax.all_gather(
-        q_rows.reshape(members * depth, half),
-        "ctx", axis=0, tiled=True, axis_index_groups=across,
+    q_rows = q_rows.reshape(members * depth, half)
+    ahead, back = [q_rows], [q_rows]
+    for _ in range(planes // 2 - 1):
+        ahead.append(to_chip(ahead[-1], chips, False))
+        back.append(to_chip(back[-1], -chips, False))
+    cut = members * depth // 2
+    opposite = jnp.concatenate(
+        [to_chip(ahead[-1][:cut], chips, False), to_chip(back[-1][cut:], -chips, False)]
     )
 
     chip_tokens = both(tokens, to_chip(tokens, 0, True))
@@ -214,18 +219,20 @@
     )
     extra = jnp.dot(low_v, value_up_weight, preferred_element_type=f32)
     mine = (mine + jnp.where(core == 1, extra, 0.0)).astype(bf16)
-    kv = jnp.stack(
-        [
-            jnp.stack([mine] + [to_chip(mine, d, False) for d in range(1, chips)]),
-            jnp.stack([to_chip(mine, d, True) for d in range(chips)]),
-        ]
-    )
+    mine = jnp.stack([mine] + [to_chip(mine, d, False) for d in range(1, chips)])
+    kv = jnp.stack([mine, to_chip(mine, 0, True)])
 
     up_mine = lax.dynamic_slice_in_dim(query_up_weight, core * half, half, axis=1)
-    query = (
-        jnp.dot(chip_tokens, q_rows, preferred_element_type=f32)
-        + jnp.dot(low_q, up_mine, preferred_element_type=f32)
-    ).astype(bf16)
+    plane = position // members
+    query = jnp.dot(low_q, up_mine, preferred_element_type=f32)
+    chunks = [(0, q_rows)]
+    for step in range(1, planes // 2):
+        chunks += [(-step, ahead[step]), (step, back[step])]
+    for step, chunk in chunks + [(planes // 2, opposite)]:
+        start = (plane + step) % planes * (members * depth)
+        part = lax.dynamic_slice_in_dim(chip_tokens, start, members * depth, axis=1)
+        query = query + jnp.dot(part, chunk, preferred_element_type=f32)
+    query = query.astype(bf16)
 
     shifts = lax.dynamic_slice_in_dim(head_shifts, core * (heads // 2), heads // 2)
     seen = jnp.where(shifts != 0, (chip + chips // 2) % chips, chip)
@@ -245,9 +252,9 @@
     value_parts = value_parts.reshape(chips, 2, rows, size).astype(bf16)
     same = lax.dynamic_index_in_dim(value_parts, core, 1, keepdims=False)
     cross = lax.dynamic_index_in_dim(value_parts, 1 - core, 1, keepdims=False)
-    arrived = [same[0]]
-    arrived += [to_chip(cross[d], -d, True) for d in range(chips)]
-    arrived += [to_chip(same[d], -d, False) for d in range(1, chips)]
+    value_parts = same.astype(f32) + to_chip(cross, 0, True).astype(f32)
+    arrived = [value_parts[0]]
+    arrived += [to_chip(value_parts[d].astype(bf16), -d, False) for d in range(1, chips)]
     value_gradient = functools.reduce(jnp.add, [a.astype(f32) for a in arrived]).astype(bf16)
 
     query_up_part = lax.dot_general(low_q, grad_query, TN, preferred_element_type=f32)

time: 273 us -> 276 us (1.011)
  blocking collectives: 38 us -> 0 us
  waiting for transfers between devices: 71.8 us -> 101 us
  starting transfers between devices: 102 us -> 115 us
  local copies, waits for them, and re-layouts: 7.33 us -> 12.2 us
  Pallas kernels: 10.1 us -> 6.07 us
    all_to_all x2 -> x0, blocking collectives: 38 us -> none  [the longest x1 20.3 us: on_device(): lax.all_to_all(kv_rows.reshape(members, depth + 2 * rank, size), 'ctx', 0...]
    ppermute x18 -> x20, waiting for transfers between devices: 14.2 us -> 47.7 us  [to_chip(): return lax.ppermute(value, 'ctx', pairs)]
    all_to_all x0 -> x2, waiting for transfers between devices: none -> 18.1 us  [the longest x1 13.7 us: on_device(): lax.all_to_all(q_rows.reshape(members, depth, half), 'ctx', 0, 0, tiled=T...]
    all_gather x1 -> x0, waiting for transfers between devices: 14.5 us -> none  [on_device(): lax.all_gather(q_rows.reshape(members * depth, half), 'ctx', axis=0, tile...]
    all_gather x1, waiting for transfers between devices: 12.2 us -> 0.02 us  [on_device(): lax.all_gather(kv_rows, 'ctx', axis=0, tiled=True, axis_index_groups=across)]
    all_to_all x0 -> x2, starting transfers between devices: none -> 7.65 us  [the longest x1 4.21 us: on_device(): lax.all_to_all(kv_rows.reshape(members, depth + 2 * rank, size), 'ctx', 0...]
    select_n x2 -> x1, other arithmetic: 5.93 us -> 0.03 us  [both(): jnp.where(core == 0, mine, theirs)]
    all_to_all x1, waiting for transfers between devices: 0.1 us -> 4.19 us  [on_device(): lax.all_to_all(query_up_part, 'ctx', 0, 0, tiled=True, axis_index_groups=...]
  transfers between devices with their start and end apart: 23 -> 26, of which waited for: 11 -> 14; matrix products, arithmetic and copies ran while one was open for 7% -> 6% of each run, Pallas kernels for 0% -> 0%
where the time goes in v3:
time: 276 us; the launch traced here: 274 us
  starting transfers between devices  115 us (42%)
  waiting for transfers between devices  101 us (37%)
  matrix products  18.4 us (7%)
  between operations  14.9 us (5%)
  local copies, waits for them, and re-layouts  12.2 us (4%)
  other arithmetic  7.28 us (3%)
  Pallas kernels  6.07 us (2%)
    ppermute x20, starting transfers between devices, to_chip(): return lax.ppermute(value, 'ctx', pairs)  82.9 us
    ppermute x20, waiting for transfers between devices, to_chip(): return lax.ppermute(value, 'ctx', pairs)  47.7 us
    all_to_all x1, waiting for transfers between devices, on_device(): payload = lax.all_to_all(payload, 'ctx', 0, 0, tiled=True)  21.5 us
    all_to_all x1, waiting for transfers between devices, on_device(): lax.all_to_all(q_rows.reshape(members, depth, half), 'ctx', 0, 0, tiled=T...  13.7 us
    all_to_all x1, starting transfers between devices, on_device(): payload = lax.all_to_all(payload, 'ctx', 0, 0, tiled=True)  10.5 us
    all_to_all x1, starting transfers between devices, spread(): lax.all_to_all(copies, axis, 0, 0, tiled=True, axis_index_groups=groups)  9.59 us
    all_to_all x1, waiting for transfers between devices, spread(): lax.all_to_all(copies, axis, 0, 0, tiled=True, axis_index_groups=groups)  9.28 us
    dot_general x1, matrix products, on_device(): lax.dot_general(chip_tokens, low_weight, NT, preferred_element_type=f32)  6.25 us
  transfers between devices with their start and end apart: 26, of which 14 were waited for; matrix products, arithmetic and copies ran while one was open for 6% of the time, Pallas kernels for 0%

profile of v3, /device:TPU:1, one launch (start us, length us, event | category | flops | bytes accessed | tf_op | source)
XLA Modules:
  0.0 274.3 jit_solution(2700939909167585604)
XLA Ops:
  7.2 8.9 %collective-permute-start = (bf16[256,8192]{1,0:T(8,128)(2,1)}, bf16[256,8192]{1,0:T(8,128)(2,1)}, u32[]{:S(2)}, u32[]{:S(2)}) collective-permute-start(bf16[256,8192]{1,0:T(8,128)(2,1)} %param.9), channel_id=1, source_target_pairs={{0,8},{8,0},{16,24},{24,16},{32,40},{40,32},{48,56},{56,48},{64,72... | collective-permute-start | bytes 12582920 | tf_op jit(solution)/shard_map/ppermute | solution.py:30
  22.1 13.7 %all-to-all-done.1 = bf16[8,128,256]{2,1,0:T(8,128)(2,1)S(1)} async-done(((bf16[8,128,256]{2,1,0:T(8,128)(2,1)}), bf16[8,128,256]{2,1,0:T(8,128)(2,1)S(1)}, u32[]{:S(2)}, u32[]{:S(2)}) %all-to-all-start.1) | async-done | bytes 524320 | tf_op jit(solution)/shard_map/all_to_all | solution.py:194
  36.6 4.2 %all-to-all-start = ((bf16[8,160,128]{2,1,0:T(8,128)(2,1)}), bf16[8,160,128]{2,1,0:T(8,128)(2,1)S(1)}, u32[]{:S(2)}, u32[]{:S(2)}) async-start(bf16[8,160,128]{2,1,0:T(8,128)(2,1)} %bitcast.4), calls=%async_computation | async-start | bytes 655360 | tf_op jit(solution)/shard_map/all_to_all | solution.py:187
  40.8 3.7 %collective-permute-start.2 = (bf16[1024,256]{1,0:T(8,128)(2,1)S(1)}, bf16[1024,256]{1,0:T(8,128)(2,1)S(1)}, u32[]{:S(2)}, u32[]{:S(2)}) collective-permute-start(bf16[1024,256]{1,0:T(8,128)(2,1)S(1)} %bitcast.95), channel_id=1, source_target_pairs={{0,448},{8,456},{16,464},{24,472},{32,480},{40,488},{48,496},{56,5... | collective-permute-start | bytes 1572872 | tf_op jit(solution)/shard_map/ppermute | solution.py:30
  46.4 4.4 %all-to-all-done = bf16[8,160,128]{2,1,0:T(8,128)(2,1)S(1)} async-done(((bf16[8,160,128]{2,1,0:T(8,128)(2,1)}), bf16[8,160,128]{2,1,0:T(8,128)(2,1)S(1)}, u32[]{:S(2)}, u32[]{:S(2)}) %all-to-all-start) | async-done | bytes 327712 | tf_op jit(solution)/shard_map/all_to_all | solution.py:187
  51.6 4.6 %collective-permute-done.2 = bf16[1024,256]{1,0:T(8,128)(2,1)S(1)} collective-permute-done((bf16[1024,256]{1,0:T(8,128)(2,1)S(1)}, bf16[1024,256]{1,0:T(8,128)(2,1)S(1)}, u32[]{:S(2)}, u32[]{:S(2)}) %collective-permute-start.2) | collective-permute-done | bytes 524320 | tf_op jit(solution)/shard_map/ppermute | solution.py:30
  56.1 4.8 %collective-permute-start.4 = (bf16[1024,256]{1,0:T(8,128)(2,1)S(1)}, bf16[1024,256]{1,0:T(8,128)(2,1)S(1)}, u32[]{:S(2)}, u32[]{:S(2)}) collective-permute-start(bf16[1024,256]{1,0:T(8,128)(2,1)S(1)} %collective-permute-done.2), channel_id=1, source_target_pairs={{0,448},{8,456},{16,464},{24,472},{32,480},{40,488},{48,496},{56,5... | collective-permute-start | bytes 1572872 | tf_op jit(solution)/shard_map/ppermute | solution.py:30
  67.7 7.4 %collective-permute-done.4 = bf16[1024,256]{1,0:T(8,128)(2,1)S(1)} collective-permute-done((bf16[1024,256]{1,0:T(8,128)(2,1)S(1)}, bf16[1024,256]{1,0:T(8,128)(2,1)S(1)}, u32[]{:S(2)}, u32[]{:S(2)}) %collective-permute-start.4) | collective-permute-done | bytes 524320 | tf_op jit(solution)/shard_map/ppermute | solution.py:30
  75.1 5.4 %collective-permute-start.6 = (bf16[1024,256]{1,0:T(8,128)(2,1)S(1)}, bf16[1024,256]{1,0:T(8,128)(2,1)S(1)}, u32[]{:S(2)}, u32[]{:S(2)}) collective-permute-start(bf16[1024,256]{1,0:T(8,128)(2,1)S(1)} %collective-permute-done.4), channel_id=1, source_target_pairs={{0,448},{8,456},{16,464},{24,472},{32,480},{40,488},{48,496},{56,5... | collective-permute-start | bytes 1572872 | tf_op jit(solution)/shard_map/ppermute | solution.py:30
  84.9 24.2 %collective-permute-done.5 = bf16[1024,256]{1,0:T(8,128)(2,1)S(1)} collective-permute-done((bf16[1024,256]{1,0:T(8,128)(2,1)}, bf16[1024,256]{1,0:T(8,128)(2,1)S(1)}, u32[]{:S(2)}, u32[]{:S(2)}) %collective-permute-start.5) | collective-permute-done | bytes 524320 | tf_op jit(solution)/shard_map/ppermute | solution.py:30
  111.2 4.6 %collective-permute-start.8 = (bf16[512,256]{1,0:T(8,128)(2,1)S(1)}, bf16[512,256]{1,0:T(8,128)(2,1)S(1)}, u32[]{:S(2)}, u32[]{:S(2)}) collective-permute-start(bf16[512,256]{1,0:T(8,128)(2,1)S(1)} %slice.70), channel_id=1, source_target_pairs={{0,448},{8,456},{16,464},{24,472},{32,480},{40,488},{48,496},{56,5... | collective-permute-start | bytes 786440 | tf_op jit(solution)/shard_map/ppermute | solution.py:30
  115.8 3.8 %broadcast_select_fusion = (bf16[256,8192]{1,0:T(8,128)(2,1)S(1)}, bf16[256,8192]{1,0:T(8,128)(2,1)S(1)}) fusion(bf16[256,8192]{1,0:T(8,128)(2,1)} %collective-permute-done, bf16[256,8192]{1,0:T(8,128)(2,1)} %param.9, pred[]{:T(512)S(6)} %eq.23), kind=kLoop, calls=%fused_computation.20 | loop fusion | flops 4194304 | bytes 16777216 | tf_op jit(solution)/shard_map/jit(_where)/select_n | solution.py:176
  123.3 6.3 %fusion.10 = bf16[512,32]{0,1:T(8,128)(2,1)S(1)} fusion(bf16[256,8192]{1,0:T(8,128)(2,1)} %copy-done.1, bf16[256,8192]{1,0:T(8,128)(2,1)} %copy-done.3, bf16[64,160,128]{2,1,0:T(8,128)(2,1)} %all-gather.2.cloned.1.call-done), kind=kOutput, calls=%fused_computation.36 | convolution fusion | flops 285229056 | bytes 8945664 | tf_op jit(solution)/shard_map/dot_general | solution.py:215
  136.4 3.7 %collective-permute-start.11 = (bf16[512,128]{1,0:T(8,128)(2,1)S(1)}, bf16[512,128]{1,0:T(8,128)(2,1)S(1)}, u32[]{:S(2)}, u32[]{:S(2)}) collective-permute-start(bf16[512,128]{1,0:T(8,128)(2,1)S(1)} %fusion.9), channel_id=1, source_target_pairs={{0,32},{8,40},{16,48},{24,56},{32,64},{40,72},{48,80},{56,88},{64,... | collective-permute-start | bytes 393224 | tf_op jit(solution)/shard_map/ppermute | solution.py:30
  148.1 11.0 %collective-permute-start.13 = (bf16[4,512,128]{2,1,0:T(8,128)(2,1)S(1)}, bf16[4,512,128]{2,1,0:T(8,128)(2,1)S(1)}, u32[]{:S(2)}, u32[]{:S(2)}) collective-permute-start(bf16[4,512,128]{2,1,0:T(8,128)(2,1)S(1)} %get-tuple-element.16), channel_id=1, source_target_pairs={{0,8},{8,0},{16,24},{24,16},{32,40},{40,32},{48,56},{56,48},{64,72... | collective-permute-start | bytes 1572872 | tf_op jit(solution)/shard_map/ppermute | solution.py:30
  161.2 6.1 %attention.1 = (bf16[512,256]{1,0:T(8,128)(2,1)S(1)}, bf16[512,256]{1,0:T(8,128)(2,1)S(1)}, f32[4,512,128]{2,1,0:T(8,128)S(1)}) custom-call(s32[3]{0:T(128)S(1)} %pad_add_fusion.info, bf16[512,256]{1,0:T(8,128)(2,1)S(1)} %fusion.7.query, bf16[512,256]{1,0:T(8,128)(2,1)S(1)} %pad_maximum_fusion.12.grad_out, bf16[2,4,512,128]{3,2,1,0:T(8,128)(2,1)S(1)} %pad_maximum_fusion.9.kv), custom_call_target="tpu_custom_call" | custom-call | flops 2684354560 | bytes 4194304 | tf_op jit(solution)/shard_map/attention/pallas_call | solution.py:122
  167.4 6.0 %collective-permute-start.15 = (bf16[4,256,128]{2,1,0:T(8,128)(2,1)S(1)}, bf16[4,256,128]{2,1,0:T(8,128)(2,1)S(1)}, u32[]{:S(2)}, u32[]{:S(2)}) collective-permute-start(bf16[4,256,128]{2,1,0:T(8,128)(2,1)S(1)} %dynamic-slice_bitcast_fusion), channel_id=1, source_target_pairs={{0,8},{8,0},{16,24},{24,16},{32,40},{40,32},{48,56},{56,48},{64,72... | collective-permute-start | bytes 786440 | tf_op jit(solution)/shard_map/ppermute | solution.py:30
  174.1 4.0 %all-to-all-start.3 = ((bf16[8,2,256]{2,1,0:T(2,128)(2,1)}), bf16[8,2,256]{2,1,0:T(2,128)(2,1)S(1)}, u32[]{:S(2)}, u32[]{:S(2)}) async-start(bf16[8,2,256]{2,1,0:T(2,128)(2,1)} %reshape.82), calls=%async_computation.3 | async-start | bytes 16384 | tf_op jit(solution)/shard_map/all_to_all | solution.py:262
  180.5 4.2 %all-to-all-done.3 = bf16[8,2,256]{2,1,0:T(2,128)(2,1)S(1)} async-done(((bf16[8,2,256]{2,1,0:T(2,128)(2,1)}), bf16[8,2,256]{2,1,0:T(2,128)(2,1)S(1)}, u32[]{:S(2)}, u32[]{:S(2)}) %all-to-all-start.3) | async-done | bytes 8224 | tf_op jit(solution)/shard_map/all_to_all | solution.py:262
  184.8 11.3 %collective-permute-start.16 = (bf16[256,128]{1,0:T(8,128)(2,1)S(1)}, bf16[256,128]{1,0:T(8,128)(2,1)S(1)}, u32[]{:S(2)}, u32[]{:S(2)}) collective-permute-start(bf16[256,128]{1,0:T(8,128)(2,1)S(1)} %get-tuple-element.21), channel_id=1, source_target_pairs={{0,496},{8,504},{16,0},{24,8},{32,16},{40,24},{48,32},{56,40},{64,... | collective-permute-start | bytes 196616 | tf_op jit(solution)/shard_map/ppermute | solution.py:30
  205.8 9.6 %all-to-all-start.2 = ((bf16[8,256,32]{1,2,0:T(8,128)(2,1)}), bf16[8,256,32]{1,2,0:T(8,128)(2,1)S(1)}, u32[]{:S(2)}, u32[]{:S(2)}) async-start(bf16[8,256,32]{1,2,0:T(8,128)(2,1)} %broadcast_in_dim.45), calls=%async_computation.2 | async-start | bytes 262144 | tf_op jit(solution)/shard_map/all_to_all | solution.py:20
  215.6 9.3 %all-to-all-done.2 = bf16[8,256,32]{1,2,0:T(8,128)(2,1)S(1)} async-done(((bf16[8,256,32]{1,2,0:T(8,128)(2,1)}), bf16[8,256,32]{1,2,0:T(8,128)(2,1)S(1)}, u32[]{:S(2)}, u32[]{:S(2)}) %all-to-all-start.2) | async-done | bytes 131104 | tf_op jit(solution)/shard_map/all_to_all | solution.py:20
  229.1 10.5 %all-to-all-start.4 = ((bf16[64,52,128]{2,1,0:T(8,128)(2,1)}), bf16[64,52,128]{2,1,0:T(8,128)(2,1)S(1)}, u32[]{:S(2)}, u32[]{:S(2)}) async-start(bf16[64,52,128]{2,1,0:T(8,128)(2,1)} %pad_maximum_fusion.10), calls=%async_computation.4 | async-start | bytes 1835008 | tf_op jit(solution)/shard_map/all_to_all | solution.py:285
  243.7 21.5 %all-to-all-done.4 = bf16[64,52,128]{2,1,0:T(8,128)(2,1)S(1)} async-done(((bf16[64,52,128]{2,1,0:T(8,128)(2,1)}), bf16[64,52,128]{2,1,0:T(8,128)(2,1)S(1)}, u32[]{:S(2)}, u32[]{:S(2)}) %all-to-all-start.4) | async-done | bytes 852000 | tf_op jit(solution)/shard_map/all_to_all | solution.py:285
  (122 shorter events, 66.5 us)
Async XLA Ops:
  7.2 108.6 %collective-permute-start = (bf16[256,8192]{1,0:T(8,128)(2,1)}, bf16[256,8192]{1,0:T(8,128)(2,1)}, u32[]{:S(2)}, u32[]{:S(2)}) collective-permute-start(bf16[256,8192]{1,0:T(8,128)(2,1)} %param.9), channel_id=1, source_target_pairs={{0,8},{8,0},{16,24},{24,16},{32,40},{40,32},{48,56},{56,48},{64,72... | collective-permute-start | bytes 12582920 | tf_op jit(solution)/shard_map/ppermute | solution.py:30
  17.9 17.9 %all-to-all-start.1 = ((bf16[8,128,256]{2,1,0:T(8,128)(2,1)}), bf16[8,128,256]{2,1,0:T(8,128)(2,1)S(1)}, u32[]{:S(2)}, u32[]{:S(2)}) async-start(bf16[8,128,256]{2,1,0:T(8,128)(2,1)} %bitcast.8), calls=%async_computation.1 | async-start | bytes 1048576 | tf_op jit(solution)/shard_map/all_to_all | solution.py:194
  36.6 14.2 %all-to-all-start = ((bf16[8,160,128]{2,1,0:T(8,128)(2,1)}), bf16[8,160,128]{2,1,0:T(8,128)(2,1)S(1)}, u32[]{:S(2)}, u32[]{:S(2)}) async-start(bf16[8,160,128]{2,1,0:T(8,128)(2,1)} %bitcast.4), calls=%async_computation | async-start | bytes 655360 | tf_op jit(solution)/shard_map/all_to_all | solution.py:187
  40.8 82.6 %all-gather.2.cloned.1.call-start = ((), (), s32[]{:S(2)}) async-start(), calls=%async_computation.5 | async-start | bytes 2949120 | tf_op jit(solution)/shard_map/all_gather | solution.py:191
  40.8 15.4 %collective-permute-start.2 = (bf16[1024,256]{1,0:T(8,128)(2,1)S(1)}, bf16[1024,256]{1,0:T(8,128)(2,1)S(1)}, u32[]{:S(2)}, u32[]{:S(2)}) collective-permute-start(bf16[1024,256]{1,0:T(8,128)(2,1)S(1)} %bitcast.95), channel_id=1, source_target_pairs={{0,448},{8,456},{16,464},{24,472},{32,480},{40,488},{48,496},{56,5... | collective-permute-start | bytes 1572872 | tf_op jit(solution)/shard_map/ppermute | solution.py:30
  44.4 16.5 %collective-permute-start.1 = (bf16[1024,256]{1,0:T(8,128)(2,1)S(1)}, bf16[1024,256]{1,0:T(8,128)(2,1)}, u32[]{:S(2)}, u32[]{:S(2)}) collective-permute-start(bf16[1024,256]{1,0:T(8,128)(2,1)S(1)} %bitcast.96), channel_id=1, source_target_pairs={{0,64},{8,72},{16,80},{24,88},{32,96},{40,104},{48,112},{56,120},{... | collective-permute-start | bytes 1572872 | tf_op jit(solution)/shard_map/ppermute | solution.py:30
  56.1 18.9 %collective-permute-start.4 = (bf16[1024,256]{1,0:T(8,128)(2,1)S(1)}, bf16[1024,256]{1,0:T(8,128)(2,1)S(1)}, u32[]{:S(2)}, u32[]{:S(2)}) collective-permute-start(bf16[1024,256]{1,0:T(8,128)(2,1)S(1)} %collective-permute-done.2), channel_id=1, source_target_pairs={{0,448},{8,456},{16,464},{24,472},{32,480},{40,488},{48,496},{56,5... | collective-permute-start | bytes 1572872 | tf_op jit(solution)/shard_map/ppermute | solution.py:30
  60.9 21.7 %collective-permute-start.3 = (bf16[1024,256]{1,0:T(8,128)(2,1)}, bf16[1024,256]{1,0:T(8,128)(2,1)}, u32[]{:S(2)}, u32[]{:S(2)}) collective-permute-start(bf16[1024,256]{1,0:T(8,128)(2,1)} %collective-permute-done.1), channel_id=1, source_target_pairs={{0,64},{8,72},{16,80},{24,88},{32,96},{40,104},{48,112},{56,120},{... | collective-permute-start | bytes 1572872 | tf_op jit(solution)/shard_map/ppermute | solution.py:30
  64.5 20.4 %collective-permute-start.9 = (bf16[256,256]{1,0:T(8,128)(2,1)S(1)}, bf16[256,256]{1,0:T(8,128)(2,1)S(1)}, u32[]{:S(2)}, u32[]{:S(2)}) collective-permute-start(bf16[256,256]{1,0:T(8,128)(2,1)S(1)} %bitcast.101), channel_id=1, source_target_pairs={{0,8},{8,0},{16,24},{24,16},{32,40},{40,32},{48,56},{56,48},{64,72... | collective-permute-start | bytes 393224 | tf_op jit(solution)/shard_map/ppermute | solution.py:30
  75.1 36.1 %collective-permute-start.6 = (bf16[1024,256]{1,0:T(8,128)(2,1)S(1)}, bf16[1024,256]{1,0:T(8,128)(2,1)S(1)}, u32[]{:S(2)}, u32[]{:S(2)}) collective-permute-start(bf16[1024,256]{1,0:T(8,128)(2,1)S(1)} %collective-permute-done.4), channel_id=1, source_target_pairs={{0,448},{8,456},{16,464},{24,472},{32,480},{40,488},{48,496},{56,5... | collective-permute-start | bytes 1572872 | tf_op jit(solution)/shard_map/ppermute | solution.py:30
  82.7 26.5 %collective-permute-start.5 = (bf16[1024,256]{1,0:T(8,128)(2,1)}, bf16[1024,256]{1,0:T(8,128)(2,1)S(1)}, u32[]{:S(2)}, u32[]{:S(2)}) collective-permute-start(bf16[1024,256]{1,0:T(8,128)(2,1)} %collective-permute-done.3), channel_id=1, source_target_pairs={{0,64},{8,72},{16,80},{24,88},{32,96},{40,104},{48,112},{56,120},{... | collective-permute-start | bytes 1572872 | tf_op jit(solution)/shard_map/ppermute | solution.py:30
  109.2 10.4 %collective-permute-start.7 = (bf16[512,256]{1,0:T(8,128)(2,1)S(1)}, bf16[512,256]{1,0:T(8,128)(2,1)S(1)}, u32[]{:S(2)}, u32[]{:S(2)}) collective-permute-start(bf16[512,256]{1,0:T(8,128)(2,1)S(1)} %slice.69), channel_id=1, source_target_pairs={{0,64},{8,72},{16,80},{24,88},{32,96},{40,104},{48,112},{56,120},{... | collective-permute-start | bytes 786440 | tf_op jit(solution)/shard_map/ppermute | solution.py:30
  111.2 8.4 %collective-permute-start.8 = (bf16[512,256]{1,0:T(8,128)(2,1)S(1)}, bf16[512,256]{1,0:T(8,128)(2,1)S(1)}, u32[]{:S(2)}, u32[]{:S(2)}) collective-permute-start(bf16[512,256]{1,0:T(8,128)(2,1)S(1)} %slice.70), channel_id=1, source_target_pairs={{0,448},{8,456},{16,464},{24,472},{32,480},{40,488},{48,496},{56,5... | collective-permute-start | bytes 786440 | tf_op jit(solution)/shard_map/ppermute | solution.py:30
  134.2 10.1 %collective-permute-start.10 = (bf16[512,128]{1,0:T(8,128)(2,1)S(1)}, bf16[512,128]{1,0:T(8,128)(2,1)S(1)}, u32[]{:S(2)}, u32[]{:S(2)}) collective-permute-start(bf16[512,128]{1,0:T(8,128)(2,1)S(1)} %fusion.9), channel_id=1, source_target_pairs={{0,16},{8,24},{16,32},{24,40},{32,48},{40,56},{48,64},{56,72},{64,... | collective-permute-start | bytes 393224 | tf_op jit(solution)/shard_map/ppermute | solution.py:30
  136.4 9.5 %collective-permute-start.11 = (bf16[512,128]{1,0:T(8,128)(2,1)S(1)}, bf16[512,128]{1,0:T(8,128)(2,1)S(1)}, u32[]{:S(2)}, u32[]{:S(2)}) collective-permute-start(bf16[512,128]{1,0:T(8,128)(2,1)S(1)} %fusion.9), channel_id=1, source_target_pairs={{0,32},{8,40},{16,48},{24,56},{32,64},{40,72},{48,80},{56,88},{64,... | collective-permute-start | bytes 393224 | tf_op jit(solution)/shard_map/ppermute | solution.py:30
  140.1 7.9 %collective-permute-start.12 = (bf16[512,128]{1,0:T(8,128)(2,1)S(1)}, bf16[512,128]{1,0:T(8,128)(2,1)S(1)}, u32[]{:S(2)}, u32[]{:S(2)}) collective-permute-start(bf16[512,128]{1,0:T(8,128)(2,1)S(1)} %fusion.9), channel_id=1, source_target_pairs={{0,48},{8,56},{16,64},{24,72},{32,80},{40,88},{48,96},{56,104},{64... | collective-permute-start | bytes 393224 | tf_op jit(solution)/shard_map/ppermute | solution.py:30
  148.1 13.0 %collective-permute-start.13 = (bf16[4,512,128]{2,1,0:T(8,128)(2,1)S(1)}, bf16[4,512,128]{2,1,0:T(8,128)(2,1)S(1)}, u32[]{:S(2)}, u32[]{:S(2)}) collective-permute-start(bf16[4,512,128]{2,1,0:T(8,128)(2,1)S(1)} %get-tuple-element.16), channel_id=1, source_target_pairs={{0,8},{8,0},{16,24},{24,16},{32,40},{40,32},{48,56},{56,48},{64,72... | collective-permute-start | bytes 1572872 | tf_op jit(solution)/shard_map/ppermute | solution.py:30
  167.4 17.3 %collective-permute-start.15 = (bf16[4,256,128]{2,1,0:T(8,128)(2,1)S(1)}, bf16[4,256,128]{2,1,0:T(8,128)(2,1)S(1)}, u32[]{:S(2)}, u32[]{:S(2)}) collective-permute-start(bf16[4,256,128]{2,1,0:T(8,128)(2,1)S(1)} %dynamic-slice_bitcast_fusion), channel_id=1, source_target_pairs={{0,8},{8,0},{16,24},{24,16},{32,40},{40,32},{48,56},{56,48},{64,72... | collective-permute-start | bytes 786440 | tf_op jit(solution)/shard_map/ppermute | solution.py:30
  174.1 10.5 %all-to-all-start.3 = ((bf16[8,2,256]{2,1,0:T(2,128)(2,1)}), bf16[8,2,256]{2,1,0:T(2,128)(2,1)S(1)}, u32[]{:S(2)}, u32[]{:S(2)}) async-start(bf16[8,2,256]{2,1,0:T(2,128)(2,1)} %reshape.82), calls=%async_computation.3 | async-start | bytes 16384 | tf_op jit(solution)/shard_map/all_to_all | solution.py:262
  178.3 22.0 %collective-permute-start.19 = (f32[256,16]{0,1:T(8,128)S(1)}, f32[256,16]{0,1:T(8,128)S(1)}, u32[]{:S(2)}, u32[]{:S(2)}) collective-permute-start(f32[256,16]{0,1:T(8,128)S(1)} %constant_dynamic-slice_fusion), channel_id=1, source_target_pairs={{0,8},{8,0},{16,24},{24,16},{32,40},{40,32},{48,56},{56,48},{64,72... | collective-permute-start | bytes 49160 | tf_op jit(solution)/shard_map/ppermute | solution.py:30
  184.8 15.5 %collective-permute-start.16 = (bf16[256,128]{1,0:T(8,128)(2,1)S(1)}, bf16[256,128]{1,0:T(8,128)(2,1)S(1)}, u32[]{:S(2)}, u32[]{:S(2)}) collective-permute-start(bf16[256,128]{1,0:T(8,128)(2,1)S(1)} %get-tuple-element.21), channel_id=1, source_target_pairs={{0,496},{8,504},{16,0},{24,8},{32,16},{40,24},{48,32},{56,40},{64,... | collective-permute-start | bytes 196616 | tf_op jit(solution)/shard_map/ppermute | solution.py:30
  198.1 6.9 %collective-permute-start.18 = (bf16[256,128]{1,0:T(8,128)(2,1)S(1)}, bf16[256,128]{1,0:T(8,128)(2,1)S(1)}, u32[]{:S(2)}, u32[]{:S(2)}) collective-permute-start(bf16[256,128]{1,0:T(8,128)(2,1)S(1)} %get-tuple-element.22), channel_id=1, source_target_pairs={{0,464},{8,472},{16,480},{24,488},{32,496},{40,504},{48,0},{56,8},... | collective-permute-start | bytes 196616 | tf_op jit(solution)/shard_map/ppermute | solution.py:30
  205.8 19.0 %all-to-all-start.2 = ((bf16[8,256,32]{1,2,0:T(8,128)(2,1)}), bf16[8,256,32]{1,2,0:T(8,128)(2,1)S(1)}, u32[]{:S(2)}, u32[]{:S(2)}) async-start(bf16[8,256,32]{1,2,0:T(8,128)(2,1)} %broadcast_in_dim.45), calls=%async_computation.2 | async-start | bytes 262144 | tf_op jit(solution)/shard_map/all_to_all | solution.py:20
  229.1 36.2 %all-to-all-start.4 = ((bf16[64,52,128]{2,1,0:T(8,128)(2,1)}), bf16[64,52,128]{2,1,0:T(8,128)(2,1)S(1)}, u32[]{:S(2)}, u32[]{:S(2)}) async-start(bf16[64,52,128]{2,1,0:T(8,128)(2,1)} %pad_maximum_fusion.10), calls=%async_computation.4 | async-start | bytes 1835008 | tf_op jit(solution)/shard_map/all_to_all | solution.py:285
  (16 other events, 342.6 us)
Sparse Core Ops, SparseCore 0:
  51.7 62.2 all-gather.1

commit v4 on v3

v4 whole, which is shorter than its diff:
```python
import functools

import jax
import jax.numpy as jnp
from jax import lax
from jax.experimental import pallas as pl
from jax.experimental.pallas import tpu as pltpu
from jax.sharding import PartitionSpec as P

GROUP = 2048
bf16 = jnp.bfloat16
f32 = jnp.float32
NT = (((1,), (1,)), ((), ()))
TN = (((0,), (0,)), ((), ()))


def spread(value, axis, groups=None):
    count = len(groups[0]) if groups else lax.axis_size(axis)
    copies = jnp.broadcast_to(value[None], (count, *value.shape))
    return lax.all_to_all(copies, axis, 0, 0, tiled=True, axis_index_groups=groups)


def to_chip(value, chips, other_core):
    count = lax.axis_size("ctx")
    pairs = []
    for source in range(count):
        core = source % 2
        target = (source - core + 2 * chips) % count + (1 - core if other_core else core)
        pairs.append((source, target))
    return lax.ppermute(value, "ctx", pairs)


def attention_kernel(scale, tile, info, query, grad_out, kv, out, grad_query, grad_value):
    rows, size = query.shape[0], kv.shape[-1]
    heads = query.shape[1] // size
    blocks, block = kv.shape[1:3]
    keys = [kv.at[info[heads], d] for d in range(blocks)]
    values = [kv.at[1 - info[heads], d] for d in range(blocks)]
    grad_value[...] = jnp.zeros_like(grad_value)

    def tile_of(index, columns, count):
        here = pl.ds(pl.multiple_of(index * tile, tile), tile)
        q = query[here, columns]
        do = grad_out[here, columns]
        row = index * tile + lax.broadcasted_iota(jnp.int32, (tile, block), 0)
        column = lax.broadcasted_iota(jnp.int32, (tile, block), 1)
        scores = [
            lax.dot_general(q, keys[d][...], NT, preferred_element_type=f32) * scale
            for d in range(count)
        ]
        scores[0] = jnp.where(column <= row, scores[0], -1e30)
        highest = functools.reduce(
            jnp.maximum, [jnp.max(s, axis=1, keepdims=True) for s in scores]
        )
        weights = [jnp.exp(s - highest) for s in scores]
        inverse = 1.0 / functools.reduce(
            jnp.add, [jnp.sum(w, axis=1, keepdims=True) for w in weights]
        )
        probs = [w * inverse for w in weights]
        low = [p.astype(bf16) for p in probs]
        result = functools.reduce(
            jnp.add,
            [
                jnp.dot(low[d], values[d][...], preferred_element_type=f32)
                for d in range(count)
            ],
        ).astype(bf16)
        out[here, columns] = result
        correction = jnp.sum(do.astype(f32) * result.astype(f32), axis=1, keepdims=True)
        total = jnp.zeros((tile, size), f32)
        for d in range(count):
            grad_value[d] += lax.dot_general(low[d], do, TN, preferred_element_type=f32)
            grad_probs = lax.dot_general(do, values[d][...], NT, preferred_element_type=f32)
            grad_scores = (probs[d] * (grad_probs - correction)).astype(bf16)
            total = total + jnp.dot(grad_scores, keys[d][...], preferred_element_type=f32)
        grad_query[here, columns] = (total * scale).astype(bf16)

    for head in range(heads):
        columns = slice(head * size, (head + 1) * size)
        for count in range(1, blocks + 1):

            @pl.when(info[head] + 1 == count)
            def _(columns=columns, count=count):
                def step(index, carry):
                    tile_of(index, columns, count)
                    return carry

                lax.fori_loop(0, rows // tile, step, 0)


def attend(info, query, grad_out, kv, tile=256):
    rows, width = query.shape
    size = kv.shape[-1]
    blocks, block = kv.shape[1:3]
    vmem = pl.BlockSpec(memory_space=pltpu.VMEM)
    return pl.pallas_call(
        functools.partial(attention_kernel, size ** (-0.5), tile),
        out_shape=(
            jax.ShapeDtypeStruct((rows, width), bf16),
            jax.ShapeDtypeStruct((rows, width), bf16),
            jax.ShapeDtypeStruct((blocks, block, size), f32),
        ),
        in_specs=[pl.BlockSpec(memory_space=pltpu.SMEM), vmem, vmem, vmem],
        out_specs=(vmem, vmem, vmem),
        compiler_params=pltpu.CompilerParams(vmem_limit_bytes=40 * 1024 * 1024),
        cost_estimate=pl.CostEstimate(
            flops=10 * rows * width * blocks * block,
            bytes_accessed=4 * 1024 * 1024,
            transcendentals=rows * width // size * blocks * block,
        ),
        name="attention",
    )(info, query, grad_out, kv)


def on_device(
    tokens,
    query_weight,
    key_weight,
    value_weight,
    adapter_down_weight,
    query_up_weight,
    value_up_weight,
    head_shifts,
    output_gradient,
):
    rows, model = tokens.shape
    heads = head_shifts.shape[0]
    width = query_weight.shape[1]
    size = width // heads
    half = width // 2
    depth = query_weight.shape[0]
    rank = adapter_down_weight.shape[1] // 2
    devices = lax.axis_size("ctx")
    chips = GROUP // (2 * rows)
    members = 2 * chips
    position = lax.axis_index("ctx")
    core = lax.rem(position, 2)
    chip = lax.rem(lax.div(position, 2), chips)
    plain = [[start + i for i in range(members)] for start in range(0, devices, members)]
    across = [[g[i] for g in plain] for i in range(members)]
    planes = devices // members

    def both(mine, theirs):
        return jnp.concatenate(
            [jnp.where(core == 0, mine, theirs), jnp.where(core == 0, theirs, mine)], axis=0
        )

    def half_of(array, which):
        return lax.dynamic_slice_in_dim(array, which * (array.shape[0] // 2), array.shape[0] // 2)

    def behind(value, *earlier):
        for other in earlier:
            value = value + (other.reshape(-1)[0] * 0).astype(value.dtype)
        return value

    def round_y(value, hold=None):
        ahead, back = [value], [value]
        for step in range(1, planes // 2):
            if hold and step in hold:
                ahead[-1] = behind(ahead[-1], *hold[step])
                back[-1] = behind(back[-1], *hold[step])
            ahead.append(to_chip(ahead[-1], chips, False))
            back.append(to_chip(back[-1], -chips, False))
        return ahead, back

    plane = lax.div(position, members)
    cut = members * depth // 2

    def project(total, ahead, back, last, weight_dim):
        chunks = [(0, 0, ahead[0])]
        for step in range(1, planes // 2):
            chunks += [(planes - step, 0, ahead[step]), (step, 0, back[step])]
        chunks += [(planes // 2, 0, last[0]), (planes // 2, cut, last[1])]
        for step, offset, chunk in chunks:
            start = lax.rem(plane + step, planes) * (members * depth) + offset
            count = chunk.shape[weight_dim]
            part = lax.dynamic_slice_in_dim(chip_tokens, start, count, axis=1)
            total = total + lax.dot_general(
                part, chunk, (((1,), (weight_dim,)), ((), ())), preferred_element_type=f32
            )
        return total

    chip_tokens = both(tokens, to_chip(tokens, 0, True))
    grad_halves = output_gradient.reshape(rows, 2, half).transpose(1, 0, 2)
    grad_mine = lax.dynamic_index_in_dim(grad_halves, core, 0, keepdims=False)
    grad_away = lax.dynamic_index_in_dim(grad_halves, 1 - core, 0, keepdims=False)
    grad_out = both(grad_mine, to_chip(grad_away, 0, True))

    down = adapter_down_weight.T
    kv_rows = jnp.stack(
        [jnp.concatenate([key_weight.T, down]), jnp.concatenate([value_weight.T, down])]
    )
    kv_rows = jnp.broadcast_to(kv_rows[None], (chips, *kv_rows.shape))
    kv_rows = lax.all_to_all(
        kv_rows.reshape(members, size + 2 * rank, depth),
        "ctx", 0, 0, tiled=True, axis_index_groups=plain,
    )
    kv_rows = kv_rows.transpose(1, 0, 2).reshape(size + 2 * rank, members * depth)
    kv_ahead, kv_back = round_y(kv_rows)
    kv_last = [
        to_chip(kv_ahead[-1][:, :cut], chips, False),
        to_chip(kv_back[-1][:, cut:], -chips, False),
    ]
    q_rows = behind(jnp.stack([query_weight[:, :half], query_weight[:, half:]]), kv_rows)
    q_rows = jnp.broadcast_to(q_rows[None], (chips, *q_rows.shape))
    q_rows = lax.all_to_all(
        q_rows.reshape(members, depth, half),
        "ctx", 0, 0, tiled=True, axis_index_groups=plain,
    )

    mine = project(0.0, kv_ahead, kv_back, kv_last, 1)
    low = mine[:, size:].astype(bf16)
    low_q, low_v = low[:, :rank], low[:, rank:]
    extra = jnp.dot(low_v, value_up_weight, preferred_element_type=f32)
    mine = (mine[:, :size] + jnp.where(core == 1, extra, 0.0)).astype(bf16)
    q_rows = behind(q_rows.reshape(members * depth, half), kv_ahead[2], kv_back[2])
    q_ahead, q_back = round_y(q_rows, {3: (mine,)})
    q_last = [
        to_chip(q_ahead[-1][:cut], chips, False),
        to_chip(q_back[-1][cut:], -chips, False),
    ]

    mine = jnp.stack([mine] + [to_chip(mine, d, False) for d in range(1, chips)])
    kv = jnp.stack([mine, to_chip(mine, 0, True)])

    up_mine = lax.dynamic_slice_in_dim(query_up_weight, core * half, half, axis=1)
    query = jnp.dot(low_q, up_mine, preferred_element_type=f32)
    query = project(query, q_ahead, q_back, q_last, 0).astype(bf16)

    shifts = lax.dynamic_slice_in_dim(head_shifts, core * (heads // 2), heads // 2)
    seen = jnp.where(shifts != 0, lax.rem(chip + chips // 2, chips), chip)
    info = jnp.concatenate([seen, core[None]]).astype(jnp.int32)
    output, grad_query, value_parts = attend(info, query, grad_out, kv)

    attention_mine = half_of(output, core)
    attention_other = to_chip(half_of(output, 1 - core), 0, True)
    attention = jnp.concatenate(
        [
            jnp.where(core == 0, attention_mine, attention_other),
            jnp.where(core == 0, attention_other, attention_mine),
        ],
        axis=1,
    )

    value_parts = value_parts.reshape(chips, 2, rows, size).astype(bf16)
    same = lax.dynamic_index_in_dim(value_parts, core, 1, keepdims=False)
    cross = lax.dynamic_index_in_dim(value_parts, 1 - core, 1, keepdims=False)
    value_parts = same.astype(f32) + to_chip(cross, 0, True).astype(f32)
    arrived = [value_parts[0]]
    arrived += [to_chip(value_parts[d].astype(bf16), -d, False) for d in range(1, chips)]
    value_gradient = functools.reduce(jnp.add, [a.astype(f32) for a in arrived]).astype(bf16)

    query_up_part = lax.dot_general(low_q, grad_query, TN, preferred_element_type=f32)
    query_up_part = behind(query_up_part.astype(bf16), value_parts)
    query_up_part = query_up_part.reshape(planes, rank // planes, half)
    query_up_part = lax.all_to_all(
        query_up_part, "ctx", 0, 0, tiled=True, axis_index_groups=across
    )
    query_up_part = jnp.sum(
        query_up_part.reshape(planes, rank // planes, half).astype(f32), axis=0
    ).astype(bf16)

    rank_q = lax.dot_general(grad_query, up_mine, NT, preferred_element_type=f32)
    rank_q = half_of(rank_q, core) + to_chip(half_of(rank_q, 1 - core), 0, True)
    rank_v = lax.dot_general(value_gradient, value_up_weight, NT, preferred_element_type=f32)
    rank_terms = jnp.concatenate([rank_q, rank_v], axis=1).astype(bf16)
    rank_grad = jnp.sum(spread(rank_terms, "fsdp").astype(f32), axis=0).astype(bf16)
    grad_down = lax.dot_general(rank_grad, tokens, TN, preferred_element_type=f32)
    grad_down = grad_down.astype(bf16).reshape(2 * rank, devices, depth).transpose(1, 0, 2)
    value_up_part = lax.dot_general(
        half_of(low_v, core), value_gradient, TN, preferred_element_type=f32
    ).astype(bf16)
    shared = jnp.concatenate(
        [value_up_part, query_up_part.reshape(-1, size)], axis=0
    )
    payload = jnp.concatenate(
        [grad_down, jnp.broadcast_to(shared[None], (devices, *shared.shape))], axis=1
    )
    payload = lax.all_to_all(payload, "ctx", 0, 0, tiled=True)
    summed = jnp.sum(payload[:, : 3 * rank].astype(f32), axis=0)
    query_up = payload[:, 3 * rank :].astype(f32)
    query_up = query_up.reshape(planes, chips, 2, rank // planes, half).sum(axis=1)
    query_up_gradient = query_up.transpose(0, 2, 1, 3).reshape(rank, width)
    return (
        attention,
        value_gradient,
        summed[: 2 * rank].T,
        query_up_gradient,
        summed[2 * rank :],
    )


def solution(mesh):
    in_specs = (
        P("ctx", None),
        P("ctx", "fsdp"),
        P("ctx", "fsdp"),
        P("ctx", "fsdp"),
        P("ctx", None),
        P(None, "fsdp"),
        P(None, "fsdp"),
        P("fsdp"),
        P("ctx", "fsdp"),
    )
    out_specs = (
        P("ctx", "fsdp"),
        P("ctx", "fsdp"),
        P("ctx", None),
        P(None, "fsdp"),
        P(None, "fsdp"),
    )
    return jax.shard_map(
        on_device, mesh=mesh, in_specs=in_specs, out_specs=out_specs, check_vma=False
    )
```

time: 276 us -> 268 us (0.971)
  waiting for transfers between devices: 101 us -> 71.3 us
  starting transfers between devices: 115 us -> 136 us
  between operations: 14.9 us -> 5.16 us
  local copies, waits for them, and re-layouts: 12.2 us -> 17.6 us
  other arithmetic: 7.28 us -> 12.6 us
    ppermute x20 -> x28, waiting for transfers between devices: 47.7 us -> 25 us  [to_chip(): return lax.ppermute(value, 'ctx', pairs)]
    ppermute x20 -> x28, starting transfers between devices: 82.9 us -> 103 us  [to_chip(): return lax.ppermute(value, 'ctx', pairs)]
    all_to_all x1, waiting for transfers between devices: 13.7 us -> 0.01 us  [on_device(): lax.all_to_all(q_rows.reshape(members, depth, half), 'ctx', 0, 0, tiled=T...]
    all_to_all x1, waiting for transfers between devices: 4.44 us -> 9.11 us  [on_device(): lax.all_to_all(kv_rows.reshape(members, size + 2 * rank, depth), 'ctx', 0...]
    slice x4 -> x9, local copies, waits for them, and re-layouts: 0.04 us -> 4.14 us  [the longest x5 2.68 us: behind(): value = value + (other.reshape(-1)[0] * 0).astype(value.dtype)]
    concatenate x1 -> x3, other arithmetic: 0.02 us -> 3.12 us  [both(): jnp.concatenate([jnp.where(core == 0, mine, theirs), jnp.where(core == 0,...]
    dot_general x10 -> x18, matrix products: 14.3 us -> 16 us  [project(): lax.dot_general(part, chunk, (((1,), (weight_dim,)), ((), ())), preferred...]
  transfers between devices with their start and end apart: 26 -> 33, of which waited for: 14 -> 10; matrix products, arithmetic and copies ran while one was open for 6% -> 15% of each run, Pallas kernels for 0% -> 0%
where the time goes in v4:
time: 268 us; the launch traced here: 267 us
  starting transfers between devices  136 us (51%)
  waiting for transfers between devices  71.3 us (27%)
  matrix products  20 us (7%)
  local copies, waits for them, and re-layouts  17.6 us (7%)
  other arithmetic  12.6 us (5%)
  between operations  5.16 us (2%)
  Pallas kernels  4.28 us (2%)
    ppermute x28, starting transfers between devices, to_chip(): return lax.ppermute(value, 'ctx', pairs)  103 us
    ppermute x28, waiting for transfers between devices, to_chip(): return lax.ppermute(value, 'ctx', pairs)  25 us
    all_to_all x1, waiting for transfers between devices, on_device(): payload = lax.all_to_all(payload, 'ctx', 0, 0, tiled=True)  21.5 us
    dot_general x18, matrix products, project(): lax.dot_general(part, chunk, (((1,), (weight_dim,)), ((), ())), preferred...  16 us
    all_to_all x1, starting transfers between devices, spread(): lax.all_to_all(copies, axis, 0, 0, tiled=True, axis_index_groups=groups)  9.77 us
    all_to_all x1, starting transfers between devices, on_device(): payload = lax.all_to_all(payload, 'ctx', 0, 0, tiled=True)  9.59 us
    all_to_all x1, waiting for transfers between devices, spread(): lax.all_to_all(copies, axis, 0, 0, tiled=True, axis_index_groups=groups)  9.16 us
    all_to_all x1, waiting for transfers between devices, on_device(): lax.all_to_all(kv_rows.reshape(members, size + 2 * rank, depth), 'ctx', 0...  9.11 us
  transfers between devices with their start and end apart: 33, of which 10 were waited for; matrix products, arithmetic and copies ran while one was open for 15% of the time, Pallas kernels for 0%

profile of v4, /device:TPU:1, one launch (start us, length us, event | category | flops | bytes accessed | tf_op | source)
XLA Modules:
  0.0 266.6 jit_solution(18405406740255130460)
XLA Ops:
  0.7 8.9 %collective-permute-start = (bf16[256,8192]{1,0:T(8,128)(2,1)}, bf16[256,8192]{1,0:T(8,128)(2,1)}, u32[]{:S(2)}, u32[]{:S(2)}) collective-permute-start(bf16[256,8192]{1,0:T(8,128)(2,1)} %param.9), channel_id=1, source_target_pairs={{0,8},{8,0},{16,24},{24,16},{32,40},{40,32},{48,56},{56,48},{64,72... | collective-permute-start | bytes 12582920 | tf_op jit(solution)/shard_map/ppermute | solution.py:30
  16.5 9.1 %all-to-all-done = bf16[8,160,128]{2,1,0:T(8,128)(2,1)S(1)} async-done(((bf16[8,160,128]{2,1,0:T(8,128)(2,1)}), bf16[8,160,128]{2,1,0:T(8,128)(2,1)S(1)}, u32[]{:S(2)}, u32[]{:S(2)}) %all-to-all-start) | async-done | bytes 327712 | tf_op jit(solution)/shard_map/all_to_all | solution.py:194
  27.9 4.5 %all-to-all-start.1 = ((bf16[8,128,256]{2,1,0:T(8,128)(2,1)}), bf16[8,128,256]{2,1,0:T(8,128)(2,1)S(1)}, u32[]{:S(2)}, u32[]{:S(2)}) async-start(bf16[8,128,256]{2,1,0:T(8,128)(2,1)} %bitcast.12), calls=%async_computation.1 | async-start | bytes 1048576 | tf_op jit(solution)/shard_map/all_to_all | solution.py:206
  34.4 4.6 %collective-permute-start.2 = (bf16[160,1024]{1,0:T(8,128)(2,1)S(1)}, bf16[160,1024]{1,0:T(8,128)(2,1)S(1)}, u32[]{:S(2)}, u32[]{:S(2)}) collective-permute-start(bf16[160,1024]{1,0:T(8,128)(2,1)S(1)} %bitcast.147), channel_id=1, source_target_pairs={{0,448},{8,456},{16,464},{24,472},{32,480},{40,488},{48,496},{56,5... | collective-permute-start | bytes 983048 | tf_op jit(solution)/shard_map/ppermute | solution.py:30
  39.0 5.8 %collective-permute-done.1 = bf16[160,1024]{1,0:T(8,128)(2,1)S(1)} collective-permute-done((bf16[160,1024]{1,0:T(8,128)(2,1)S(1)}, bf16[160,1024]{1,0:T(8,128)(2,1)S(1)}, u32[]{:S(2)}, u32[]{:S(2)}) %collective-permute-start.1) | collective-permute-done | bytes 327712 | tf_op jit(solution)/shard_map/ppermute | solution.py:30
  46.8 4.6 %collective-permute-start.4 = (bf16[160,1024]{1,0:T(8,128)(2,1)S(1)}, bf16[160,1024]{1,0:T(8,128)(2,1)S(1)}, u32[]{:S(2)}, u32[]{:S(2)}) collective-permute-start(bf16[160,1024]{1,0:T(8,128)(2,1)S(1)} %collective-permute-done.2), channel_id=1, source_target_pairs={{0,448},{8,456},{16,464},{24,472},{32,480},{40,488},{48,496},{56,5... | collective-permute-start | bytes 983048 | tf_op jit(solution)/shard_map/ppermute | solution.py:30
  58.9 4.9 %collective-permute-start.10 = (bf16[1024,256]{1,0:T(8,128)(2,1)S(1)}, bf16[1024,256]{1,0:T(8,128)(2,1)}, u32[]{:S(2)}, u32[]{:S(2)}) collective-permute-start(bf16[1024,256]{1,0:T(8,128)(2,1)S(1)} %bitcast.134), channel_id=1, source_target_pairs={{0,448},{8,456},{16,464},{24,472},{32,480},{40,488},{48,496},{56,5... | collective-permute-start | bytes 1572872 | tf_op jit(solution)/shard_map/ppermute | solution.py:30
  66.0 4.6 %collective-permute-start.6 = (bf16[160,1024]{1,0:T(8,128)(2,1)S(1)}, bf16[160,1024]{1,0:T(8,128)(2,1)S(1)}, u32[]{:S(2)}, u32[]{:S(2)}) collective-permute-start(bf16[160,1024]{1,0:T(8,128)(2,1)S(1)} %collective-permute-done.4), channel_id=1, source_target_pairs={{0,448},{8,456},{16,464},{24,472},{32,480},{40,488},{48,496},{56,5... | collective-permute-start | bytes 983048 | tf_op jit(solution)/shard_map/ppermute | solution.py:30
  72.6 12.4 %collective-permute-done.5 = bf16[160,1024]{1,0:T(8,128)(2,1)S(1)} collective-permute-done((bf16[160,1024]{1,0:T(8,128)(2,1)S(1)}, bf16[160,1024]{1,0:T(8,128)(2,1)S(1)}, u32[]{:S(2)}, u32[]{:S(2)}) %collective-permute-start.5) | collective-permute-done | bytes 327712 | tf_op jit(solution)/shard_map/ppermute | solution.py:30
  88.4 4.6 %collective-permute-start.8 = (bf16[160,512]{1,0:T(8,128)(2,1)}, bf16[160,512]{1,0:T(8,128)(2,1)}, u32[]{:S(2)}, u32[]{:S(2)}) collective-permute-start(bf16[160,512]{1,0:T(8,128)(2,1)} %slice.97), channel_id=1, source_target_pairs={{0,448},{8,456},{16,464},{24,472},{32,480},{40,488},{48,496},{56,5... | collective-permute-start | bytes 491528 | tf_op jit(solution)/shard_map/ppermute | solution.py:30
  98.3 3.8 %broadcast_select_fusion = (bf16[256,8192]{1,0:T(8,128)(2,1)S(1)}, bf16[256,8192]{1,0:T(8,128)(2,1)S(1)}) fusion(bf16[256,8192]{1,0:T(8,128)(2,1)} %collective-permute-done, bf16[256,8192]{1,0:T(8,128)(2,1)} %param.9, pred[]{:T(512)S(6)} %eq.4), kind=kLoop, calls=%fused_computation.19 | loop fusion | flops 4194304 | bytes 16777216 | tf_op jit(solution)/shard_map/jit(_where)/select_n | solution.py:145
  123.7 4.0 %collective-permute-start.19 = (bf16[512,128]{1,0:T(8,128)(2,1)S(1)}, bf16[512,128]{1,0:T(8,128)(2,1)S(1)}, u32[]{:S(2)}, u32[]{:S(2)}) collective-permute-start(bf16[512,128]{1,0:T(8,128)(2,1)S(1)} %fusion.22), channel_id=1, source_target_pairs={{0,32},{8,40},{16,48},{24,56},{32,64},{40,72},{48,80},{56,88},{64,... | collective-permute-start | bytes 393224 | tf_op jit(solution)/shard_map/ppermute | solution.py:30
  137.4 3.7 %collective-permute-start.14 = (bf16[1024,256]{1,0:T(8,128)(2,1)S(1)}, bf16[1024,256]{1,0:T(8,128)(2,1)S(1)}, u32[]{:S(2)}, u32[]{:S(2)}) collective-permute-start(bf16[1024,256]{1,0:T(8,128)(2,1)S(1)} %broadcast_add_fusion), channel_id=1, source_target_pairs={{0,448},{8,456},{16,464},{24,472},{32,480},{40,488},{48,496},{56,5... | collective-permute-start | bytes 1572872 | tf_op jit(solution)/shard_map/ppermute | solution.py:30
  144.7 7.7 %collective-permute-start.21 = (bf16[4,512,128]{2,1,0:T(8,128)(2,1)S(1)}, bf16[4,512,128]{2,1,0:T(8,128)(2,1)S(1)}, u32[]{:S(2)}, u32[]{:S(2)}) collective-permute-start(bf16[4,512,128]{2,1,0:T(8,128)(2,1)S(1)} %get-tuple-element.24), channel_id=1, source_target_pairs={{0,8},{8,0},{16,24},{24,16},{32,40},{40,32},{48,56},{56,48},{64,72... | collective-permute-start | bytes 1572872 | tf_op jit(solution)/shard_map/ppermute | solution.py:30
  155.1 4.0 %collective-permute-start.16 = (bf16[512,256]{1,0:T(8,128)(2,1)S(1)}, bf16[512,256]{1,0:T(8,128)(2,1)S(1)}, u32[]{:S(2)}, u32[]{:S(2)}) collective-permute-start(bf16[512,256]{1,0:T(8,128)(2,1)S(1)} %slice.106), channel_id=1, source_target_pairs={{0,448},{8,456},{16,464},{24,472},{32,480},{40,488},{48,496},{56,5... | collective-permute-start | bytes 786440 | tf_op jit(solution)/shard_map/ppermute | solution.py:30
  165.9 4.3 %attention.1 = (bf16[512,256]{1,0:T(8,128)(2,1)S(1)}, bf16[512,256]{1,0:T(8,128)(2,1)S(1)}, f32[4,512,128]{2,1,0:T(8,128)S(1)}) custom-call(s32[3]{0:T(128)S(1)} %pad_add_fusion.info, bf16[512,256]{1,0:T(8,128)(2,1)S(1)} %fusion.11.query, bf16[512,256]{1,0:T(8,128)(2,1)S(1)} %pad_maximum_fusion.3.grad_out, bf16[2,4,512,128]{3,2,1,0:T(8,128)(2,1)S(1)} %pad_maximum_fusion.kv), custom_call_target="tpu_custom_call" | custom-call | flops 2684354560 | bytes 4194304 | tf_op jit(solution)/shard_map/attention/pallas_call | solution.py:96
  170.3 6.3 %collective-permute-start.23 = (bf16[4,256,128]{2,1,0:T(8,128)(2,1)S(1)}, bf16[4,256,128]{2,1,0:T(8,128)(2,1)S(1)}, u32[]{:S(2)}, u32[]{:S(2)}) collective-permute-start(bf16[4,256,128]{2,1,0:T(8,128)(2,1)S(1)} %dynamic-slice_bitcast_fusion), channel_id=1, source_target_pairs={{0,8},{8,0},{16,24},{24,16},{32,40},{40,32},{48,56},{56,48},{64,72... | collective-permute-start | bytes 786440 | tf_op jit(solution)/shard_map/ppermute | solution.py:30
  178.9 6.6 %collective-permute-start.24 = (bf16[256,128]{1,0:T(8,128)(2,1)S(1)}, bf16[256,128]{1,0:T(8,128)(2,1)S(1)}, u32[]{:S(2)}, u32[]{:S(2)}) collective-permute-start(bf16[256,128]{1,0:T(8,128)(2,1)S(1)} %get-tuple-element.31), channel_id=1, source_target_pairs={{0,496},{8,504},{16,0},{24,8},{32,16},{40,24},{48,32},{56,40},{64,... | collective-permute-start | bytes 196616 | tf_op jit(solution)/shard_map/ppermute | solution.py:30
  192.8 5.4 %all-to-all-start.3 = ((bf16[8,2,256]{2,1,0:T(2,128)(2,1)}), bf16[8,2,256]{2,1,0:T(2,128)(2,1)S(1)}, u32[]{:S(2)}, u32[]{:S(2)}) async-start(bf16[8,2,256]{2,1,0:T(2,128)(2,1)} %reshape.123), calls=%async_computation.3 | async-start | bytes 16384 | tf_op jit(solution)/shard_map/all_to_all | solution.py:256
  198.3 6.5 %all-to-all-done.3 = bf16[8,2,256]{2,1,0:T(2,128)(2,1)S(1)} async-done(((bf16[8,2,256]{2,1,0:T(2,128)(2,1)}), bf16[8,2,256]{2,1,0:T(2,128)(2,1)S(1)}, u32[]{:S(2)}, u32[]{:S(2)}) %all-to-all-start.3) | async-done | bytes 8224 | tf_op jit(solution)/shard_map/all_to_all | solution.py:256
  205.8 9.8 %all-to-all-start.2 = ((bf16[8,256,32]{1,2,0:T(8,128)(2,1)}), bf16[8,256,32]{1,2,0:T(8,128)(2,1)S(1)}, u32[]{:S(2)}, u32[]{:S(2)}) async-start(bf16[8,256,32]{1,2,0:T(8,128)(2,1)} %broadcast_in_dim.45), calls=%async_computation.2 | async-start | bytes 262144 | tf_op jit(solution)/shard_map/all_to_all | solution.py:20
  215.7 9.2 %all-to-all-done.2 = bf16[8,256,32]{1,2,0:T(8,128)(2,1)S(1)} async-done(((bf16[8,256,32]{1,2,0:T(8,128)(2,1)}), bf16[8,256,32]{1,2,0:T(8,128)(2,1)S(1)}, u32[]{:S(2)}, u32[]{:S(2)}) %all-to-all-start.2) | async-done | bytes 131104 | tf_op jit(solution)/shard_map/all_to_all | solution.py:20
  229.1 9.6 %all-to-all-start.4 = ((bf16[64,52,128]{2,1,0:T(8,128)(2,1)}), bf16[64,52,128]{2,1,0:T(8,128)(2,1)S(1)}, u32[]{:S(2)}, u32[]{:S(2)}) async-start(bf16[64,52,128]{2,1,0:T(8,128)(2,1)} %pad_maximum_fusion.1), calls=%async_computation.4 | async-start | bytes 1835008 | tf_op jit(solution)/shard_map/all_to_all | solution.py:279
  242.9 21.5 %all-to-all-done.4 = bf16[64,52,128]{2,1,0:T(8,128)(2,1)S(1)} async-done(((bf16[64,52,128]{2,1,0:T(8,128)(2,1)}), bf16[64,52,128]{2,1,0:T(8,128)(2,1)S(1)}, u32[]{:S(2)}, u32[]{:S(2)}) %all-to-all-start.4) | async-done | bytes 852000 | tf_op jit(solution)/shard_map/all_to_all | solution.py:279
  (186 shorter events, 95.0 us)
Async XLA Ops:
  0.7 97.7 %collective-permute-start = (bf16[256,8192]{1,0:T(8,128)(2,1)}, bf16[256,8192]{1,0:T(8,128)(2,1)}, u32[]{:S(2)}, u32[]{:S(2)}) collective-permute-start(bf16[256,8192]{1,0:T(8,128)(2,1)} %param.9), channel_id=1, source_target_pairs={{0,8},{8,0},{16,24},{24,16},{32,40},{40,32},{48,56},{56,48},{64,72... | collective-permute-start | bytes 12582920 | tf_op jit(solution)/shard_map/ppermute | solution.py:30
  12.1 13.5 %all-to-all-start = ((bf16[8,160,128]{2,1,0:T(8,128)(2,1)}), bf16[8,160,128]{2,1,0:T(8,128)(2,1)S(1)}, u32[]{:S(2)}, u32[]{:S(2)}) async-start(bf16[8,160,128]{2,1,0:T(8,128)(2,1)} %bitcast.6), calls=%async_computation | async-start | bytes 655360 | tf_op jit(solution)/shard_map/all_to_all | solution.py:194
  27.9 31.0 %all-to-all-start.1 = ((bf16[8,128,256]{2,1,0:T(8,128)(2,1)}), bf16[8,128,256]{2,1,0:T(8,128)(2,1)S(1)}, u32[]{:S(2)}, u32[]{:S(2)}) async-start(bf16[8,128,256]{2,1,0:T(8,128)(2,1)} %bitcast.12), calls=%async_computation.1 | async-start | bytes 1048576 | tf_op jit(solution)/shard_map/all_to_all | solution.py:206
  52.0 18.6 %collective-permute-start.17 = (bf16[256,256]{1,0:T(8,128)(2,1)S(1)}, bf16[256,256]{1,0:T(8,128)(2,1)S(1)}, u32[]{:S(2)}, u32[]{:S(2)}) collective-permute-start(bf16[256,256]{1,0:T(8,128)(2,1)S(1)} %bitcast.150), channel_id=1, source_target_pairs={{0,8},{8,0},{16,24},{24,16},{32,40},{40,32},{48,56},{56,48},{64,72... | collective-permute-start | bytes 393224 | tf_op jit(solution)/shard_map/ppermute | solution.py:30
  58.9 34.1 %collective-permute-start.10 = (bf16[1024,256]{1,0:T(8,128)(2,1)S(1)}, bf16[1024,256]{1,0:T(8,128)(2,1)}, u32[]{:S(2)}, u32[]{:S(2)}) collective-permute-start(bf16[1024,256]{1,0:T(8,128)(2,1)S(1)} %bitcast.134), channel_id=1, source_target_pairs={{0,448},{8,456},{16,464},{24,472},{32,480},{40,488},{48,496},{56,5... | collective-permute-start | bytes 1572872 | tf_op jit(solution)/shard_map/ppermute | solution.py:30
  63.9 31.1 %collective-permute-start.9 = (bf16[1024,256]{1,0:T(8,128)(2,1)S(1)}, bf16[1024,256]{1,0:T(8,128)(2,1)}, u32[]{:S(2)}, u32[]{:S(2)}) collective-permute-start(bf16[1024,256]{1,0:T(8,128)(2,1)S(1)} %bitcast.135), channel_id=1, source_target_pairs={{0,64},{8,72},{16,80},{24,88},{32,96},{40,104},{48,112},{56,120},{... | collective-permute-start | bytes 1572872 | tf_op jit(solution)/shard_map/ppermute | solution.py:30
  66.0 21.7 %collective-permute-start.6 = (bf16[160,1024]{1,0:T(8,128)(2,1)S(1)}, bf16[160,1024]{1,0:T(8,128)(2,1)S(1)}, u32[]{:S(2)}, u32[]{:S(2)}) collective-permute-start(bf16[160,1024]{1,0:T(8,128)(2,1)S(1)} %collective-permute-done.4), channel_id=1, source_target_pairs={{0,448},{8,456},{16,464},{24,472},{32,480},{40,488},{48,496},{56,5... | collective-permute-start | bytes 983048 | tf_op jit(solution)/shard_map/ppermute | solution.py:30
  70.6 14.4 %collective-permute-start.5 = (bf16[160,1024]{1,0:T(8,128)(2,1)S(1)}, bf16[160,1024]{1,0:T(8,128)(2,1)S(1)}, u32[]{:S(2)}, u32[]{:S(2)}) collective-permute-start(bf16[160,1024]{1,0:T(8,128)(2,1)S(1)} %collective-permute-done.3), channel_id=1, source_target_pairs={{0,64},{8,72},{16,80},{24,88},{32,96},{40,104},{48,112},{56,120},{... | collective-permute-start | bytes 983048 | tf_op jit(solution)/shard_map/ppermute | solution.py:30
  85.8 30.9 %collective-permute-start.7 = (bf16[160,512]{1,0:T(8,128)(2,1)}, bf16[160,512]{1,0:T(8,128)(2,1)}, u32[]{:S(2)}, u32[]{:S(2)}) collective-permute-start(bf16[160,512]{1,0:T(8,128)(2,1)} %slice.96), channel_id=1, source_target_pairs={{0,64},{8,72},{16,80},{24,88},{32,96},{40,104},{48,112},{56,120},{... | collective-permute-start | bytes 491528 | tf_op jit(solution)/shard_map/ppermute | solution.py:30
  88.4 29.6 %collective-permute-start.8 = (bf16[160,512]{1,0:T(8,128)(2,1)}, bf16[160,512]{1,0:T(8,128)(2,1)}, u32[]{:S(2)}, u32[]{:S(2)}) collective-permute-start(bf16[160,512]{1,0:T(8,128)(2,1)} %slice.97), channel_id=1, source_target_pairs={{0,448},{8,456},{16,464},{24,472},{32,480},{40,488},{48,496},{56,5... | collective-permute-start | bytes 491528 | tf_op jit(solution)/shard_map/ppermute | solution.py:30
  93.0 43.3 %collective-permute-start.12 = (bf16[1024,256]{1,0:T(8,128)(2,1)}, bf16[1024,256]{1,0:T(8,128)(2,1)}, u32[]{:S(2)}, u32[]{:S(2)}) collective-permute-start(bf16[1024,256]{1,0:T(8,128)(2,1)} %collective-permute-done.10), channel_id=1, source_target_pairs={{0,448},{8,456},{16,464},{24,472},{32,480},{40,488},{48,496},{56,5... | collective-permute-start | bytes 1572872 | tf_op jit(solution)/shard_map/ppermute | solution.py:30
  94.9 36.7 %collective-permute-start.11 = (bf16[1024,256]{1,0:T(8,128)(2,1)}, bf16[1024,256]{1,0:T(8,128)(2,1)}, u32[]{:S(2)}, u32[]{:S(2)}) collective-permute-start(bf16[1024,256]{1,0:T(8,128)(2,1)} %collective-permute-done.9), channel_id=1, source_target_pairs={{0,64},{8,72},{16,80},{24,88},{32,96},{40,104},{48,112},{56,120},{... | collective-permute-start | bytes 1572872 | tf_op jit(solution)/shard_map/ppermute | solution.py:30
  121.3 23.3 %collective-permute-start.18 = (bf16[512,128]{1,0:T(8,128)(2,1)S(1)}, bf16[512,128]{1,0:T(8,128)(2,1)S(1)}, u32[]{:S(2)}, u32[]{:S(2)}) collective-permute-start(bf16[512,128]{1,0:T(8,128)(2,1)S(1)} %fusion.22), channel_id=1, source_target_pairs={{0,16},{8,24},{16,32},{24,40},{32,48},{40,56},{48,64},{56,72},{64,... | collective-permute-start | bytes 393224 | tf_op jit(solution)/shard_map/ppermute | solution.py:30
  123.7 21.0 %collective-permute-start.19 = (bf16[512,128]{1,0:T(8,128)(2,1)S(1)}, bf16[512,128]{1,0:T(8,128)(2,1)S(1)}, u32[]{:S(2)}, u32[]{:S(2)}) collective-permute-start(bf16[512,128]{1,0:T(8,128)(2,1)S(1)} %fusion.22), channel_id=1, source_target_pairs={{0,32},{8,40},{16,48},{24,56},{32,64},{40,72},{48,80},{56,88},{64,... | collective-permute-start | bytes 393224 | tf_op jit(solution)/shard_map/ppermute | solution.py:30
  127.7 16.9 %collective-permute-start.20 = (bf16[512,128]{1,0:T(8,128)(2,1)S(1)}, bf16[512,128]{1,0:T(8,128)(2,1)S(1)}, u32[]{:S(2)}, u32[]{:S(2)}) collective-permute-start(bf16[512,128]{1,0:T(8,128)(2,1)S(1)} %fusion.22), channel_id=1, source_target_pairs={{0,48},{8,56},{16,64},{24,72},{32,80},{40,88},{48,96},{56,104},{64... | collective-permute-start | bytes 393224 | tf_op jit(solution)/shard_map/ppermute | solution.py:30
  132.8 19.7 %collective-permute-start.13 = (bf16[1024,256]{1,0:T(8,128)(2,1)S(1)}, bf16[1024,256]{1,0:T(8,128)(2,1)S(1)}, u32[]{:S(2)}, u32[]{:S(2)}) collective-permute-start(bf16[1024,256]{1,0:T(8,128)(2,1)S(1)} %broadcast_add_fusion.1), channel_id=1, source_target_pairs={{0,64},{8,72},{16,80},{24,88},{32,96},{40,104},{48,112},{56,120},{... | collective-permute-start | bytes 1572872 | tf_op jit(solution)/shard_map/ppermute | solution.py:30
  137.4 17.7 %collective-permute-start.14 = (bf16[1024,256]{1,0:T(8,128)(2,1)S(1)}, bf16[1024,256]{1,0:T(8,128)(2,1)S(1)}, u32[]{:S(2)}, u32[]{:S(2)}) collective-permute-start(bf16[1024,256]{1,0:T(8,128)(2,1)S(1)} %broadcast_add_fusion), channel_id=1, source_target_pairs={{0,448},{8,456},{16,464},{24,472},{32,480},{40,488},{48,496},{56,5... | collective-permute-start | bytes 1572872 | tf_op jit(solution)/shard_map/ppermute | solution.py:30
  144.7 15.2 %collective-permute-start.21 = (bf16[4,512,128]{2,1,0:T(8,128)(2,1)S(1)}, bf16[4,512,128]{2,1,0:T(8,128)(2,1)S(1)}, u32[]{:S(2)}, u32[]{:S(2)}) collective-permute-start(bf16[4,512,128]{2,1,0:T(8,128)(2,1)S(1)} %get-tuple-element.24), channel_id=1, source_target_pairs={{0,8},{8,0},{16,24},{24,16},{32,40},{40,32},{48,56},{56,48},{64,72... | collective-permute-start | bytes 1572872 | tf_op jit(solution)/shard_map/ppermute | solution.py:30
  176.8 21.4 %collective-permute-start.27 = (f32[256,16]{0,1:T(8,128)S(1)}, f32[256,16]{0,1:T(8,128)S(1)}, u32[]{:S(2)}, u32[]{:S(2)}) collective-permute-start(f32[256,16]{0,1:T(8,128)S(1)} %constant_dynamic-slice_fusion), channel_id=1, source_target_pairs={{0,8},{8,0},{16,24},{24,16},{32,40},{40,32},{48,56},{56,48},{64,72... | collective-permute-start | bytes 49160 | tf_op jit(solution)/shard_map/ppermute | solution.py:30
  178.9 26.0 %collective-permute-start.24 = (bf16[256,128]{1,0:T(8,128)(2,1)S(1)}, bf16[256,128]{1,0:T(8,128)(2,1)S(1)}, u32[]{:S(2)}, u32[]{:S(2)}) collective-permute-start(bf16[256,128]{1,0:T(8,128)(2,1)S(1)} %get-tuple-element.31), channel_id=1, source_target_pairs={{0,496},{8,504},{16,0},{24,8},{32,16},{40,24},{48,32},{56,40},{64,... | collective-permute-start | bytes 196616 | tf_op jit(solution)/shard_map/ppermute | solution.py:30
  185.5 19.4 %collective-permute-start.25 = (bf16[256,128]{1,0:T(8,128)(2,1)S(1)}, bf16[256,128]{1,0:T(8,128)(2,1)S(1)}, u32[]{:S(2)}, u32[]{:S(2)}) collective-permute-start(bf16[256,128]{1,0:T(8,128)(2,1)S(1)} %get-tuple-element.33), channel_id=1, source_target_pairs={{0,480},{8,488},{16,496},{24,504},{32,0},{40,8},{48,16},{56,24},{6... | collective-permute-start | bytes 196616 | tf_op jit(solution)/shard_map/ppermute | solution.py:30
  188.9 16.0 %collective-permute-start.26 = (bf16[256,128]{1,0:T(8,128)(2,1)S(1)}, bf16[256,128]{1,0:T(8,128)(2,1)S(1)}, u32[]{:S(2)}, u32[]{:S(2)}) collective-permute-start(bf16[256,128]{1,0:T(8,128)(2,1)S(1)} %get-tuple-element.32), channel_id=1, source_target_pairs={{0,464},{8,472},{16,480},{24,488},{32,496},{40,504},{48,0},{56,8},... | collective-permute-start | bytes 196616 | tf_op jit(solution)/shard_map/ppermute | solution.py:30
  205.8 19.1 %all-to-all-start.2 = ((bf16[8,256,32]{1,2,0:T(8,128)(2,1)}), bf16[8,256,32]{1,2,0:T(8,128)(2,1)S(1)}, u32[]{:S(2)}, u32[]{:S(2)}) async-start(bf16[8,256,32]{1,2,0:T(8,128)(2,1)} %broadcast_in_dim.45), calls=%async_computation.2 | async-start | bytes 262144 | tf_op jit(solution)/shard_map/all_to_all | solution.py:20
  229.1 35.3 %all-to-all-start.4 = ((bf16[64,52,128]{2,1,0:T(8,128)(2,1)}), bf16[64,52,128]{2,1,0:T(8,128)(2,1)S(1)}, u32[]{:S(2)}, u32[]{:S(2)}) async-start(bf16[64,52,128]{2,1,0:T(8,128)(2,1)} %pad_maximum_fusion.1), calls=%async_computation.4 | async-start | bytes 1835008 | tf_op jit(solution)/shard_map/all_to_all | solution.py:279
  (35 other events, 755.3 us)

commit v5 on v4

--- a/solution.py
+++ b/solution.py
@@ -30,13 +30,29 @@
     return lax.ppermute(value, "ctx", pairs)
 
 
-def attention_kernel(scale, tile, info, query, grad_out, kv, out, grad_query, grad_value):
+def attention_kernel(
+    scale, tile, info, tokens, weight, start, grad_out, kv,
+    out, grad_query, grad_value, query, parts, arrivals,
+):
     rows, size = query.shape[0], kv.shape[-1]
     heads = query.shape[1] // size
     blocks, block = kv.shape[1:3]
     keys = [kv.at[info[heads], d] for d in range(blocks)]
     values = [kv.at[1 - info[heads], d] for d in range(blocks)]
+    count, depth = parts.shape[:2]
+    copies = [
+        pltpu.make_async_copy(weight.at[pl.ds(i * depth, depth)], parts.at[i], arrivals.at[i])
+        for i in range(count)
+    ]
+    for copy in copies:
+        copy.start()
     grad_value[...] = jnp.zeros_like(grad_value)
+    total = start[...]
+    for i, copy in enumerate(copies):
+        copy.wait()
+        part = tokens[:, i * depth : (i + 1) * depth]
+        total = total + jnp.dot(part, parts[i], preferred_element_type=f32)
+    query[...] = total.astype(bf16)
 
     def tile_of(index, columns, count):
         here = pl.ds(pl.multiple_of(index * tile, tile), tile)
@@ -88,8 +104,9 @@
                 lax.fori_loop(0, rows // tile, step, 0)
 
 
-def attend(info, query, grad_out, kv, tile=256):
-    rows, width = query.shape
+def attend(info, tokens, weight, start, grad_out, kv, tile=256, parts=8):
+    rows, width = start.shape
+    model = tokens.shape[1]
     size = kv.shape[-1]
     blocks, block = kv.shape[1:3]
     vmem = pl.BlockSpec(memory_space=pltpu.VMEM)
@@ -100,16 +117,64 @@
             jax.ShapeDtypeStruct((rows, width), bf16),
             jax.ShapeDtypeStruct((blocks, block, size), f32),
         ),
-        in_specs=[pl.BlockSpec(memory_space=pltpu.SMEM), vmem, vmem, vmem],
+        in_specs=[
+            pl.BlockSpec(memory_space=pltpu.SMEM),
+            vmem,
+            pl.BlockSpec(memory_space=pl.ANY),
+            vmem,
+            vmem,
+            vmem,
+        ],
         out_specs=(vmem, vmem, vmem),
-        compiler_params=pltpu.CompilerParams(vmem_limit_bytes=40 * 1024 * 1024),
+        scratch_shapes=[
+            pltpu.VMEM((rows, width), bf16),
+            pltpu.VMEM((parts, model // parts, width), bf16),
+            pltpu.SemaphoreType.DMA((parts,)),
+        ],
+        compiler_params=pltpu.CompilerParams(vmem_limit_bytes=48 * 1024 * 1024),
         cost_estimate=pl.CostEstimate(
-            flops=10 * rows * width * blocks * block,
-            bytes_accessed=4 * 1024 * 1024,
+            flops=10 * rows * width * blocks * block + 2 * rows * width * model,
+            bytes_accessed=16 * 1024 * 1024,
             transcendentals=rows * width // size * blocks * block,
         ),
         name="attention",
-    )(info, query, grad_out, kv)
+    )(info, tokens, weight, start, grad_out, kv)
+
+
+def blocks_kernel(rank_terms, tokens, shared, out):
+    ranks, size = rank_terms.shape[0], out.shape[2]
+    product = jnp.dot(rank_terms[...], tokens[...], preferred_element_type=f32).astype(bf16)
+    for i in range(out.shape[0]):
+        out[i, :ranks] = product[:, i * size : (i + 1) * size]
+        if out.shape[1] > ranks:
+            out[i, ranks:] = shared[...]
+
+
+def down_blocks(rank_terms, tokens, devices, shared=None, steps=8):
+    ranks, rows = rank_terms.shape
+    size = tokens.shape[1] // devices
+    extra = 0 if shared is None else shared.shape[0]
+    if shared is None:
+        shared = rank_terms
+    step = devices // steps
+    return pl.pallas_call(
+        blocks_kernel,
+        out_shape=jax.ShapeDtypeStruct((devices, ranks + extra, size), bf16),
+        grid=(steps,),
+        in_specs=[
+            pl.BlockSpec((ranks, rows), lambda i: (0, 0)),
+            pl.BlockSpec((rows, step * size), lambda i: (0, i)),
+            pl.BlockSpec(shared.shape, lambda i: (0, 0)),
+        ],
+        out_specs=pl.BlockSpec((step, ranks + extra, size), lambda i: (i, 0, 0)),
+        compiler_params=pltpu.CompilerParams(vmem_limit_bytes=24 * 1024 * 1024),
+        cost_estimate=pl.CostEstimate(
+            flops=2 * ranks * rows * devices * size,
+            bytes_accessed=2 * rows * devices * size,
+            transcendentals=0,
+        ),
+        name="down_blocks",
+    )(rank_terms, tokens, shared)
 
 
 def on_device(
@@ -148,38 +213,6 @@
     def half_of(array, which):
         return lax.dynamic_slice_in_dim(array, which * (array.shape[0] // 2), array.shape[0] // 2)
 
-    def behind(value, *earlier):
-        for other in earlier:
-            value = value + (other.reshape(-1)[0] * 0).astype(value.dtype)
-        return value
-
-    def round_y(value, hold=None):
-        ahead, back = [value], [value]
-        for step in range(1, planes // 2):
-            if hold and step in hold:
-                ahead[-1] = behind(ahead[-1], *hold[step])
-                back[-1] = behind(back[-1], *hold[step])
-            ahead.append(to_chip(ahead[-1], chips, False))
-            back.append(to_chip(back[-1], -chips, False))
-        return ahead, back
-
-    plane = lax.div(position, members)
-    cut = members * depth // 2
-
-    def project(total, ahead, back, last, weight_dim):
-        chunks = [(0, 0, ahead[0])]
-        for step in range(1, planes // 2):
-            chunks += [(planes - step, 0, ahead[step]), (step, 0, back[step])]
-        chunks += [(planes // 2, 0, last[0]), (planes // 2, cut, last[1])]
-        for step, offset, chunk in chunks:
-            start = lax.rem(plane + step, planes) * (members * depth) + offset
-            count = chunk.shape[weight_dim]
-            part = lax.dynamic_slice_in_dim(chip_tokens, start, count, axis=1)
-            total = total + lax.dot_general(
-                part, chunk, (((1,), (weight_dim,)), ((), ())), preferred_element_type=f32
-            )
-        return total
-
     chip_tokens = both(tokens, to_chip(tokens, 0, True))
     grad_halves = output_gradient.reshape(rows, 2, half).transpose(1, 0, 2)
     grad_mine = lax.dynamic_index_in_dim(grad_halves, core, 0, keepdims=False)
@@ -195,42 +228,33 @@
         kv_rows.reshape(members, size + 2 * rank, depth),
         "ctx", 0, 0, tiled=True, axis_index_groups=plain,
     )
-    kv_rows = kv_rows.transpose(1, 0, 2).reshape(size + 2 * rank, members * depth)
-    kv_ahead, kv_back = round_y(kv_rows)
-    kv_last = [
-        to_chip(kv_ahead[-1][:, :cut], chips, False),
-        to_chip(kv_back[-1][:, cut:], -chips, False),
-    ]
-    q_rows = behind(jnp.stack([query_weight[:, :half], query_weight[:, half:]]), kv_rows)
+    kv_rows = lax.all_gather(kv_rows, "ctx", axis=0, tiled=True, axis_index_groups=across)
+    q_rows = jnp.stack([query_weight[:, :half], query_weight[:, half:]])
     q_rows = jnp.broadcast_to(q_rows[None], (chips, *q_rows.shape))
     q_rows = lax.all_to_all(
         q_rows.reshape(members, depth, half),
         "ctx", 0, 0, tiled=True, axis_index_groups=plain,
     )
-
-    mine = project(0.0, kv_ahead, kv_back, kv_last, 1)
+    q_rows = lax.all_gather(
+        q_rows.reshape(members * depth, half),
+        "ctx", axis=0, tiled=True, axis_index_groups=across,
+    )
+
+    kv_weight = kv_rows.transpose(1, 0, 2).reshape(size + 2 * rank, model)
+    mine = lax.dot_general(chip_tokens, kv_weight, NT, preferred_element_type=f32)
     low = mine[:, size:].astype(bf16)
     low_q, low_v = low[:, :rank], low[:, rank:]
     extra = jnp.dot(low_v, value_up_weight, preferred_element_type=f32)
     mine = (mine[:, :size] + jnp.where(core == 1, extra, 0.0)).astype(bf16)
-    q_rows = behind(q_rows.reshape(members * depth, half), kv_ahead[2], kv_back[2])
-    q_ahead, q_back = round_y(q_rows, {3: (mine,)})
-    q_last = [
-        to_chip(q_ahead[-1][:cut], chips, False),
-        to_chip(q_back[-1][cut:], -chips, False),
-    ]
-
     mine = jnp.stack([mine] + [to_chip(mine, d, False) for d in range(1, chips)])
     kv = jnp.stack([mine, to_chip(mine, 0, True)])
 
     up_mine = lax.dynamic_slice_in_dim(query_up_weight, core * half, half, axis=1)
-    query = jnp.dot(low_q, up_mine, preferred_element_type=f32)
-    query = project(query, q_ahead, q_back, q_last, 0).astype(bf16)
-
+    start = jnp.dot(low_q, up_mine, preferred_element_type=f32)
     shifts = lax.dynamic_slice_in_dim(head_shifts, core * (heads // 2), heads // 2)
     seen = jnp.where(shifts != 0, lax.rem(chip + chips // 2, chips), chip)
     info = jnp.concatenate([seen, core[None]]).astype(jnp.int32)
-    output, grad_query, value_parts = attend(info, query, grad_out, kv)
+    output, grad_query, value_parts = attend(info, chip_tokens, q_rows, start, grad_out, kv)
 
     attention_mine = half_of(output, core)
     attention_other = to_chip(half_of(output, 1 - core), 0, True)
@@ -242,52 +266,52 @@
         axis=1,
     )
 
+    rank_q = lax.dot_general(up_mine, grad_query, NT, preferred_element_type=f32).astype(bf16)
+    q_blocks = lax.all_to_all(
+        down_blocks(rank_q, chip_tokens, devices), "ctx", 0, 0, tiled=True
+    )
+
+    query_up_part = lax.dot_general(low_q, grad_query, TN, preferred_element_type=f32)
+    query_up_part = query_up_part.reshape(chips, -1, size)
     value_parts = value_parts.reshape(chips, 2, rows, size).astype(bf16)
     same = lax.dynamic_index_in_dim(value_parts, core, 1, keepdims=False)
     cross = lax.dynamic_index_in_dim(value_parts, 1 - core, 1, keepdims=False)
     value_parts = same.astype(f32) + to_chip(cross, 0, True).astype(f32)
-    arrived = [value_parts[0]]
-    arrived += [to_chip(value_parts[d].astype(bf16), -d, False) for d in range(1, chips)]
-    value_gradient = functools.reduce(jnp.add, [a.astype(f32) for a in arrived]).astype(bf16)
-
-    query_up_part = lax.dot_general(low_q, grad_query, TN, preferred_element_type=f32)
-    query_up_part = behind(query_up_part.astype(bf16), value_parts)
-    query_up_part = query_up_part.reshape(planes, rank // planes, half)
-    query_up_part = lax.all_to_all(
-        query_up_part, "ctx", 0, 0, tiled=True, axis_index_groups=across
-    )
-    query_up_part = jnp.sum(
-        query_up_part.reshape(planes, rank // planes, half).astype(f32), axis=0
+
+    def with_share(d):
+        share = lax.dynamic_index_in_dim(
+            query_up_part, lax.rem(chip + chips - d, chips), 0, keepdims=False
+        )
+        return jnp.concatenate([value_parts[d], share], axis=0)
+
+    arrived = [with_share(0)]
+    arrived += [to_chip(with_share(d).astype(bf16), -d, False) for d in range(1, chips)]
+    arrived = functools.reduce(jnp.add, [a.astype(f32) for a in arrived]).astype(bf16)
+    value_gradient = arrived[:rows]
+
+    rank_v = lax.dot_general(
+        value_up_weight, value_gradient, NT, preferred_element_type=f32
     ).astype(bf16)
-
-    rank_q = lax.dot_general(grad_query, up_mine, NT, preferred_element_type=f32)
-    rank_q = half_of(rank_q, core) + to_chip(half_of(rank_q, 1 - core), 0, True)
-    rank_v = lax.dot_general(value_gradient, value_up_weight, NT, preferred_element_type=f32)
-    rank_terms = jnp.concatenate([rank_q, rank_v], axis=1).astype(bf16)
-    rank_grad = jnp.sum(spread(rank_terms, "fsdp").astype(f32), axis=0).astype(bf16)
-    grad_down = lax.dot_general(rank_grad, tokens, TN, preferred_element_type=f32)
-    grad_down = grad_down.astype(bf16).reshape(2 * rank, devices, depth).transpose(1, 0, 2)
     value_up_part = lax.dot_general(
         half_of(low_v, core), value_gradient, TN, preferred_element_type=f32
     ).astype(bf16)
-    shared = jnp.concatenate(
-        [value_up_part, query_up_part.reshape(-1, size)], axis=0
-    )
-    payload = jnp.concatenate(
-        [grad_down, jnp.broadcast_to(shared[None], (devices, *shared.shape))], axis=1
-    )
-    payload = lax.all_to_all(payload, "ctx", 0, 0, tiled=True)
-    summed = jnp.sum(payload[:, : 3 * rank].astype(f32), axis=0)
-    query_up = payload[:, 3 * rank :].astype(f32)
-    query_up = query_up.reshape(planes, chips, 2, rank // planes, half).sum(axis=1)
+    shared = jnp.concatenate([value_up_part, arrived[rows:]], axis=0)
+    v_blocks = lax.all_to_all(
+        down_blocks(rank_v, tokens, devices, shared), "ctx", 0, 0, tiled=True
+    )
+    grad_down = jnp.concatenate(
+        [
+            jnp.sum(q_blocks.astype(f32), axis=0),
+            jnp.sum(v_blocks[:, :rank].astype(f32), axis=0),
+        ],
+        axis=0,
+    ).astype(bf16)
+    grad_down = jnp.sum(spread(grad_down, "fsdp").astype(f32), axis=0)
+    value_up_gradient = jnp.sum(v_blocks[:, rank : 2 * rank].astype(f32), axis=0)
+    query_up = v_blocks[:, 2 * rank :].astype(f32)
+    query_up = query_up.reshape(planes, chips, 2, rank // chips, half).sum(axis=0)
     query_up_gradient = query_up.transpose(0, 2, 1, 3).reshape(rank, width)
-    return (
-        attention,
-        value_gradient,
-        summed[: 2 * rank].T,
-        query_up_gradient,
-        summed[2 * rank :],
-    )
+    return (attention, value_gradient, grad_down.T, query_up_gradient, value_up_gradient)
 
 
 def solution(mesh):

time: 268 us -> 252 us (0.940)
  starting transfers between devices: 136 us -> 71.5 us
  blocking collectives: 0 us -> 38.1 us
  Pallas kernels: 4.28 us -> 24.4 us
  matrix products: 20 us -> 8.2 us
  between operations: 5.16 us -> 14.6 us
  local copies, waits for them, and re-layouts: 17.6 us -> 9.84 us
  other arithmetic: 12.6 us -> 17.4 us
  waiting for transfers between devices: 71.3 us -> 66.9 us
    ppermute x28 -> x11, starting transfers between devices: 103 us -> 41.8 us  [to_chip(): return lax.ppermute(value, 'ctx', pairs)]
    all_to_all x0 -> x2, blocking collectives: none -> 38.1 us  [the longest x1 20.4 us: on_device(): lax.all_to_all(kv_rows.reshape(members, size + 2 * rank, depth), 'ctx', 0...]
    all_gather x0 -> x2, waiting for transfers between devices: none -> 32.2 us  [the longest x1 19.8 us: on_device(): lax.all_gather(q_rows.reshape(members * depth, half), 'ctx', axis=0, tile...]
    all_to_all x4 -> x2, waiting for transfers between devices: 37.1 us -> 16.3 us  [the longest x1 16.3 us: on_device(): lax.all_to_all(down_blocks(rank_v, tokens, devices, shared), 'ctx', 0, 0,...]
    ppermute x28 -> x11, waiting for transfers between devices: 25 us -> 9.97 us  [to_chip(): return lax.ppermute(value, 'ctx', pairs)]
    pallas_call x1, Pallas kernels: 4.28 us -> 16.7 us  [attend(): pl.pallas_call(functools.partial(attention_kernel, size ** (-0.5), tile),...]
    dot_general x22 -> x4, matrix products: 19.5 us -> 7.7 us  [the longest x1 7.15 us: on_device(): lax.dot_general(chip_tokens, kv_weight, NT, preferred_element_type=f32)]
    pallas_call x0 -> x2, Pallas kernels: none -> 7.71 us  [down_blocks(): pl.pallas_call(blocks_kernel, out_shape=jax.ShapeDtypeStruct((devices, ra...]
  transfers between devices with their start and end apart: 33 -> 16, of which waited for: 10 -> 9; matrix products, arithmetic and copies ran while one was open for 15% -> 10% of each run, Pallas kernels for 0% -> 3%
where the time goes in v5:
time: 252 us; the launch traced here: 251 us
  starting transfers between devices  71.5 us (28%)
  waiting for transfers between devices  66.9 us (27%)
  blocking collectives  38.1 us (15%)
  Pallas kernels  24.4 us (10%)
  other arithmetic  17.4 us (7%)
  between operations  14.6 us (6%)
  local copies, waits for them, and re-layouts  9.84 us (4%)
  matrix products  8.2 us (3%)
    ppermute x11, starting transfers between devices, to_chip(): return lax.ppermute(value, 'ctx', pairs)  41.8 us
    all_to_all x1, blocking collectives, on_device(): lax.all_to_all(kv_rows.reshape(members, size + 2 * rank, depth), 'ctx', 0...  20.4 us
    all_gather x1, waiting for transfers between devices, on_device(): lax.all_gather(q_rows.reshape(members * depth, half), 'ctx', axis=0, tile...  19.8 us
    all_to_all x1, blocking collectives, on_device(): lax.all_to_all(q_rows.reshape(members, depth, half), 'ctx', 0, 0, tiled=T...  17.7 us
    pallas_call x1, Pallas kernels, attend(): pl.pallas_call(functools.partial(attention_kernel, size ** (-0.5), tile),...  16.7 us
    all_to_all x1, waiting for transfers between devices, on_device(): lax.all_to_all(down_blocks(rank_v, tokens, devices, shared), 'ctx', 0, 0,...  16.3 us
    all_to_all x1, starting transfers between devices, on_device(): lax.all_to_all(down_blocks(rank_q, chip_tokens, devices), 'ctx', 0, 0, ti...  13.1 us
    all_gather x1, waiting for transfers between devices, on_device(): lax.all_gather(kv_rows, 'ctx', axis=0, tiled=True, axis_index_groups=across)  12.3 us
  transfers between devices with their start and end apart: 16, of which 9 were waited for; matrix products, arithmetic and copies ran while one was open for 10% of the time, Pallas kernels for 3%

profile of v5, /device:TPU:1, one launch (start us, length us, event | category | flops | bytes accessed | tf_op | source)
XLA Modules:
  0.0 250.9 jit_solution(17514340615922616972)
XLA Ops:
  9.1 20.4 %all_to_all.25 = bf16[8,160,128]{2,1,0:T(8,128)(2,1)} all-to-all(bf16[8,160,128]{2,1,0:T(8,128)(2,1)S(1)} %bitcast.83), channel_id=1, replica_groups={{0,8,16,24,32,40,48,56},{64,72,80,88,96,104,112,120},{128,136,144,152,1..., dimensions={0} | all-to-all | bytes 655360 | tf_op jit(solution)/shard_map/all_to_all | solution.py:227
  33.1 17.7 %all_to_all.26 = bf16[8,128,256]{2,1,0:T(8,128)(2,1)} all-to-all(bf16[8,128,256]{2,1,0:T(8,128)(2,1)S(1)} %bitcast.81), channel_id=1, replica_groups={{0,8,16,24,32,40,48,56},{64,72,80,88,96,104,112,120},{128,136,144,152,1..., dimensions={0} | all-to-all | bytes 1048576 | tf_op jit(solution)/shard_map/all_to_all | solution.py:234
  54.5 5.9 %broadcast_select_fusion.1 = (bf16[256,8192]{1,0:T(8,128)(2,1)}, bf16[256,8192]{1,0:T(8,128)(2,1)}) fusion(bf16[256,8192]{1,0:T(8,128)(2,1)} %tokens.1, bf16[256,8192]{1,0:T(8,128)(2,1)} %collective-permute-done, pred[]{:T(512)S(6)} %eq.4), kind=kLoop, calls=%fused_computation.2 | loop fusion | flops 4194304 | bytes 16777216 | tf_op jit(solution)/shard_map/jit(_where)/select_n | solution.py:210
  60.3 12.3 %all-gather.5.cloned.1.call-done = bf16[64,160,128]{2,1,0:T(8,128)(2,1)} async-done(((bf16[8,160,128]{2,1,0:T(8,128)(2,1)}), bf16[64,160,128]{2,1,0:T(8,128)(2,1)}) %all-gather.5.cloned.1.call-update) | async-done | bytes 2621456 | tf_op jit(solution)/shard_map/all_gather | solution.py:231
  72.7 7.1 %fusion.25 = (bf16[512,160]{0,1:T(8,128)(2,1)S(1)}, f32[512,160]{0,1:T(8,128)S(1)}) fusion(bf16[256,8192]{1,0:T(8,128)(2,1)} %get-tuple-element.14, bf16[256,8192]{1,0:T(8,128)(2,1)} %get-tuple-element.13, bf16[64,160,128]{2,1,0:T(8,128)(2,1)} %all-gather.5.cloned.1.call-done), kind=kOutput, calls=%fused_computation.74 | convolution fusion | flops 1359036416 | bytes 11501568 | tf_op jit(solution)/shard_map/dot_general | solution.py:244
  80.2 3.0 %collective-permute-start.2 = (bf16[512,128]{1,0:T(8,128)(2,1)S(1)}, bf16[512,128]{1,0:T(8,128)(2,1)S(1)}, u32[]{:S(2)}, u32[]{:S(2)}) collective-permute-start(bf16[512,128]{1,0:T(8,128)(2,1)S(1)} %add_convert_fusion), channel_id=1, source_target_pairs={{0,16},{8,24},{16,32},{24,40},{32,48},{40,56},{48,64},{56,72},{64,... | collective-permute-start | bytes 393224 | tf_op jit(solution)/shard_map/ppermute | solution.py:30
  83.2 4.2 %collective-permute-start.3 = (bf16[512,128]{1,0:T(8,128)(2,1)S(1)}, bf16[512,128]{1,0:T(8,128)(2,1)S(1)}, u32[]{:S(2)}, u32[]{:S(2)}) collective-permute-start(bf16[512,128]{1,0:T(8,128)(2,1)S(1)} %add_convert_fusion), channel_id=1, source_target_pairs={{0,32},{8,40},{16,48},{24,56},{32,64},{40,72},{48,80},{56,88},{64,... | collective-permute-start | bytes 393224 | tf_op jit(solution)/shard_map/ppermute | solution.py:30
  87.4 4.0 %collective-permute-start.4 = (bf16[512,128]{1,0:T(8,128)(2,1)S(1)}, bf16[512,128]{1,0:T(8,128)(2,1)S(1)}, u32[]{:S(2)}, u32[]{:S(2)}) collective-permute-start(bf16[512,128]{1,0:T(8,128)(2,1)S(1)} %add_convert_fusion), channel_id=1, source_target_pairs={{0,48},{8,56},{16,64},{24,72},{32,80},{40,88},{48,96},{56,104},{64... | collective-permute-start | bytes 393224 | tf_op jit(solution)/shard_map/ppermute | solution.py:30
  92.4 4.5 %collective-permute-done.4 = bf16[512,128]{1,0:T(8,128)(2,1)S(1)} collective-permute-done((bf16[512,128]{1,0:T(8,128)(2,1)S(1)}, bf16[512,128]{1,0:T(8,128)(2,1)S(1)}, u32[]{:S(2)}, u32[]{:S(2)}) %collective-permute-start.4) | collective-permute-done | bytes 131104 | tf_op jit(solution)/shard_map/ppermute | solution.py:30
  97.0 8.4 %collective-permute-start.5 = (bf16[4,512,128]{2,1,0:T(8,128)(2,1)S(1)}, bf16[4,512,128]{2,1,0:T(8,128)(2,1)S(1)}, u32[]{:S(2)}, u32[]{:S(2)}) collective-permute-start(bf16[4,512,128]{2,1,0:T(8,128)(2,1)S(1)} %get-tuple-element.16), channel_id=1, source_target_pairs={{0,8},{8,0},{16,24},{24,16},{32,40},{40,32},{48,56},{56,48},{64,72... | collective-permute-start | bytes 1572872 | tf_op jit(solution)/shard_map/ppermute | solution.py:30
  105.4 7.8 %pad_maximum_fusion.tokens = bf16[512,8192]{1,0:T(8,128)(2,1)} fusion(bf16[256,8192]{1,0:T(8,128)(2,1)} %get-tuple-element.14, bf16[256,8192]{1,0:T(8,128)(2,1)} %get-tuple-element.13), kind=kLoop, calls=%fused_computation | loop fusion | flops 16777216 | bytes 16777216 | tf_op jit(solution)/shard_map/concatenate | solution.py:209
  113.6 19.8 %all-gather.3.cloned.1.call-done.weight = bf16[8192,256]{1,0:T(8,128)(2,1)} async-done(((bf16[1024,256]{1,0:T(8,128)(2,1)}), bf16[8192,256]{1,0:T(8,128)(2,1)}) %all-gather.3.cloned.1.call-update) | async-done | bytes 4194320 | tf_op jit(solution)/shard_map/all_gather | solution.py:238
  133.4 16.7 %attention.1 = (bf16[512,256]{1,0:T(8,128)(2,1)S(1)}, bf16[512,256]{1,0:T(8,128)(2,1)S(1)}, f32[4,512,128]{2,1,0:T(8,128)S(1)}) custom-call(s32[3]{0:T(128)S(1)} %pad_add_fusion.info, bf16[512,8192]{1,0:T(8,128)(2,1)} %pad_maximum_fusion.tokens, bf16[8192,256]{1,0:T(8,128)(2,1)} %all-gather.3.cloned.1.call-done.weight, f32[512,256]{1,0:T(8,128)S(1)} %fusion.11.start, ...), custom_call_target="tpu_custom_call" | custom-call | flops 4831838208 | bytes 16777216 | tf_op jit(solution)/shard_map/attention/pallas_call | solution.py:113
  152.4 3.4 %copy-done.1 = bf16[512,8192]{1,0:T(8,128)(2,1)S(1)} copy-done((bf16[512,8192]{1,0:T(8,128)(2,1)S(1)}, bf16[512,8192]{1,0:T(8,128)(2,1)}, u32[]{:S(2)}) %copy-start.1) | copy-done | bytes 8388632
  155.8 4.1 %down_blocks.2 = bf16[64,16,128]{2,1,0:T(8,128)(2,1)} custom-call(bf16[16,512]{1,0:T(8,128)(2,1)S(1)} %convolution_convert_fusion.rank_terms.shared, bf16[512,8192]{1,0:T(8,128)(2,1)S(1)} %copy-done.1, bf16[16,512]{1,0:T(8,128)(2,1)S(1)} %convolution_convert_fusion.rank_terms.shared), custom_call_target="tpu_custom_call" | custom-call | flops 134217728 | bytes 8388608 | tf_op jit(solution)/shard_map/down_blocks/pallas_call | solution.py:160
  159.9 13.1 %all-to-all-start.2 = ((bf16[64,16,128]{2,1,0:T(8,128)(2,1)}), bf16[64,16,128]{2,1,0:T(8,128)(2,1)S(1)}, u32[]{:S(2)}, u32[]{:S(2)}) async-start(bf16[64,16,128]{2,1,0:T(8,128)(2,1)} %down_blocks.2), calls=%async_computation.2 | async-start | bytes 524288 | tf_op jit(solution)/shard_map/all_to_all | solution.py:270
  173.2 7.5 %collective-permute-start.8 = (bf16[264,128]{1,0:T(8,128)(2,1)S(1)}, bf16[264,128]{1,0:T(8,128)(2,1)S(1)}, u32[]{:S(2)}, u32[]{:S(2)}) collective-permute-start(bf16[264,128]{1,0:T(8,128)(2,1)S(1)} %pad_maximum_fusion.9), channel_id=1, source_target_pairs={{0,496},{8,504},{16,0},{24,8},{32,16},{40,24},{48,32},{56,40},{64,... | collective-permute-start | bytes 202760 | tf_op jit(solution)/shard_map/ppermute | solution.py:30
  182.7 3.3 %collective-permute-start.10 = (bf16[264,128]{1,0:T(8,128)(2,1)S(1)}, bf16[264,128]{1,0:T(8,128)(2,1)S(1)}, u32[]{:S(2)}, u32[]{:S(2)}) collective-permute-start(bf16[264,128]{1,0:T(8,128)(2,1)S(1)} %pad_maximum_fusion.11), channel_id=1, source_target_pairs={{0,464},{8,472},{16,480},{24,488},{32,496},{40,504},{48,0},{56,8},... | collective-permute-start | bytes 202760 | tf_op jit(solution)/shard_map/ppermute | solution.py:30
  186.8 2.7 %collective-permute-done.10 = bf16[264,128]{1,0:T(8,128)(2,1)S(1)} collective-permute-done((bf16[264,128]{1,0:T(8,128)(2,1)S(1)}, bf16[264,128]{1,0:T(8,128)(2,1)S(1)}, u32[]{:S(2)}, u32[]{:S(2)}) %collective-permute-start.10) | collective-permute-done | bytes 67616 | tf_op jit(solution)/shard_map/ppermute | solution.py:30
  192.1 3.6 %down_blocks.3 = bf16[64,40,128]{2,1,0:T(8,128)(2,1)} custom-call(bf16[16,256]{1,0:T(8,128)(2,1)S(1)} %fusion.3.rank_terms, bf16[256,8192]{1,0:T(8,128)(2,1)S(1)} %copy-done.2, bf16[24,128]{1,0:T(8,128)(2,1)S(1)} %pad_maximum_fusion.13.shared), custom_call_target="tpu_custom_call" | custom-call | flops 67108864 | bytes 4194304 | tf_op jit(solution)/shard_map/down_blocks/pallas_call | solution.py:160
  195.7 8.2 %all-to-all-start.3 = ((bf16[64,40,128]{2,1,0:T(8,128)(2,1)}), bf16[64,40,128]{2,1,0:T(8,128)(2,1)S(1)}, u32[]{:S(2)}, u32[]{:S(2)}) async-start(bf16[64,40,128]{2,1,0:T(8,128)(2,1)} %down_blocks.3), calls=%async_computation.3 | async-start | bytes 1310720 | tf_op jit(solution)/shard_map/all_to_all | solution.py:299
  208.2 16.3 %all-to-all-done.3 = bf16[64,40,128]{2,1,0:T(8,128)(2,1)S(1)} async-done(((bf16[64,40,128]{2,1,0:T(8,128)(2,1)}), bf16[64,40,128]{2,1,0:T(8,128)(2,1)S(1)}, u32[]{:S(2)}, u32[]{:S(2)}) %all-to-all-start.3) | async-done | bytes 655392 | tf_op jit(solution)/shard_map/all_to_all | solution.py:299
  226.0 8.3 %all-to-all-start.4 = ((bf16[8,32,128]{2,1,0:T(8,128)(2,1)}), bf16[8,32,128]{2,1,0:T(8,128)(2,1)S(1)}, u32[]{:S(2)}, u32[]{:S(2)}) async-start(bf16[8,32,128]{2,1,0:T(8,128)(2,1)} %broadcast_in_dim.39), calls=%async_computation.4 | async-start | bytes 131072 | tf_op jit(solution)/shard_map/all_to_all | solution.py:20
  235.0 8.4 %all-to-all-done.4 = bf16[8,32,128]{2,1,0:T(8,128)(2,1)S(1)} async-done(((bf16[8,32,128]{2,1,0:T(8,128)(2,1)}), bf16[8,32,128]{2,1,0:T(8,128)(2,1)S(1)}, u32[]{:S(2)}, u32[]{:S(2)}) %all-to-all-start.4) | async-done | bytes 65568 | tf_op jit(solution)/shard_map/all_to_all | solution.py:20
  (87 shorter events, 25.6 us)
Async XLA Ops:
  7.2 106.1 %copy-start = (bf16[16,512]{1,0:T(8,128)(2,1)S(1)}, bf16[16,512]{1,0:T(8,128)(2,1)}, u32[]{:S(2)}) copy-start(bf16[16,512]{1,0:T(8,128)(2,1)} %param.14) | copy-start | bytes 49156
  7.2 43.7 %copy-start.4 = (bf16[256,512]{1,0:T(8,128)(2,1)S(1)}, bf16[256,512]{1,0:T(8,128)(2,1)}, u32[]{:S(2)}) copy-start(bf16[256,512]{1,0:T(8,128)(2,1)} %param.17) | copy-start | bytes 786436
  7.2 47.1 %copy-start.6 = (s32[4]{0:T(128)S(1)}, s32[4]{0:T(128)}, u32[]{:S(2)}) copy-start(s32[4]{0:T(128)} %param.16) | copy-start | bytes 52
  7.2 65.5 %all-gather.5.cloned.1.call-start = ((), (), s32[]{:S(2)}) async-start(), calls=%async_computation.6 | async-start | bytes 2949120 | tf_op jit(solution)/shard_map/all_gather | solution.py:231
  29.5 103.9 %all-gather.3.cloned.1.call-start = ((), (), s32[]{:S(2)}) async-start(), calls=%async_computation.5 | async-start | bytes 4718592 | tf_op jit(solution)/shard_map/all_gather | solution.py:238
  29.5 24.9 %collective-permute-start = (bf16[256,8192]{1,0:T(8,128)(2,1)}, bf16[256,8192]{1,0:T(8,128)(2,1)}, u32[]{:S(2)}, u32[]{:S(2)}) collective-permute-start(bf16[256,8192]{1,0:T(8,128)(2,1)} %tokens.1), channel_id=1, source_target_pairs={{0,8},{8,0},{16,24},{24,16},{32,40},{40,32},{48,56},{56,48},{64,72... | collective-permute-start | bytes 12582920 | tf_op jit(solution)/shard_map/ppermute | solution.py:30
  51.6 39.8 %collective-permute-start.1 = (bf16[256,256]{1,0:T(8,128)(2,1)S(1)}, bf16[256,256]{1,0:T(8,128)(2,1)S(1)}, u32[]{:S(2)}, u32[]{:S(2)}) collective-permute-start(bf16[256,256]{1,0:T(8,128)(2,1)S(1)} %bitcast.86), channel_id=1, source_target_pairs={{0,8},{8,0},{16,24},{24,16},{32,40},{40,32},{48,56},{56,48},{64,72... | collective-permute-start | bytes 393224 | tf_op jit(solution)/shard_map/ppermute | solution.py:30
  72.7 7.3 %copy-start.5 = (bf16[16,128]{1,0:T(8,128)(2,1)S(1)}, bf16[16,128]{1,0:T(8,128)(2,1)}, u32[]{:S(2)}) copy-start(bf16[16,128]{1,0:T(8,128)(2,1)} %param.15) | copy-start | bytes 12292
  80.2 11.2 %collective-permute-start.2 = (bf16[512,128]{1,0:T(8,128)(2,1)S(1)}, bf16[512,128]{1,0:T(8,128)(2,1)S(1)}, u32[]{:S(2)}, u32[]{:S(2)}) collective-permute-start(bf16[512,128]{1,0:T(8,128)(2,1)S(1)} %add_convert_fusion), channel_id=1, source_target_pairs={{0,16},{8,24},{16,32},{24,40},{32,48},{40,56},{48,64},{56,72},{64,... | collective-permute-start | bytes 393224 | tf_op jit(solution)/shard_map/ppermute | solution.py:30
  83.2 9.2 %collective-permute-start.3 = (bf16[512,128]{1,0:T(8,128)(2,1)S(1)}, bf16[512,128]{1,0:T(8,128)(2,1)S(1)}, u32[]{:S(2)}, u32[]{:S(2)}) collective-permute-start(bf16[512,128]{1,0:T(8,128)(2,1)S(1)} %add_convert_fusion), channel_id=1, source_target_pairs={{0,32},{8,40},{16,48},{24,56},{32,64},{40,72},{48,80},{56,88},{64,... | collective-permute-start | bytes 393224 | tf_op jit(solution)/shard_map/ppermute | solution.py:30
  87.4 9.5 %collective-permute-start.4 = (bf16[512,128]{1,0:T(8,128)(2,1)S(1)}, bf16[512,128]{1,0:T(8,128)(2,1)S(1)}, u32[]{:S(2)}, u32[]{:S(2)}) collective-permute-start(bf16[512,128]{1,0:T(8,128)(2,1)S(1)} %add_convert_fusion), channel_id=1, source_target_pairs={{0,48},{8,56},{16,64},{24,72},{32,80},{40,88},{48,96},{56,104},{64... | collective-permute-start | bytes 393224 | tf_op jit(solution)/shard_map/ppermute | solution.py:30
  97.0 16.5 %collective-permute-start.5 = (bf16[4,512,128]{2,1,0:T(8,128)(2,1)S(1)}, bf16[4,512,128]{2,1,0:T(8,128)(2,1)S(1)}, u32[]{:S(2)}, u32[]{:S(2)}) collective-permute-start(bf16[4,512,128]{2,1,0:T(8,128)(2,1)S(1)} %get-tuple-element.16), channel_id=1, source_target_pairs={{0,8},{8,0},{16,24},{24,16},{32,40},{40,32},{48,56},{56,48},{64,72... | collective-permute-start | bytes 1572872 | tf_op jit(solution)/shard_map/ppermute | solution.py:30
  150.2 22.9 %collective-permute-start.7 = (bf16[4,256,128]{2,1,0:T(8,128)(2,1)S(1)}, bf16[4,256,128]{2,1,0:T(8,128)(2,1)S(1)}, u32[]{:S(2)}, u32[]{:S(2)}) collective-permute-start(bf16[4,256,128]{2,1,0:T(8,128)(2,1)S(1)} %dynamic-slice_bitcast_fusion), channel_id=1, source_target_pairs={{0,8},{8,0},{16,24},{24,16},{32,40},{40,32},{48,56},{56,48},{64,72... | collective-permute-start | bytes 786440 | tf_op jit(solution)/shard_map/ppermute | solution.py:30
  152.4 3.4 %copy-start.1 = (bf16[512,8192]{1,0:T(8,128)(2,1)S(1)}, bf16[512,8192]{1,0:T(8,128)(2,1)}, u32[]{:S(2)}) copy-start(bf16[512,8192]{1,0:T(8,128)(2,1)} %pad_maximum_fusion.tokens) | copy-start | bytes 25165828
  159.9 35.8 %all-to-all-start.2 = ((bf16[64,16,128]{2,1,0:T(8,128)(2,1)}), bf16[64,16,128]{2,1,0:T(8,128)(2,1)S(1)}, u32[]{:S(2)}, u32[]{:S(2)}) async-start(bf16[64,16,128]{2,1,0:T(8,128)(2,1)} %down_blocks.2), calls=%async_computation.2 | async-start | bytes 524288 | tf_op jit(solution)/shard_map/all_to_all | solution.py:270
  173.2 12.8 %collective-permute-start.8 = (bf16[264,128]{1,0:T(8,128)(2,1)S(1)}, bf16[264,128]{1,0:T(8,128)(2,1)S(1)}, u32[]{:S(2)}, u32[]{:S(2)}) collective-permute-start(bf16[264,128]{1,0:T(8,128)(2,1)S(1)} %pad_maximum_fusion.9), channel_id=1, source_target_pairs={{0,496},{8,504},{16,0},{24,8},{32,16},{40,24},{48,32},{56,40},{64,... | collective-permute-start | bytes 202760 | tf_op jit(solution)/shard_map/ppermute | solution.py:30
  180.8 6.1 %collective-permute-start.9 = (bf16[264,128]{1,0:T(8,128)(2,1)S(1)}, bf16[264,128]{1,0:T(8,128)(2,1)S(1)}, u32[]{:S(2)}, u32[]{:S(2)}) collective-permute-start(bf16[264,128]{1,0:T(8,128)(2,1)S(1)} %pad_maximum_fusion.10), channel_id=1, source_target_pairs={{0,480},{8,488},{16,496},{24,504},{32,0},{40,8},{48,16},{56,24},{6... | collective-permute-start | bytes 202760 | tf_op jit(solution)/shard_map/ppermute | solution.py:30
  182.7 6.8 %collective-permute-start.10 = (bf16[264,128]{1,0:T(8,128)(2,1)S(1)}, bf16[264,128]{1,0:T(8,128)(2,1)S(1)}, u32[]{:S(2)}, u32[]{:S(2)}) collective-permute-start(bf16[264,128]{1,0:T(8,128)(2,1)S(1)} %pad_maximum_fusion.11), channel_id=1, source_target_pairs={{0,464},{8,472},{16,480},{24,488},{32,496},{40,504},{48,0},{56,8},... | collective-permute-start | bytes 202760 | tf_op jit(solution)/shard_map/ppermute | solution.py:30
  189.6 35.0 %copy-start.3 = (bf16[256,128]{1,0:T(8,128)(2,1)}, bf16[256,128]{1,0:T(8,128)(2,1)S(1)}, u32[]{:S(2)}) copy-start(bf16[256,128]{1,0:T(8,128)(2,1)S(1)} %slice.70) | copy-start | bytes 196612
  189.9 2.2 copy-start.2
  195.7 28.7 %all-to-all-start.3 = ((bf16[64,40,128]{2,1,0:T(8,128)(2,1)}), bf16[64,40,128]{2,1,0:T(8,128)(2,1)S(1)}, u32[]{:S(2)}, u32[]{:S(2)}) async-start(bf16[64,40,128]{2,1,0:T(8,128)(2,1)} %down_blocks.3), calls=%async_computation.3 | async-start | bytes 1310720 | tf_op jit(solution)/shard_map/all_to_all | solution.py:299
  203.9 3.3 %collective-permute-start.6 = (bf16[256,256]{1,0:T(8,128)(2,1)S(1)}, bf16[256,256]{1,0:T(8,128)(2,1)S(1)}, u32[]{:S(2)}, u32[]{:S(2)}) collective-permute-start(bf16[256,256]{1,0:T(8,128)(2,1)S(1)} %constant_dynamic-slice_fusion), channel_id=1, source_target_pairs={{0,8},{8,0},{16,24},{24,16},{32,40},{40,32},{48,56},{56,48},{64,72... | collective-permute-start | bytes 393224 | tf_op jit(solution)/shard_map/ppermute | solution.py:30
  226.0 17.4 %all-to-all-start.4 = ((bf16[8,32,128]{2,1,0:T(8,128)(2,1)}), bf16[8,32,128]{2,1,0:T(8,128)(2,1)S(1)}, u32[]{:S(2)}, u32[]{:S(2)}) async-start(bf16[8,32,128]{2,1,0:T(8,128)(2,1)} %broadcast_in_dim.39), calls=%async_computation.4 | async-start | bytes 131072 | tf_op jit(solution)/shard_map/all_to_all | solution.py:20
Sparse Core Ops, SparseCore 0:
  29.6 43.0 all-gather.4
  74.7 58.6 all-gather.2

commit v6 on v5

--- a/solution.py
+++ b/solution.py
@@ -32,26 +32,29 @@
 
 def attention_kernel(
     scale, tile, info, tokens, weight, start, grad_out, kv,
-    out, grad_query, grad_value, query, parts, arrivals,
+    out, grad_query, grad_value, query, columns_in, rows_in, arrivals,
 ):
     rows, size = query.shape[0], kv.shape[-1]
     heads = query.shape[1] // size
     blocks, block = kv.shape[1:3]
     keys = [kv.at[info[heads], d] for d in range(blocks)]
     values = [kv.at[1 - info[heads], d] for d in range(blocks)]
-    count, depth = parts.shape[:2]
-    copies = [
-        pltpu.make_async_copy(weight.at[pl.ds(i * depth, depth)], parts.at[i], arrivals.at[i])
-        for i in range(count)
-    ]
+    parts, depth = rows_in.shape[:2]
+    copies = []
+    for i in range(parts):
+        here = pl.ds(i * depth, depth)
+        copies += [
+            pltpu.make_async_copy(tokens.at[:, here], columns_in.at[i], arrivals.at[2 * i]),
+            pltpu.make_async_copy(weight.at[here], rows_in.at[i], arrivals.at[2 * i + 1]),
+        ]
     for copy in copies:
         copy.start()
     grad_value[...] = jnp.zeros_like(grad_value)
     total = start[...]
-    for i, copy in enumerate(copies):
-        copy.wait()
-        part = tokens[:, i * depth : (i + 1) * depth]
-        total = total + jnp.dot(part, parts[i], preferred_element_type=f32)
+    for i in range(parts):
+        copies[2 * i].wait()
+        copies[2 * i + 1].wait()
+        total = total + jnp.dot(columns_in[i], rows_in[i], preferred_element_type=f32)
     query[...] = total.astype(bf16)
 
     def tile_of(index, columns, count):
@@ -119,7 +122,7 @@
         ),
         in_specs=[
             pl.BlockSpec(memory_space=pltpu.SMEM),
-            vmem,
+            pl.BlockSpec(memory_space=pl.ANY),
             pl.BlockSpec(memory_space=pl.ANY),
             vmem,
             vmem,
@@ -128,8 +131,9 @@
         out_specs=(vmem, vmem, vmem),
         scratch_shapes=[
             pltpu.VMEM((rows, width), bf16),
+            pltpu.VMEM((parts, rows, model // parts), bf16),
             pltpu.VMEM((parts, model // parts, width), bf16),
-            pltpu.SemaphoreType.DMA((parts,)),
+            pltpu.SemaphoreType.DMA((2 * parts,)),
         ],
         compiler_params=pltpu.CompilerParams(vmem_limit_bytes=48 * 1024 * 1024),
         cost_estimate=pl.CostEstimate(
@@ -141,40 +145,53 @@
     )(info, tokens, weight, start, grad_out, kv)
 
 
-def blocks_kernel(rank_terms, tokens, shared, out):
-    ranks, size = rank_terms.shape[0], out.shape[2]
+def blocks_kernel(rank_terms, tokens, above, below, out):
+    top, size = above.shape[1], out.shape[2]
+    bottom = top + rank_terms.shape[0]
     product = jnp.dot(rank_terms[...], tokens[...], preferred_element_type=f32).astype(bf16)
     for i in range(out.shape[0]):
-        out[i, :ranks] = product[:, i * size : (i + 1) * size]
-        if out.shape[1] > ranks:
-            out[i, ranks:] = shared[...]
-
-
-def down_blocks(rank_terms, tokens, devices, shared=None, steps=8):
+        out[i, :top] = above[i]
+        out[i, top:bottom] = product[:, i * size : (i + 1) * size]
+        out[i, bottom:] = below[...]
+
+
+def first_blocks_kernel(rank_terms, tokens, out):
+    size = out.shape[2]
+    product = jnp.dot(rank_terms[...], tokens[...], preferred_element_type=f32).astype(bf16)
+    for i in range(out.shape[0]):
+        out[i] = product[:, i * size : (i + 1) * size]
+
+
+def down_blocks(rank_terms, tokens, devices, above=None, below=None, steps=4):
     ranks, rows = rank_terms.shape
     size = tokens.shape[1] // devices
-    extra = 0 if shared is None else shared.shape[0]
-    if shared is None:
-        shared = rank_terms
     step = devices // steps
+    in_specs = [
+        pl.BlockSpec((ranks, rows), lambda i: (0, 0)),
+        pl.BlockSpec((rows, step * size), lambda i: (0, i)),
+    ]
+    more, height, kernel = (), ranks, first_blocks_kernel
+    if above is not None:
+        more, kernel = (above, below), blocks_kernel
+        height += above.shape[1] + below.shape[0]
+        in_specs += [
+            pl.BlockSpec((step, *above.shape[1:]), lambda i: (i, 0, 0)),
+            pl.BlockSpec(below.shape, lambda i: (0, 0)),
+        ]
     return pl.pallas_call(
-        blocks_kernel,
-        out_shape=jax.ShapeDtypeStruct((devices, ranks + extra, size), bf16),
+        kernel,
+        out_shape=jax.ShapeDtypeStruct((devices, height, size), bf16),
         grid=(steps,),
-        in_specs=[
-            pl.BlockSpec((ranks, rows), lambda i: (0, 0)),
-            pl.BlockSpec((rows, step * size), lambda i: (0, i)),
-            pl.BlockSpec(shared.shape, lambda i: (0, 0)),
-        ],
-        out_specs=pl.BlockSpec((step, ranks + extra, size), lambda i: (i, 0, 0)),
-        compiler_params=pltpu.CompilerParams(vmem_limit_bytes=24 * 1024 * 1024),
+        in_specs=in_specs,
+        out_specs=pl.BlockSpec((step, height, size), lambda i: (i, 0, 0)),
+        compiler_params=pltpu.CompilerParams(vmem_limit_bytes=56 * 1024 * 1024),
         cost_estimate=pl.CostEstimate(
             flops=2 * ranks * rows * devices * size,
             bytes_accessed=2 * rows * devices * size,
             transcendentals=0,
         ),
         name="down_blocks",
-    )(rank_terms, tokens, shared)
+    )(rank_terms, tokens, *more)
 
 
 def on_device(
@@ -267,9 +284,7 @@
     )
 
     rank_q = lax.dot_general(up_mine, grad_query, NT, preferred_element_type=f32).astype(bf16)
-    q_blocks = lax.all_to_all(
-        down_blocks(rank_q, chip_tokens, devices), "ctx", 0, 0, tiled=True
-    )
+    q_blocks = down_blocks(rank_q, chip_tokens, devices)
 
     query_up_part = lax.dot_general(low_q, grad_query, TN, preferred_element_type=f32)
     query_up_part = query_up_part.reshape(chips, -1, size)
@@ -296,19 +311,12 @@
         half_of(low_v, core), value_gradient, TN, preferred_element_type=f32
     ).astype(bf16)
     shared = jnp.concatenate([value_up_part, arrived[rows:]], axis=0)
-    v_blocks = lax.all_to_all(
-        down_blocks(rank_v, tokens, devices, shared), "ctx", 0, 0, tiled=True
-    )
-    grad_down = jnp.concatenate(
-        [
-            jnp.sum(q_blocks.astype(f32), axis=0),
-            jnp.sum(v_blocks[:, :rank].astype(f32), axis=0),
-        ],
-        axis=0,
-    ).astype(bf16)
-    grad_down = jnp.sum(spread(grad_down, "fsdp").astype(f32), axis=0)
-    value_up_gradient = jnp.sum(v_blocks[:, rank : 2 * rank].astype(f32), axis=0)
-    query_up = v_blocks[:, 2 * rank :].astype(f32)
+    blocks = down_blocks(rank_v, tokens, devices, q_blocks, shared)
+    blocks = lax.all_to_all(blocks, "ctx", 0, 0, tiled=True)
+    summed = jnp.sum(blocks[:, : 3 * rank].astype(f32), axis=0)
+    grad_down = jnp.sum(spread(summed[: 2 * rank].astype(bf16), "fsdp").astype(f32), axis=0)
+    value_up_gradient = summed[2 * rank :]
+    query_up = blocks[:, 3 * rank :].astype(f32)
     query_up = query_up.reshape(planes, chips, 2, rank // chips, half).sum(axis=0)
     query_up_gradient = query_up.transpose(0, 2, 1, 3).reshape(rank, width)
     return (attention, value_gradient, grad_down.T, query_up_gradient, value_up_gradient)

time: 252 us -> 241 us (0.956)
  starting transfers between devices: 71.5 us -> 61.5 us
  local copies, waits for them, and re-layouts: 9.84 us -> 4.8 us
  waiting for transfers between devices: 66.9 us -> 71.6 us
    all_to_all x2 -> x1, starting transfers between devices: 21.3 us -> 8.08 us  [on_device(): blocks = lax.all_to_all(blocks, 'ctx', 0, 0, tiled=True)]
    unnamed x17 -> x13, local copies, waits for them, and re-layouts: 6.41 us -> 0.79 us
    all_to_all x2 -> x1, waiting for transfers between devices: 16.3 us -> 21.5 us  [on_device(): blocks = lax.all_to_all(blocks, 'ctx', 0, 0, tiled=True)]
    ppermute x11, starting transfers between devices: 41.8 us -> 46.4 us  [to_chip(): return lax.ppermute(value, 'ctx', pairs)]
    pallas_call x1, Pallas kernels: 16.7 us -> 12.4 us  [attend(): pl.pallas_call(functools.partial(attention_kernel, size ** (-0.5), tile),...]
  transfers between devices with their start and end apart: 16 -> 15, of which waited for: 9 -> 9; matrix products, arithmetic and copies ran while one was open for 10% -> 11% of each run, Pallas kernels for 3% -> 2%
where the time goes in v6:
time: 241 us; the launch traced here: 240 us
  waiting for transfers between devices  71.6 us (30%)
  starting transfers between devices  61.5 us (26%)
  blocking collectives  38.1 us (16%)
  Pallas kernels  22.3 us (9%)
  other arithmetic  17.4 us (7%)
  between operations  14.6 us (6%)
  matrix products  9.44 us (4%)
  local copies, waits for them, and re-layouts  4.8 us (2%)
    ppermute x11, starting transfers between devices, to_chip(): return lax.ppermute(value, 'ctx', pairs)  46.4 us
    all_to_all x1, waiting for transfers between devices, on_device(): blocks = lax.all_to_all(blocks, 'ctx', 0, 0, tiled=True)  21.5 us
    all_to_all x1, blocking collectives, on_device(): lax.all_to_all(kv_rows.reshape(members, size + 2 * rank, depth), 'ctx', 0...  20.4 us
    all_gather x1, waiting for transfers between devices, on_device(): lax.all_gather(q_rows.reshape(members * depth, half), 'ctx', axis=0, tile...  19.8 us
    all_to_all x1, blocking collectives, on_device(): lax.all_to_all(q_rows.reshape(members, depth, half), 'ctx', 0, 0, tiled=T...  17.7 us
    pallas_call x1, Pallas kernels, attend(): pl.pallas_call(functools.partial(attention_kernel, size ** (-0.5), tile),...  12.4 us
    all_gather x1, waiting for transfers between devices, on_device(): lax.all_gather(kv_rows, 'ctx', axis=0, tiled=True, axis_index_groups=across)  12.1 us
    ppermute x11, waiting for transfers between devices, to_chip(): return lax.ppermute(value, 'ctx', pairs)  10.5 us
  transfers between devices with their start and end apart: 15, of which 9 were waited for; matrix products, arithmetic and copies ran while one was open for 11% of the time, Pallas kernels for 2%

profile of v6, /device:TPU:1, one launch (start us, length us, event | category | flops | bytes accessed | tf_op | source)
XLA Modules:
  0.0 239.7 jit_solution(6960807271709841841)
XLA Ops:
  9.1 20.4 %all_to_all.20 = bf16[8,160,128]{2,1,0:T(8,128)(2,1)} all-to-all(bf16[8,160,128]{2,1,0:T(8,128)(2,1)S(1)} %bitcast.83), channel_id=1, replica_groups={{0,8,16,24,32,40,48,56},{64,72,80,88,96,104,112,120},{128,136,144,152,1..., dimensions={0} | all-to-all | bytes 655360 | tf_op jit(solution)/shard_map/all_to_all | solution.py:244
  29.5 2.7 %collective-permute-start = (bf16[256,8192]{1,0:T(8,128)(2,1)}, bf16[256,8192]{1,0:T(8,128)(2,1)}, u32[]{:S(2)}, u32[]{:S(2)}) collective-permute-start(bf16[256,8192]{1,0:T(8,128)(2,1)} %tokens.1), channel_id=1, source_target_pairs={{0,8},{8,0},{16,24},{24,16},{32,40},{40,32},{48,56},{56,48},{64,72... | collective-permute-start | bytes 12582920 | tf_op jit(solution)/shard_map/ppermute | solution.py:30
  33.2 17.7 %all_to_all.21 = bf16[8,128,256]{2,1,0:T(8,128)(2,1)} all-to-all(bf16[8,128,256]{2,1,0:T(8,128)(2,1)S(1)} %bitcast.81), channel_id=1, replica_groups={{0,8,16,24,32,40,48,56},{64,72,80,88,96,104,112,120},{128,136,144,152,1..., dimensions={0} | all-to-all | bytes 1048576 | tf_op jit(solution)/shard_map/all_to_all | solution.py:251
  51.6 2.7 %collective-permute-start.1 = (bf16[256,256]{1,0:T(8,128)(2,1)S(1)}, bf16[256,256]{1,0:T(8,128)(2,1)S(1)}, u32[]{:S(2)}, u32[]{:S(2)}) collective-permute-start(bf16[256,256]{1,0:T(8,128)(2,1)S(1)} %bitcast.86), channel_id=1, source_target_pairs={{0,8},{8,0},{16,24},{24,16},{32,40},{40,32},{48,56},{56,48},{64,72... | collective-permute-start | bytes 393224 | tf_op jit(solution)/shard_map/ppermute | solution.py:30
  54.5 5.9 %broadcast_select_fusion.1 = (bf16[256,8192]{1,0:T(8,128)(2,1)}, bf16[256,8192]{1,0:T(8,128)(2,1)}) fusion(bf16[256,8192]{1,0:T(8,128)(2,1)} %tokens.1, bf16[256,8192]{1,0:T(8,128)(2,1)} %collective-permute-done, pred[]{:T(512)S(6)} %eq.4), kind=kLoop, calls=%fused_computation.2 | loop fusion | flops 4194304 | bytes 16777216 | tf_op jit(solution)/shard_map/jit(_where)/select_n | solution.py:227
  60.3 12.1 %all-gather.5.cloned.1.call-done = bf16[64,160,128]{2,1,0:T(8,128)(2,1)} async-done(((bf16[8,160,128]{2,1,0:T(8,128)(2,1)}), bf16[64,160,128]{2,1,0:T(8,128)(2,1)}) %all-gather.5.cloned.1.call-update) | async-done | bytes 2621456 | tf_op jit(solution)/shard_map/all_gather | solution.py:248
  72.4 7.1 %fusion.25 = (bf16[512,160]{0,1:T(8,128)(2,1)S(1)}, f32[512,160]{0,1:T(8,128)S(1)}) fusion(bf16[256,8192]{1,0:T(8,128)(2,1)} %get-tuple-element.14, bf16[256,8192]{1,0:T(8,128)(2,1)} %get-tuple-element.13, bf16[64,160,128]{2,1,0:T(8,128)(2,1)} %all-gather.5.cloned.1.call-done), kind=kOutput, calls=%fused_computation.73 | convolution fusion | flops 1359036416 | bytes 11501568 | tf_op jit(solution)/shard_map/dot_general | solution.py:261
  80.0 3.4 %collective-permute-start.2 = (bf16[512,128]{1,0:T(8,128)(2,1)S(1)}, bf16[512,128]{1,0:T(8,128)(2,1)S(1)}, u32[]{:S(2)}, u32[]{:S(2)}) collective-permute-start(bf16[512,128]{1,0:T(8,128)(2,1)S(1)} %add_convert_fusion), channel_id=1, source_target_pairs={{0,16},{8,24},{16,32},{24,40},{32,48},{40,56},{48,64},{56,72},{64,... | collective-permute-start | bytes 393224 | tf_op jit(solution)/shard_map/ppermute | solution.py:30
  83.4 4.0 %collective-permute-start.3 = (bf16[512,128]{1,0:T(8,128)(2,1)S(1)}, bf16[512,128]{1,0:T(8,128)(2,1)S(1)}, u32[]{:S(2)}, u32[]{:S(2)}) collective-permute-start(bf16[512,128]{1,0:T(8,128)(2,1)S(1)} %add_convert_fusion), channel_id=1, source_target_pairs={{0,32},{8,40},{16,48},{24,56},{32,64},{40,72},{48,80},{56,88},{64,... | collective-permute-start | bytes 393224 | tf_op jit(solution)/shard_map/ppermute | solution.py:30
  87.5 3.9 %collective-permute-start.4 = (bf16[512,128]{1,0:T(8,128)(2,1)S(1)}, bf16[512,128]{1,0:T(8,128)(2,1)S(1)}, u32[]{:S(2)}, u32[]{:S(2)}) collective-permute-start(bf16[512,128]{1,0:T(8,128)(2,1)S(1)} %add_convert_fusion), channel_id=1, source_target_pairs={{0,48},{8,56},{16,64},{24,72},{32,80},{40,88},{48,96},{56,104},{64... | collective-permute-start | bytes 393224 | tf_op jit(solution)/shard_map/ppermute | solution.py:30
  92.8 4.2 %collective-permute-done.4 = bf16[512,128]{1,0:T(8,128)(2,1)S(1)} collective-permute-done((bf16[512,128]{1,0:T(8,128)(2,1)S(1)}, bf16[512,128]{1,0:T(8,128)(2,1)S(1)}, u32[]{:S(2)}, u32[]{:S(2)}) %collective-permute-start.4) | collective-permute-done | bytes 131104 | tf_op jit(solution)/shard_map/ppermute | solution.py:30
  97.1 8.3 %collective-permute-start.5 = (bf16[4,512,128]{2,1,0:T(8,128)(2,1)S(1)}, bf16[4,512,128]{2,1,0:T(8,128)(2,1)S(1)}, u32[]{:S(2)}, u32[]{:S(2)}) collective-permute-start(bf16[4,512,128]{2,1,0:T(8,128)(2,1)S(1)} %get-tuple-element.16), channel_id=1, source_target_pairs={{0,8},{8,0},{16,24},{24,16},{32,40},{40,32},{48,56},{56,48},{64,72... | collective-permute-start | bytes 1572872 | tf_op jit(solution)/shard_map/ppermute | solution.py:30
  105.4 7.8 %pad_maximum_fusion.tokens = bf16[512,8192]{1,0:T(8,128)(2,1)} fusion(bf16[256,8192]{1,0:T(8,128)(2,1)} %get-tuple-element.14, bf16[256,8192]{1,0:T(8,128)(2,1)} %get-tuple-element.13), kind=kLoop, calls=%fused_computation | loop fusion | flops 16777216 | bytes 16777216 | tf_op jit(solution)/shard_map/concatenate | solution.py:226
  113.6 19.8 %all-gather.3.cloned.1.call-done.weight = bf16[8192,256]{1,0:T(8,128)(2,1)} async-done(((bf16[1024,256]{1,0:T(8,128)(2,1)}), bf16[8192,256]{1,0:T(8,128)(2,1)}) %all-gather.3.cloned.1.call-update) | async-done | bytes 4194320 | tf_op jit(solution)/shard_map/all_gather | solution.py:255
  133.4 12.4 %attention.1 = (bf16[512,256]{1,0:T(8,128)(2,1)S(1)}, bf16[512,256]{1,0:T(8,128)(2,1)S(1)}, f32[4,512,128]{2,1,0:T(8,128)S(1)}) custom-call(s32[3]{0:T(128)S(1)} %pad_add_fusion.info, bf16[512,8192]{1,0:T(8,128)(2,1)} %pad_maximum_fusion.tokens, bf16[8192,256]{1,0:T(8,128)(2,1)} %all-gather.3.cloned.1.call-done.weight, f32[512,256]{1,0:T(8,128)S(1)} %fusion.11.start, ...), custom_call_target="tpu_custom_call" | custom-call | flops 4831838208 | bytes 16777216 | tf_op jit(solution)/shard_map/attention/pallas_call | solution.py:116
  148.9 5.4 %down_blocks.2.above = bf16[64,16,128]{2,1,0:T(8,128)(2,1)} custom-call(bf16[16,512]{1,0:T(8,128)(2,1)} %convolution_convert_fusion.rank_terms, bf16[512,8192]{1,0:T(8,128)(2,1)} %pad_maximum_fusion.tokens), custom_call_target="tpu_custom_call" | custom-call | flops 134217728 | bytes 8388608 | tf_op jit(solution)/shard_map/down_blocks/pallas_call | solution.py:181
  154.4 12.4 %collective-permute-start.8 = (bf16[264,128]{1,0:T(8,128)(2,1)S(1)}, bf16[264,128]{1,0:T(8,128)(2,1)S(1)}, u32[]{:S(2)}, u32[]{:S(2)}) collective-permute-start(bf16[264,128]{1,0:T(8,128)(2,1)S(1)} %pad_maximum_fusion.9), channel_id=1, source_target_pairs={{0,496},{8,504},{16,0},{24,8},{32,16},{40,24},{48,32},{56,40},{64,... | collective-permute-start | bytes 202760 | tf_op jit(solution)/shard_map/ppermute | solution.py:30
  168.8 2.9 %collective-permute-start.10 = (bf16[264,128]{1,0:T(8,128)(2,1)S(1)}, bf16[264,128]{1,0:T(8,128)(2,1)S(1)}, u32[]{:S(2)}, u32[]{:S(2)}) collective-permute-start(bf16[264,128]{1,0:T(8,128)(2,1)S(1)} %pad_maximum_fusion.11), channel_id=1, source_target_pairs={{0,464},{8,472},{16,480},{24,488},{32,496},{40,504},{48,0},{56,8},... | collective-permute-start | bytes 202760 | tf_op jit(solution)/shard_map/ppermute | solution.py:30
  172.8 2.8 %collective-permute-done.10 = bf16[264,128]{1,0:T(8,128)(2,1)S(1)} collective-permute-done((bf16[264,128]{1,0:T(8,128)(2,1)S(1)}, bf16[264,128]{1,0:T(8,128)(2,1)S(1)}, u32[]{:S(2)}, u32[]{:S(2)}) %collective-permute-start.10) | collective-permute-done | bytes 67616 | tf_op jit(solution)/shard_map/ppermute | solution.py:30
  177.2 4.4 %down_blocks.3 = bf16[64,56,128]{2,1,0:T(8,128)(2,1)} custom-call(bf16[16,256]{1,0:T(8,128)(2,1)} %fusion.3.rank_terms, bf16[256,8192]{1,0:T(8,128)(2,1)} %tokens.1, bf16[64,16,128]{2,1,0:T(8,128)(2,1)} %down_blocks.2.above, bf16[24,128]{1,0:T(8,128)(2,1)} %pad_maximum_fusion.12.below), custom_call_target="tpu_custom_call" | custom-call | flops 67108864 | bytes 4194304 | tf_op jit(solution)/shard_map/down_blocks/pallas_call | solution.py:181
  181.6 8.1 %all-to-all-start.2 = ((bf16[64,56,128]{2,1,0:T(8,128)(2,1)}), bf16[64,56,128]{2,1,0:T(8,128)(2,1)S(1)}, u32[]{:S(2)}, u32[]{:S(2)}) async-start(bf16[64,56,128]{2,1,0:T(8,128)(2,1)} %down_blocks.3), calls=%async_computation.2 | async-start | bytes 1835008 | tf_op jit(solution)/shard_map/all_to_all | solution.py:315
  193.9 21.5 %all-to-all-done.2 = bf16[64,56,128]{2,1,0:T(8,128)(2,1)S(1)} async-done(((bf16[64,56,128]{2,1,0:T(8,128)(2,1)}), bf16[64,56,128]{2,1,0:T(8,128)(2,1)S(1)}, u32[]{:S(2)}, u32[]{:S(2)}) %all-to-all-start.2) | async-done | bytes 917536 | tf_op jit(solution)/shard_map/all_to_all | solution.py:315
  216.1 7.0 %all-to-all-start.3 = ((bf16[8,32,128]{2,1,0:T(8,128)(2,1)}), bf16[8,32,128]{2,1,0:T(8,128)(2,1)S(1)}, u32[]{:S(2)}, u32[]{:S(2)}) async-start(bf16[8,32,128]{2,1,0:T(8,128)(2,1)} %broadcast_in_dim.39), calls=%async_computation.3 | async-start | bytes 131072 | tf_op jit(solution)/shard_map/all_to_all | solution.py:20
  224.6 7.7 %all-to-all-done.3 = bf16[8,32,128]{2,1,0:T(8,128)(2,1)S(1)} async-done(((bf16[8,32,128]{2,1,0:T(8,128)(2,1)}), bf16[8,32,128]{2,1,0:T(8,128)(2,1)S(1)}, u32[]{:S(2)}, u32[]{:S(2)}) %all-to-all-start.3) | async-done | bytes 65568 | tf_op jit(solution)/shard_map/all_to_all | solution.py:20
  (80 shorter events, 20.5 us)
Async XLA Ops:
  7.2 106.1 %copy-start = (bf16[16,512]{1,0:T(8,128)(2,1)S(1)}, bf16[16,512]{1,0:T(8,128)(2,1)}, u32[]{:S(2)}) copy-start(bf16[16,512]{1,0:T(8,128)(2,1)} %param.14) | copy-start | bytes 49156
  7.2 43.7 %copy-start.2 = (bf16[256,512]{1,0:T(8,128)(2,1)S(1)}, bf16[256,512]{1,0:T(8,128)(2,1)}, u32[]{:S(2)}) copy-start(bf16[256,512]{1,0:T(8,128)(2,1)} %param.17) | copy-start | bytes 786436
  7.2 47.1 %copy-start.4 = (s32[4]{0:T(128)S(1)}, s32[4]{0:T(128)}, u32[]{:S(2)}) copy-start(s32[4]{0:T(128)} %param.16) | copy-start | bytes 52
  7.2 65.2 %all-gather.5.cloned.1.call-start = ((), (), s32[]{:S(2)}) async-start(), calls=%async_computation.5 | async-start | bytes 2949120 | tf_op jit(solution)/shard_map/all_gather | solution.py:248
  29.5 104.0 %all-gather.3.cloned.1.call-start = ((), (), s32[]{:S(2)}) async-start(), calls=%async_computation.4 | async-start | bytes 4718592 | tf_op jit(solution)/shard_map/all_gather | solution.py:255
  29.5 24.9 %collective-permute-start = (bf16[256,8192]{1,0:T(8,128)(2,1)}, bf16[256,8192]{1,0:T(8,128)(2,1)}, u32[]{:S(2)}, u32[]{:S(2)}) collective-permute-start(bf16[256,8192]{1,0:T(8,128)(2,1)} %tokens.1), channel_id=1, source_target_pairs={{0,8},{8,0},{16,24},{24,16},{32,40},{40,32},{48,56},{56,48},{64,72... | collective-permute-start | bytes 12582920 | tf_op jit(solution)/shard_map/ppermute | solution.py:30
  51.6 39.8 %collective-permute-start.1 = (bf16[256,256]{1,0:T(8,128)(2,1)S(1)}, bf16[256,256]{1,0:T(8,128)(2,1)S(1)}, u32[]{:S(2)}, u32[]{:S(2)}) collective-permute-start(bf16[256,256]{1,0:T(8,128)(2,1)S(1)} %bitcast.86), channel_id=1, source_target_pairs={{0,8},{8,0},{16,24},{24,16},{32,40},{40,32},{48,56},{56,48},{64,72... | collective-permute-start | bytes 393224 | tf_op jit(solution)/shard_map/ppermute | solution.py:30
  72.4 7.3 %copy-start.3 = (bf16[16,128]{1,0:T(8,128)(2,1)S(1)}, bf16[16,128]{1,0:T(8,128)(2,1)}, u32[]{:S(2)}) copy-start(bf16[16,128]{1,0:T(8,128)(2,1)} %param.15) | copy-start | bytes 12292
  80.0 11.5 %collective-permute-start.2 = (bf16[512,128]{1,0:T(8,128)(2,1)S(1)}, bf16[512,128]{1,0:T(8,128)(2,1)S(1)}, u32[]{:S(2)}, u32[]{:S(2)}) collective-permute-start(bf16[512,128]{1,0:T(8,128)(2,1)S(1)} %add_convert_fusion), channel_id=1, source_target_pairs={{0,16},{8,24},{16,32},{24,40},{32,48},{40,56},{48,64},{56,72},{64,... | collective-permute-start | bytes 393224 | tf_op jit(solution)/shard_map/ppermute | solution.py:30
  83.4 9.4 %collective-permute-start.3 = (bf16[512,128]{1,0:T(8,128)(2,1)S(1)}, bf16[512,128]{1,0:T(8,128)(2,1)S(1)}, u32[]{:S(2)}, u32[]{:S(2)}) collective-permute-start(bf16[512,128]{1,0:T(8,128)(2,1)S(1)} %add_convert_fusion), channel_id=1, source_target_pairs={{0,32},{8,40},{16,48},{24,56},{32,64},{40,72},{48,80},{56,88},{64,... | collective-permute-start | bytes 393224 | tf_op jit(solution)/shard_map/ppermute | solution.py:30
  87.5 9.6 %collective-permute-start.4 = (bf16[512,128]{1,0:T(8,128)(2,1)S(1)}, bf16[512,128]{1,0:T(8,128)(2,1)S(1)}, u32[]{:S(2)}, u32[]{:S(2)}) collective-permute-start(bf16[512,128]{1,0:T(8,128)(2,1)S(1)} %add_convert_fusion), channel_id=1, source_target_pairs={{0,48},{8,56},{16,64},{24,72},{32,80},{40,88},{48,96},{56,104},{64... | collective-permute-start | bytes 393224 | tf_op jit(solution)/shard_map/ppermute | solution.py:30
  97.1 16.3 %collective-permute-start.5 = (bf16[4,512,128]{2,1,0:T(8,128)(2,1)S(1)}, bf16[4,512,128]{2,1,0:T(8,128)(2,1)S(1)}, u32[]{:S(2)}, u32[]{:S(2)}) collective-permute-start(bf16[4,512,128]{2,1,0:T(8,128)(2,1)S(1)} %get-tuple-element.16), channel_id=1, source_target_pairs={{0,8},{8,0},{16,24},{24,16},{32,40},{40,32},{48,56},{56,48},{64,72... | collective-permute-start | bytes 1572872 | tf_op jit(solution)/shard_map/ppermute | solution.py:30
  146.0 8.3 %collective-permute-start.7 = (bf16[4,256,128]{2,1,0:T(8,128)(2,1)S(1)}, bf16[4,256,128]{2,1,0:T(8,128)(2,1)S(1)}, u32[]{:S(2)}, u32[]{:S(2)}) collective-permute-start(bf16[4,256,128]{2,1,0:T(8,128)(2,1)S(1)} %dynamic-slice_bitcast_fusion), channel_id=1, source_target_pairs={{0,8},{8,0},{16,24},{24,16},{32,40},{40,32},{48,56},{56,48},{64,72... | collective-permute-start | bytes 786440 | tf_op jit(solution)/shard_map/ppermute | solution.py:30
  154.4 17.2 %collective-permute-start.8 = (bf16[264,128]{1,0:T(8,128)(2,1)S(1)}, bf16[264,128]{1,0:T(8,128)(2,1)S(1)}, u32[]{:S(2)}, u32[]{:S(2)}) collective-permute-start(bf16[264,128]{1,0:T(8,128)(2,1)S(1)} %pad_maximum_fusion.9), channel_id=1, source_target_pairs={{0,496},{8,504},{16,0},{24,8},{32,16},{40,24},{48,32},{56,40},{64,... | collective-permute-start | bytes 202760 | tf_op jit(solution)/shard_map/ppermute | solution.py:30
  166.8 5.9 %collective-permute-start.9 = (bf16[264,128]{1,0:T(8,128)(2,1)S(1)}, bf16[264,128]{1,0:T(8,128)(2,1)S(1)}, u32[]{:S(2)}, u32[]{:S(2)}) collective-permute-start(bf16[264,128]{1,0:T(8,128)(2,1)S(1)} %pad_maximum_fusion.10), channel_id=1, source_target_pairs={{0,480},{8,488},{16,496},{24,504},{32,0},{40,8},{48,16},{56,24},{6... | collective-permute-start | bytes 202760 | tf_op jit(solution)/shard_map/ppermute | solution.py:30
  168.8 6.8 %collective-permute-start.10 = (bf16[264,128]{1,0:T(8,128)(2,1)S(1)}, bf16[264,128]{1,0:T(8,128)(2,1)S(1)}, u32[]{:S(2)}, u32[]{:S(2)}) collective-permute-start(bf16[264,128]{1,0:T(8,128)(2,1)S(1)} %pad_maximum_fusion.11), channel_id=1, source_target_pairs={{0,464},{8,472},{16,480},{24,488},{32,496},{40,504},{48,0},{56,8},... | collective-permute-start | bytes 202760 | tf_op jit(solution)/shard_map/ppermute | solution.py:30
  175.7 18.2 %copy-start.1 = (bf16[256,128]{1,0:T(8,128)(2,1)}, bf16[256,128]{1,0:T(8,128)(2,1)S(1)}, u32[]{:S(2)}) copy-start(bf16[256,128]{1,0:T(8,128)(2,1)S(1)} %slice.75) | copy-start | bytes 196612
  181.6 33.8 %all-to-all-start.2 = ((bf16[64,56,128]{2,1,0:T(8,128)(2,1)}), bf16[64,56,128]{2,1,0:T(8,128)(2,1)S(1)}, u32[]{:S(2)}, u32[]{:S(2)}) async-start(bf16[64,56,128]{2,1,0:T(8,128)(2,1)} %down_blocks.3), calls=%async_computation.2 | async-start | bytes 1835008 | tf_op jit(solution)/shard_map/all_to_all | solution.py:315
  189.7 3.3 %collective-permute-start.6 = (bf16[256,256]{1,0:T(8,128)(2,1)S(1)}, bf16[256,256]{1,0:T(8,128)(2,1)S(1)}, u32[]{:S(2)}, u32[]{:S(2)}) collective-permute-start(bf16[256,256]{1,0:T(8,128)(2,1)S(1)} %constant_dynamic-slice_fusion), channel_id=1, source_target_pairs={{0,8},{8,0},{16,24},{24,16},{32,40},{40,32},{48,56},{56,48},{64,72... | collective-permute-start | bytes 393224 | tf_op jit(solution)/shard_map/ppermute | solution.py:30
  216.1 16.1 %all-to-all-start.3 = ((bf16[8,32,128]{2,1,0:T(8,128)(2,1)}), bf16[8,32,128]{2,1,0:T(8,128)(2,1)S(1)}, u32[]{:S(2)}, u32[]{:S(2)}) async-start(bf16[8,32,128]{2,1,0:T(8,128)(2,1)} %broadcast_in_dim.39), calls=%async_computation.3 | async-start | bytes 131072 | tf_op jit(solution)/shard_map/all_to_all | solution.py:20
Sparse Core Ops, SparseCore 0:
  29.6 42.7 all-gather.4
  74.5 58.8 all-gather.2

commit v7 on v6

--- a/solution.py
+++ b/solution.py
@@ -30,8 +30,77 @@
     return lax.ppermute(value, "ctx", pairs)
 
 
+def rows_of(tokens, theirs, columns, core, target, arrivals, first):
+    rows = tokens.shape[0]
+    mine = target.at[pl.ds(pl.multiple_of(core * rows, rows), rows)]
+    other = target.at[pl.ds(pl.multiple_of((1 - core) * rows, rows), rows)]
+    return [
+        pltpu.make_async_copy(tokens.at[:, columns], mine, arrivals.at[first]),
+        pltpu.make_async_copy(theirs.at[:, columns], other, arrivals.at[first + 1]),
+    ]
+
+
+def project_kernel(steps, info, tokens, theirs, up, *rest):
+    chunks, (out, low_out, columns_in, arrivals) = rest[: len(steps)], rest[len(steps) :]
+    planes, _, depth = columns_in.shape
+    size = out.shape[1]
+    plane, core = info[0], info[1]
+    copies = []
+    for i in range(planes):
+        start = lax.rem(plane + i, planes) * depth
+        here = pl.ds(pl.multiple_of(start, depth), depth)
+        copies.append(rows_of(tokens, theirs, here, core, columns_in.at[i], arrivals, 2 * i))
+    order = list(dict.fromkeys(step for step, _ in steps))
+    for step in order:
+        for copy in copies[step]:
+            copy.start()
+    total = jnp.zeros((out.shape[0], chunks[0].shape[0]), f32)
+    waited = set()
+    for (step, place), chunk in zip(steps, chunks):
+        if step not in waited:
+            waited.add(step)
+            for copy in copies[step]:
+                copy.wait()
+        part = columns_in[step, :, place : place + chunk.shape[1]]
+        total = total + lax.dot_general(part, chunk[...], NT, preferred_element_type=f32)
+    low = total[:, size:].astype(bf16)
+    low_out[...] = low
+    rank = low.shape[1] // 2
+    extra = jnp.dot(low[:, rank:], up[...], preferred_element_type=f32)
+    out[...] = (total[:, :size] + jnp.where(core == 1, extra, 0.0)).astype(bf16)
+
+
+def project(info, tokens, theirs, up, steps, chunks, planes):
+    rows, model = tokens.shape
+    size = up.shape[1]
+    ranks = chunks[0].shape[0] - size
+    vmem = pl.BlockSpec(memory_space=pltpu.VMEM)
+    anywhere = pl.BlockSpec(memory_space=pl.ANY)
+    return pl.pallas_call(
+        functools.partial(project_kernel, steps),
+        out_shape=(
+            jax.ShapeDtypeStruct((2 * rows, size), bf16),
+            jax.ShapeDtypeStruct((2 * rows, ranks), bf16),
+        ),
+        in_specs=[pl.BlockSpec(memory_space=pltpu.SMEM), anywhere, anywhere, vmem]
+        + [vmem] * len(chunks),
+        out_specs=(vmem, vmem),
+        scratch_shapes=[
+            pltpu.VMEM((planes, 2 * rows, model // planes), bf16),
+            pltpu.SemaphoreType.DMA((2 * planes,)),
+        ],
+        compiler_params=pltpu.CompilerParams(vmem_limit_bytes=48 * 1024 * 1024),
+        cost_estimate=pl.CostEstimate(
+            flops=4 * rows * model * (size + ranks),
+            bytes_accessed=4 * rows * model,
+            transcendentals=0,
+        ),
+        name="project",
+    )(info, tokens, theirs, up, *chunks)
+
+
 def attention_kernel(
-    scale, tile, info, tokens, weight, start, grad_out, kv,
+    scale, tile, info, tokens, theirs, weight, start, grad_out, kv,
     out, grad_query, grad_value, query, columns_in, rows_in, arrivals,
 ):
     rows, size = query.shape[0], kv.shape[-1]
@@ -43,17 +112,17 @@
     copies = []
     for i in range(parts):
         here = pl.ds(i * depth, depth)
-        copies += [
-            pltpu.make_async_copy(tokens.at[:, here], columns_in.at[i], arrivals.at[2 * i]),
-            pltpu.make_async_copy(weight.at[here], rows_in.at[i], arrivals.at[2 * i + 1]),
-        ]
-    for copy in copies:
+        copies.append(
+            rows_of(tokens, theirs, here, info[heads], columns_in.at[i], arrivals, 3 * i)
+            + [pltpu.make_async_copy(weight.at[here], rows_in.at[i], arrivals.at[3 * i + 2])]
+        )
+    for copy in sum(copies, []):
         copy.start()
     grad_value[...] = jnp.zeros_like(grad_value)
     total = start[...]
     for i in range(parts):
-        copies[2 * i].wait()
-        copies[2 * i + 1].wait()
+        for copy in copies[i]:
+            copy.wait()
         total = total + jnp.dot(columns_in[i], rows_in[i], preferred_element_type=f32)
     query[...] = total.astype(bf16)
 
@@ -107,7 +176,7 @@
                 lax.fori_loop(0, rows // tile, step, 0)
 
 
-def attend(info, tokens, weight, start, grad_out, kv, tile=256, parts=8):
+def attend(info, tokens, theirs, weight, start, grad_out, kv, tile=256, parts=8):
     rows, width = start.shape
     model = tokens.shape[1]
     size = kv.shape[-1]
@@ -124,6 +193,7 @@
             pl.BlockSpec(memory_space=pltpu.SMEM),
             pl.BlockSpec(memory_space=pl.ANY),
             pl.BlockSpec(memory_space=pl.ANY),
+            pl.BlockSpec(memory_space=pl.ANY),
             vmem,
             vmem,
             vmem,
@@ -133,7 +203,7 @@
             pltpu.VMEM((rows, width), bf16),
             pltpu.VMEM((parts, rows, model // parts), bf16),
             pltpu.VMEM((parts, model // parts, width), bf16),
-            pltpu.SemaphoreType.DMA((2 * parts,)),
+            pltpu.SemaphoreType.DMA((3 * parts,)),
         ],
         compiler_params=pltpu.CompilerParams(vmem_limit_bytes=48 * 1024 * 1024),
         cost_estimate=pl.CostEstimate(
@@ -142,7 +212,7 @@
             transcendentals=rows * width // size * blocks * block,
         ),
         name="attention",
-    )(info, tokens, weight, start, grad_out, kv)
+    )(info, tokens, theirs, weight, start, grad_out, kv)
 
 
 def blocks_kernel(rank_terms, tokens, above, below, out):
@@ -155,24 +225,25 @@
         out[i, bottom:] = below[...]
 
 
-def first_blocks_kernel(rank_terms, tokens, out):
+def first_blocks_kernel(rank_mine, rank_theirs, tokens, theirs, out):
     size = out.shape[2]
-    product = jnp.dot(rank_terms[...], tokens[...], preferred_element_type=f32).astype(bf16)
+    product = jnp.dot(rank_mine[...], tokens[...], preferred_element_type=f32)
+    product += jnp.dot(rank_theirs[...], theirs[...], preferred_element_type=f32)
+    product = product.astype(bf16)
     for i in range(out.shape[0]):
         out[i] = product[:, i * size : (i + 1) * size]
 
 
-def down_blocks(rank_terms, tokens, devices, above=None, below=None, steps=4):
-    ranks, rows = rank_terms.shape
-    size = tokens.shape[1] // devices
+def down_blocks(kernel, ranks, tokens, devices, above=None, below=None, steps=8):
+    rows, model = tokens[0].shape
+    size = model // devices
     step = devices // steps
-    in_specs = [
-        pl.BlockSpec((ranks, rows), lambda i: (0, 0)),
-        pl.BlockSpec((rows, step * size), lambda i: (0, i)),
-    ]
-    more, height, kernel = (), ranks, first_blocks_kernel
+    height = ranks[0].shape[0]
+    in_specs = [pl.BlockSpec(r.shape, lambda i: (0, 0)) for r in ranks]
+    in_specs += [pl.BlockSpec((rows, step * size), lambda i: (0, i)) for _ in tokens]
+    more = ()
     if above is not None:
-        more, kernel = (above, below), blocks_kernel
+        more = (above, below)
         height += above.shape[1] + below.shape[0]
         in_specs += [
             pl.BlockSpec((step, *above.shape[1:]), lambda i: (i, 0, 0)),
@@ -186,12 +257,12 @@
         out_specs=pl.BlockSpec((step, height, size), lambda i: (i, 0, 0)),
         compiler_params=pltpu.CompilerParams(vmem_limit_bytes=56 * 1024 * 1024),
         cost_estimate=pl.CostEstimate(
-            flops=2 * ranks * rows * devices * size,
-            bytes_accessed=2 * rows * devices * size,
+            flops=2 * ranks[0].shape[0] * rows * model * len(tokens),
+            bytes_accessed=2 * rows * model * len(tokens),
             transcendentals=0,
         ),
         name="down_blocks",
-    )(rank_terms, tokens, *more)
+    )(*ranks, *tokens, *more)
 
 
 def on_device(
@@ -230,7 +301,17 @@
     def half_of(array, which):
         return lax.dynamic_slice_in_dim(array, which * (array.shape[0] // 2), array.shape[0] // 2)
 
-    chip_tokens = both(tokens, to_chip(tokens, 0, True))
+    def round_y(value):
+        ahead, back = [value], [value]
+        for _ in range(planes // 2 - 1):
+            ahead.append(to_chip(ahead[-1], chips, False))
+            back.append(to_chip(back[-1], -chips, False))
+        return ahead, back
+
+    def behind(value, earlier):
+        return value + (earlier.reshape(-1)[0] * 0).astype(value.dtype)
+
+    theirs = to_chip(tokens, 0, True)
     grad_halves = output_gradient.reshape(rows, 2, half).transpose(1, 0, 2)
     grad_mine = lax.dynamic_index_in_dim(grad_halves, core, 0, keepdims=False)
     grad_away = lax.dynamic_index_in_dim(grad_halves, 1 - core, 0, keepdims=False)
@@ -245,8 +326,20 @@
         kv_rows.reshape(members, size + 2 * rank, depth),
         "ctx", 0, 0, tiled=True, axis_index_groups=plain,
     )
-    kv_rows = lax.all_gather(kv_rows, "ctx", axis=0, tiled=True, axis_index_groups=across)
-    q_rows = jnp.stack([query_weight[:, :half], query_weight[:, half:]])
+    kv_rows = kv_rows.transpose(1, 0, 2).reshape(size + 2 * rank, members * depth)
+    kv_ahead, kv_back = round_y(kv_rows)
+    cut = members * depth // 2
+    opposite = planes // 2
+    steps, chunks = [(0, 0)], [kv_rows]
+    for step in range(1, opposite):
+        steps += [(planes - step, 0), (step, 0)]
+        chunks += [kv_ahead[step], kv_back[step]]
+    steps += [(opposite, 0), (opposite, cut)]
+    chunks += [
+        to_chip(kv_ahead[-1][:, :cut], chips, False),
+        to_chip(kv_back[-1][:, cut:], -chips, False),
+    ]
+    q_rows = behind(jnp.stack([query_weight[:, :half], query_weight[:, half:]]), kv_rows)
     q_rows = jnp.broadcast_to(q_rows[None], (chips, *q_rows.shape))
     q_rows = lax.all_to_all(
         q_rows.reshape(members, depth, half),
@@ -257,12 +350,9 @@
         "ctx", axis=0, tiled=True, axis_index_groups=across,
     )
 
-    kv_weight = kv_rows.transpose(1, 0, 2).reshape(size + 2 * rank, model)
-    mine = lax.dot_general(chip_tokens, kv_weight, NT, preferred_element_type=f32)
-    low = mine[:, size:].astype(bf16)
+    place = jnp.stack([lax.div(position, members), core]).astype(jnp.int32)
+    mine, low = project(place, tokens, theirs, value_up_weight, steps, chunks, planes)
     low_q, low_v = low[:, :rank], low[:, rank:]
-    extra = jnp.dot(low_v, value_up_weight, preferred_element_type=f32)
-    mine = (mine[:, :size] + jnp.where(core == 1, extra, 0.0)).astype(bf16)
     mine = jnp.stack([mine] + [to_chip(mine, d, False) for d in range(1, chips)])
     kv = jnp.stack([mine, to_chip(mine, 0, True)])
 
@@ -271,7 +361,9 @@
     shifts = lax.dynamic_slice_in_dim(head_shifts, core * (heads // 2), heads // 2)
     seen = jnp.where(shifts != 0, lax.rem(chip + chips // 2, chips), chip)
     info = jnp.concatenate([seen, core[None]]).astype(jnp.int32)
-    output, grad_query, value_parts = attend(info, chip_tokens, q_rows, start, grad_out, kv)
+    output, grad_query, value_parts = attend(
+        info, tokens, theirs, q_rows, start, grad_out, kv
+    )
 
     attention_mine = half_of(output, core)
     attention_other = to_chip(half_of(output, 1 - core), 0, True)
@@ -284,7 +376,12 @@
     )
 
     rank_q = lax.dot_general(up_mine, grad_query, NT, preferred_element_type=f32).astype(bf16)
-    q_blocks = down_blocks(rank_q, chip_tokens, devices)
+    rank_halves = rank_q.reshape(rank, 2, rows)
+    rank_mine = lax.dynamic_index_in_dim(rank_halves, core, 1, keepdims=False)
+    rank_theirs = lax.dynamic_index_in_dim(rank_halves, 1 - core, 1, keepdims=False)
+    q_blocks = down_blocks(
+        first_blocks_kernel, (rank_mine, rank_theirs), (tokens, theirs), devices
+    )
 
     query_up_part = lax.dot_general(low_q, grad_query, TN, preferred_element_type=f32)
     query_up_part = query_up_part.reshape(chips, -1, size)
@@ -311,7 +408,7 @@
         half_of(low_v, core), value_gradient, TN, preferred_element_type=f32
     ).astype(bf16)
     shared = jnp.concatenate([value_up_part, arrived[rows:]], axis=0)
-    blocks = down_blocks(rank_v, tokens, devices, q_blocks, shared)
+    blocks = down_blocks(blocks_kernel, (rank_v,), (tokens,), devices, q_blocks, shared)
     blocks = lax.all_to_all(blocks, "ctx", 0, 0, tiled=True)
     summed = jnp.sum(blocks[:, : 3 * rank].astype(f32), axis=0)
     grad_down = jnp.sum(spread(summed[: 2 * rank].astype(bf16), "fsdp").astype(f32), axis=0)

time: 241 us -> 261 us (1.083)
  starting transfers between devices: 61.5 us -> 99.5 us
  blocking collectives: 38.1 us -> 18.5 us
  other arithmetic: 17.4 us -> 4.7 us
  Pallas kernels: 22.3 us -> 31.6 us
  waiting for transfers between devices: 71.6 us -> 80 us
  matrix products: 9.44 us -> 1.47 us
  local copies, waits for them, and re-layouts: 4.8 us -> 8.86 us
    ppermute x11 -> x19, waiting for transfers between devices: 10.5 us -> 41.7 us  [to_chip(): return lax.ppermute(value, 'ctx', pairs)]
    ppermute x11 -> x19, starting transfers between devices: 46.4 us -> 69.5 us  [to_chip(): return lax.ppermute(value, 'ctx', pairs)]
    all_to_all x1 -> x0, blocking collectives: 20.4 us -> none  [on_device(): lax.all_to_all(kv_rows.reshape(members, size + 2 * rank, depth), 'ctx', 0...]
    all_gather x1, waiting for transfers between devices: 19.8 us -> 0.02 us  [on_device(): lax.all_gather(q_rows.reshape(members * depth, half), 'ctx', axis=0, tile...]
    all_gather x1 -> x0, waiting for transfers between devices: 12.1 us -> none  [on_device(): lax.all_gather(kv_rows, 'ctx', axis=0, tiled=True, axis_index_groups=across)]
    all_to_all x0 -> x1, starting transfers between devices: none -> 10.2 us  [on_device(): lax.all_to_all(kv_rows.reshape(members, size + 2 * rank, depth), 'ctx', 0...]
    all_to_all x0 -> x1, waiting for transfers between devices: none -> 9.16 us  [on_device(): lax.all_to_all(kv_rows.reshape(members, size + 2 * rank, depth), 'ctx', 0...]
    concatenate x2 -> x1, other arithmetic: 7.83 us -> 0.02 us  [both(): jnp.concatenate([jnp.where(core == 0, mine, theirs), jnp.where(core == 0,...]
  transfers between devices with their start and end apart: 15 -> 23, of which waited for: 9 -> 13; matrix products, arithmetic and copies ran while one was open for 11% -> 3% of each run, Pallas kernels for 2% -> 6%
where the time goes in v7:
time: 261 us; the launch traced here: 260 us
  starting transfers between devices  99.5 us (38%)
  waiting for transfers between devices  80 us (31%)
  Pallas kernels  31.6 us (12%)
  blocking collectives  18.5 us (7%)
  between operations  15.3 us (6%)
  local copies, waits for them, and re-layouts  8.86 us (3%)
  other arithmetic  4.7 us (2%)
    ppermute x19, starting transfers between devices, to_chip(): return lax.ppermute(value, 'ctx', pairs)  69.5 us
    ppermute x19, waiting for transfers between devices, to_chip(): return lax.ppermute(value, 'ctx', pairs)  41.7 us
    all_to_all x1, waiting for transfers between devices, on_device(): blocks = lax.all_to_all(blocks, 'ctx', 0, 0, tiled=True)  21.5 us
    all_to_all x1, blocking collectives, on_device(): lax.all_to_all(q_rows.reshape(members, depth, half), 'ctx', 0, 0, tiled=T...  18.5 us
    pallas_call x2, Pallas kernels, down_blocks(): pl.pallas_call(kernel, out_shape=jax.ShapeDtypeStruct((devices, height, s...  13.7 us
    pallas_call x1, Pallas kernels, attend(): pl.pallas_call(functools.partial(attention_kernel, size ** (-0.5), tile),...  10.7 us
    all_to_all x1, starting transfers between devices, on_device(): blocks = lax.all_to_all(blocks, 'ctx', 0, 0, tiled=True)  10.2 us
    all_to_all x1, starting transfers between devices, on_device(): lax.all_to_all(kv_rows.reshape(members, size + 2 * rank, depth), 'ctx', 0...  10.2 us
  transfers between devices with their start and end apart: 23, of which 13 were waited for; matrix products, arithmetic and copies ran while one was open for 3% of the time, Pallas kernels for 6%

profile of v7, /device:TPU:1, one launch (start us, length us, event | category | flops | bytes accessed | tf_op | source)
XLA Modules:
  0.0 259.9 jit_solution(9738601346647329891)
XLA Ops:
  9.8 10.2 %all-to-all-start = ((bf16[8,160,128]{2,1,0:T(8,128)(2,1)}), bf16[8,160,128]{2,1,0:T(8,128)(2,1)S(1)}, u32[]{:S(2)}, u32[]{:S(2)}) async-start(bf16[8,160,128]{2,1,0:T(8,128)(2,1)} %bitcast.8), calls=%async_computation | async-start | bytes 655360 | tf_op jit(solution)/shard_map/all_to_all | solution.py:325
  20.9 9.2 %all-to-all-done = bf16[8,160,128]{2,1,0:T(8,128)(2,1)S(1)} async-done(((bf16[8,160,128]{2,1,0:T(8,128)(2,1)}), bf16[8,160,128]{2,1,0:T(8,128)(2,1)S(1)}, u32[]{:S(2)}, u32[]{:S(2)}) %all-to-all-start) | async-done | bytes 327712 | tf_op jit(solution)/shard_map/all_to_all | solution.py:325
  31.4 18.5 %all_to_all.20 = bf16[8,128,256]{2,1,0:T(8,128)(2,1)} all-to-all(bf16[8,128,256]{2,1,0:T(8,128)(2,1)S(1)} %bitcast.88), channel_id=1, replica_groups={{0,8,16,24,32,40,48,56},{64,72,80,88,96,104,112,120},{128,136,144,152,1..., dimensions={0} | all-to-all | bytes 1048576 | tf_op jit(solution)/shard_map/all_to_all | solution.py:344
  54.9 4.6 %collective-permute-start.2 = (bf16[160,1024]{1,0:T(8,128)(2,1)S(1)}, bf16[160,1024]{1,0:T(8,128)(2,1)S(1)}, u32[]{:S(2)}, u32[]{:S(2)}) collective-permute-start(bf16[160,1024]{1,0:T(8,128)(2,1)S(1)} %bitcast.83), channel_id=1, source_target_pairs={{0,448},{8,456},{16,464},{24,472},{32,480},{40,488},{48,496},{56,5... | collective-permute-start | bytes 983048 | tf_op jit(solution)/shard_map/ppermute | solution.py:30
  59.5 5.9 %collective-permute-done.1.rest_1_ = bf16[160,1024]{1,0:T(8,128)(2,1)S(1)} collective-permute-done((bf16[160,1024]{1,0:T(8,128)(2,1)S(1)}, bf16[160,1024]{1,0:T(8,128)(2,1)S(1)}, u32[]{:S(2)}, u32[]{:S(2)}) %collective-permute-start.1) | collective-permute-done | bytes 327712 | tf_op jit(solution)/shard_map/ppermute | solution.py:30
  67.4 5.1 %collective-permute-start.4 = (bf16[160,1024]{1,0:T(8,128)(2,1)S(1)}, bf16[160,1024]{1,0:T(8,128)(2,1)S(1)}, u32[]{:S(2)}, u32[]{:S(2)}) collective-permute-start(bf16[160,1024]{1,0:T(8,128)(2,1)S(1)} %collective-permute-done.2.rest_2_), channel_id=1, source_target_pairs={{0,448},{8,456},{16,464},{24,472},{32,480},{40,488},{48,496},{56,5... | collective-permute-start | bytes 983048 | tf_op jit(solution)/shard_map/ppermute | solution.py:30
  72.5 12.4 %collective-permute-done.3.rest_3_ = bf16[160,1024]{1,0:T(8,128)(2,1)S(1)} collective-permute-done((bf16[160,1024]{1,0:T(8,128)(2,1)S(1)}, bf16[160,1024]{1,0:T(8,128)(2,1)S(1)}, u32[]{:S(2)}, u32[]{:S(2)}) %collective-permute-start.3) | collective-permute-done | bytes 327712 | tf_op jit(solution)/shard_map/ppermute | solution.py:30
  86.9 4.6 %collective-permute-start.6 = (bf16[160,1024]{1,0:T(8,128)(2,1)S(1)}, bf16[160,1024]{1,0:T(8,128)(2,1)S(1)}, u32[]{:S(2)}, u32[]{:S(2)}) collective-permute-start(bf16[160,1024]{1,0:T(8,128)(2,1)S(1)} %collective-permute-done.4.rest_4_), channel_id=1, source_target_pairs={{0,448},{8,456},{16,464},{24,472},{32,480},{40,488},{48,496},{56,5... | collective-permute-start | bytes 983048 | tf_op jit(solution)/shard_map/ppermute | solution.py:30
  91.5 12.6 %collective-permute-done.5.rest_5_ = bf16[160,1024]{1,0:T(8,128)(2,1)S(1)} collective-permute-done((bf16[160,1024]{1,0:T(8,128)(2,1)S(1)}, bf16[160,1024]{1,0:T(8,128)(2,1)S(1)}, u32[]{:S(2)}, u32[]{:S(2)}) %collective-permute-start.5) | collective-permute-done | bytes 327712 | tf_op jit(solution)/shard_map/ppermute | solution.py:30
  107.5 4.6 %collective-permute-start.8 = (bf16[160,512]{1,0:T(8,128)(2,1)}, bf16[160,512]{1,0:T(8,128)(2,1)S(1)}, u32[]{:S(2)}, u32[]{:S(2)}) collective-permute-start(bf16[160,512]{1,0:T(8,128)(2,1)} %slice.74), channel_id=1, source_target_pairs={{0,448},{8,456},{16,464},{24,472},{32,480},{40,488},{48,496},{56,5... | collective-permute-start | bytes 491528 | tf_op jit(solution)/shard_map/ppermute | solution.py:30
  113.3 4.9 %collective-permute-start.9 = (bf16[256,256]{1,0:T(8,128)(2,1)}, bf16[256,256]{1,0:T(8,128)(2,1)}, u32[]{:S(2)}, u32[]{:S(2)}) collective-permute-start(bf16[256,256]{1,0:T(8,128)(2,1)} %bitcast.81), channel_id=1, source_target_pairs={{0,8},{8,0},{16,24},{24,16},{32,40},{40,32},{48,56},{56,48},{64,72... | collective-permute-start | bytes 393224 | tf_op jit(solution)/shard_map/ppermute | solution.py:30
  118.8 7.1 %project.1 = (bf16[512,128]{1,0:T(8,128)(2,1)S(1)}, bf16[512,32]{1,0:T(8,128)(2,1)S(1)}) custom-call(s32[2]{0:T(128)S(1)} %pad_add_fusion.1.info, bf16[256,8192]{1,0:T(8,128)(2,1)} %tokens.7, bf16[256,8192]{1,0:T(8,128)(2,1)} %collective-permute-done.theirs, bf16[16,128]{1,0:T(8,128)(2,1)S(1)} %copy-done.1, bf16[160,1024]{1,0:T(8,128)(2,1)S(1)} %bitcast.84, ...), custom_call_target="tpu_custom_call" | custom-call | flops 1342177280 | bytes 8388608 | tf_op jit(solution)/shard_map/project/pallas_call | solution.py:79
  130.4 3.8 %collective-permute-start.12 = (bf16[512,128]{1,0:T(8,128)(2,1)S(1)}, bf16[512,128]{1,0:T(8,128)(2,1)S(1)}, u32[]{:S(2)}, u32[]{:S(2)}) collective-permute-start(bf16[512,128]{1,0:T(8,128)(2,1)S(1)} %get-tuple-element.11), channel_id=1, source_target_pairs={{0,48},{8,56},{16,64},{24,72},{32,80},{40,88},{48,96},{56,104},{64... | collective-permute-start | bytes 393224 | tf_op jit(solution)/shard_map/ppermute | solution.py:30
  140.5 6.5 %collective-permute-start.13 = (bf16[4,512,128]{2,1,0:T(8,128)(2,1)S(1)}, bf16[4,512,128]{2,1,0:T(8,128)(2,1)S(1)}, u32[]{:S(2)}, u32[]{:S(2)}) collective-permute-start(bf16[4,512,128]{2,1,0:T(8,128)(2,1)S(1)} %get-tuple-element.18), channel_id=1, source_target_pairs={{0,8},{8,0},{16,24},{24,16},{32,40},{40,32},{48,56},{56,48},{64,72... | collective-permute-start | bytes 1572872 | tf_op jit(solution)/shard_map/ppermute | solution.py:30
  148.7 10.7 %attention.1 = (bf16[512,256]{1,0:T(8,128)(2,1)S(1)}, bf16[512,256]{1,0:T(8,128)(2,1)S(1)}, f32[4,512,128]{2,1,0:T(8,128)S(1)}) custom-call(s32[3]{0:T(128)S(1)} %pad_add_fusion.info, bf16[256,8192]{1,0:T(8,128)(2,1)} %tokens.7, bf16[256,8192]{1,0:T(8,128)(2,1)} %collective-permute-done.theirs, bf16[8192,256]{1,0:T(8,128)(2,1)} %all-gather.2.cloned.1.call-done.weight, ...), custom_call_target="tpu_custom_call" | custom-call | flops 4831838208 | bytes 16777216 | tf_op jit(solution)/shard_map/attention/pallas_call | solution.py:185
  159.9 4.1 %collective-permute-start.15 = (bf16[4,256,128]{2,1,0:T(8,128)(2,1)S(1)}, bf16[4,256,128]{2,1,0:T(8,128)(2,1)S(1)}, u32[]{:S(2)}, u32[]{:S(2)}) collective-permute-start(bf16[4,256,128]{2,1,0:T(8,128)(2,1)S(1)} %dynamic-slice_bitcast_fusion), channel_id=1, source_target_pairs={{0,8},{8,0},{16,24},{24,16},{32,40},{40,32},{48,56},{56,48},{64,72... | collective-permute-start | bytes 786440 | tf_op jit(solution)/shard_map/ppermute | solution.py:30
  164.7 7.3 %down_blocks.2.above = bf16[64,16,128]{2,1,0:T(8,128)(2,1)} custom-call(bf16[16,256]{1,0:T(8,128)(2,1)} %get-tuple-element.40.rank_mine, bf16[16,256]{1,0:T(8,128)(2,1)} %get-tuple-element.39.rank_theirs, bf16[256,8192]{1,0:T(8,128)(2,1)} %tokens.7, bf16[256,8192]{1,0:T(8,128)(2,1)} %collective-permute-done.theirs), custom_call_target="tpu_custom_call" | custom-call | flops 134217728 | bytes 8388608 | tf_op jit(solution)/shard_map/down_blocks/pallas_call | solution.py:252
  172.2 8.0 %collective-permute-start.16 = (bf16[264,128]{1,0:T(8,128)(2,1)S(1)}, bf16[264,128]{1,0:T(8,128)(2,1)S(1)}, u32[]{:S(2)}, u32[]{:S(2)}) collective-permute-start(bf16[264,128]{1,0:T(8,128)(2,1)S(1)} %pad_maximum_fusion.7), channel_id=1, source_target_pairs={{0,496},{8,504},{16,0},{24,8},{32,16},{40,24},{48,32},{56,40},{64,... | collective-permute-start | bytes 202760 | tf_op jit(solution)/shard_map/ppermute | solution.py:30
  182.3 3.9 %collective-permute-start.18 = (bf16[264,128]{1,0:T(8,128)(2,1)S(1)}, bf16[264,128]{1,0:T(8,128)(2,1)S(1)}, u32[]{:S(2)}, u32[]{:S(2)}) collective-permute-start(bf16[264,128]{1,0:T(8,128)(2,1)S(1)} %pad_maximum_fusion.9), channel_id=1, source_target_pairs={{0,464},{8,472},{16,480},{24,488},{32,496},{40,504},{48,0},{56,8},... | collective-permute-start | bytes 202760 | tf_op jit(solution)/shard_map/ppermute | solution.py:30
  190.7 6.4 %down_blocks.3 = bf16[64,56,128]{2,1,0:T(8,128)(2,1)} custom-call(bf16[16,256]{1,0:T(8,128)(2,1)} %fusion.rank_terms, bf16[256,8192]{1,0:T(8,128)(2,1)} %tokens.7, bf16[64,16,128]{2,1,0:T(8,128)(2,1)} %down_blocks.2.above, bf16[24,128]{1,0:T(8,128)(2,1)} %pad_maximum_fusion.10.below), custom_call_target="tpu_custom_call" | custom-call | flops 67108864 | bytes 4194304 | tf_op jit(solution)/shard_map/down_blocks/pallas_call | solution.py:252
  197.1 10.2 %all-to-all-start.2 = ((bf16[64,56,128]{2,1,0:T(8,128)(2,1)}), bf16[64,56,128]{2,1,0:T(8,128)(2,1)S(1)}, u32[]{:S(2)}, u32[]{:S(2)}) async-start(bf16[64,56,128]{2,1,0:T(8,128)(2,1)} %down_blocks.3), calls=%async_computation.2 | async-start | bytes 1835008 | tf_op jit(solution)/shard_map/all_to_all | solution.py:412
  211.6 21.5 %all-to-all-done.2 = bf16[64,56,128]{2,1,0:T(8,128)(2,1)S(1)} async-done(((bf16[64,56,128]{2,1,0:T(8,128)(2,1)}), bf16[64,56,128]{2,1,0:T(8,128)(2,1)S(1)}, u32[]{:S(2)}, u32[]{:S(2)}) %all-to-all-start.2) | async-done | bytes 917536 | tf_op jit(solution)/shard_map/all_to_all | solution.py:412
  233.8 9.5 %all-to-all-start.3 = ((bf16[8,32,128]{2,1,0:T(8,128)(2,1)}), bf16[8,32,128]{2,1,0:T(8,128)(2,1)S(1)}, u32[]{:S(2)}, u32[]{:S(2)}) async-start(bf16[8,32,128]{2,1,0:T(8,128)(2,1)} %broadcast_in_dim.34), calls=%async_computation.3 | async-start | bytes 131072 | tf_op jit(solution)/shard_map/all_to_all | solution.py:20
  244.7 7.7 %all-to-all-done.3 = bf16[8,32,128]{2,1,0:T(8,128)(2,1)S(1)} async-done(((bf16[8,32,128]{2,1,0:T(8,128)(2,1)}), bf16[8,32,128]{2,1,0:T(8,128)(2,1)S(1)}, u32[]{:S(2)}, u32[]{:S(2)}) %all-to-all-start.3) | async-done | bytes 65568 | tf_op jit(solution)/shard_map/all_to_all | solution.py:20
  (98 shorter events, 45.2 us)
Async XLA Ops:
  7.2 140.9 %copy-start = (bf16[16,512]{1,0:T(8,128)(2,1)S(1)}, bf16[16,512]{1,0:T(8,128)(2,1)}, u32[]{:S(2)}) copy-start(bf16[16,512]{1,0:T(8,128)(2,1)} %param.14) | copy-start | bytes 49156
  9.8 20.3 %all-to-all-start = ((bf16[8,160,128]{2,1,0:T(8,128)(2,1)}), bf16[8,160,128]{2,1,0:T(8,128)(2,1)S(1)}, u32[]{:S(2)}, u32[]{:S(2)}) async-start(bf16[8,160,128]{2,1,0:T(8,128)(2,1)} %bitcast.8), calls=%async_computation | async-start | bytes 655360 | tf_op jit(solution)/shard_map/all_to_all | solution.py:325
  20.0 128.7 %all-gather.2.cloned.1.call-start = ((), (), s32[]{:S(2)}) async-start(), calls=%async_computation.4 | async-start | bytes 4718592 | tf_op jit(solution)/shard_map/all_gather | solution.py:348
  50.0 68.8 %collective-permute-start = (bf16[256,8192]{1,0:T(8,128)(2,1)}, bf16[256,8192]{1,0:T(8,128)(2,1)}, u32[]{:S(2)}, u32[]{:S(2)}) collective-permute-start(bf16[256,8192]{1,0:T(8,128)(2,1)} %tokens.7), channel_id=1, source_target_pairs={{0,8},{8,0},{16,24},{24,16},{32,40},{40,32},{48,56},{56,48},{64,72... | collective-permute-start | bytes 12582920 | tf_op jit(solution)/shard_map/ppermute | solution.py:30
  53.0 12.4 %collective-permute-start.1 = (bf16[160,1024]{1,0:T(8,128)(2,1)S(1)}, bf16[160,1024]{1,0:T(8,128)(2,1)S(1)}, u32[]{:S(2)}, u32[]{:S(2)}) collective-permute-start(bf16[160,1024]{1,0:T(8,128)(2,1)S(1)} %bitcast.82), channel_id=1, source_target_pairs={{0,64},{8,72},{16,80},{24,88},{32,96},{40,104},{48,112},{56,120},{... | collective-permute-start | bytes 983048 | tf_op jit(solution)/shard_map/ppermute | solution.py:30
  54.9 12.4 %collective-permute-start.2 = (bf16[160,1024]{1,0:T(8,128)(2,1)S(1)}, bf16[160,1024]{1,0:T(8,128)(2,1)S(1)}, u32[]{:S(2)}, u32[]{:S(2)}) collective-permute-start(bf16[160,1024]{1,0:T(8,128)(2,1)S(1)} %bitcast.83), channel_id=1, source_target_pairs={{0,448},{8,456},{16,464},{24,472},{32,480},{40,488},{48,496},{56,5... | collective-permute-start | bytes 983048 | tf_op jit(solution)/shard_map/ppermute | solution.py:30
  65.4 19.5 %collective-permute-start.3 = (bf16[160,1024]{1,0:T(8,128)(2,1)S(1)}, bf16[160,1024]{1,0:T(8,128)(2,1)S(1)}, u32[]{:S(2)}, u32[]{:S(2)}) collective-permute-start(bf16[160,1024]{1,0:T(8,128)(2,1)S(1)} %collective-permute-done.1.rest_1_), channel_id=1, source_target_pairs={{0,64},{8,72},{16,80},{24,88},{32,96},{40,104},{48,112},{56,120},{... | collective-permute-start | bytes 983048 | tf_op jit(solution)/shard_map/ppermute | solution.py:30
  67.4 19.5 %collective-permute-start.4 = (bf16[160,1024]{1,0:T(8,128)(2,1)S(1)}, bf16[160,1024]{1,0:T(8,128)(2,1)S(1)}, u32[]{:S(2)}, u32[]{:S(2)}) collective-permute-start(bf16[160,1024]{1,0:T(8,128)(2,1)S(1)} %collective-permute-done.2.rest_2_), channel_id=1, source_target_pairs={{0,448},{8,456},{16,464},{24,472},{32,480},{40,488},{48,496},{56,5... | collective-permute-start | bytes 983048 | tf_op jit(solution)/shard_map/ppermute | solution.py:30
  84.9 19.3 %collective-permute-start.5 = (bf16[160,1024]{1,0:T(8,128)(2,1)S(1)}, bf16[160,1024]{1,0:T(8,128)(2,1)S(1)}, u32[]{:S(2)}, u32[]{:S(2)}) collective-permute-start(bf16[160,1024]{1,0:T(8,128)(2,1)S(1)} %collective-permute-done.3.rest_3_), channel_id=1, source_target_pairs={{0,64},{8,72},{16,80},{24,88},{32,96},{40,104},{48,112},{56,120},{... | collective-permute-start | bytes 983048 | tf_op jit(solution)/shard_map/ppermute | solution.py:30
  86.9 19.9 %collective-permute-start.6 = (bf16[160,1024]{1,0:T(8,128)(2,1)S(1)}, bf16[160,1024]{1,0:T(8,128)(2,1)S(1)}, u32[]{:S(2)}, u32[]{:S(2)}) collective-permute-start(bf16[160,1024]{1,0:T(8,128)(2,1)S(1)} %collective-permute-done.4.rest_4_), channel_id=1, source_target_pairs={{0,448},{8,456},{16,464},{24,472},{32,480},{40,488},{48,496},{56,5... | collective-permute-start | bytes 983048 | tf_op jit(solution)/shard_map/ppermute | solution.py:30
  104.9 13.4 %collective-permute-start.7 = (bf16[160,512]{1,0:T(8,128)(2,1)}, bf16[160,512]{1,0:T(8,128)(2,1)S(1)}, u32[]{:S(2)}, u32[]{:S(2)}) collective-permute-start(bf16[160,512]{1,0:T(8,128)(2,1)} %slice.73), channel_id=1, source_target_pairs={{0,64},{8,72},{16,80},{24,88},{32,96},{40,104},{48,112},{56,120},{... | collective-permute-start | bytes 491528 | tf_op jit(solution)/shard_map/ppermute | solution.py:30
  107.5 11.3 %collective-permute-start.8 = (bf16[160,512]{1,0:T(8,128)(2,1)}, bf16[160,512]{1,0:T(8,128)(2,1)S(1)}, u32[]{:S(2)}, u32[]{:S(2)}) collective-permute-start(bf16[160,512]{1,0:T(8,128)(2,1)} %slice.74), channel_id=1, source_target_pairs={{0,448},{8,456},{16,464},{24,472},{32,480},{40,488},{48,496},{56,5... | collective-permute-start | bytes 491528 | tf_op jit(solution)/shard_map/ppermute | solution.py:30
  113.3 33.8 %collective-permute-start.9 = (bf16[256,256]{1,0:T(8,128)(2,1)}, bf16[256,256]{1,0:T(8,128)(2,1)}, u32[]{:S(2)}, u32[]{:S(2)}) collective-permute-start(bf16[256,256]{1,0:T(8,128)(2,1)} %bitcast.81), channel_id=1, source_target_pairs={{0,8},{8,0},{16,24},{24,16},{32,40},{40,32},{48,56},{56,48},{64,72... | collective-permute-start | bytes 393224 | tf_op jit(solution)/shard_map/ppermute | solution.py:30
  125.9 10.0 %collective-permute-start.10 = (bf16[512,128]{1,0:T(8,128)(2,1)S(1)}, bf16[512,128]{1,0:T(8,128)(2,1)S(1)}, u32[]{:S(2)}, u32[]{:S(2)}) collective-permute-start(bf16[512,128]{1,0:T(8,128)(2,1)S(1)} %get-tuple-element.11), channel_id=1, source_target_pairs={{0,16},{8,24},{16,32},{24,40},{32,48},{40,56},{48,64},{56,72},{64,... | collective-permute-start | bytes 393224 | tf_op jit(solution)/shard_map/ppermute | solution.py:30
  127.8 9.6 %collective-permute-start.11 = (bf16[512,128]{1,0:T(8,128)(2,1)S(1)}, bf16[512,128]{1,0:T(8,128)(2,1)S(1)}, u32[]{:S(2)}, u32[]{:S(2)}) collective-permute-start(bf16[512,128]{1,0:T(8,128)(2,1)S(1)} %get-tuple-element.11), channel_id=1, source_target_pairs={{0,32},{8,40},{16,48},{24,56},{32,64},{40,72},{48,80},{56,88},{64,... | collective-permute-start | bytes 393224 | tf_op jit(solution)/shard_map/ppermute | solution.py:30
  130.4 10.1 %collective-permute-start.12 = (bf16[512,128]{1,0:T(8,128)(2,1)S(1)}, bf16[512,128]{1,0:T(8,128)(2,1)S(1)}, u32[]{:S(2)}, u32[]{:S(2)}) collective-permute-start(bf16[512,128]{1,0:T(8,128)(2,1)S(1)} %get-tuple-element.11), channel_id=1, source_target_pairs={{0,48},{8,56},{16,64},{24,72},{32,80},{40,88},{48,96},{56,104},{64... | collective-permute-start | bytes 393224 | tf_op jit(solution)/shard_map/ppermute | solution.py:30
  140.5 8.0 %collective-permute-start.13 = (bf16[4,512,128]{2,1,0:T(8,128)(2,1)S(1)}, bf16[4,512,128]{2,1,0:T(8,128)(2,1)S(1)}, u32[]{:S(2)}, u32[]{:S(2)}) collective-permute-start(bf16[4,512,128]{2,1,0:T(8,128)(2,1)S(1)} %get-tuple-element.18), channel_id=1, source_target_pairs={{0,8},{8,0},{16,24},{24,16},{32,40},{40,32},{48,56},{56,48},{64,72... | collective-permute-start | bytes 1572872 | tf_op jit(solution)/shard_map/ppermute | solution.py:30
  159.9 12.2 %collective-permute-start.15 = (bf16[4,256,128]{2,1,0:T(8,128)(2,1)S(1)}, bf16[4,256,128]{2,1,0:T(8,128)(2,1)S(1)}, u32[]{:S(2)}, u32[]{:S(2)}) collective-permute-start(bf16[4,256,128]{2,1,0:T(8,128)(2,1)S(1)} %dynamic-slice_bitcast_fusion), channel_id=1, source_target_pairs={{0,8},{8,0},{16,24},{24,16},{32,40},{40,32},{48,56},{56,48},{64,72... | collective-permute-start | bytes 786440 | tf_op jit(solution)/shard_map/ppermute | solution.py:30
  172.2 14.0 %collective-permute-start.16 = (bf16[264,128]{1,0:T(8,128)(2,1)S(1)}, bf16[264,128]{1,0:T(8,128)(2,1)S(1)}, u32[]{:S(2)}, u32[]{:S(2)}) collective-permute-start(bf16[264,128]{1,0:T(8,128)(2,1)S(1)} %pad_maximum_fusion.7), channel_id=1, source_target_pairs={{0,496},{8,504},{16,0},{24,8},{32,16},{40,24},{48,32},{56,40},{64,... | collective-permute-start | bytes 202760 | tf_op jit(solution)/shard_map/ppermute | solution.py:30
  180.2 6.0 %collective-permute-start.17 = (bf16[264,128]{1,0:T(8,128)(2,1)S(1)}, bf16[264,128]{1,0:T(8,128)(2,1)S(1)}, u32[]{:S(2)}, u32[]{:S(2)}) collective-permute-start(bf16[264,128]{1,0:T(8,128)(2,1)S(1)} %pad_maximum_fusion.8), channel_id=1, source_target_pairs={{0,480},{8,488},{16,496},{24,504},{32,0},{40,8},{48,16},{56,24},{6... | collective-permute-start | bytes 202760 | tf_op jit(solution)/shard_map/ppermute | solution.py:30
  182.3 6.8 %collective-permute-start.18 = (bf16[264,128]{1,0:T(8,128)(2,1)S(1)}, bf16[264,128]{1,0:T(8,128)(2,1)S(1)}, u32[]{:S(2)}, u32[]{:S(2)}) collective-permute-start(bf16[264,128]{1,0:T(8,128)(2,1)S(1)} %pad_maximum_fusion.9), channel_id=1, source_target_pairs={{0,464},{8,472},{16,480},{24,488},{32,496},{40,504},{48,0},{56,8},... | collective-permute-start | bytes 202760 | tf_op jit(solution)/shard_map/ppermute | solution.py:30
  197.1 35.9 %all-to-all-start.2 = ((bf16[64,56,128]{2,1,0:T(8,128)(2,1)}), bf16[64,56,128]{2,1,0:T(8,128)(2,1)S(1)}, u32[]{:S(2)}, u32[]{:S(2)}) async-start(bf16[64,56,128]{2,1,0:T(8,128)(2,1)} %down_blocks.3), calls=%async_computation.2 | async-start | bytes 1835008 | tf_op jit(solution)/shard_map/all_to_all | solution.py:412
  207.4 3.3 %collective-permute-start.14 = (bf16[256,256]{1,0:T(8,128)(2,1)S(1)}, bf16[256,256]{1,0:T(8,128)(2,1)S(1)}, u32[]{:S(2)}, u32[]{:S(2)}) collective-permute-start(bf16[256,256]{1,0:T(8,128)(2,1)S(1)} %constant_dynamic-slice_fusion.2), channel_id=1, source_target_pairs={{0,8},{8,0},{16,24},{24,16},{32,40},{40,32},{48,56},{56,48},{64,72... | collective-permute-start | bytes 393224 | tf_op jit(solution)/shard_map/ppermute | solution.py:30
  233.8 18.6 %all-to-all-start.3 = ((bf16[8,32,128]{2,1,0:T(8,128)(2,1)}), bf16[8,32,128]{2,1,0:T(8,128)(2,1)S(1)}, u32[]{:S(2)}, u32[]{:S(2)}) async-start(bf16[8,32,128]{2,1,0:T(8,128)(2,1)} %broadcast_in_dim.34), calls=%async_computation.3 | async-start | bytes 131072 | tf_op jit(solution)/shard_map/all_to_all | solution.py:20
  (4 other events, 232.5 us)
Sparse Core Ops, SparseCore 0:
  50.1 75.5 all-gather.1

commit v8 on v6

--- a/solution.py
+++ b/solution.py
@@ -31,8 +31,8 @@
 
 
 def attention_kernel(
-    scale, tile, info, tokens, weight, start, grad_out, kv,
-    out, grad_query, grad_value, query, columns_in, rows_in, arrivals,
+    scale, tile, info, tokens, theirs, weight, start, grad_out, kv,
+    out, grad_query, grad_value, query, rows_in, arrivals,
 ):
     rows, size = query.shape[0], kv.shape[-1]
     heads = query.shape[1] // size
@@ -43,19 +43,21 @@
     copies = []
     for i in range(parts):
         here = pl.ds(i * depth, depth)
-        copies += [
-            pltpu.make_async_copy(tokens.at[:, here], columns_in.at[i], arrivals.at[2 * i]),
-            pltpu.make_async_copy(weight.at[here], rows_in.at[i], arrivals.at[2 * i + 1]),
-        ]
+        copies.append(pltpu.make_async_copy(weight.at[here], rows_in.at[i], arrivals.at[i]))
     for copy in copies:
         copy.start()
     grad_value[...] = jnp.zeros_like(grad_value)
-    total = start[...]
-    for i in range(parts):
-        copies[2 * i].wait()
-        copies[2 * i + 1].wait()
-        total = total + jnp.dot(columns_in[i], rows_in[i], preferred_element_type=f32)
-    query[...] = total.astype(bf16)
+    core, each = info[heads], rows // 2
+    mine = pl.ds(pl.multiple_of(core * each, each), each)
+    other = pl.ds(pl.multiple_of((1 - core) * each, each), each)
+    totals = [start[mine, :], start[other, :]]
+    for i, copy in enumerate(copies):
+        copy.wait()
+        here = slice(i * depth, (i + 1) * depth)
+        for which, source in enumerate((tokens, theirs)):
+            totals[which] += jnp.dot(source[:, here], rows_in[i], preferred_element_type=f32)
+    query[mine, :] = totals[0].astype(bf16)
+    query[other, :] = totals[1].astype(bf16)
 
     def tile_of(index, columns, count):
         here = pl.ds(pl.multiple_of(index * tile, tile), tile)
@@ -107,7 +109,7 @@
                 lax.fori_loop(0, rows // tile, step, 0)
 
 
-def attend(info, tokens, weight, start, grad_out, kv, tile=256, parts=8):
+def attend(info, tokens, theirs, weight, start, grad_out, kv, tile=256, parts=8):
     rows, width = start.shape
     model = tokens.shape[1]
     size = kv.shape[-1]
@@ -122,7 +124,8 @@
         ),
         in_specs=[
             pl.BlockSpec(memory_space=pltpu.SMEM),
-            pl.BlockSpec(memory_space=pl.ANY),
+            vmem,
+            vmem,
             pl.BlockSpec(memory_space=pl.ANY),
             vmem,
             vmem,
@@ -131,67 +134,136 @@
         out_specs=(vmem, vmem, vmem),
         scratch_shapes=[
             pltpu.VMEM((rows, width), bf16),
-            pltpu.VMEM((parts, rows, model // parts), bf16),
             pltpu.VMEM((parts, model // parts, width), bf16),
-            pltpu.SemaphoreType.DMA((2 * parts,)),
+            pltpu.SemaphoreType.DMA((parts,)),
         ],
-        compiler_params=pltpu.CompilerParams(vmem_limit_bytes=48 * 1024 * 1024),
+        compiler_params=pltpu.CompilerParams(vmem_limit_bytes=30 * 1024 * 1024),
         cost_estimate=pl.CostEstimate(
             flops=10 * rows * width * blocks * block + 2 * rows * width * model,
             bytes_accessed=16 * 1024 * 1024,
             transcendentals=rows * width // size * blocks * block,
         ),
         name="attention",
-    )(info, tokens, weight, start, grad_out, kv)
-
-
-def blocks_kernel(rank_terms, tokens, above, below, out):
-    top, size = above.shape[1], out.shape[2]
-    bottom = top + rank_terms.shape[0]
-    product = jnp.dot(rank_terms[...], tokens[...], preferred_element_type=f32).astype(bf16)
-    for i in range(out.shape[0]):
-        out[i, :top] = above[i]
-        out[i, top:bottom] = product[:, i * size : (i + 1) * size]
-        out[i, bottom:] = below[...]
-
-
-def first_blocks_kernel(rank_terms, tokens, out):
+    )(info, tokens, theirs, weight, start, grad_out, kv)
+
+
+def column_copies(sources, buffer, arrivals):
+    parts, width = buffer.shape[0], buffer.shape[-1]
+    copies = [
+        [
+            pltpu.make_async_copy(
+                source.at[:, pl.ds(i * width, width)],
+                buffer.at[i, which],
+                arrivals.at[len(sources) * i + which],
+            )
+            for which, source in enumerate(sources)
+        ]
+        for i in range(parts)
+    ]
+    for copy in sum(copies, []):
+        copy.start()
+    return copies
+
+
+def multiply_parts(ranks, copies, buffer, store):
+    for i, part in enumerate(copies):
+        for copy in part:
+            copy.wait()
+        product = functools.reduce(
+            jnp.add,
+            [
+                jnp.dot(r, buffer[i, which], preferred_element_type=f32)
+                for which, r in enumerate(ranks)
+            ],
+        ).astype(bf16)
+        store(i, product)
+
+
+def query_blocks_kernel(rank_mine, rank_theirs, tokens, theirs, out, buffer, arrivals):
+    copies = column_copies((tokens, theirs), buffer, arrivals)
     size = out.shape[2]
-    product = jnp.dot(rank_terms[...], tokens[...], preferred_element_type=f32).astype(bf16)
-    for i in range(out.shape[0]):
-        out[i] = product[:, i * size : (i + 1) * size]
-
-
-def down_blocks(rank_terms, tokens, devices, above=None, below=None, steps=4):
-    ranks, rows = rank_terms.shape
-    size = tokens.shape[1] // devices
-    step = devices // steps
-    in_specs = [
-        pl.BlockSpec((ranks, rows), lambda i: (0, 0)),
-        pl.BlockSpec((rows, step * size), lambda i: (0, i)),
-    ]
-    more, height, kernel = (), ranks, first_blocks_kernel
-    if above is not None:
-        more, kernel = (above, below), blocks_kernel
-        height += above.shape[1] + below.shape[0]
-        in_specs += [
-            pl.BlockSpec((step, *above.shape[1:]), lambda i: (i, 0, 0)),
-            pl.BlockSpec(below.shape, lambda i: (0, 0)),
-        ]
+    each = buffer.shape[-1] // size
+
+    def store(i, product):
+        for j in range(each):
+            out[i * each + j] = product[:, j * size : (j + 1) * size]
+
+    multiply_parts((rank_mine[...], rank_theirs[...]), copies, buffer, store)
+
+
+def query_blocks(rank_mine, rank_theirs, tokens, theirs, devices, parts=4):
+    rows, model = tokens.shape
+    vmem = pl.BlockSpec(memory_space=pltpu.VMEM)
+    anywhere = pl.BlockSpec(memory_space=pl.ANY)
+    ranks = rank_mine.shape[0]
     return pl.pallas_call(
-        kernel,
-        out_shape=jax.ShapeDtypeStruct((devices, height, size), bf16),
-        grid=(steps,),
-        in_specs=in_specs,
-        out_specs=pl.BlockSpec((step, height, size), lambda i: (i, 0, 0)),
-        compiler_params=pltpu.CompilerParams(vmem_limit_bytes=56 * 1024 * 1024),
+        query_blocks_kernel,
+        out_shape=jax.ShapeDtypeStruct((devices, ranks, model // devices), bf16),
+        in_specs=[vmem, vmem, anywhere, anywhere],
+        out_specs=vmem,
+        scratch_shapes=[
+            pltpu.VMEM((parts, 2, rows, model // parts), bf16),
+            pltpu.SemaphoreType.DMA((2 * parts,)),
+        ],
+        compiler_params=pltpu.CompilerParams(vmem_limit_bytes=40 * 1024 * 1024),
         cost_estimate=pl.CostEstimate(
-            flops=2 * ranks * rows * devices * size,
-            bytes_accessed=2 * rows * devices * size,
-            transcendentals=0,
+            flops=4 * ranks * rows * model, bytes_accessed=4 * rows * model, transcendentals=0
         ),
-        name="down_blocks",
-    )(rank_terms, tokens, *more)
+        name="query_blocks",
+    )(rank_mine, rank_theirs, tokens, theirs)
+
+
+def all_blocks_kernel(own, *refs):
+    arrived, (up, low, above, tokens, out, gradient, buffer, arrivals) = refs[:-8], refs[-8:]
+    copies = column_copies((tokens,), buffer, arrivals)
+    rows, size = gradient.shape
+    each = buffer.shape[-1] // size
+    total = own[...]
+    for other in arrived:
+        total += other[...].astype(f32)
+    total = total.astype(bf16)
+    mine = total[:rows]
+    gradient[...] = mine
+    ranks = lax.dot_general(up[...], mine, NT, preferred_element_type=f32).astype(bf16)
+    up_part = lax.dot_general(low[...], mine, TN, preferred_element_type=f32).astype(bf16)
+    top = above.shape[1]
+    bottom = top + ranks.shape[0]
+    last = bottom + up_part.shape[0]
+
+    def store(i, product):
+        for j in range(each):
+            block = i * each + j
+            out[block, :top] = above[block]
+            out[block, top:bottom] = product[:, j * size : (j + 1) * size]
+            out[block, bottom:last] = up_part
+            out[block, last:] = total[rows:]
+
+    multiply_parts((ranks,), copies, buffer, store)
+
+
+def all_blocks(own, arrived, up, low, above, tokens, parts=4):
+    rows, model = tokens.shape
+    devices, ranks, size = above.shape
+    vmem = pl.BlockSpec(memory_space=pltpu.VMEM)
+    height = 3 * ranks + own.shape[0] - rows
+    return pl.pallas_call(
+        all_blocks_kernel,
+        out_shape=(
+            jax.ShapeDtypeStruct((devices, height, size), bf16),
+            jax.ShapeDtypeStruct((rows, size), bf16),
+        ),
+        in_specs=[vmem] * (4 + len(arrived)) + [pl.BlockSpec(memory_space=pl.ANY)],
+        out_specs=(vmem, vmem),
+        scratch_shapes=[
+            pltpu.VMEM((parts, 1, rows, model // parts), bf16),
+            pltpu.SemaphoreType.DMA((parts,)),
+        ],
+        compiler_params=pltpu.CompilerParams(vmem_limit_bytes=40 * 1024 * 1024),
+        cost_estimate=pl.CostEstimate(
+            flops=2 * ranks * rows * model, bytes_accessed=3 * rows * model, transcendentals=0
+        ),
+        name="all_blocks",
+    )(own, *arrived, up, low, above, tokens)
 
 
 def on_device(
@@ -230,7 +302,7 @@
     def half_of(array, which):
         return lax.dynamic_slice_in_dim(array, which * (array.shape[0] // 2), array.shape[0] // 2)
 
-    chip_tokens = both(tokens, to_chip(tokens, 0, True))
+    theirs = to_chip(tokens, 0, True)
     grad_halves = output_gradient.reshape(rows, 2, half).transpose(1, 0, 2)
     grad_mine = lax.dynamic_index_in_dim(grad_halves, core, 0, keepdims=False)
     grad_away = lax.dynamic_index_in_dim(grad_halves, 1 - core, 0, keepdims=False)
@@ -238,11 +310,14 @@
 
     down = adapter_down_weight.T
     kv_rows = jnp.stack(
-        [jnp.concatenate([key_weight.T, down]), jnp.concatenate([value_weight.T, down])]
+        [
+            jnp.concatenate([key_weight.T, down[:rank]]),
+            jnp.concatenate([value_weight.T, down[rank:]]),
+        ]
     )
     kv_rows = jnp.broadcast_to(kv_rows[None], (chips, *kv_rows.shape))
     kv_rows = lax.all_to_all(
-        kv_rows.reshape(members, size + 2 * rank, depth),
+        kv_rows.reshape(members, size + rank, depth),
         "ctx", 0, 0, tiled=True, axis_index_groups=plain,
     )
     kv_rows = lax.all_gather(kv_rows, "ctx", axis=0, tiled=True, axis_index_groups=across)
@@ -257,12 +332,17 @@
         "ctx", axis=0, tiled=True, axis_index_groups=across,
     )
 
-    kv_weight = kv_rows.transpose(1, 0, 2).reshape(size + 2 * rank, model)
-    mine = lax.dot_general(chip_tokens, kv_weight, NT, preferred_element_type=f32)
+    kv_weight = kv_rows.transpose(1, 0, 2).reshape(size + rank, model)
+    mine = both(
+        lax.dot_general(tokens, kv_weight, NT, preferred_element_type=f32),
+        lax.dot_general(theirs, kv_weight, NT, preferred_element_type=f32),
+    )
     low = mine[:, size:].astype(bf16)
-    low_q, low_v = low[:, :rank], low[:, rank:]
-    extra = jnp.dot(low_v, value_up_weight, preferred_element_type=f32)
+    extra = jnp.dot(low, value_up_weight, preferred_element_type=f32)
     mine = (mine[:, :size] + jnp.where(core == 1, extra, 0.0)).astype(bf16)
+    low_away = to_chip(low, 0, True)
+    low_q = jnp.where(core == 0, low, low_away)
+    low_v = jnp.where(core == 0, low_away, low)
     mine = jnp.stack([mine] + [to_chip(mine, d, False) for d in range(1, chips)])
     kv = jnp.stack([mine, to_chip(mine, 0, True)])
 
@@ -271,7 +351,9 @@
     shifts = lax.dynamic_slice_in_dim(head_shifts, core * (heads // 2), heads // 2)
     seen = jnp.where(shifts != 0, lax.rem(chip + chips // 2, chips), chip)
     info = jnp.concatenate([seen, core[None]]).astype(jnp.int32)
-    output, grad_query, value_parts = attend(info, chip_tokens, q_rows, start, grad_out, kv)
+    output, grad_query, value_parts = attend(
+        info, tokens, theirs, q_rows, start, grad_out, kv
+    )
 
     attention_mine = half_of(output, core)
     attention_other = to_chip(half_of(output, 1 - core), 0, True)
@@ -283,9 +365,6 @@
         axis=1,
     )
 
-    rank_q = lax.dot_general(up_mine, grad_query, NT, preferred_element_type=f32).astype(bf16)
-    q_blocks = down_blocks(rank_q, chip_tokens, devices)
-
     query_up_part = lax.dot_general(low_q, grad_query, TN, preferred_element_type=f32)
     query_up_part = query_up_part.reshape(chips, -1, size)
     value_parts = value_parts.reshape(chips, 2, rows, size).astype(bf16)
@@ -301,17 +380,16 @@
 
     arrived = [with_share(0)]
     arrived += [to_chip(with_share(d).astype(bf16), -d, False) for d in range(1, chips)]
-    arrived = functools.reduce(jnp.add, [a.astype(f32) for a in arrived]).astype(bf16)
-    value_gradient = arrived[:rows]
-
-    rank_v = lax.dot_general(
-        value_up_weight, value_gradient, NT, preferred_element_type=f32
-    ).astype(bf16)
-    value_up_part = lax.dot_general(
-        half_of(low_v, core), value_gradient, TN, preferred_element_type=f32
-    ).astype(bf16)
-    shared = jnp.concatenate([value_up_part, arrived[rows:]], axis=0)
-    blocks = down_blocks(rank_v, tokens, devices, q_blocks, shared)
+
+    rank_q = lax.dot_general(up_mine, grad_query, NT, preferred_element_type=f32).astype(bf16)
+    rank_q = rank_q + (value_parts[0, 0, 0] * 0).astype(bf16)
+    rank_halves = rank_q.reshape(rank, 2, rows)
+    rank_mine = lax.dynamic_index_in_dim(rank_halves, core, 1, keepdims=False)
+    rank_theirs = lax.dynamic_index_in_dim(rank_halves, 1 - core, 1, keepdims=False)
+    blocks = query_blocks(rank_mine, rank_theirs, tokens, theirs, devices)
+    blocks, value_gradient = all_blocks(
+        arrived[0], arrived[1:], value_up_weight, half_of(low_v, core), blocks, tokens
+    )
     blocks = lax.all_to_all(blocks, "ctx", 0, 0, tiled=True)
     summed = jnp.sum(blocks[:, : 3 * rank].astype(f32), axis=0)
     grad_down = jnp.sum(spread(summed[: 2 * rank].astype(bf16), "fsdp").astype(f32), axis=0)

time: 241 us -> 237 us (0.983)
  other arithmetic: 17.4 us -> 3.14 us
  waiting for transfers between devices: 71.6 us -> 80.4 us
  local copies, waits for them, and re-layouts: 4.8 us -> 12.3 us
  Pallas kernels: 22.3 us -> 16.4 us
    concatenate x2 -> x1, other arithmetic: 7.83 us -> 0.02 us  [both(): jnp.concatenate([jnp.where(core == 0, mine, theirs), jnp.where(core == 0,...]
    unnamed x13 -> x22, local copies, waits for them, and re-layouts: 0.79 us -> 7.56 us
    select_n x2 -> x1, other arithmetic: 5.89 us -> 0.03 us  [both(): jnp.where(core == 0, mine, theirs)]
    all_gather x1, waiting for transfers between devices: 12.1 us -> 17.3 us  [on_device(): lax.all_gather(kv_rows, 'ctx', axis=0, tiled=True, axis_index_groups=across)]
    pallas_call x2, Pallas kernels: 9.83 us -> 5.54 us  [the longest x1 3.07 us: query_blocks(): pl.pallas_call(query_blocks_kernel, out_shape=jax.ShapeDtypeStruct((devic...]
    all_gather x1, waiting for transfers between devices: 19.8 us -> 23.7 us  [on_device(): lax.all_gather(q_rows.reshape(members * depth, half), 'ctx', axis=0, tile...]
    ppermute x11 -> x12, starting transfers between devices: 46.4 us -> 45.7 us  [to_chip(): return lax.ppermute(value, 'ctx', pairs)]
    dot_general x4 -> x3, matrix products: 8.25 us -> 7.92 us  [the longest x1 4.29 us: on_device(): lax.dot_general(tokens, kv_weight, NT, preferred_element_type=f32)]
  transfers between devices with their start and end apart: 15 -> 16, of which waited for: 9 -> 9; matrix products, arithmetic and copies ran while one was open for 11% -> 5% of each run, Pallas kernels for 2% -> 1%
where the time goes in v8:
time: 237 us; the launch traced here: 236 us
  waiting for transfers between devices  80.4 us (34%)
  starting transfers between devices  61.6 us (26%)
  blocking collectives  38.1 us (16%)
  Pallas kernels  16.4 us (7%)
  between operations  15.3 us (6%)
  local copies, waits for them, and re-layouts  12.3 us (5%)
  matrix products  8.44 us (4%)
  other arithmetic  3.14 us (1%)
    ppermute x12, starting transfers between devices, to_chip(): return lax.ppermute(value, 'ctx', pairs)  45.7 us
    all_gather x1, waiting for transfers between devices, on_device(): lax.all_gather(q_rows.reshape(members * depth, half), 'ctx', axis=0, tile...  23.7 us
    all_to_all x1, waiting for transfers between devices, on_device(): blocks = lax.all_to_all(blocks, 'ctx', 0, 0, tiled=True)  21.5 us
    all_to_all x1, blocking collectives, on_device(): lax.all_to_all(kv_rows.reshape(members, size + rank, depth), 'ctx', 0, 0,...  19.8 us
    all_to_all x1, blocking collectives, on_device(): lax.all_to_all(q_rows.reshape(members, depth, half), 'ctx', 0, 0, tiled=T...  18.3 us
    all_gather x1, waiting for transfers between devices, on_device(): lax.all_gather(kv_rows, 'ctx', axis=0, tiled=True, axis_index_groups=across)  17.3 us
    pallas_call x1, Pallas kernels, attend(): pl.pallas_call(functools.partial(attention_kernel, size ** (-0.5), tile),...  10.8 us
    ppermute x12, waiting for transfers between devices, to_chip(): return lax.ppermute(value, 'ctx', pairs)  10.2 us
  transfers between devices with their start and end apart: 16, of which 9 were waited for; matrix products, arithmetic and copies ran while one was open for 5% of the time, Pallas kernels for 1%

profile of v8, /device:TPU:1, one launch (start us, length us, event | category | flops | bytes accessed | tf_op | source)
XLA Modules:
  0.0 235.6 jit_solution(653301550876288978)
XLA Ops:
  9.2 19.8 %all_to_all.20 = bf16[8,144,128]{2,1,0:T(8,128)(2,1)} all-to-all(bf16[8,144,128]{2,1,0:T(8,128)(2,1)S(1)} %bitcast.99), channel_id=1, replica_groups={{0,8,16,24,32,40,48,56},{64,72,80,88,96,104,112,120},{128,136,144,152,1..., dimensions={0} | all-to-all | bytes 589824 | tf_op jit(solution)/shard_map/all_to_all | solution.py:319
  30.1 18.3 %all_to_all.21 = bf16[8,128,256]{2,1,0:T(8,128)(2,1)} all-to-all(bf16[8,128,256]{2,1,0:T(8,128)(2,1)S(1)} %bitcast.97), channel_id=1, replica_groups={{0,8,16,24,32,40,48,56},{64,72,80,88,96,104,112,120},{128,136,144,152,1..., dimensions={0} | all-to-all | bytes 1048576 | tf_op jit(solution)/shard_map/all_to_all | solution.py:326
  48.4 2.7 %collective-permute-start = (bf16[256,8192]{1,0:T(8,128)(2,1)}, bf16[256,8192]{1,0:T(8,128)(2,1)}, u32[]{:S(2)}, u32[]{:S(2)}) collective-permute-start(bf16[256,8192]{1,0:T(8,128)(2,1)} %refs_6_.1), channel_id=1, source_target_pairs={{0,8},{8,0},{16,24},{24,16},{32,40},{40,32},{48,56},{56,48},{64,72... | collective-permute-start | bytes 12582920 | tf_op jit(solution)/shard_map/ppermute | solution.py:30
  53.7 17.3 %all-gather.5.cloned.1.call-done = bf16[64,144,128]{2,1,0:T(8,128)(2,1)} async-done(((bf16[8,144,128]{2,1,0:T(8,128)(2,1)}), bf16[64,144,128]{2,1,0:T(8,128)(2,1)}) %all-gather.5.cloned.1.call-update) | async-done | bytes 2359312 | tf_op jit(solution)/shard_map/all_gather | solution.py:323
  70.9 4.3 %fusion.2 = f32[144,256]{0,1:T(8,128)S(1)} fusion(bf16[256,8192]{1,0:T(8,128)(2,1)} %refs_6_.1, bf16[64,144,128]{2,1,0:T(8,128)(2,1)} %all-gather.5.cloned.1.call-done), kind=kOutput, calls=%fused_computation.2 | convolution fusion | flops 603979776 | bytes 6701056 | tf_op jit(solution)/shard_map/dot_general | solution.py:337
  75.3 3.5 %select_bitcast_fusion = (f32[256,144]{1,0:T(8,128)S(1)}, f32[256,144]{1,0:T(8,128)S(1)}) fusion(f32[144,256]{0,1:T(8,128)S(1)} %fusion.2, pred[]{:T(512)S(6)} %eq.4, bf16[256,8192]{1,0:T(8,128)(2,1)} %collective-permute-done.theirs, bf16[64,144,128]{2,1,0:T(8,128)(2,1)S(1)} %copy-done.8), kind=kOutput, calls=%fused_computation.23 | convolution fusion | flops 604053504 | bytes 6995969 | tf_op jit(solution)/shard_map/dot_general | solution.py:338
  79.0 3.3 %collective-permute-start.3 = (bf16[512,128]{1,0:T(8,128)(2,1)S(1)}, bf16[512,128]{1,0:T(8,128)(2,1)S(1)}, u32[]{:S(2)}, u32[]{:S(2)}) collective-permute-start(bf16[512,128]{1,0:T(8,128)(2,1)S(1)} %fusion.7), channel_id=1, source_target_pairs={{0,16},{8,24},{16,32},{24,40},{32,48},{40,56},{48,64},{56,72},{64,... | collective-permute-start | bytes 393224 | tf_op jit(solution)/shard_map/ppermute | solution.py:30
  82.2 4.4 %collective-permute-start.4 = (bf16[512,128]{1,0:T(8,128)(2,1)S(1)}, bf16[512,128]{1,0:T(8,128)(2,1)S(1)}, u32[]{:S(2)}, u32[]{:S(2)}) collective-permute-start(bf16[512,128]{1,0:T(8,128)(2,1)S(1)} %fusion.7), channel_id=1, source_target_pairs={{0,32},{8,40},{16,48},{24,56},{32,64},{40,72},{48,80},{56,88},{64,... | collective-permute-start | bytes 393224 | tf_op jit(solution)/shard_map/ppermute | solution.py:30
  86.6 3.2 %collective-permute-start.5 = (bf16[512,128]{1,0:T(8,128)(2,1)S(1)}, bf16[512,128]{1,0:T(8,128)(2,1)S(1)}, u32[]{:S(2)}, u32[]{:S(2)}) collective-permute-start(bf16[512,128]{1,0:T(8,128)(2,1)S(1)} %fusion.7), channel_id=1, source_target_pairs={{0,48},{8,56},{16,64},{24,72},{32,80},{40,88},{48,96},{56,104},{64... | collective-permute-start | bytes 393224 | tf_op jit(solution)/shard_map/ppermute | solution.py:30
  91.3 5.7 %collective-permute-done.5 = bf16[512,128]{1,0:T(8,128)(2,1)S(1)} collective-permute-done((bf16[512,128]{1,0:T(8,128)(2,1)S(1)}, bf16[512,128]{1,0:T(8,128)(2,1)S(1)}, u32[]{:S(2)}, u32[]{:S(2)}) %collective-permute-start.5) | collective-permute-done | bytes 131104 | tf_op jit(solution)/shard_map/ppermute | solution.py:30
  97.1 7.7 %collective-permute-start.6 = (bf16[4,512,128]{2,1,0:T(8,128)(2,1)S(1)}, bf16[4,512,128]{2,1,0:T(8,128)(2,1)S(1)}, u32[]{:S(2)}, u32[]{:S(2)}) collective-permute-start(bf16[4,512,128]{2,1,0:T(8,128)(2,1)S(1)} %get-tuple-element.18), channel_id=1, source_target_pairs={{0,8},{8,0},{16,24},{24,16},{32,40},{40,32},{48,56},{56,48},{64,72... | collective-permute-start | bytes 1572872 | tf_op jit(solution)/shard_map/ppermute | solution.py:30
  108.4 23.7 %all-gather.3.cloned.1.call-done.weight = bf16[8192,256]{1,0:T(8,128)(2,1)} async-done(((bf16[1024,256]{1,0:T(8,128)(2,1)}), bf16[8192,256]{1,0:T(8,128)(2,1)}) %all-gather.3.cloned.1.call-update) | async-done | bytes 4194320 | tf_op jit(solution)/shard_map/all_gather | solution.py:330
  136.5 10.8 %attention.1 = (bf16[512,256]{1,0:T(8,128)(2,1)S(1)}, bf16[512,256]{1,0:T(8,128)(2,1)S(1)}, f32[4,512,128]{2,1,0:T(8,128)S(1)}) custom-call(s32[3]{0:T(128)S(1)} %pad_add_fusion.info, bf16[256,8192]{1,0:T(8,128)(2,1)S(1)} %copy-done.1, bf16[256,8192]{1,0:T(8,128)(2,1)} %collective-permute-done.theirs, bf16[8192,256]{1,0:T(8,128)(2,1)S(1)} %copy-done.5, ...), custom_call_target="tpu_custom_call" | custom-call | flops 4831838208 | bytes 16777216 | tf_op jit(solution)/shard_map/attention/pallas_call | solution.py:118
  147.5 4.4 %collective-permute-start.8 = (bf16[4,256,128]{2,1,0:T(8,128)(2,1)S(1)}, bf16[4,256,128]{2,1,0:T(8,128)(2,1)S(1)}, u32[]{:S(2)}, u32[]{:S(2)}) collective-permute-start(bf16[4,256,128]{2,1,0:T(8,128)(2,1)S(1)} %dynamic-slice_bitcast_fusion), channel_id=1, source_target_pairs={{0,8},{8,0},{16,24},{24,16},{32,40},{40,32},{48,56},{56,48},{64,72... | collective-permute-start | bytes 786440 | tf_op jit(solution)/shard_map/ppermute | solution.py:30
  154.7 8.0 %collective-permute-start.11 = (bf16[264,128]{1,0:T(8,128)(2,1)S(1)}, bf16[264,128]{1,0:T(8,128)(2,1)S(1)}, u32[]{:S(2)}, u32[]{:S(2)}) collective-permute-start(bf16[264,128]{1,0:T(8,128)(2,1)S(1)} %pad_maximum_fusion.10), channel_id=1, source_target_pairs={{0,464},{8,472},{16,480},{24,488},{32,496},{40,504},{48,0},{56,8},... | collective-permute-start | bytes 202760 | tf_op jit(solution)/shard_map/ppermute | solution.py:30
  162.7 2.4 %collective-permute-start.10 = (bf16[264,128]{1,0:T(8,128)(2,1)S(1)}, bf16[264,128]{1,0:T(8,128)(2,1)S(1)}, u32[]{:S(2)}, u32[]{:S(2)}) collective-permute-start(bf16[264,128]{1,0:T(8,128)(2,1)S(1)} %pad_maximum_fusion.9), channel_id=1, source_target_pairs={{0,480},{8,488},{16,496},{24,504},{32,0},{40,8},{48,16},{56,24},{6... | collective-permute-start | bytes 202760 | tf_op jit(solution)/shard_map/ppermute | solution.py:30
  165.1 3.5 %collective-permute-start.9 = (bf16[264,128]{1,0:T(8,128)(2,1)S(1)}, bf16[264,128]{1,0:T(8,128)(2,1)S(1)}, u32[]{:S(2)}, u32[]{:S(2)}) collective-permute-start(bf16[264,128]{1,0:T(8,128)(2,1)S(1)} %pad_maximum_fusion.8), channel_id=1, source_target_pairs={{0,496},{8,504},{16,0},{24,8},{32,16},{40,24},{48,32},{56,40},{64,... | collective-permute-start | bytes 202760 | tf_op jit(solution)/shard_map/ppermute | solution.py:30
  170.8 3.1 %query_blocks.1.refs_5_ = bf16[64,16,128]{2,1,0:T(8,128)(2,1)S(1)} custom-call(bf16[16,256]{1,0:T(8,128)(2,1)S(1)} %bitcast.94, bf16[16,256]{1,0:T(8,128)(2,1)S(1)} %bitcast.93, bf16[256,8192]{1,0:T(8,128)(2,1)S(1)} %copy-done.2, bf16[256,8192]{1,0:T(8,128)(2,1)} %collective-permute-done.theirs), custom_call_target="tpu_custom_call" | custom-call | flops 134217728 | bytes 8388608 | tf_op jit(solution)/shard_map/query_blocks/pallas_call | solution.py:199
  174.3 2.5 %all_blocks.1 = (bf16[64,56,128]{2,1,0:T(8,128)(2,1)}, bf16[256,128]{1,0:T(8,128)(2,1)}) custom-call(f32[264,128]{1,0:T(8,128)S(1)} %pad_maximum_fusion.5.own, bf16[264,128]{1,0:T(8,128)(2,1)S(1)} %collective-permute-done.9.refs_0_, bf16[264,128]{1,0:T(8,128)(2,1)S(1)} %collective-permute-done.10.refs_1_, ...), custom_call_target="tpu_custom_call" | custom-call | flops 67108864 | bytes 6291456 | tf_op jit(solution)/shard_map/all_blocks/pallas_call | solution.py:249
  176.8 7.1 %all-to-all-start.2 = ((bf16[64,56,128]{2,1,0:T(8,128)(2,1)}), bf16[64,56,128]{2,1,0:T(8,128)(2,1)S(1)}, u32[]{:S(2)}, u32[]{:S(2)}) async-start(bf16[64,56,128]{2,1,0:T(8,128)(2,1)} %get-tuple-element.14), calls=%async_computation.2 | async-start | bytes 1835008 | tf_op jit(solution)/shard_map/all_to_all | solution.py:393
  183.9 2.4 %collective-permute-start.7 = (bf16[256,256]{1,0:T(8,128)(2,1)S(1)}, bf16[256,256]{1,0:T(8,128)(2,1)S(1)}, u32[]{:S(2)}, u32[]{:S(2)}) collective-permute-start(bf16[256,256]{1,0:T(8,128)(2,1)S(1)} %constant_dynamic-slice_fusion.2), channel_id=1, source_target_pairs={{0,8},{8,0},{16,24},{24,16},{32,40},{40,32},{48,56},{56,48},{64,72... | collective-permute-start | bytes 393224 | tf_op jit(solution)/shard_map/ppermute | solution.py:30
  188.1 21.5 %all-to-all-done.2 = bf16[64,56,128]{2,1,0:T(8,128)(2,1)S(1)} async-done(((bf16[64,56,128]{2,1,0:T(8,128)(2,1)}), bf16[64,56,128]{2,1,0:T(8,128)(2,1)S(1)}, u32[]{:S(2)}, u32[]{:S(2)}) %all-to-all-start.2) | async-done | bytes 917536 | tf_op jit(solution)/shard_map/all_to_all | solution.py:393
  210.3 8.7 %all-to-all-start.3 = ((bf16[8,32,128]{2,1,0:T(8,128)(2,1)}), bf16[8,32,128]{2,1,0:T(8,128)(2,1)S(1)}, u32[]{:S(2)}, u32[]{:S(2)}) async-start(bf16[8,32,128]{2,1,0:T(8,128)(2,1)} %broadcast_in_dim.39), calls=%async_computation.3 | async-start | bytes 131072 | tf_op jit(solution)/shard_map/all_to_all | solution.py:20
  220.5 7.7 %all-to-all-done.3 = bf16[8,32,128]{2,1,0:T(8,128)(2,1)S(1)} async-done(((bf16[8,32,128]{2,1,0:T(8,128)(2,1)}), bf16[8,32,128]{2,1,0:T(8,128)(2,1)S(1)}, u32[]{:S(2)}, u32[]{:S(2)}) %all-to-all-start.3) | async-done | bytes 65568 | tf_op jit(solution)/shard_map/all_to_all | solution.py:20
  (90 shorter events, 24.5 us)
Async XLA Ops:
  7.2 100.9 %copy-start = (bf16[16,512]{1,0:T(8,128)(2,1)S(1)}, bf16[16,512]{1,0:T(8,128)(2,1)}, u32[]{:S(2)}) copy-start(bf16[16,512]{1,0:T(8,128)(2,1)} %param.14) | copy-start | bytes 49156
  7.2 63.8 %all-gather.5.cloned.1.call-start = ((), (), s32[]{:S(2)}) async-start(), calls=%async_computation.5 | async-start | bytes 2654208 | tf_op jit(solution)/shard_map/all_gather | solution.py:323
  8.2 42.9 %copy-start.6 = (bf16[256,512]{1,0:T(8,128)(2,1)S(1)}, bf16[256,512]{1,0:T(8,128)(2,1)}, u32[]{:S(2)}) copy-start(bf16[256,512]{1,0:T(8,128)(2,1)} %param.17) | copy-start | bytes 786436
  29.1 103.1 %all-gather.3.cloned.1.call-start = ((), (), s32[]{:S(2)}) async-start(), calls=%async_computation.4 | async-start | bytes 4718592 | tf_op jit(solution)/shard_map/all_gather | solution.py:330
  48.4 26.9 %collective-permute-start = (bf16[256,8192]{1,0:T(8,128)(2,1)}, bf16[256,8192]{1,0:T(8,128)(2,1)}, u32[]{:S(2)}, u32[]{:S(2)}) collective-permute-start(bf16[256,8192]{1,0:T(8,128)(2,1)} %refs_6_.1), channel_id=1, source_target_pairs={{0,8},{8,0},{16,24},{24,16},{32,40},{40,32},{48,56},{56,48},{64,72... | collective-permute-start | bytes 12582920 | tf_op jit(solution)/shard_map/ppermute | solution.py:30
  51.7 53.1 %collective-permute-start.2 = (bf16[256,256]{1,0:T(8,128)(2,1)S(1)}, bf16[256,256]{1,0:T(8,128)(2,1)S(1)}, u32[]{:S(2)}, u32[]{:S(2)}) collective-permute-start(bf16[256,256]{1,0:T(8,128)(2,1)S(1)} %bitcast.102), channel_id=1, source_target_pairs={{0,8},{8,0},{16,24},{24,16},{32,40},{40,32},{48,56},{56,48},{64,72... | collective-permute-start | bytes 393224 | tf_op jit(solution)/shard_map/ppermute | solution.py:30
  70.9 4.3 %copy-start.8 = (bf16[64,144,128]{2,1,0:T(8,128)(2,1)S(1)}, bf16[64,144,128]{2,1,0:T(8,128)(2,1)}, u32[]{:S(2)}) copy-start(bf16[64,144,128]{2,1,0:T(8,128)(2,1)} %all-gather.5.cloned.1.call-done) | copy-start | bytes 7077892
  75.2 3.6 %copy-start.4 = (bf16[16,128]{1,0:T(8,128)(2,1)S(1)}, bf16[16,128]{1,0:T(8,128)(2,1)}, u32[]{:S(2)}) copy-start(bf16[16,128]{1,0:T(8,128)(2,1)} %refs_3_.1) | copy-start | bytes 12292
  75.2 14.6 %copy-start.7 = (s32[4]{0:T(128)S(1)}, s32[4]{0:T(128)}, u32[]{:S(2)}) copy-start(s32[4]{0:T(128)} %param.16) | copy-start | bytes 52
  79.0 11.0 %collective-permute-start.3 = (bf16[512,128]{1,0:T(8,128)(2,1)S(1)}, bf16[512,128]{1,0:T(8,128)(2,1)S(1)}, u32[]{:S(2)}, u32[]{:S(2)}) collective-permute-start(bf16[512,128]{1,0:T(8,128)(2,1)S(1)} %fusion.7), channel_id=1, source_target_pairs={{0,16},{8,24},{16,32},{24,40},{32,48},{40,56},{48,64},{56,72},{64,... | collective-permute-start | bytes 393224 | tf_op jit(solution)/shard_map/ppermute | solution.py:30
  82.2 9.0 %collective-permute-start.4 = (bf16[512,128]{1,0:T(8,128)(2,1)S(1)}, bf16[512,128]{1,0:T(8,128)(2,1)S(1)}, u32[]{:S(2)}, u32[]{:S(2)}) collective-permute-start(bf16[512,128]{1,0:T(8,128)(2,1)S(1)} %fusion.7), channel_id=1, source_target_pairs={{0,32},{8,40},{16,48},{24,56},{32,64},{40,72},{48,80},{56,88},{64,... | collective-permute-start | bytes 393224 | tf_op jit(solution)/shard_map/ppermute | solution.py:30
  86.6 10.4 %collective-permute-start.5 = (bf16[512,128]{1,0:T(8,128)(2,1)S(1)}, bf16[512,128]{1,0:T(8,128)(2,1)S(1)}, u32[]{:S(2)}, u32[]{:S(2)}) collective-permute-start(bf16[512,128]{1,0:T(8,128)(2,1)S(1)} %fusion.7), channel_id=1, source_target_pairs={{0,48},{8,56},{16,64},{24,72},{32,80},{40,88},{48,96},{56,104},{64... | collective-permute-start | bytes 393224 | tf_op jit(solution)/shard_map/ppermute | solution.py:30
  97.1 11.2 %collective-permute-start.6 = (bf16[4,512,128]{2,1,0:T(8,128)(2,1)S(1)}, bf16[4,512,128]{2,1,0:T(8,128)(2,1)S(1)}, u32[]{:S(2)}, u32[]{:S(2)}) collective-permute-start(bf16[4,512,128]{2,1,0:T(8,128)(2,1)S(1)} %get-tuple-element.18), channel_id=1, source_target_pairs={{0,8},{8,0},{16,24},{24,16},{32,40},{40,32},{48,56},{56,48},{64,72... | collective-permute-start | bytes 1572872 | tf_op jit(solution)/shard_map/ppermute | solution.py:30
  104.8 3.2 %collective-permute-start.1 = (bf16[512,16]{1,0:T(8,128)(2,1)S(1)}, bf16[512,16]{1,0:T(8,128)(2,1)S(1)}, u32[]{:S(2)}, u32[]{:S(2)}) collective-permute-start(bf16[512,16]{1,0:T(8,128)(2,1)S(1)} %fusion.10), channel_id=1, source_target_pairs={{0,8},{8,0},{16,24},{24,16},{32,40},{40,32},{48,56},{56,48},{64,72... | collective-permute-start | bytes 49160 | tf_op jit(solution)/shard_map/ppermute | solution.py:30
  132.2 2.2 copy-start.1
  147.5 5.6 %collective-permute-start.8 = (bf16[4,256,128]{2,1,0:T(8,128)(2,1)S(1)}, bf16[4,256,128]{2,1,0:T(8,128)(2,1)S(1)}, u32[]{:S(2)}, u32[]{:S(2)}) collective-permute-start(bf16[4,256,128]{2,1,0:T(8,128)(2,1)S(1)} %dynamic-slice_bitcast_fusion), channel_id=1, source_target_pairs={{0,8},{8,0},{16,24},{24,16},{32,40},{40,32},{48,56},{56,48},{64,72... | collective-permute-start | bytes 786440 | tf_op jit(solution)/shard_map/ppermute | solution.py:30
  154.7 19.3 %collective-permute-start.11 = (bf16[264,128]{1,0:T(8,128)(2,1)S(1)}, bf16[264,128]{1,0:T(8,128)(2,1)S(1)}, u32[]{:S(2)}, u32[]{:S(2)}) collective-permute-start(bf16[264,128]{1,0:T(8,128)(2,1)S(1)} %pad_maximum_fusion.10), channel_id=1, source_target_pairs={{0,464},{8,472},{16,480},{24,488},{32,496},{40,504},{48,0},{56,8},... | collective-permute-start | bytes 202760 | tf_op jit(solution)/shard_map/ppermute | solution.py:30
  162.7 11.2 %collective-permute-start.10 = (bf16[264,128]{1,0:T(8,128)(2,1)S(1)}, bf16[264,128]{1,0:T(8,128)(2,1)S(1)}, u32[]{:S(2)}, u32[]{:S(2)}) collective-permute-start(bf16[264,128]{1,0:T(8,128)(2,1)S(1)} %pad_maximum_fusion.9), channel_id=1, source_target_pairs={{0,480},{8,488},{16,496},{24,504},{32,0},{40,8},{48,16},{56,24},{6... | collective-permute-start | bytes 202760 | tf_op jit(solution)/shard_map/ppermute | solution.py:30
  165.1 8.8 %collective-permute-start.9 = (bf16[264,128]{1,0:T(8,128)(2,1)S(1)}, bf16[264,128]{1,0:T(8,128)(2,1)S(1)}, u32[]{:S(2)}, u32[]{:S(2)}) collective-permute-start(bf16[264,128]{1,0:T(8,128)(2,1)S(1)} %pad_maximum_fusion.8), channel_id=1, source_target_pairs={{0,496},{8,504},{16,0},{24,8},{32,16},{40,24},{48,32},{56,40},{64,... | collective-permute-start | bytes 202760 | tf_op jit(solution)/shard_map/ppermute | solution.py:30
  168.6 2.2 copy-start.2
  170.8 3.5 %copy-start.3 = (bf16[256,8192]{1,0:T(8,128)(2,1)S(1)}, bf16[256,8192]{1,0:T(8,128)(2,1)}, u32[]{:S(2)}) copy-start(bf16[256,8192]{1,0:T(8,128)(2,1)} %refs_6_.1) | copy-start | bytes 12582916
  176.8 32.8 %all-to-all-start.2 = ((bf16[64,56,128]{2,1,0:T(8,128)(2,1)}), bf16[64,56,128]{2,1,0:T(8,128)(2,1)S(1)}, u32[]{:S(2)}, u32[]{:S(2)}) async-start(bf16[64,56,128]{2,1,0:T(8,128)(2,1)} %get-tuple-element.14), calls=%async_computation.2 | async-start | bytes 1835008 | tf_op jit(solution)/shard_map/all_to_all | solution.py:393
  183.9 3.3 %collective-permute-start.7 = (bf16[256,256]{1,0:T(8,128)(2,1)S(1)}, bf16[256,256]{1,0:T(8,128)(2,1)S(1)}, u32[]{:S(2)}, u32[]{:S(2)}) collective-permute-start(bf16[256,256]{1,0:T(8,128)(2,1)S(1)} %constant_dynamic-slice_fusion.2), channel_id=1, source_target_pairs={{0,8},{8,0},{16,24},{24,16},{32,40},{40,32},{48,56},{56,48},{64,72... | collective-permute-start | bytes 393224 | tf_op jit(solution)/shard_map/ppermute | solution.py:30
  210.3 17.8 %all-to-all-start.3 = ((bf16[8,32,128]{2,1,0:T(8,128)(2,1)}), bf16[8,32,128]{2,1,0:T(8,128)(2,1)S(1)}, u32[]{:S(2)}, u32[]{:S(2)}) async-start(bf16[8,32,128]{2,1,0:T(8,128)(2,1)} %broadcast_in_dim.39), calls=%async_computation.3 | async-start | bytes 131072 | tf_op jit(solution)/shard_map/all_to_all | solution.py:20
  (1 other events, 2.2 us)
Sparse Core Ops, SparseCore 0:
  29.2 41.6 all-gather.4
  73.0 59.1 all-gather.2

commit v9 on v8

--- a/solution.py
+++ b/solution.py
@@ -30,9 +30,19 @@
     return lax.ppermute(value, "ctx", pairs)
 
 
+def rows_of(tokens, theirs, columns, core, target, arrivals, first):
+    rows = tokens.shape[0]
+    mine = target.at[pl.ds(pl.multiple_of(core * rows, rows), rows)]
+    other = target.at[pl.ds(pl.multiple_of((1 - core) * rows, rows), rows)]
+    return [
+        pltpu.make_async_copy(tokens.at[:, columns], mine, arrivals.at[first]),
+        pltpu.make_async_copy(theirs.at[:, columns], other, arrivals.at[first + 1]),
+    ]
+
+
 def attention_kernel(
     scale, tile, info, tokens, theirs, weight, start, grad_out, kv,
-    out, grad_query, grad_value, query, rows_in, arrivals,
+    out, grad_query, grad_value, query, columns_in, rows_in, arrivals,
 ):
     rows, size = query.shape[0], kv.shape[-1]
     heads = query.shape[1] // size
@@ -43,21 +53,19 @@
     copies = []
     for i in range(parts):
         here = pl.ds(i * depth, depth)
-        copies.append(pltpu.make_async_copy(weight.at[here], rows_in.at[i], arrivals.at[i]))
-    for copy in copies:
+        copies.append(
+            rows_of(tokens, theirs, here, info[heads], columns_in.at[i], arrivals, 3 * i)
+            + [pltpu.make_async_copy(weight.at[here], rows_in.at[i], arrivals.at[3 * i + 2])]
+        )
+    for copy in sum(copies, []):
         copy.start()
     grad_value[...] = jnp.zeros_like(grad_value)
-    core, each = info[heads], rows // 2
-    mine = pl.ds(pl.multiple_of(core * each, each), each)
-    other = pl.ds(pl.multiple_of((1 - core) * each, each), each)
-    totals = [start[mine, :], start[other, :]]
-    for i, copy in enumerate(copies):
-        copy.wait()
-        here = slice(i * depth, (i + 1) * depth)
-        for which, source in enumerate((tokens, theirs)):
-            totals[which] += jnp.dot(source[:, here], rows_in[i], preferred_element_type=f32)
-    query[mine, :] = totals[0].astype(bf16)
-    query[other, :] = totals[1].astype(bf16)
+    total = start[...]
+    for i in range(parts):
+        for copy in copies[i]:
+            copy.wait()
+        total = total + jnp.dot(columns_in[i], rows_in[i], preferred_element_type=f32)
+    query[...] = total.astype(bf16)
 
     def tile_of(index, columns, count):
         here = pl.ds(pl.multiple_of(index * tile, tile), tile)
@@ -124,8 +132,8 @@
         ),
         in_specs=[
             pl.BlockSpec(memory_space=pltpu.SMEM),
-            vmem,
-            vmem,
+            pl.BlockSpec(memory_space=pl.ANY),
+            pl.BlockSpec(memory_space=pl.ANY),
             pl.BlockSpec(memory_space=pl.ANY),
             vmem,
             vmem,
@@ -134,10 +142,11 @@
         out_specs=(vmem, vmem, vmem),
         scratch_shapes=[
             pltpu.VMEM((rows, width), bf16),
+            pltpu.VMEM((parts, rows, model // parts), bf16),
             pltpu.VMEM((parts, model // parts, width), bf16),
-            pltpu.SemaphoreType.DMA((parts,)),
+            pltpu.SemaphoreType.DMA((3 * parts,)),
         ],
-        compiler_params=pltpu.CompilerParams(vmem_limit_bytes=30 * 1024 * 1024),
+        compiler_params=pltpu.CompilerParams(vmem_limit_bytes=48 * 1024 * 1024),
         cost_estimate=pl.CostEstimate(
             flops=10 * rows * width * blocks * block + 2 * rows * width * model,
             bytes_accessed=16 * 1024 * 1024,
@@ -147,123 +156,70 @@
     )(info, tokens, theirs, weight, start, grad_out, kv)
 
 
-def column_copies(sources, buffer, arrivals):
-    parts, width = buffer.shape[0], buffer.shape[-1]
-    copies = [
-        [
-            pltpu.make_async_copy(
-                source.at[:, pl.ds(i * width, width)],
-                buffer.at[i, which],
-                arrivals.at[len(sources) * i + which],
-            )
-            for which, source in enumerate(sources)
-        ]
-        for i in range(parts)
-    ]
+def all_blocks_kernel(info, own, *refs):
+    arrived, refs = refs[:-9], refs[-9:]
+    up, low, rank_q, tokens, theirs, out, gradient, buffer, arrivals = refs
+    core = info[0]
+    size = gradient.shape[1]
+    each = buffer.shape[-1] // size
+    copies = []
+    for block in range(out.shape[0]):
+        part, lane = block // each, block % each * size
+        columns = pl.ds(pl.multiple_of((2 * block + core) * size, size), size)
+        target = buffer.at[part, :, pl.ds(lane, size)]
+        copies.append(rows_of(tokens, theirs, columns, core, target, arrivals, 2 * block))
     for copy in sum(copies, []):
         copy.start()
-    return copies
-
-
-def multiply_parts(ranks, copies, buffer, store):
-    for i, part in enumerate(copies):
-        for copy in part:
-            copy.wait()
-        product = functools.reduce(
-            jnp.add,
-            [
-                jnp.dot(r, buffer[i, which], preferred_element_type=f32)
-                for which, r in enumerate(ranks)
-            ],
-        ).astype(bf16)
-        store(i, product)
-
-
-def query_blocks_kernel(rank_mine, rank_theirs, tokens, theirs, out, buffer, arrivals):
-    copies = column_copies((tokens, theirs), buffer, arrivals)
-    size = out.shape[2]
-    each = buffer.shape[-1] // size
-
-    def store(i, product):
-        for j in range(each):
-            out[i * each + j] = product[:, j * size : (j + 1) * size]
-
-    multiply_parts((rank_mine[...], rank_theirs[...]), copies, buffer, store)
-
-
-def query_blocks(rank_mine, rank_theirs, tokens, theirs, devices, parts=4):
-    rows, model = tokens.shape
-    vmem = pl.BlockSpec(memory_space=pltpu.VMEM)
-    anywhere = pl.BlockSpec(memory_space=pl.ANY)
-    ranks = rank_mine.shape[0]
-    return pl.pallas_call(
-        query_blocks_kernel,
-        out_shape=jax.ShapeDtypeStruct((devices, ranks, model // devices), bf16),
-        in_specs=[vmem, vmem, anywhere, anywhere],
-        out_specs=vmem,
-        scratch_shapes=[
-            pltpu.VMEM((parts, 2, rows, model // parts), bf16),
-            pltpu.SemaphoreType.DMA((2 * parts,)),
-        ],
-        compiler_params=pltpu.CompilerParams(vmem_limit_bytes=40 * 1024 * 1024),
-        cost_estimate=pl.CostEstimate(
-            flops=4 * ranks * rows * model, bytes_accessed=4 * rows * model, transcendentals=0
-        ),
-        name="query_blocks",
-    )(rank_mine, rank_theirs, tokens, theirs)
-
-
-def all_blocks_kernel(own, *refs):
-    arrived, (up, low, above, tokens, out, gradient, buffer, arrivals) = refs[:-8], refs[-8:]
-    copies = column_copies((tokens,), buffer, arrivals)
-    rows, size = gradient.shape
-    each = buffer.shape[-1] // size
+    rows = gradient.shape[0]
     total = own[...]
     for other in arrived:
         total += other[...].astype(f32)
     total = total.astype(bf16)
     mine = total[:rows]
     gradient[...] = mine
-    ranks = lax.dot_general(up[...], mine, NT, preferred_element_type=f32).astype(bf16)
+    rank_v = lax.dot_general(up[...], mine, NT, preferred_element_type=f32).astype(bf16)
+    ranks = jnp.concatenate([rank_q[...], rank_v], axis=0)
     up_part = lax.dot_general(low[...], mine, TN, preferred_element_type=f32).astype(bf16)
-    top = above.shape[1]
-    bottom = top + ranks.shape[0]
+    bottom = ranks.shape[0]
     last = bottom + up_part.shape[0]
-
-    def store(i, product):
+    for part in range(buffer.shape[0]):
+        for copy in sum(copies[part * each : (part + 1) * each], []):
+            copy.wait()
+        product = jnp.dot(ranks, buffer[part], preferred_element_type=f32).astype(bf16)
         for j in range(each):
-            block = i * each + j
-            out[block, :top] = above[block]
-            out[block, top:bottom] = product[:, j * size : (j + 1) * size]
+            block = part * each + j
+            out[block, :bottom] = product[:, j * size : (j + 1) * size]
             out[block, bottom:last] = up_part
             out[block, last:] = total[rows:]
 
-    multiply_parts((ranks,), copies, buffer, store)
-
-
-def all_blocks(own, arrived, up, low, above, tokens, parts=4):
+
+def all_blocks(info, own, arrived, up, low, rank_q, tokens, theirs, parts=4):
     rows, model = tokens.shape
-    devices, ranks, size = above.shape
+    ranks, size = up.shape
+    count = model // (2 * size)
     vmem = pl.BlockSpec(memory_space=pltpu.VMEM)
-    height = 3 * ranks + own.shape[0] - rows
+    anywhere = pl.BlockSpec(memory_space=pl.ANY)
+    height = 3 * ranks + own.shape[0] - 2 * rows
     return pl.pallas_call(
         all_blocks_kernel,
         out_shape=(
-            jax.ShapeDtypeStruct((devices, height, size), bf16),
-            jax.ShapeDtypeStruct((rows, size), bf16),
+            jax.ShapeDtypeStruct((count, height, size), bf16),
+            jax.ShapeDtypeStruct((2 * rows, size), bf16),
         ),
-        in_specs=[vmem] * (4 + len(arrived)) + [pl.BlockSpec(memory_space=pl.ANY)],
+        in_specs=[pl.BlockSpec(memory_space=pltpu.SMEM)]
+        + [vmem] * (4 + len(arrived))
+        + [anywhere, anywhere],
         out_specs=(vmem, vmem),
         scratch_shapes=[
-            pltpu.VMEM((parts, 1, rows, model // parts), bf16),
-            pltpu.SemaphoreType.DMA((parts,)),
+            pltpu.VMEM((parts, 2 * rows, model // (2 * parts)), bf16),
+            pltpu.SemaphoreType.DMA((2 * count,)),
         ],
-        compiler_params=pltpu.CompilerParams(vmem_limit_bytes=40 * 1024 * 1024),
+        compiler_params=pltpu.CompilerParams(vmem_limit_bytes=56 * 1024 * 1024),
         cost_estimate=pl.CostEstimate(
-            flops=2 * ranks * rows * model, bytes_accessed=3 * rows * model, transcendentals=0
+            flops=4 * ranks * rows * model, bytes_accessed=3 * rows * model, transcendentals=0
         ),
         name="all_blocks",
-    )(own, *arrived, up, low, above, tokens)
+    )(info, own, *arrived, up, low, rank_q, tokens, theirs)
 
 
 def on_device(
@@ -365,39 +321,58 @@
         axis=1,
     )
 
+    count = value_parts.shape[0] * value_parts.shape[1]
     query_up_part = lax.dot_general(low_q, grad_query, TN, preferred_element_type=f32)
-    query_up_part = query_up_part.reshape(chips, -1, size)
-    value_parts = value_parts.reshape(chips, 2, rows, size).astype(bf16)
-    same = lax.dynamic_index_in_dim(value_parts, core, 1, keepdims=False)
-    cross = lax.dynamic_index_in_dim(value_parts, 1 - core, 1, keepdims=False)
-    value_parts = same.astype(f32) + to_chip(cross, 0, True).astype(f32)
+    rank_q = lax.dot_general(up_mine, grad_query, NT, preferred_element_type=f32)
+    swapped = [value_parts, query_up_part, rank_q]
+    swapped = jnp.concatenate([part.astype(bf16).reshape(-1, size) for part in swapped])
+    swapped = [swapped, to_chip(swapped, 0, True)]
+    value_parts = (swapped[0][:count].astype(f32) + swapped[1][:count].astype(f32)).reshape(
+        value_parts.shape
+    )
+    last = count + rank * half // size
+    rank_q = [part[last:].reshape(rank, -1).astype(f32) for part in swapped]
+    rank_q = (rank_q[0] + rank_q[1]).astype(bf16)
+    query_up_part = [part[count:last].reshape(rank, half) for part in swapped]
+    query_up_part = jnp.concatenate(
+        [jnp.where(core == 0, *query_up_part), jnp.where(core == 0, *query_up_part[::-1])], axis=1
+    ).reshape(chips, -1, size)
 
     def with_share(d):
         share = lax.dynamic_index_in_dim(
             query_up_part, lax.rem(chip + chips - d, chips), 0, keepdims=False
         )
-        return jnp.concatenate([value_parts[d], share], axis=0)
-
-    arrived = [with_share(0)]
-    arrived += [to_chip(with_share(d).astype(bf16), -d, False) for d in range(1, chips)]
-
-    rank_q = lax.dot_general(up_mine, grad_query, NT, preferred_element_type=f32).astype(bf16)
-    rank_q = rank_q + (value_parts[0, 0, 0] * 0).astype(bf16)
-    rank_halves = rank_q.reshape(rank, 2, rows)
-    rank_mine = lax.dynamic_index_in_dim(rank_halves, core, 1, keepdims=False)
-    rank_theirs = lax.dynamic_index_in_dim(rank_halves, 1 - core, 1, keepdims=False)
-    blocks = query_blocks(rank_mine, rank_theirs, tokens, theirs, devices)
+        return jnp.concatenate([value_parts[d].astype(bf16), share], axis=0)
+
+    arrived = [to_chip(with_share(d), -d, False) for d in range(1, chips)]
+
     blocks, value_gradient = all_blocks(
-        arrived[0], arrived[1:], value_up_weight, half_of(low_v, core), blocks, tokens
-    )
-    blocks = lax.all_to_all(blocks, "ctx", 0, 0, tiled=True)
+        core[None].astype(jnp.int32),
+        with_share(0).astype(f32),
+        arrived,
+        value_up_weight,
+        low_v,
+        rank_q,
+        tokens,
+        theirs,
+    )
+    same_core = [[i for i in range(devices) if i % 2 == c] for c in range(2)]
+    blocks = lax.all_to_all(
+        blocks, "ctx", 0, 0, tiled=True, axis_index_groups=same_core
+    )
     summed = jnp.sum(blocks[:, : 3 * rank].astype(f32), axis=0)
     grad_down = jnp.sum(spread(summed[: 2 * rank].astype(bf16), "fsdp").astype(f32), axis=0)
     value_up_gradient = summed[2 * rank :]
     query_up = blocks[:, 3 * rank :].astype(f32)
-    query_up = query_up.reshape(planes, chips, 2, rank // chips, half).sum(axis=0)
-    query_up_gradient = query_up.transpose(0, 2, 1, 3).reshape(rank, width)
-    return (attention, value_gradient, grad_down.T, query_up_gradient, value_up_gradient)
+    query_up = query_up.reshape(planes, chips, -1, size).sum(axis=0)
+    query_up_gradient = query_up.reshape(rank, width)
+    return (
+        attention,
+        half_of(value_gradient, core),
+        grad_down.T,
+        query_up_gradient,
+        value_up_gradient,
+    )
 
 
 def solution(mesh):

time: 237 us -> 230 us (0.970)
  local copies, waits for them, and re-layouts: 12.3 us -> 6.01 us
  waiting for transfers between devices: 80.4 us -> 74.6 us
    all_to_all x1, waiting for transfers between devices: 21.5 us -> 10.6 us  [on_device(): lax.all_to_all(blocks, 'ctx', 0, 0, tiled=True, axis_index_groups=same_core)]
    unnamed x22 -> x19, local copies, waits for them, and re-layouts: 7.56 us -> 0.72 us
    ppermute x12, waiting for transfers between devices: 10.2 us -> 14.4 us  [to_chip(): return lax.ppermute(value, 'ctx', pairs)]
    pallas_call x2 -> x1, Pallas kernels: 5.54 us -> 5.19 us  [all_blocks(): pl.pallas_call(all_blocks_kernel, out_shape=(jax.ShapeDtypeStruct((count,...]
  transfers between devices with their start and end apart: 16 -> 16, of which waited for: 9 -> 11; matrix products, arithmetic and copies ran while one was open for 5% -> 6% of each run, Pallas kernels for 1% -> 0%
where the time goes in v9:
time: 230 us; the launch traced here: 227 us
  waiting for transfers between devices  74.6 us (32%)
  starting transfers between devices  62.2 us (27%)
  blocking collectives  38.1 us (17%)
  Pallas kernels  17.8 us (8%)
  between operations  14.6 us (6%)
  matrix products  8.48 us (4%)
  local copies, waits for them, and re-layouts  6.01 us (3%)
  other arithmetic  5.09 us (2%)
    ppermute x12, starting transfers between devices, to_chip(): return lax.ppermute(value, 'ctx', pairs)  46.4 us
    all_gather x1, waiting for transfers between devices, on_device(): lax.all_gather(q_rows.reshape(members * depth, half), 'ctx', axis=0, tile...  23.8 us
    all_to_all x1, blocking collectives, on_device(): lax.all_to_all(kv_rows.reshape(members, size + rank, depth), 'ctx', 0, 0,...  19.8 us
    all_to_all x1, blocking collectives, on_device(): lax.all_to_all(q_rows.reshape(members, depth, half), 'ctx', 0, 0, tiled=T...  18.3 us
    all_gather x1, waiting for transfers between devices, on_device(): lax.all_gather(kv_rows, 'ctx', axis=0, tiled=True, axis_index_groups=across)  17.3 us
    ppermute x12, waiting for transfers between devices, to_chip(): return lax.ppermute(value, 'ctx', pairs)  14.4 us
    pallas_call x1, Pallas kernels, attend(): pl.pallas_call(functools.partial(attention_kernel, size ** (-0.5), tile),...  12.6 us
    all_to_all x1, waiting for transfers between devices, on_device(): lax.all_to_all(blocks, 'ctx', 0, 0, tiled=True, axis_index_groups=same_core)  10.6 us
  transfers between devices with their start and end apart: 16, of which 11 were waited for; matrix products, arithmetic and copies ran while one was open for 6% of the time, Pallas kernels for 0%

profile of v9, /device:TPU:1, one launch (start us, length us, event | category | flops | bytes accessed | tf_op | source)
XLA Modules:
  0.0 226.8 jit_solution(307994805476411601)
XLA Ops:
  9.2 19.8 %all_to_all.20 = bf16[8,144,128]{2,1,0:T(8,128)(2,1)} all-to-all(bf16[8,144,128]{2,1,0:T(8,128)(2,1)S(1)} %bitcast.72), channel_id=1, replica_groups={{0,8,16,24,32,40,48,56},{64,72,80,88,96,104,112,120},{128,136,144,152,1..., dimensions={0} | all-to-all | bytes 589824 | tf_op jit(solution)/shard_map/all_to_all | solution.py:275
  30.1 18.3 %all_to_all.21 = bf16[8,128,256]{2,1,0:T(8,128)(2,1)} all-to-all(bf16[8,128,256]{2,1,0:T(8,128)(2,1)S(1)} %bitcast.70), channel_id=1, replica_groups={{0,8,16,24,32,40,48,56},{64,72,80,88,96,104,112,120},{128,136,144,152,1..., dimensions={0} | all-to-all | bytes 1048576 | tf_op jit(solution)/shard_map/all_to_all | solution.py:282
  48.4 2.7 %collective-permute-start = (bf16[256,8192]{1,0:T(8,128)(2,1)}, bf16[256,8192]{1,0:T(8,128)(2,1)}, u32[]{:S(2)}, u32[]{:S(2)}) collective-permute-start(bf16[256,8192]{1,0:T(8,128)(2,1)} %refs_6_.1), channel_id=1, source_target_pairs={{0,8},{8,0},{16,24},{24,16},{32,40},{40,32},{48,56},{56,48},{64,72... | collective-permute-start | bytes 12582920 | tf_op jit(solution)/shard_map/ppermute | solution.py:30
  53.7 17.3 %all-gather.5.cloned.1.call-done = bf16[64,144,128]{2,1,0:T(8,128)(2,1)} async-done(((bf16[8,144,128]{2,1,0:T(8,128)(2,1)}), bf16[64,144,128]{2,1,0:T(8,128)(2,1)}) %all-gather.5.cloned.1.call-update) | async-done | bytes 2359312 | tf_op jit(solution)/shard_map/all_gather | solution.py:279
  70.9 4.3 %fusion.2 = f32[144,256]{0,1:T(8,128)S(1)} fusion(bf16[256,8192]{1,0:T(8,128)(2,1)} %refs_6_.1, bf16[64,144,128]{2,1,0:T(8,128)(2,1)} %all-gather.5.cloned.1.call-done), kind=kOutput, calls=%fused_computation.2 | convolution fusion | flops 603979776 | bytes 6701056 | tf_op jit(solution)/shard_map/dot_general | solution.py:293
  75.3 3.5 %select_bitcast_fusion = (f32[256,144]{1,0:T(8,128)S(1)}, f32[256,144]{1,0:T(8,128)S(1)}) fusion(f32[144,256]{0,1:T(8,128)S(1)} %fusion.2, pred[]{:T(512)S(6)} %eq.4, bf16[256,8192]{1,0:T(8,128)(2,1)} %collective-permute-done.theirs.refs_7_, bf16[64,144,128]{2,1,0:T(8,128)(2,1)S(1)} %copy-done.8), kind=kOutput, calls=%fused_computation.24 | convolution fusion | flops 604053504 | bytes 6995969 | tf_op jit(solution)/shard_map/dot_general | solution.py:294
  79.0 3.3 %collective-permute-start.3 = (bf16[512,128]{1,0:T(8,128)(2,1)S(1)}, bf16[512,128]{1,0:T(8,128)(2,1)S(1)}, u32[]{:S(2)}, u32[]{:S(2)}) collective-permute-start(bf16[512,128]{1,0:T(8,128)(2,1)S(1)} %fusion.7), channel_id=1, source_target_pairs={{0,16},{8,24},{16,32},{24,40},{32,48},{40,56},{48,64},{56,72},{64,... | collective-permute-start | bytes 393224 | tf_op jit(solution)/shard_map/ppermute | solution.py:30
  82.2 4.4 %collective-permute-start.4 = (bf16[512,128]{1,0:T(8,128)(2,1)S(1)}, bf16[512,128]{1,0:T(8,128)(2,1)S(1)}, u32[]{:S(2)}, u32[]{:S(2)}) collective-permute-start(bf16[512,128]{1,0:T(8,128)(2,1)S(1)} %fusion.7), channel_id=1, source_target_pairs={{0,32},{8,40},{16,48},{24,56},{32,64},{40,72},{48,80},{56,88},{64,... | collective-permute-start | bytes 393224 | tf_op jit(solution)/shard_map/ppermute | solution.py:30
  86.6 3.2 %collective-permute-start.5 = (bf16[512,128]{1,0:T(8,128)(2,1)S(1)}, bf16[512,128]{1,0:T(8,128)(2,1)S(1)}, u32[]{:S(2)}, u32[]{:S(2)}) collective-permute-start(bf16[512,128]{1,0:T(8,128)(2,1)S(1)} %fusion.7), channel_id=1, source_target_pairs={{0,48},{8,56},{16,64},{24,72},{32,80},{40,88},{48,96},{56,104},{64... | collective-permute-start | bytes 393224 | tf_op jit(solution)/shard_map/ppermute | solution.py:30
  91.3 5.8 %collective-permute-done.5 = bf16[512,128]{1,0:T(8,128)(2,1)S(1)} collective-permute-done((bf16[512,128]{1,0:T(8,128)(2,1)S(1)}, bf16[512,128]{1,0:T(8,128)(2,1)S(1)}, u32[]{:S(2)}, u32[]{:S(2)}) %collective-permute-start.5) | collective-permute-done | bytes 131104 | tf_op jit(solution)/shard_map/ppermute | solution.py:30
  97.2 7.6 %collective-permute-start.6 = (bf16[4,512,128]{2,1,0:T(8,128)(2,1)S(1)}, bf16[4,512,128]{2,1,0:T(8,128)(2,1)S(1)}, u32[]{:S(2)}, u32[]{:S(2)}) collective-permute-start(bf16[4,512,128]{2,1,0:T(8,128)(2,1)S(1)} %get-tuple-element.20), channel_id=1, source_target_pairs={{0,8},{8,0},{16,24},{24,16},{32,40},{40,32},{48,56},{56,48},{64,72... | collective-permute-start | bytes 1572872 | tf_op jit(solution)/shard_map/ppermute | solution.py:30
  108.4 23.8 %all-gather.3.cloned.1.call-done.weight = bf16[8192,256]{1,0:T(8,128)(2,1)} async-done(((bf16[1024,256]{1,0:T(8,128)(2,1)}), bf16[8192,256]{1,0:T(8,128)(2,1)}) %all-gather.3.cloned.1.call-update) | async-done | bytes 4194320 | tf_op jit(solution)/shard_map/all_gather | solution.py:286
  132.2 12.6 %attention.1 = (bf16[512,256]{1,0:T(8,128)(2,1)S(1)}, bf16[512,256]{1,0:T(8,128)(2,1)S(1)}, f32[4,512,128]{2,1,0:T(8,128)S(1)}) custom-call(s32[3]{0:T(128)S(1)} %pad_add_fusion.info, bf16[256,8192]{1,0:T(8,128)(2,1)} %refs_6_.1, bf16[256,8192]{1,0:T(8,128)(2,1)} %collective-permute-done.theirs.refs_7_, ...), custom_call_target="tpu_custom_call" | custom-call | flops 4831838208 | bytes 16777216 | tf_op jit(solution)/shard_map/attention/pallas_call | solution.py:126
  145.3 4.4 %collective-permute-start.8 = (bf16[2144,128]{1,0:T(8,128)(2,1)S(1)}, bf16[2144,128]{1,0:T(8,128)(2,1)S(1)}, u32[]{:S(2)}, u32[]{:S(2)}) collective-permute-start(bf16[2144,128]{1,0:T(8,128)(2,1)S(1)} %pad_maximum_fusion.1), channel_id=1, source_target_pairs={{0,8},{8,0},{16,24},{24,16},{32,40},{40,32},{48,56},{56,48},{64,72... | collective-permute-start | bytes 1646600 | tf_op jit(solution)/shard_map/ppermute | solution.py:30
  151.6 8.1 %collective-permute-start.11 = (bf16[528,128]{1,0:T(8,128)(2,1)S(1)}, bf16[528,128]{1,0:T(8,128)(2,1)S(1)}, u32[]{:S(2)}, u32[]{:S(2)}) collective-permute-start(bf16[528,128]{1,0:T(8,128)(2,1)S(1)} %pad_maximum_fusion.8), channel_id=1, source_target_pairs={{0,464},{8,472},{16,480},{24,488},{32,496},{40,504},{48,0},{56,8},... | collective-permute-start | bytes 405512 | tf_op jit(solution)/shard_map/ppermute | solution.py:30
  159.7 2.4 %collective-permute-start.10 = (bf16[528,128]{1,0:T(8,128)(2,1)S(1)}, bf16[528,128]{1,0:T(8,128)(2,1)S(1)}, u32[]{:S(2)}, u32[]{:S(2)}) collective-permute-start(bf16[528,128]{1,0:T(8,128)(2,1)S(1)} %pad_maximum_fusion.7), channel_id=1, source_target_pairs={{0,480},{8,488},{16,496},{24,504},{32,0},{40,8},{48,16},{56,24},{6... | collective-permute-start | bytes 405512 | tf_op jit(solution)/shard_map/ppermute | solution.py:30
  162.1 3.5 %collective-permute-start.9 = (bf16[528,128]{1,0:T(8,128)(2,1)S(1)}, bf16[528,128]{1,0:T(8,128)(2,1)S(1)}, u32[]{:S(2)}, u32[]{:S(2)}) collective-permute-start(bf16[528,128]{1,0:T(8,128)(2,1)S(1)} %pad_maximum_fusion.6), channel_id=1, source_target_pairs={{0,496},{8,504},{16,0},{24,8},{32,16},{40,24},{48,32},{56,40},{64,... | collective-permute-start | bytes 405512 | tf_op jit(solution)/shard_map/ppermute | solution.py:30
  166.9 3.5 %collective-permute-done.10.refs_1_ = bf16[528,128]{1,0:T(8,128)(2,1)S(1)} collective-permute-done((bf16[528,128]{1,0:T(8,128)(2,1)S(1)}, bf16[528,128]{1,0:T(8,128)(2,1)S(1)}, u32[]{:S(2)}, u32[]{:S(2)}) %collective-permute-start.10) | collective-permute-done | bytes 135200 | tf_op jit(solution)/shard_map/ppermute | solution.py:30
  171.9 5.2 %all_blocks.1 = (bf16[32,64,128]{2,1,0:T(8,128)(2,1)}, bf16[512,128]{1,0:T(8,128)(2,1)}) custom-call(s32[1]{0:T(128)} %bitcast.info, f32[528,128]{1,0:T(8,128)} %maximum_convert_fusion.own, bf16[528,128]{1,0:T(8,128)(2,1)} %copy-done.4, bf16[528,128]{1,0:T(8,128)(2,1)} %copy-done.3, bf16[528,128]{1,0:T(8,128)(2,1)} %copy-done.2, bf16[16,128]{1,0:T(8,128)(2,1)} %refs_3_.1, ...), custom_call_target="tpu_custom_call" | custom-call | flops 134217728 | bytes 6291456 | tf_op jit(solution)/shard_map/all_blocks/pallas_call | solution.py:203
  177.1 7.2 %all-to-all-start.2 = ((bf16[32,64,128]{2,1,0:T(8,128)(2,1)}), bf16[32,64,128]{2,1,0:T(8,128)(2,1)S(1)}, u32[]{:S(2)}, u32[]{:S(2)}) async-start(bf16[32,64,128]{2,1,0:T(8,128)(2,1)} %get-tuple-element.14), calls=%async_computation.2 | async-start | bytes 1048576 | tf_op jit(solution)/shard_map/all_to_all | solution.py:360
  184.3 3.0 %collective-permute-start.7 = (bf16[256,256]{1,0:T(8,128)(2,1)S(1)}, bf16[256,256]{1,0:T(8,128)(2,1)S(1)}, u32[]{:S(2)}, u32[]{:S(2)}) collective-permute-start(bf16[256,256]{1,0:T(8,128)(2,1)S(1)} %constant_dynamic-slice_fusion.1), channel_id=1, source_target_pairs={{0,8},{8,0},{16,24},{24,16},{32,40},{40,32},{48,56},{56,48},{64,72... | collective-permute-start | bytes 393224 | tf_op jit(solution)/shard_map/ppermute | solution.py:30
  189.7 10.6 %all-to-all-done.2 = bf16[32,64,128]{2,1,0:T(8,128)(2,1)S(1)} async-done(((bf16[32,64,128]{2,1,0:T(8,128)(2,1)}), bf16[32,64,128]{2,1,0:T(8,128)(2,1)S(1)}, u32[]{:S(2)}, u32[]{:S(2)}) %all-to-all-start.2) | async-done | bytes 524320 | tf_op jit(solution)/shard_map/all_to_all | solution.py:360
  201.6 8.6 %all-to-all-start.3 = ((bf16[8,32,128]{2,1,0:T(8,128)(2,1)}), bf16[8,32,128]{2,1,0:T(8,128)(2,1)S(1)}, u32[]{:S(2)}, u32[]{:S(2)}) async-start(bf16[8,32,128]{2,1,0:T(8,128)(2,1)} %broadcast_in_dim.40), calls=%async_computation.3 | async-start | bytes 131072 | tf_op jit(solution)/shard_map/all_to_all | solution.py:20
  210.9 8.4 %all-to-all-done.3 = bf16[8,32,128]{2,1,0:T(8,128)(2,1)S(1)} async-done(((bf16[8,32,128]{2,1,0:T(8,128)(2,1)}), bf16[8,32,128]{2,1,0:T(8,128)(2,1)S(1)}, u32[]{:S(2)}, u32[]{:S(2)}) %all-to-all-start.3) | async-done | bytes 65568 | tf_op jit(solution)/shard_map/all_to_all | solution.py:20
  (90 shorter events, 20.8 us)
Async XLA Ops:
  7.2 100.9 %copy-start = (bf16[16,512]{1,0:T(8,128)(2,1)S(1)}, bf16[16,512]{1,0:T(8,128)(2,1)}, u32[]{:S(2)}) copy-start(bf16[16,512]{1,0:T(8,128)(2,1)} %param.14) | copy-start | bytes 49156
  7.2 63.8 %all-gather.5.cloned.1.call-start = ((), (), s32[]{:S(2)}) async-start(), calls=%async_computation.5 | async-start | bytes 2654208 | tf_op jit(solution)/shard_map/all_gather | solution.py:279
  8.2 42.9 %copy-start.1 = (bf16[256,512]{1,0:T(8,128)(2,1)S(1)}, bf16[256,512]{1,0:T(8,128)(2,1)}, u32[]{:S(2)}) copy-start(bf16[256,512]{1,0:T(8,128)(2,1)} %param.17) | copy-start | bytes 786436
  29.1 103.1 %all-gather.3.cloned.1.call-start = ((), (), s32[]{:S(2)}) async-start(), calls=%async_computation.4 | async-start | bytes 4718592 | tf_op jit(solution)/shard_map/all_gather | solution.py:286
  48.4 26.9 %collective-permute-start = (bf16[256,8192]{1,0:T(8,128)(2,1)}, bf16[256,8192]{1,0:T(8,128)(2,1)}, u32[]{:S(2)}, u32[]{:S(2)}) collective-permute-start(bf16[256,8192]{1,0:T(8,128)(2,1)} %refs_6_.1), channel_id=1, source_target_pairs={{0,8},{8,0},{16,24},{24,16},{32,40},{40,32},{48,56},{56,48},{64,72... | collective-permute-start | bytes 12582920 | tf_op jit(solution)/shard_map/ppermute | solution.py:30
  51.7 53.1 %collective-permute-start.2 = (bf16[256,256]{1,0:T(8,128)(2,1)S(1)}, bf16[256,256]{1,0:T(8,128)(2,1)S(1)}, u32[]{:S(2)}, u32[]{:S(2)}) collective-permute-start(bf16[256,256]{1,0:T(8,128)(2,1)S(1)} %bitcast.76), channel_id=1, source_target_pairs={{0,8},{8,0},{16,24},{24,16},{32,40},{40,32},{48,56},{56,48},{64,72... | collective-permute-start | bytes 393224 | tf_op jit(solution)/shard_map/ppermute | solution.py:30
  70.9 4.3 %copy-start.8 = (bf16[64,144,128]{2,1,0:T(8,128)(2,1)S(1)}, bf16[64,144,128]{2,1,0:T(8,128)(2,1)}, u32[]{:S(2)}) copy-start(bf16[64,144,128]{2,1,0:T(8,128)(2,1)} %all-gather.5.cloned.1.call-done) | copy-start | bytes 7077892
  75.2 3.6 %copy-start.6 = (bf16[16,128]{1,0:T(8,128)(2,1)S(1)}, bf16[16,128]{1,0:T(8,128)(2,1)}, u32[]{:S(2)}) copy-start(bf16[16,128]{1,0:T(8,128)(2,1)} %refs_3_.1) | copy-start | bytes 12292
  75.2 14.6 %copy-start.7 = (s32[4]{0:T(128)S(1)}, s32[4]{0:T(128)}, u32[]{:S(2)}) copy-start(s32[4]{0:T(128)} %param.16) | copy-start | bytes 52
  79.0 11.0 %collective-permute-start.3 = (bf16[512,128]{1,0:T(8,128)(2,1)S(1)}, bf16[512,128]{1,0:T(8,128)(2,1)S(1)}, u32[]{:S(2)}, u32[]{:S(2)}) collective-permute-start(bf16[512,128]{1,0:T(8,128)(2,1)S(1)} %fusion.7), channel_id=1, source_target_pairs={{0,16},{8,24},{16,32},{24,40},{32,48},{40,56},{48,64},{56,72},{64,... | collective-permute-start | bytes 393224 | tf_op jit(solution)/shard_map/ppermute | solution.py:30
  82.2 9.0 %collective-permute-start.4 = (bf16[512,128]{1,0:T(8,128)(2,1)S(1)}, bf16[512,128]{1,0:T(8,128)(2,1)S(1)}, u32[]{:S(2)}, u32[]{:S(2)}) collective-permute-start(bf16[512,128]{1,0:T(8,128)(2,1)S(1)} %fusion.7), channel_id=1, source_target_pairs={{0,32},{8,40},{16,48},{24,56},{32,64},{40,72},{48,80},{56,88},{64,... | collective-permute-start | bytes 393224 | tf_op jit(solution)/shard_map/ppermute | solution.py:30
  86.6 10.4 %collective-permute-start.5 = (bf16[512,128]{1,0:T(8,128)(2,1)S(1)}, bf16[512,128]{1,0:T(8,128)(2,1)S(1)}, u32[]{:S(2)}, u32[]{:S(2)}) collective-permute-start(bf16[512,128]{1,0:T(8,128)(2,1)S(1)} %fusion.7), channel_id=1, source_target_pairs={{0,48},{8,56},{16,64},{24,72},{32,80},{40,88},{48,96},{56,104},{64... | collective-permute-start | bytes 393224 | tf_op jit(solution)/shard_map/ppermute | solution.py:30
  97.2 11.1 %collective-permute-start.6 = (bf16[4,512,128]{2,1,0:T(8,128)(2,1)S(1)}, bf16[4,512,128]{2,1,0:T(8,128)(2,1)S(1)}, u32[]{:S(2)}, u32[]{:S(2)}) collective-permute-start(bf16[4,512,128]{2,1,0:T(8,128)(2,1)S(1)} %get-tuple-element.20), channel_id=1, source_target_pairs={{0,8},{8,0},{16,24},{24,16},{32,40},{40,32},{48,56},{56,48},{64,72... | collective-permute-start | bytes 1572872 | tf_op jit(solution)/shard_map/ppermute | solution.py:30
  104.8 3.2 %collective-permute-start.1 = (bf16[512,16]{1,0:T(8,128)(2,1)S(1)}, bf16[512,16]{1,0:T(8,128)(2,1)S(1)}, u32[]{:S(2)}, u32[]{:S(2)}) collective-permute-start(bf16[512,16]{1,0:T(8,128)(2,1)S(1)} %fusion.9), channel_id=1, source_target_pairs={{0,8},{8,0},{16,24},{24,16},{32,40},{40,32},{48,56},{56,48},{64,72... | collective-permute-start | bytes 49160 | tf_op jit(solution)/shard_map/ppermute | solution.py:30
  145.3 6.0 %collective-permute-start.8 = (bf16[2144,128]{1,0:T(8,128)(2,1)S(1)}, bf16[2144,128]{1,0:T(8,128)(2,1)S(1)}, u32[]{:S(2)}, u32[]{:S(2)}) collective-permute-start(bf16[2144,128]{1,0:T(8,128)(2,1)S(1)} %pad_maximum_fusion.1), channel_id=1, source_target_pairs={{0,8},{8,0},{16,24},{24,16},{32,40},{40,32},{48,56},{56,48},{64,72... | collective-permute-start | bytes 1646600 | tf_op jit(solution)/shard_map/ppermute | solution.py:30
  151.6 15.4 %collective-permute-start.11 = (bf16[528,128]{1,0:T(8,128)(2,1)S(1)}, bf16[528,128]{1,0:T(8,128)(2,1)S(1)}, u32[]{:S(2)}, u32[]{:S(2)}) collective-permute-start(bf16[528,128]{1,0:T(8,128)(2,1)S(1)} %pad_maximum_fusion.8), channel_id=1, source_target_pairs={{0,464},{8,472},{16,480},{24,488},{32,496},{40,504},{48,0},{56,8},... | collective-permute-start | bytes 405512 | tf_op jit(solution)/shard_map/ppermute | solution.py:30
  159.7 10.8 %collective-permute-start.10 = (bf16[528,128]{1,0:T(8,128)(2,1)S(1)}, bf16[528,128]{1,0:T(8,128)(2,1)S(1)}, u32[]{:S(2)}, u32[]{:S(2)}) collective-permute-start(bf16[528,128]{1,0:T(8,128)(2,1)S(1)} %pad_maximum_fusion.7), channel_id=1, source_target_pairs={{0,480},{8,488},{16,496},{24,504},{32,0},{40,8},{48,16},{56,24},{6... | collective-permute-start | bytes 405512 | tf_op jit(solution)/shard_map/ppermute | solution.py:30
  162.1 9.1 %collective-permute-start.9 = (bf16[528,128]{1,0:T(8,128)(2,1)S(1)}, bf16[528,128]{1,0:T(8,128)(2,1)S(1)}, u32[]{:S(2)}, u32[]{:S(2)}) collective-permute-start(bf16[528,128]{1,0:T(8,128)(2,1)S(1)} %pad_maximum_fusion.6), channel_id=1, source_target_pairs={{0,496},{8,504},{16,0},{24,8},{32,16},{40,24},{48,32},{56,40},{64,... | collective-permute-start | bytes 405512 | tf_op jit(solution)/shard_map/ppermute | solution.py:30
  166.9 4.3 %copy-start.2 = (bf16[528,128]{1,0:T(8,128)(2,1)}, bf16[528,128]{1,0:T(8,128)(2,1)S(1)}, u32[]{:S(2)}) copy-start(bf16[528,128]{1,0:T(8,128)(2,1)S(1)} %collective-permute-done.11.refs_2_) | copy-start | bytes 405508
  170.5 0.7 copy-start.3
  177.1 12.0 %copy-start.5 = (bf16[512,128]{1,0:T(8,128)(2,1)S(1)}, bf16[512,128]{1,0:T(8,128)(2,1)}, u32[]{:S(2)}) copy-start(bf16[512,128]{1,0:T(8,128)(2,1)} %get-tuple-element.13) | copy-start | bytes 393220
  177.1 23.3 %all-to-all-start.2 = ((bf16[32,64,128]{2,1,0:T(8,128)(2,1)}), bf16[32,64,128]{2,1,0:T(8,128)(2,1)S(1)}, u32[]{:S(2)}, u32[]{:S(2)}) async-start(bf16[32,64,128]{2,1,0:T(8,128)(2,1)} %get-tuple-element.14), calls=%async_computation.2 | async-start | bytes 1048576 | tf_op jit(solution)/shard_map/all_to_all | solution.py:360
  184.3 4.0 %collective-permute-start.7 = (bf16[256,256]{1,0:T(8,128)(2,1)S(1)}, bf16[256,256]{1,0:T(8,128)(2,1)S(1)}, u32[]{:S(2)}, u32[]{:S(2)}) collective-permute-start(bf16[256,256]{1,0:T(8,128)(2,1)S(1)} %constant_dynamic-slice_fusion.1), channel_id=1, source_target_pairs={{0,8},{8,0},{16,24},{24,16},{32,40},{40,32},{48,56},{56,48},{64,72... | collective-permute-start | bytes 393224 | tf_op jit(solution)/shard_map/ppermute | solution.py:30
  201.6 17.7 %all-to-all-start.3 = ((bf16[8,32,128]{2,1,0:T(8,128)(2,1)}), bf16[8,32,128]{2,1,0:T(8,128)(2,1)S(1)}, u32[]{:S(2)}, u32[]{:S(2)}) async-start(bf16[8,32,128]{2,1,0:T(8,128)(2,1)} %broadcast_in_dim.40), calls=%async_computation.3 | async-start | bytes 131072 | tf_op jit(solution)/shard_map/all_to_all | solution.py:20
  (1 other events, 0.7 us)
Sparse Core Ops, SparseCore 0:
  29.2 41.6 all-gather.4
  73.0 59.0 all-gather.2

commit v10 on v9

--- a/solution.py
+++ b/solution.py
@@ -12,12 +12,6 @@
 f32 = jnp.float32
 NT = (((1,), (1,)), ((), ()))
 TN = (((0,), (0,)), ((), ()))
-
-
-def spread(value, axis, groups=None):
-    count = len(groups[0]) if groups else lax.axis_size(axis)
-    copies = jnp.broadcast_to(value[None], (count, *value.shape))
-    return lax.all_to_all(copies, axis, 0, 0, tiled=True, axis_index_groups=groups)
 
 
 def to_chip(value, chips, other_core):
@@ -28,6 +22,61 @@
         target = (source - core + 2 * chips) % count + (1 - core if other_core else core)
         pairs.append((source, target))
     return lax.ppermute(value, "ctx", pairs)
+
+
+def payload_kernel(key_weight, value_weight, down, out):
+    size, rank = key_weight.shape[1], down.shape[0] // 2
+    adapters = down[...]
+    for core, weight in enumerate((key_weight, value_weight)):
+        turned = weight[...].astype(f32).T.astype(bf16)
+        for member in range(core, out.shape[0], 2):
+            out[member, :size] = turned
+            out[member, size:] = adapters[core * rank : (core + 1) * rank]
+
+
+def payload(key_weight, value_weight, down, members):
+    depth, size = key_weight.shape
+    vmem = pl.BlockSpec(memory_space=pltpu.VMEM)
+    return pl.pallas_call(
+        payload_kernel,
+        out_shape=jax.ShapeDtypeStruct((members, size + down.shape[0] // 2, depth), bf16),
+        in_specs=[vmem] * 3,
+        out_specs=vmem,
+        name="payload",
+    )(key_weight, value_weight, down)
+
+
+def sum_kernel(blocks, copies, value_up, query_up):
+    ranks, shares = copies.shape[1], query_up.shape[0]
+    last = ranks + value_up.shape[0]
+    total = blocks[0, :last].astype(f32)
+    for chip in range(1, blocks.shape[0]):
+        total += blocks[chip, :last].astype(f32)
+    low = total[:ranks].astype(bf16)
+    for copy in range(copies.shape[0]):
+        copies[copy] = low
+    value_up[...] = total[ranks:]
+    for share in range(shares):
+        total = blocks[share, last:].astype(f32)
+        for chip in range(share + shares, blocks.shape[0], shares):
+            total += blocks[chip, last:].astype(f32)
+        query_up[share] = total
+
+
+def sum_blocks(blocks, rank, count, shares):
+    size = blocks.shape[2]
+    vmem = pl.BlockSpec(memory_space=pltpu.VMEM)
+    return pl.pallas_call(
+        sum_kernel,
+        out_shape=(
+            jax.ShapeDtypeStruct((count, 2 * rank, size), bf16),
+            jax.ShapeDtypeStruct((rank, size), f32),
+            jax.ShapeDtypeStruct((shares, blocks.shape[1] - 3 * rank, size), f32),
+        ),
+        in_specs=[vmem],
+        out_specs=(vmem, vmem, vmem),
+        name="sum_blocks",
+    )(blocks)
 
 
 def rows_of(tokens, theirs, columns, core, target, arrivals, first):
@@ -264,16 +313,8 @@
     grad_away = lax.dynamic_index_in_dim(grad_halves, 1 - core, 0, keepdims=False)
     grad_out = both(grad_mine, to_chip(grad_away, 0, True))
 
-    down = adapter_down_weight.T
-    kv_rows = jnp.stack(
-        [
-            jnp.concatenate([key_weight.T, down[:rank]]),
-            jnp.concatenate([value_weight.T, down[rank:]]),
-        ]
-    )
-    kv_rows = jnp.broadcast_to(kv_rows[None], (chips, *kv_rows.shape))
     kv_rows = lax.all_to_all(
-        kv_rows.reshape(members, size + rank, depth),
+        payload(key_weight, value_weight, adapter_down_weight.T, members),
         "ctx", 0, 0, tiled=True, axis_index_groups=plain,
     )
     kv_rows = lax.all_gather(kv_rows, "ctx", axis=0, tiled=True, axis_index_groups=across)
@@ -360,11 +401,11 @@
     blocks = lax.all_to_all(
         blocks, "ctx", 0, 0, tiled=True, axis_index_groups=same_core
     )
-    summed = jnp.sum(blocks[:, : 3 * rank].astype(f32), axis=0)
-    grad_down = jnp.sum(spread(summed[: 2 * rank].astype(bf16), "fsdp").astype(f32), axis=0)
-    value_up_gradient = summed[2 * rank :]
-    query_up = blocks[:, 3 * rank :].astype(f32)
-    query_up = query_up.reshape(planes, chips, -1, size).sum(axis=0)
+    copies, value_up_gradient, query_up = sum_blocks(
+        blocks, rank, lax.axis_size("fsdp"), chips
+    )
+    copies = lax.all_to_all(copies, "fsdp", 0, 0, tiled=True)
+    grad_down = jnp.sum(copies.astype(f32), axis=0)
     query_up_gradient = query_up.reshape(rank, width)
     return (
         attention,

time: 230 us -> 232 us (level)
  Pallas kernels: 17.8 us -> 21.1 us
    pallas_call x0 -> x2, Pallas kernels: none -> 3.36 us  [the longest x1 1.74 us: sum_blocks(): pl.pallas_call(sum_kernel, out_shape=(jax.ShapeDtypeStruct((count, 2 * ra...]
  transfers between devices with their start and end apart: 16 -> 16, of which waited for: 11 -> 11; matrix products, arithmetic and copies ran while one was open for 6% -> 7% of each run, Pallas kernels for 0% -> 0%
where the time goes in v10:
time: 232 us; the launch traced here: 229 us
  waiting for transfers between devices  74.7 us (32%)
  starting transfers between devices  61.8 us (27%)
  blocking collectives  39 us (17%)
  Pallas kernels  21.1 us (9%)
  between operations  14.6 us (6%)
  matrix products  8.49 us (4%)
  local copies, waits for them, and re-layouts  5.19 us (2%)
  other arithmetic  4.17 us (2%)
    ppermute x12, starting transfers between devices, to_chip(): return lax.ppermute(value, 'ctx', pairs)  45.8 us
    all_gather x1, waiting for transfers between devices, on_device(): lax.all_gather(q_rows.reshape(members * depth, half), 'ctx', axis=0, tile...  23.8 us
    all_to_all x1, blocking collectives, on_device(): lax.all_to_all(payload(key_weight, value_weight, adapter_down_weight.T, m...  20.8 us
    all_to_all x1, blocking collectives, on_device(): lax.all_to_all(q_rows.reshape(members, depth, half), 'ctx', 0, 0, tiled=T...  18.3 us
    ppermute x12, waiting for transfers between devices, to_chip(): return lax.ppermute(value, 'ctx', pairs)  16.7 us
    all_gather x1, waiting for transfers between devices, on_device(): lax.all_gather(kv_rows, 'ctx', axis=0, tiled=True, axis_index_groups=across)  16.5 us
    pallas_call x1, Pallas kernels, attend(): pl.pallas_call(functools.partial(attention_kernel, size ** (-0.5), tile),...  12.6 us
    all_to_all x1, waiting for transfers between devices, on_device(): lax.all_to_all(blocks, 'ctx', 0, 0, tiled=True, axis_index_groups=same_core)  11.3 us
  transfers between devices with their start and end apart: 16, of which 11 were waited for; matrix products, arithmetic and copies ran while one was open for 7% of the time, Pallas kernels for 0%

profile of v10, /device:TPU:1, one launch (start us, length us, event | category | flops | bytes accessed | tf_op | source)
XLA Modules:
  0.0 229.1 jit_solution(12499337433554789433)
XLA Ops:
  8.9 20.8 %all_to_all.20 = bf16[8,144,128]{2,1,0:T(8,128)(2,1)} all-to-all(bf16[8,144,128]{2,1,0:T(8,128)(2,1)} %payload.1), channel_id=1, replica_groups={{0,8,16,24,32,40,48,56},{64,72,80,88,96,104,112,120},{128,136,144,152,1..., dimensions={0} | all-to-all | bytes 589824 | tf_op jit(solution)/shard_map/all_to_all | solution.py:316
  30.7 18.3 %all_to_all.21 = bf16[8,128,256]{2,1,0:T(8,128)(2,1)} all-to-all(bf16[8,128,256]{2,1,0:T(8,128)(2,1)S(1)} %bitcast.61), channel_id=1, replica_groups={{0,8,16,24,32,40,48,56},{64,72,80,88,96,104,112,120},{128,136,144,152,1..., dimensions={0} | all-to-all | bytes 1048576 | tf_op jit(solution)/shard_map/all_to_all | solution.py:323
  49.0 2.7 %collective-permute-start = (bf16[256,8192]{1,0:T(8,128)(2,1)}, bf16[256,8192]{1,0:T(8,128)(2,1)}, u32[]{:S(2)}, u32[]{:S(2)}) collective-permute-start(bf16[256,8192]{1,0:T(8,128)(2,1)} %refs_6_.1), channel_id=1, source_target_pairs={{0,8},{8,0},{16,24},{24,16},{32,40},{40,32},{48,56},{56,48},{64,72... | collective-permute-start | bytes 12582920 | tf_op jit(solution)/shard_map/ppermute | solution.py:24
  54.3 16.5 %all-gather.5.cloned.1.call-done = bf16[64,144,128]{2,1,0:T(8,128)(2,1)} async-done(((bf16[8,144,128]{2,1,0:T(8,128)(2,1)}), bf16[64,144,128]{2,1,0:T(8,128)(2,1)}) %all-gather.5.cloned.1.call-update) | async-done | bytes 2359312 | tf_op jit(solution)/shard_map/all_gather | solution.py:320
  70.8 4.3 %fusion.2 = f32[144,256]{0,1:T(8,128)S(1)} fusion(bf16[256,8192]{1,0:T(8,128)(2,1)} %refs_6_.1, bf16[64,144,128]{2,1,0:T(8,128)(2,1)} %all-gather.5.cloned.1.call-done), kind=kOutput, calls=%fused_computation.2 | convolution fusion | flops 603979776 | bytes 6701056 | tf_op jit(solution)/shard_map/dot_general | solution.py:334
  75.1 3.5 %select_bitcast_fusion = (f32[256,144]{1,0:T(8,128)S(1)}, f32[256,144]{1,0:T(8,128)S(1)}) fusion(f32[144,256]{0,1:T(8,128)S(1)} %fusion.2, pred[]{:T(512)S(6)} %eq.4, bf16[256,8192]{1,0:T(8,128)(2,1)} %collective-permute-done.theirs.refs_7_, bf16[64,144,128]{2,1,0:T(8,128)(2,1)S(1)} %copy-done.9), kind=kOutput, calls=%fused_computation.22 | convolution fusion | flops 604053504 | bytes 6995969 | tf_op jit(solution)/shard_map/dot_general | solution.py:335
  78.8 3.3 %collective-permute-start.3 = (bf16[512,128]{1,0:T(8,128)(2,1)S(1)}, bf16[512,128]{1,0:T(8,128)(2,1)S(1)}, u32[]{:S(2)}, u32[]{:S(2)}) collective-permute-start(bf16[512,128]{1,0:T(8,128)(2,1)S(1)} %fusion.7), channel_id=1, source_target_pairs={{0,16},{8,24},{16,32},{24,40},{32,48},{40,56},{48,64},{56,72},{64,... | collective-permute-start | bytes 393224 | tf_op jit(solution)/shard_map/ppermute | solution.py:24
  82.1 4.4 %collective-permute-start.4 = (bf16[512,128]{1,0:T(8,128)(2,1)S(1)}, bf16[512,128]{1,0:T(8,128)(2,1)S(1)}, u32[]{:S(2)}, u32[]{:S(2)}) collective-permute-start(bf16[512,128]{1,0:T(8,128)(2,1)S(1)} %fusion.7), channel_id=1, source_target_pairs={{0,32},{8,40},{16,48},{24,56},{32,64},{40,72},{48,80},{56,88},{64,... | collective-permute-start | bytes 393224 | tf_op jit(solution)/shard_map/ppermute | solution.py:24
  86.4 3.2 %collective-permute-start.5 = (bf16[512,128]{1,0:T(8,128)(2,1)S(1)}, bf16[512,128]{1,0:T(8,128)(2,1)S(1)}, u32[]{:S(2)}, u32[]{:S(2)}) collective-permute-start(bf16[512,128]{1,0:T(8,128)(2,1)S(1)} %fusion.7), channel_id=1, source_target_pairs={{0,48},{8,56},{16,64},{24,72},{32,80},{40,88},{48,96},{56,104},{64... | collective-permute-start | bytes 393224 | tf_op jit(solution)/shard_map/ppermute | solution.py:24
  91.1 5.7 %collective-permute-done.5 = bf16[512,128]{1,0:T(8,128)(2,1)S(1)} collective-permute-done((bf16[512,128]{1,0:T(8,128)(2,1)S(1)}, bf16[512,128]{1,0:T(8,128)(2,1)S(1)}, u32[]{:S(2)}, u32[]{:S(2)}) %collective-permute-start.5) | collective-permute-done | bytes 131104 | tf_op jit(solution)/shard_map/ppermute | solution.py:24
  96.9 7.7 %collective-permute-start.6 = (bf16[4,512,128]{2,1,0:T(8,128)(2,1)S(1)}, bf16[4,512,128]{2,1,0:T(8,128)(2,1)S(1)}, u32[]{:S(2)}, u32[]{:S(2)}) collective-permute-start(bf16[4,512,128]{2,1,0:T(8,128)(2,1)S(1)} %get-tuple-element.26), channel_id=1, source_target_pairs={{0,8},{8,0},{16,24},{24,16},{32,40},{40,32},{48,56},{56,48},{64,72... | collective-permute-start | bytes 1572872 | tf_op jit(solution)/shard_map/ppermute | solution.py:24
  108.2 23.8 %all-gather.3.cloned.1.call-done.weight = bf16[8192,256]{1,0:T(8,128)(2,1)} async-done(((bf16[1024,256]{1,0:T(8,128)(2,1)}), bf16[8192,256]{1,0:T(8,128)(2,1)}) %all-gather.3.cloned.1.call-update) | async-done | bytes 4194320 | tf_op jit(solution)/shard_map/all_gather | solution.py:327
  132.0 12.6 %attention.1 = (bf16[512,256]{1,0:T(8,128)(2,1)S(1)}, bf16[512,256]{1,0:T(8,128)(2,1)S(1)}, f32[4,512,128]{2,1,0:T(8,128)S(1)}) custom-call(s32[3]{0:T(128)S(1)} %pad_add_fusion.info, bf16[256,8192]{1,0:T(8,128)(2,1)} %refs_6_.1, bf16[256,8192]{1,0:T(8,128)(2,1)} %collective-permute-done.theirs.refs_7_, ...), custom_call_target="tpu_custom_call" | custom-call | flops 4831838208 | bytes 16777216 | tf_op jit(solution)/shard_map/attention/pallas_call | solution.py:175
  145.1 2.6 %collective-permute-start.8 = (bf16[2144,128]{1,0:T(8,128)(2,1)S(1)}, bf16[2144,128]{1,0:T(8,128)(2,1)S(1)}, u32[]{:S(2)}, u32[]{:S(2)}) collective-permute-start(bf16[2144,128]{1,0:T(8,128)(2,1)S(1)} %pad_maximum_fusion.1), channel_id=1, source_target_pairs={{0,8},{8,0},{16,24},{24,16},{32,40},{40,32},{48,56},{56,48},{64,72... | collective-permute-start | bytes 1646600 | tf_op jit(solution)/shard_map/ppermute | solution.py:24
  149.6 7.8 %collective-permute-start.11 = (bf16[528,128]{1,0:T(8,128)(2,1)S(1)}, bf16[528,128]{1,0:T(8,128)(2,1)S(1)}, u32[]{:S(2)}, u32[]{:S(2)}) collective-permute-start(bf16[528,128]{1,0:T(8,128)(2,1)S(1)} %pad_maximum_fusion.8), channel_id=1, source_target_pairs={{0,464},{8,472},{16,480},{24,488},{32,496},{40,504},{48,0},{56,8},... | collective-permute-start | bytes 405512 | tf_op jit(solution)/shard_map/ppermute | solution.py:24
  157.4 4.8 %collective-permute-start.10 = (bf16[528,128]{1,0:T(8,128)(2,1)S(1)}, bf16[528,128]{1,0:T(8,128)(2,1)S(1)}, u32[]{:S(2)}, u32[]{:S(2)}) collective-permute-start(bf16[528,128]{1,0:T(8,128)(2,1)S(1)} %pad_maximum_fusion.7), channel_id=1, source_target_pairs={{0,480},{8,488},{16,496},{24,504},{32,0},{40,8},{48,16},{56,24},{6... | collective-permute-start | bytes 405512 | tf_op jit(solution)/shard_map/ppermute | solution.py:24
  165.5 3.8 %collective-permute-done.10.refs_1_ = bf16[528,128]{1,0:T(8,128)(2,1)S(1)} collective-permute-done((bf16[528,128]{1,0:T(8,128)(2,1)S(1)}, bf16[528,128]{1,0:T(8,128)(2,1)S(1)}, u32[]{:S(2)}, u32[]{:S(2)}) %collective-permute-start.10) | collective-permute-done | bytes 135200 | tf_op jit(solution)/shard_map/ppermute | solution.py:24
  169.3 2.8 %collective-permute-done.9.refs_0_ = bf16[528,128]{1,0:T(8,128)(2,1)S(1)} collective-permute-done((bf16[528,128]{1,0:T(8,128)(2,1)S(1)}, bf16[528,128]{1,0:T(8,128)(2,1)S(1)}, u32[]{:S(2)}, u32[]{:S(2)}) %collective-permute-start.9) | collective-permute-done | bytes 135200 | tf_op jit(solution)/shard_map/ppermute | solution.py:24
  172.8 5.2 %all_blocks.1 = (bf16[32,64,128]{2,1,0:T(8,128)(2,1)}, bf16[512,128]{1,0:T(8,128)(2,1)}) custom-call(s32[1]{0:T(128)} %bitcast.info, f32[528,128]{1,0:T(8,128)} %maximum_convert_fusion.own, bf16[528,128]{1,0:T(8,128)(2,1)} %copy-done.5, bf16[528,128]{1,0:T(8,128)(2,1)} %copy-done.4, bf16[528,128]{1,0:T(8,128)(2,1)} %copy-done.3, bf16[16,128]{1,0:T(8,128)(2,1)} %refs_3_.1, ...), custom_call_target="tpu_custom_call" | custom-call | flops 134217728 | bytes 6291456 | tf_op jit(solution)/shard_map/all_blocks/pallas_call | solution.py:252
  178.0 5.5 %all-to-all-start.2 = ((bf16[32,64,128]{2,1,0:T(8,128)(2,1)}), bf16[32,64,128]{2,1,0:T(8,128)(2,1)S(1)}, u32[]{:S(2)}, u32[]{:S(2)}) async-start(bf16[32,64,128]{2,1,0:T(8,128)(2,1)} %get-tuple-element.17), calls=%async_computation.2 | async-start | bytes 1048576 | tf_op jit(solution)/shard_map/all_to_all | solution.py:401
  183.5 3.7 %collective-permute-start.7 = (bf16[256,256]{1,0:T(8,128)(2,1)S(1)}, bf16[256,256]{1,0:T(8,128)(2,1)S(1)}, u32[]{:S(2)}, u32[]{:S(2)}) collective-permute-start(bf16[256,256]{1,0:T(8,128)(2,1)S(1)} %constant_dynamic-slice_fusion.1), channel_id=1, source_target_pairs={{0,8},{8,0},{16,24},{24,16},{32,40},{40,32},{48,56},{56,48},{64,72... | collective-permute-start | bytes 393224 | tf_op jit(solution)/shard_map/ppermute | solution.py:24
  188.3 11.3 %all-to-all-done.2.blocks = bf16[32,64,128]{2,1,0:T(8,128)(2,1)S(1)} async-done(((bf16[32,64,128]{2,1,0:T(8,128)(2,1)}), bf16[32,64,128]{2,1,0:T(8,128)(2,1)S(1)}, u32[]{:S(2)}, u32[]{:S(2)}) %all-to-all-start.2) | async-done | bytes 524320 | tf_op jit(solution)/shard_map/all_to_all | solution.py:401
  202.1 10.4 %all-to-all-start.3 = ((bf16[8,32,128]{2,1,0:T(8,128)(2,1)}), bf16[8,32,128]{2,1,0:T(8,128)(2,1)S(1)}, u32[]{:S(2)}, u32[]{:S(2)}) async-start(bf16[8,32,128]{2,1,0:T(8,128)(2,1)} %get-tuple-element.18), calls=%async_computation.3 | async-start | bytes 131072 | tf_op jit(solution)/shard_map/all_to_all | solution.py:407
  215.2 6.4 %all-to-all-done.3 = bf16[8,32,128]{2,1,0:T(8,128)(2,1)S(1)} async-done(((bf16[8,32,128]{2,1,0:T(8,128)(2,1)}), bf16[8,32,128]{2,1,0:T(8,128)(2,1)S(1)}, u32[]{:S(2)}, u32[]{:S(2)}) %all-to-all-start.3) | async-done | bytes 65568 | tf_op jit(solution)/shard_map/all_to_all | solution.py:407
  (81 shorter events, 23.7 us)
Async XLA Ops:
  7.2 100.7 %copy-start = (bf16[16,512]{1,0:T(8,128)(2,1)S(1)}, bf16[16,512]{1,0:T(8,128)(2,1)}, u32[]{:S(2)}) copy-start(bf16[16,512]{1,0:T(8,128)(2,1)} %param.14) | copy-start | bytes 49156
  7.2 44.5 %copy-start.2 = (bf16[256,512]{1,0:T(8,128)(2,1)S(1)}, bf16[256,512]{1,0:T(8,128)(2,1)}, u32[]{:S(2)}) copy-start(bf16[256,512]{1,0:T(8,128)(2,1)} %param.17) | copy-start | bytes 786436
  7.2 63.6 %all-gather.5.cloned.1.call-start = ((), (), s32[]{:S(2)}) async-start(), calls=%async_computation.5 | async-start | bytes 2654208 | tf_op jit(solution)/shard_map/all_gather | solution.py:320
  29.7 102.3 %all-gather.3.cloned.1.call-start = ((), (), s32[]{:S(2)}) async-start(), calls=%async_computation.4 | async-start | bytes 4718592 | tf_op jit(solution)/shard_map/all_gather | solution.py:327
  49.0 26.1 %collective-permute-start = (bf16[256,8192]{1,0:T(8,128)(2,1)}, bf16[256,8192]{1,0:T(8,128)(2,1)}, u32[]{:S(2)}, u32[]{:S(2)}) collective-permute-start(bf16[256,8192]{1,0:T(8,128)(2,1)} %refs_6_.1), channel_id=1, source_target_pairs={{0,8},{8,0},{16,24},{24,16},{32,40},{40,32},{48,56},{56,48},{64,72... | collective-permute-start | bytes 12582920 | tf_op jit(solution)/shard_map/ppermute | solution.py:24
  52.3 52.3 %collective-permute-start.2 = (bf16[256,256]{1,0:T(8,128)(2,1)S(1)}, bf16[256,256]{1,0:T(8,128)(2,1)S(1)}, u32[]{:S(2)}, u32[]{:S(2)}) collective-permute-start(bf16[256,256]{1,0:T(8,128)(2,1)S(1)} %bitcast.65), channel_id=1, source_target_pairs={{0,8},{8,0},{16,24},{24,16},{32,40},{40,32},{48,56},{56,48},{64,72... | collective-permute-start | bytes 393224 | tf_op jit(solution)/shard_map/ppermute | solution.py:24
  70.8 4.4 %copy-start.9 = (bf16[64,144,128]{2,1,0:T(8,128)(2,1)S(1)}, bf16[64,144,128]{2,1,0:T(8,128)(2,1)}, u32[]{:S(2)}) copy-start(bf16[64,144,128]{2,1,0:T(8,128)(2,1)} %all-gather.5.cloned.1.call-done) | copy-start | bytes 7077892
  75.1 3.6 %copy-start.7 = (bf16[16,128]{1,0:T(8,128)(2,1)S(1)}, bf16[16,128]{1,0:T(8,128)(2,1)}, u32[]{:S(2)}) copy-start(bf16[16,128]{1,0:T(8,128)(2,1)} %refs_3_.1) | copy-start | bytes 12292
  75.1 14.6 %copy-start.8 = (s32[4]{0:T(128)S(1)}, s32[4]{0:T(128)}, u32[]{:S(2)}) copy-start(s32[4]{0:T(128)} %param.16) | copy-start | bytes 52
  78.8 11.0 %collective-permute-start.3 = (bf16[512,128]{1,0:T(8,128)(2,1)S(1)}, bf16[512,128]{1,0:T(8,128)(2,1)S(1)}, u32[]{:S(2)}, u32[]{:S(2)}) collective-permute-start(bf16[512,128]{1,0:T(8,128)(2,1)S(1)} %fusion.7), channel_id=1, source_target_pairs={{0,16},{8,24},{16,32},{24,40},{32,48},{40,56},{48,64},{56,72},{64,... | collective-permute-start | bytes 393224 | tf_op jit(solution)/shard_map/ppermute | solution.py:24
  82.1 9.0 %collective-permute-start.4 = (bf16[512,128]{1,0:T(8,128)(2,1)S(1)}, bf16[512,128]{1,0:T(8,128)(2,1)S(1)}, u32[]{:S(2)}, u32[]{:S(2)}) collective-permute-start(bf16[512,128]{1,0:T(8,128)(2,1)S(1)} %fusion.7), channel_id=1, source_target_pairs={{0,32},{8,40},{16,48},{24,56},{32,64},{40,72},{48,80},{56,88},{64,... | collective-permute-start | bytes 393224 | tf_op jit(solution)/shard_map/ppermute | solution.py:24
  86.4 10.4 %collective-permute-start.5 = (bf16[512,128]{1,0:T(8,128)(2,1)S(1)}, bf16[512,128]{1,0:T(8,128)(2,1)S(1)}, u32[]{:S(2)}, u32[]{:S(2)}) collective-permute-start(bf16[512,128]{1,0:T(8,128)(2,1)S(1)} %fusion.7), channel_id=1, source_target_pairs={{0,48},{8,56},{16,64},{24,72},{32,80},{40,88},{48,96},{56,104},{64... | collective-permute-start | bytes 393224 | tf_op jit(solution)/shard_map/ppermute | solution.py:24
  96.9 11.2 %collective-permute-start.6 = (bf16[4,512,128]{2,1,0:T(8,128)(2,1)S(1)}, bf16[4,512,128]{2,1,0:T(8,128)(2,1)S(1)}, u32[]{:S(2)}, u32[]{:S(2)}) collective-permute-start(bf16[4,512,128]{2,1,0:T(8,128)(2,1)S(1)} %get-tuple-element.26), channel_id=1, source_target_pairs={{0,8},{8,0},{16,24},{24,16},{32,40},{40,32},{48,56},{56,48},{64,72... | collective-permute-start | bytes 1572872 | tf_op jit(solution)/shard_map/ppermute | solution.py:24
  104.7 3.2 %collective-permute-start.1 = (bf16[512,16]{1,0:T(8,128)(2,1)S(1)}, bf16[512,16]{1,0:T(8,128)(2,1)S(1)}, u32[]{:S(2)}, u32[]{:S(2)}) collective-permute-start(bf16[512,16]{1,0:T(8,128)(2,1)S(1)} %fusion.9), channel_id=1, source_target_pairs={{0,8},{8,0},{16,24},{24,16},{32,40},{40,32},{48,56},{56,48},{64,72... | collective-permute-start | bytes 49160 | tf_op jit(solution)/shard_map/ppermute | solution.py:24
  145.1 4.2 %collective-permute-start.8 = (bf16[2144,128]{1,0:T(8,128)(2,1)S(1)}, bf16[2144,128]{1,0:T(8,128)(2,1)S(1)}, u32[]{:S(2)}, u32[]{:S(2)}) collective-permute-start(bf16[2144,128]{1,0:T(8,128)(2,1)S(1)} %pad_maximum_fusion.1), channel_id=1, source_target_pairs={{0,8},{8,0},{16,24},{24,16},{32,40},{40,32},{48,56},{56,48},{64,72... | collective-permute-start | bytes 1646600 | tf_op jit(solution)/shard_map/ppermute | solution.py:24
  149.6 15.9 %collective-permute-start.11 = (bf16[528,128]{1,0:T(8,128)(2,1)S(1)}, bf16[528,128]{1,0:T(8,128)(2,1)S(1)}, u32[]{:S(2)}, u32[]{:S(2)}) collective-permute-start(bf16[528,128]{1,0:T(8,128)(2,1)S(1)} %pad_maximum_fusion.8), channel_id=1, source_target_pairs={{0,464},{8,472},{16,480},{24,488},{32,496},{40,504},{48,0},{56,8},... | collective-permute-start | bytes 405512 | tf_op jit(solution)/shard_map/ppermute | solution.py:24
  157.4 11.9 %collective-permute-start.10 = (bf16[528,128]{1,0:T(8,128)(2,1)S(1)}, bf16[528,128]{1,0:T(8,128)(2,1)S(1)}, u32[]{:S(2)}, u32[]{:S(2)}) collective-permute-start(bf16[528,128]{1,0:T(8,128)(2,1)S(1)} %pad_maximum_fusion.7), channel_id=1, source_target_pairs={{0,480},{8,488},{16,496},{24,504},{32,0},{40,8},{48,16},{56,24},{6... | collective-permute-start | bytes 405512 | tf_op jit(solution)/shard_map/ppermute | solution.py:24
  162.2 9.9 %collective-permute-start.9 = (bf16[528,128]{1,0:T(8,128)(2,1)S(1)}, bf16[528,128]{1,0:T(8,128)(2,1)S(1)}, u32[]{:S(2)}, u32[]{:S(2)}) collective-permute-start(bf16[528,128]{1,0:T(8,128)(2,1)S(1)} %pad_maximum_fusion.6), channel_id=1, source_target_pairs={{0,496},{8,504},{16,0},{24,8},{32,16},{40,24},{48,32},{56,40},{64,... | collective-permute-start | bytes 405512 | tf_op jit(solution)/shard_map/ppermute | solution.py:24
  165.5 6.6 %copy-start.3 = (bf16[528,128]{1,0:T(8,128)(2,1)}, bf16[528,128]{1,0:T(8,128)(2,1)S(1)}, u32[]{:S(2)}) copy-start(bf16[528,128]{1,0:T(8,128)(2,1)S(1)} %collective-permute-done.11.refs_2_) | copy-start | bytes 405508
  169.3 2.8 %copy-start.4 = (bf16[528,128]{1,0:T(8,128)(2,1)}, bf16[528,128]{1,0:T(8,128)(2,1)S(1)}, u32[]{:S(2)}) copy-start(bf16[528,128]{1,0:T(8,128)(2,1)S(1)} %collective-permute-done.10.refs_1_) | copy-start | bytes 405508
  178.0 35.2 %copy-start.6 = (bf16[512,128]{1,0:T(8,128)(2,1)S(1)}, bf16[512,128]{1,0:T(8,128)(2,1)}, u32[]{:S(2)}) copy-start(bf16[512,128]{1,0:T(8,128)(2,1)} %get-tuple-element.16) | copy-start | bytes 393220
  178.0 21.6 %all-to-all-start.2 = ((bf16[32,64,128]{2,1,0:T(8,128)(2,1)}), bf16[32,64,128]{2,1,0:T(8,128)(2,1)S(1)}, u32[]{:S(2)}, u32[]{:S(2)}) async-start(bf16[32,64,128]{2,1,0:T(8,128)(2,1)} %get-tuple-element.17), calls=%async_computation.2 | async-start | bytes 1048576 | tf_op jit(solution)/shard_map/all_to_all | solution.py:401
  183.5 4.6 %collective-permute-start.7 = (bf16[256,256]{1,0:T(8,128)(2,1)S(1)}, bf16[256,256]{1,0:T(8,128)(2,1)S(1)}, u32[]{:S(2)}, u32[]{:S(2)}) collective-permute-start(bf16[256,256]{1,0:T(8,128)(2,1)S(1)} %constant_dynamic-slice_fusion.1), channel_id=1, source_target_pairs={{0,8},{8,0},{16,24},{24,16},{32,40},{40,32},{48,56},{56,48},{64,72... | collective-permute-start | bytes 393224 | tf_op jit(solution)/shard_map/ppermute | solution.py:24
  202.1 19.5 %all-to-all-start.3 = ((bf16[8,32,128]{2,1,0:T(8,128)(2,1)}), bf16[8,32,128]{2,1,0:T(8,128)(2,1)S(1)}, u32[]{:S(2)}, u32[]{:S(2)}) async-start(bf16[8,32,128]{2,1,0:T(8,128)(2,1)} %get-tuple-element.18), calls=%async_computation.3 | async-start | bytes 131072 | tf_op jit(solution)/shard_map/all_to_all | solution.py:407
  (2 other events, 1.4 us)
Sparse Core Ops, SparseCore 0:
  29.8 40.9 all-gather.4
  72.8 59.1 all-gather.2

commit v11 on v10

--- a/solution.py
+++ b/solution.py
@@ -44,39 +44,6 @@
         out_specs=vmem,
         name="payload",
     )(key_weight, value_weight, down)
-
-
-def sum_kernel(blocks, copies, value_up, query_up):
-    ranks, shares = copies.shape[1], query_up.shape[0]
-    last = ranks + value_up.shape[0]
-    total = blocks[0, :last].astype(f32)
-    for chip in range(1, blocks.shape[0]):
-        total += blocks[chip, :last].astype(f32)
-    low = total[:ranks].astype(bf16)
-    for copy in range(copies.shape[0]):
-        copies[copy] = low
-    value_up[...] = total[ranks:]
-    for share in range(shares):
-        total = blocks[share, last:].astype(f32)
-        for chip in range(share + shares, blocks.shape[0], shares):
-            total += blocks[chip, last:].astype(f32)
-        query_up[share] = total
-
-
-def sum_blocks(blocks, rank, count, shares):
-    size = blocks.shape[2]
-    vmem = pl.BlockSpec(memory_space=pltpu.VMEM)
-    return pl.pallas_call(
-        sum_kernel,
-        out_shape=(
-            jax.ShapeDtypeStruct((count, 2 * rank, size), bf16),
-            jax.ShapeDtypeStruct((rank, size), f32),
-            jax.ShapeDtypeStruct((shares, blocks.shape[1] - 3 * rank, size), f32),
-        ),
-        in_specs=[vmem],
-        out_specs=(vmem, vmem, vmem),
-        name="sum_blocks",
-    )(blocks)
 
 
 def rows_of(tokens, theirs, columns, core, target, arrivals, first):
@@ -401,11 +368,15 @@
     blocks = lax.all_to_all(
         blocks, "ctx", 0, 0, tiled=True, axis_index_groups=same_core
     )
-    copies, value_up_gradient, query_up = sum_blocks(
-        blocks, rank, lax.axis_size("fsdp"), chips
+    summed = jnp.sum(blocks[:, : 3 * rank].astype(f32), axis=0)
+    value_up_gradient = summed[2 * rank :]
+    copies = jnp.broadcast_to(
+        summed[None, : 2 * rank].astype(bf16), (lax.axis_size("fsdp"), 2 * rank, size)
     )
     copies = lax.all_to_all(copies, "fsdp", 0, 0, tiled=True)
     grad_down = jnp.sum(copies.astype(f32), axis=0)
+    query_up = blocks[:, 3 * rank :].astype(f32)
+    query_up = query_up.reshape(planes, chips, -1, size).sum(axis=0)
     query_up_gradient = query_up.reshape(rank, width)
     return (
         attention,

time: 232 us -> 230 us (level)
  Pallas kernels: 21.1 us -> 17.5 us
    ppermute x12, starting transfers between devices: 45.8 us -> 49.3 us  [to_chip(): return lax.ppermute(value, 'ctx', pairs)]
    all_to_all x1, starting transfers between devices: 10.4 us -> 6.98 us  [on_device(): copies = lax.all_to_all(copies, 'fsdp', 0, 0, tiled=True)]
  transfers between devices with their start and end apart: 16 -> 16, of which waited for: 11 -> 11; matrix products, arithmetic and copies ran while one was open for 7% -> 6% of each run, Pallas kernels for 0% -> 0%
where the time goes in v11:
time: 230 us; the launch traced here: 227 us
  waiting for transfers between devices  75.8 us (33%)
  starting transfers between devices  62 us (27%)
  blocking collectives  39.1 us (17%)
  Pallas kernels  17.5 us (8%)
  between operations  14.6 us (6%)
  matrix products  8.48 us (4%)
  local copies, waits for them, and re-layouts  4.9 us (2%)
  other arithmetic  4.24 us (2%)
    ppermute x12, starting transfers between devices, to_chip(): return lax.ppermute(value, 'ctx', pairs)  49.3 us
    all_gather x1, waiting for transfers between devices, on_device(): lax.all_gather(q_rows.reshape(members * depth, half), 'ctx', axis=0, tile...  23.8 us
    all_to_all x1, blocking collectives, on_device(): lax.all_to_all(payload(key_weight, value_weight, adapter_down_weight.T, m...  20.8 us
    all_to_all x1, blocking collectives, on_device(): lax.all_to_all(q_rows.reshape(members, depth, half), 'ctx', 0, 0, tiled=T...  18.3 us
    ppermute x12, waiting for transfers between devices, to_chip(): return lax.ppermute(value, 'ctx', pairs)  16.9 us
    all_gather x1, waiting for transfers between devices, on_device(): lax.all_gather(kv_rows, 'ctx', axis=0, tiled=True, axis_index_groups=across)  16.5 us
    pallas_call x1, Pallas kernels, attend(): pl.pallas_call(functools.partial(attention_kernel, size ** (-0.5), tile),...  10.7 us
    all_to_all x1, waiting for transfers between devices, on_device(): lax.all_to_all(blocks, 'ctx', 0, 0, tiled=True, axis_index_groups=same_core)  10.2 us
  transfers between devices with their start and end apart: 16, of which 11 were waited for; matrix products, arithmetic and copies ran while one was open for 6% of the time, Pallas kernels for 0%

profile of v11, /device:TPU:1, one launch (start us, length us, event | category | flops | bytes accessed | tf_op | source)
XLA Modules:
  0.0 226.6 jit_solution(4376877793613832410)
XLA Ops:
  8.9 20.8 %all_to_all.20 = bf16[8,144,128]{2,1,0:T(8,128)(2,1)} all-to-all(bf16[8,144,128]{2,1,0:T(8,128)(2,1)} %payload.1), channel_id=1, replica_groups={{0,8,16,24,32,40,48,56},{64,72,80,88,96,104,112,120},{128,136,144,152,1..., dimensions={0} | all-to-all | bytes 589824 | tf_op jit(solution)/shard_map/all_to_all | solution.py:283
  30.7 18.3 %all_to_all.21 = bf16[8,128,256]{2,1,0:T(8,128)(2,1)} all-to-all(bf16[8,128,256]{2,1,0:T(8,128)(2,1)S(1)} %bitcast.63), channel_id=1, replica_groups={{0,8,16,24,32,40,48,56},{64,72,80,88,96,104,112,120},{128,136,144,152,1..., dimensions={0} | all-to-all | bytes 1048576 | tf_op jit(solution)/shard_map/all_to_all | solution.py:290
  49.0 2.7 %collective-permute-start = (bf16[256,8192]{1,0:T(8,128)(2,1)}, bf16[256,8192]{1,0:T(8,128)(2,1)}, u32[]{:S(2)}, u32[]{:S(2)}) collective-permute-start(bf16[256,8192]{1,0:T(8,128)(2,1)} %refs_6_.1), channel_id=1, source_target_pairs={{0,8},{8,0},{16,24},{24,16},{32,40},{40,32},{48,56},{56,48},{64,72... | collective-permute-start | bytes 12582920 | tf_op jit(solution)/shard_map/ppermute | solution.py:24
  54.3 16.5 %all-gather.5.cloned.1.call-done = bf16[64,144,128]{2,1,0:T(8,128)(2,1)} async-done(((bf16[8,144,128]{2,1,0:T(8,128)(2,1)}), bf16[64,144,128]{2,1,0:T(8,128)(2,1)}) %all-gather.5.cloned.1.call-update) | async-done | bytes 2359312 | tf_op jit(solution)/shard_map/all_gather | solution.py:287
  70.8 4.3 %fusion.2 = f32[144,256]{0,1:T(8,128)S(1)} fusion(bf16[256,8192]{1,0:T(8,128)(2,1)} %refs_6_.1, bf16[64,144,128]{2,1,0:T(8,128)(2,1)} %all-gather.5.cloned.1.call-done), kind=kOutput, calls=%fused_computation.2 | convolution fusion | flops 603979776 | bytes 6701056 | tf_op jit(solution)/shard_map/dot_general | solution.py:301
  75.1 3.5 %select_bitcast_fusion = (f32[256,144]{1,0:T(8,128)S(1)}, f32[256,144]{1,0:T(8,128)S(1)}) fusion(f32[144,256]{0,1:T(8,128)S(1)} %fusion.2, pred[]{:T(512)S(6)} %eq.4, bf16[256,8192]{1,0:T(8,128)(2,1)} %collective-permute-done.theirs.refs_7_, bf16[64,144,128]{2,1,0:T(8,128)(2,1)S(1)} %copy-done.8), kind=kOutput, calls=%fused_computation.24 | convolution fusion | flops 604053504 | bytes 6995969 | tf_op jit(solution)/shard_map/dot_general | solution.py:302
  78.8 3.3 %collective-permute-start.3 = (bf16[512,128]{1,0:T(8,128)(2,1)S(1)}, bf16[512,128]{1,0:T(8,128)(2,1)S(1)}, u32[]{:S(2)}, u32[]{:S(2)}) collective-permute-start(bf16[512,128]{1,0:T(8,128)(2,1)S(1)} %fusion.7), channel_id=1, source_target_pairs={{0,16},{8,24},{16,32},{24,40},{32,48},{40,56},{48,64},{56,72},{64,... | collective-permute-start | bytes 393224 | tf_op jit(solution)/shard_map/ppermute | solution.py:24
  82.1 4.4 %collective-permute-start.4 = (bf16[512,128]{1,0:T(8,128)(2,1)S(1)}, bf16[512,128]{1,0:T(8,128)(2,1)S(1)}, u32[]{:S(2)}, u32[]{:S(2)}) collective-permute-start(bf16[512,128]{1,0:T(8,128)(2,1)S(1)} %fusion.7), channel_id=1, source_target_pairs={{0,32},{8,40},{16,48},{24,56},{32,64},{40,72},{48,80},{56,88},{64,... | collective-permute-start | bytes 393224 | tf_op jit(solution)/shard_map/ppermute | solution.py:24
  86.4 3.2 %collective-permute-start.5 = (bf16[512,128]{1,0:T(8,128)(2,1)S(1)}, bf16[512,128]{1,0:T(8,128)(2,1)S(1)}, u32[]{:S(2)}, u32[]{:S(2)}) collective-permute-start(bf16[512,128]{1,0:T(8,128)(2,1)S(1)} %fusion.7), channel_id=1, source_target_pairs={{0,48},{8,56},{16,64},{24,72},{32,80},{40,88},{48,96},{56,104},{64... | collective-permute-start | bytes 393224 | tf_op jit(solution)/shard_map/ppermute | solution.py:24
  91.1 5.7 %collective-permute-done.5 = bf16[512,128]{1,0:T(8,128)(2,1)S(1)} collective-permute-done((bf16[512,128]{1,0:T(8,128)(2,1)S(1)}, bf16[512,128]{1,0:T(8,128)(2,1)S(1)}, u32[]{:S(2)}, u32[]{:S(2)}) %collective-permute-start.5) | collective-permute-done | bytes 131104 | tf_op jit(solution)/shard_map/ppermute | solution.py:24
  96.9 7.7 %collective-permute-start.6 = (bf16[4,512,128]{2,1,0:T(8,128)(2,1)S(1)}, bf16[4,512,128]{2,1,0:T(8,128)(2,1)S(1)}, u32[]{:S(2)}, u32[]{:S(2)}) collective-permute-start(bf16[4,512,128]{2,1,0:T(8,128)(2,1)S(1)} %get-tuple-element.20), channel_id=1, source_target_pairs={{0,8},{8,0},{16,24},{24,16},{32,40},{40,32},{48,56},{56,48},{64,72... | collective-permute-start | bytes 1572872 | tf_op jit(solution)/shard_map/ppermute | solution.py:24
  108.2 23.8 %all-gather.3.cloned.1.call-done.weight = bf16[8192,256]{1,0:T(8,128)(2,1)} async-done(((bf16[1024,256]{1,0:T(8,128)(2,1)}), bf16[8192,256]{1,0:T(8,128)(2,1)}) %all-gather.3.cloned.1.call-update) | async-done | bytes 4194320 | tf_op jit(solution)/shard_map/all_gather | solution.py:294
  132.0 10.7 %attention.1 = (bf16[512,256]{1,0:T(8,128)(2,1)S(1)}, bf16[512,256]{1,0:T(8,128)(2,1)S(1)}, f32[4,512,128]{2,1,0:T(8,128)S(1)}) custom-call(s32[3]{0:T(128)S(1)} %pad_add_fusion.info, bf16[256,8192]{1,0:T(8,128)(2,1)} %refs_6_.1, bf16[256,8192]{1,0:T(8,128)(2,1)} %collective-permute-done.theirs.refs_7_, ...), custom_call_target="tpu_custom_call" | custom-call | flops 4831838208 | bytes 16777216 | tf_op jit(solution)/shard_map/attention/pallas_call | solution.py:142
  143.3 4.4 %collective-permute-start.8 = (bf16[2144,128]{1,0:T(8,128)(2,1)S(1)}, bf16[2144,128]{1,0:T(8,128)(2,1)S(1)}, u32[]{:S(2)}, u32[]{:S(2)}) collective-permute-start(bf16[2144,128]{1,0:T(8,128)(2,1)S(1)} %pad_maximum_fusion.1), channel_id=1, source_target_pairs={{0,8},{8,0},{16,24},{24,16},{32,40},{40,32},{48,56},{56,48},{64,72... | collective-permute-start | bytes 1646600 | tf_op jit(solution)/shard_map/ppermute | solution.py:24
  149.6 7.8 %collective-permute-start.11 = (bf16[528,128]{1,0:T(8,128)(2,1)S(1)}, bf16[528,128]{1,0:T(8,128)(2,1)S(1)}, u32[]{:S(2)}, u32[]{:S(2)}) collective-permute-start(bf16[528,128]{1,0:T(8,128)(2,1)S(1)} %pad_maximum_fusion.8), channel_id=1, source_target_pairs={{0,464},{8,472},{16,480},{24,488},{32,496},{40,504},{48,0},{56,8},... | collective-permute-start | bytes 405512 | tf_op jit(solution)/shard_map/ppermute | solution.py:24
  157.4 6.6 %collective-permute-start.10 = (bf16[528,128]{1,0:T(8,128)(2,1)S(1)}, bf16[528,128]{1,0:T(8,128)(2,1)S(1)}, u32[]{:S(2)}, u32[]{:S(2)}) collective-permute-start(bf16[528,128]{1,0:T(8,128)(2,1)S(1)} %pad_maximum_fusion.7), channel_id=1, source_target_pairs={{0,480},{8,488},{16,496},{24,504},{32,0},{40,8},{48,16},{56,24},{6... | collective-permute-start | bytes 405512 | tf_op jit(solution)/shard_map/ppermute | solution.py:24
  167.3 4.0 %collective-permute-done.10.refs_1_ = bf16[528,128]{1,0:T(8,128)(2,1)S(1)} collective-permute-done((bf16[528,128]{1,0:T(8,128)(2,1)S(1)}, bf16[528,128]{1,0:T(8,128)(2,1)S(1)}, u32[]{:S(2)}, u32[]{:S(2)}) %collective-permute-start.10) | collective-permute-done | bytes 135200 | tf_op jit(solution)/shard_map/ppermute | solution.py:24
  171.3 2.8 %collective-permute-done.9.refs_0_ = bf16[528,128]{1,0:T(8,128)(2,1)S(1)} collective-permute-done((bf16[528,128]{1,0:T(8,128)(2,1)S(1)}, bf16[528,128]{1,0:T(8,128)(2,1)S(1)}, u32[]{:S(2)}, u32[]{:S(2)}) %collective-permute-start.9) | collective-permute-done | bytes 135200 | tf_op jit(solution)/shard_map/ppermute | solution.py:24
  174.8 5.2 %all_blocks.1 = (bf16[32,64,128]{2,1,0:T(8,128)(2,1)}, bf16[512,128]{1,0:T(8,128)(2,1)}) custom-call(s32[1]{0:T(128)} %bitcast.info, f32[528,128]{1,0:T(8,128)} %maximum_convert_fusion.own, bf16[528,128]{1,0:T(8,128)(2,1)} %copy-done.4, bf16[528,128]{1,0:T(8,128)(2,1)} %copy-done.3, bf16[528,128]{1,0:T(8,128)(2,1)} %copy-done.2, bf16[16,128]{1,0:T(8,128)(2,1)} %refs_3_.1, ...), custom_call_target="tpu_custom_call" | custom-call | flops 134217728 | bytes 6291456 | tf_op jit(solution)/shard_map/all_blocks/pallas_call | solution.py:219
  180.0 5.6 %all-to-all-start.2 = ((bf16[32,64,128]{2,1,0:T(8,128)(2,1)}), bf16[32,64,128]{2,1,0:T(8,128)(2,1)S(1)}, u32[]{:S(2)}, u32[]{:S(2)}) async-start(bf16[32,64,128]{2,1,0:T(8,128)(2,1)} %get-tuple-element.14), calls=%async_computation.2 | async-start | bytes 1048576 | tf_op jit(solution)/shard_map/all_to_all | solution.py:368
  185.6 3.6 %collective-permute-start.7 = (bf16[256,256]{1,0:T(8,128)(2,1)S(1)}, bf16[256,256]{1,0:T(8,128)(2,1)S(1)}, u32[]{:S(2)}, u32[]{:S(2)}) collective-permute-start(bf16[256,256]{1,0:T(8,128)(2,1)S(1)} %constant_dynamic-slice_fusion.1), channel_id=1, source_target_pairs={{0,8},{8,0},{16,24},{24,16},{32,40},{40,32},{48,56},{56,48},{64,72... | collective-permute-start | bytes 393224 | tf_op jit(solution)/shard_map/ppermute | solution.py:24
  191.6 10.2 %all-to-all-done.2 = bf16[32,64,128]{2,1,0:T(8,128)(2,1)S(1)} async-done(((bf16[32,64,128]{2,1,0:T(8,128)(2,1)}), bf16[32,64,128]{2,1,0:T(8,128)(2,1)S(1)}, u32[]{:S(2)}, u32[]{:S(2)}) %all-to-all-start.2) | async-done | bytes 524320 | tf_op jit(solution)/shard_map/all_to_all | solution.py:368
  203.1 7.0 %all-to-all-start.3 = ((bf16[8,32,128]{2,1,0:T(8,128)(2,1)}), bf16[8,32,128]{2,1,0:T(8,128)(2,1)S(1)}, u32[]{:S(2)}, u32[]{:S(2)}) async-start(bf16[8,32,128]{2,1,0:T(8,128)(2,1)} %broadcast_in_dim.33), calls=%async_computation.3 | async-start | bytes 131072 | tf_op jit(solution)/shard_map/all_to_all | solution.py:376
  210.7 8.4 %all-to-all-done.3 = bf16[8,32,128]{2,1,0:T(8,128)(2,1)S(1)} async-done(((bf16[8,32,128]{2,1,0:T(8,128)(2,1)}), bf16[8,32,128]{2,1,0:T(8,128)(2,1)S(1)}, u32[]{:S(2)}, u32[]{:S(2)}) %all-to-all-start.3) | async-done | bytes 65568 | tf_op jit(solution)/shard_map/all_to_all | solution.py:376
  (84 shorter events, 21.7 us)
Async XLA Ops:
  7.2 100.7 %copy-start = (bf16[16,512]{1,0:T(8,128)(2,1)S(1)}, bf16[16,512]{1,0:T(8,128)(2,1)}, u32[]{:S(2)}) copy-start(bf16[16,512]{1,0:T(8,128)(2,1)} %param.14) | copy-start | bytes 49156
  7.2 44.5 %copy-start.1 = (bf16[256,512]{1,0:T(8,128)(2,1)S(1)}, bf16[256,512]{1,0:T(8,128)(2,1)}, u32[]{:S(2)}) copy-start(bf16[256,512]{1,0:T(8,128)(2,1)} %param.17) | copy-start | bytes 786436
  7.2 63.6 %all-gather.5.cloned.1.call-start = ((), (), s32[]{:S(2)}) async-start(), calls=%async_computation.5 | async-start | bytes 2654208 | tf_op jit(solution)/shard_map/all_gather | solution.py:287
  29.7 102.3 %all-gather.3.cloned.1.call-start = ((), (), s32[]{:S(2)}) async-start(), calls=%async_computation.4 | async-start | bytes 4718592 | tf_op jit(solution)/shard_map/all_gather | solution.py:294
  49.0 26.1 %collective-permute-start = (bf16[256,8192]{1,0:T(8,128)(2,1)}, bf16[256,8192]{1,0:T(8,128)(2,1)}, u32[]{:S(2)}, u32[]{:S(2)}) collective-permute-start(bf16[256,8192]{1,0:T(8,128)(2,1)} %refs_6_.1), channel_id=1, source_target_pairs={{0,8},{8,0},{16,24},{24,16},{32,40},{40,32},{48,56},{56,48},{64,72... | collective-permute-start | bytes 12582920 | tf_op jit(solution)/shard_map/ppermute | solution.py:24
  52.3 52.3 %collective-permute-start.2 = (bf16[256,256]{1,0:T(8,128)(2,1)S(1)}, bf16[256,256]{1,0:T(8,128)(2,1)S(1)}, u32[]{:S(2)}, u32[]{:S(2)}) collective-permute-start(bf16[256,256]{1,0:T(8,128)(2,1)S(1)} %bitcast.68), channel_id=1, source_target_pairs={{0,8},{8,0},{16,24},{24,16},{32,40},{40,32},{48,56},{56,48},{64,72... | collective-permute-start | bytes 393224 | tf_op jit(solution)/shard_map/ppermute | solution.py:24
  70.8 4.3 %copy-start.8 = (bf16[64,144,128]{2,1,0:T(8,128)(2,1)S(1)}, bf16[64,144,128]{2,1,0:T(8,128)(2,1)}, u32[]{:S(2)}) copy-start(bf16[64,144,128]{2,1,0:T(8,128)(2,1)} %all-gather.5.cloned.1.call-done) | copy-start | bytes 7077892
  75.1 3.6 %copy-start.6 = (bf16[16,128]{1,0:T(8,128)(2,1)S(1)}, bf16[16,128]{1,0:T(8,128)(2,1)}, u32[]{:S(2)}) copy-start(bf16[16,128]{1,0:T(8,128)(2,1)} %refs_3_.1) | copy-start | bytes 12292
  75.1 14.6 %copy-start.7 = (s32[4]{0:T(128)S(1)}, s32[4]{0:T(128)}, u32[]{:S(2)}) copy-start(s32[4]{0:T(128)} %param.16) | copy-start | bytes 52
  78.8 11.0 %collective-permute-start.3 = (bf16[512,128]{1,0:T(8,128)(2,1)S(1)}, bf16[512,128]{1,0:T(8,128)(2,1)S(1)}, u32[]{:S(2)}, u32[]{:S(2)}) collective-permute-start(bf16[512,128]{1,0:T(8,128)(2,1)S(1)} %fusion.7), channel_id=1, source_target_pairs={{0,16},{8,24},{16,32},{24,40},{32,48},{40,56},{48,64},{56,72},{64,... | collective-permute-start | bytes 393224 | tf_op jit(solution)/shard_map/ppermute | solution.py:24
  82.1 9.0 %collective-permute-start.4 = (bf16[512,128]{1,0:T(8,128)(2,1)S(1)}, bf16[512,128]{1,0:T(8,128)(2,1)S(1)}, u32[]{:S(2)}, u32[]{:S(2)}) collective-permute-start(bf16[512,128]{1,0:T(8,128)(2,1)S(1)} %fusion.7), channel_id=1, source_target_pairs={{0,32},{8,40},{16,48},{24,56},{32,64},{40,72},{48,80},{56,88},{64,... | collective-permute-start | bytes 393224 | tf_op jit(solution)/shard_map/ppermute | solution.py:24
  86.4 10.4 %collective-permute-start.5 = (bf16[512,128]{1,0:T(8,128)(2,1)S(1)}, bf16[512,128]{1,0:T(8,128)(2,1)S(1)}, u32[]{:S(2)}, u32[]{:S(2)}) collective-permute-start(bf16[512,128]{1,0:T(8,128)(2,1)S(1)} %fusion.7), channel_id=1, source_target_pairs={{0,48},{8,56},{16,64},{24,72},{32,80},{40,88},{48,96},{56,104},{64... | collective-permute-start | bytes 393224 | tf_op jit(solution)/shard_map/ppermute | solution.py:24
  96.9 11.2 %collective-permute-start.6 = (bf16[4,512,128]{2,1,0:T(8,128)(2,1)S(1)}, bf16[4,512,128]{2,1,0:T(8,128)(2,1)S(1)}, u32[]{:S(2)}, u32[]{:S(2)}) collective-permute-start(bf16[4,512,128]{2,1,0:T(8,128)(2,1)S(1)} %get-tuple-element.20), channel_id=1, source_target_pairs={{0,8},{8,0},{16,24},{24,16},{32,40},{40,32},{48,56},{56,48},{64,72... | collective-permute-start | bytes 1572872 | tf_op jit(solution)/shard_map/ppermute | solution.py:24
  104.7 3.2 %collective-permute-start.1 = (bf16[512,16]{1,0:T(8,128)(2,1)S(1)}, bf16[512,16]{1,0:T(8,128)(2,1)S(1)}, u32[]{:S(2)}, u32[]{:S(2)}) collective-permute-start(bf16[512,16]{1,0:T(8,128)(2,1)S(1)} %fusion.9), channel_id=1, source_target_pairs={{0,8},{8,0},{16,24},{24,16},{32,40},{40,32},{48,56},{56,48},{64,72... | collective-permute-start | bytes 49160 | tf_op jit(solution)/shard_map/ppermute | solution.py:24
  143.3 6.0 %collective-permute-start.8 = (bf16[2144,128]{1,0:T(8,128)(2,1)S(1)}, bf16[2144,128]{1,0:T(8,128)(2,1)S(1)}, u32[]{:S(2)}, u32[]{:S(2)}) collective-permute-start(bf16[2144,128]{1,0:T(8,128)(2,1)S(1)} %pad_maximum_fusion.1), channel_id=1, source_target_pairs={{0,8},{8,0},{16,24},{24,16},{32,40},{40,32},{48,56},{56,48},{64,72... | collective-permute-start | bytes 1646600 | tf_op jit(solution)/shard_map/ppermute | solution.py:24
  149.6 17.7 %collective-permute-start.11 = (bf16[528,128]{1,0:T(8,128)(2,1)S(1)}, bf16[528,128]{1,0:T(8,128)(2,1)S(1)}, u32[]{:S(2)}, u32[]{:S(2)}) collective-permute-start(bf16[528,128]{1,0:T(8,128)(2,1)S(1)} %pad_maximum_fusion.8), channel_id=1, source_target_pairs={{0,464},{8,472},{16,480},{24,488},{32,496},{40,504},{48,0},{56,8},... | collective-permute-start | bytes 405512 | tf_op jit(solution)/shard_map/ppermute | solution.py:24
  157.4 13.9 %collective-permute-start.10 = (bf16[528,128]{1,0:T(8,128)(2,1)S(1)}, bf16[528,128]{1,0:T(8,128)(2,1)S(1)}, u32[]{:S(2)}, u32[]{:S(2)}) collective-permute-start(bf16[528,128]{1,0:T(8,128)(2,1)S(1)} %pad_maximum_fusion.7), channel_id=1, source_target_pairs={{0,480},{8,488},{16,496},{24,504},{32,0},{40,8},{48,16},{56,24},{6... | collective-permute-start | bytes 405512 | tf_op jit(solution)/shard_map/ppermute | solution.py:24
  164.0 10.1 %collective-permute-start.9 = (bf16[528,128]{1,0:T(8,128)(2,1)S(1)}, bf16[528,128]{1,0:T(8,128)(2,1)S(1)}, u32[]{:S(2)}, u32[]{:S(2)}) collective-permute-start(bf16[528,128]{1,0:T(8,128)(2,1)S(1)} %pad_maximum_fusion.6), channel_id=1, source_target_pairs={{0,496},{8,504},{16,0},{24,8},{32,16},{40,24},{48,32},{56,40},{64,... | collective-permute-start | bytes 405512 | tf_op jit(solution)/shard_map/ppermute | solution.py:24
  167.3 6.9 %copy-start.2 = (bf16[528,128]{1,0:T(8,128)(2,1)}, bf16[528,128]{1,0:T(8,128)(2,1)S(1)}, u32[]{:S(2)}) copy-start(bf16[528,128]{1,0:T(8,128)(2,1)S(1)} %collective-permute-done.11.refs_2_) | copy-start | bytes 405508
  171.3 2.8 %copy-start.3 = (bf16[528,128]{1,0:T(8,128)(2,1)}, bf16[528,128]{1,0:T(8,128)(2,1)S(1)}, u32[]{:S(2)}) copy-start(bf16[528,128]{1,0:T(8,128)(2,1)S(1)} %collective-permute-done.10.refs_1_) | copy-start | bytes 405508
  180.0 11.0 %copy-start.5 = (bf16[512,128]{1,0:T(8,128)(2,1)S(1)}, bf16[512,128]{1,0:T(8,128)(2,1)}, u32[]{:S(2)}) copy-start(bf16[512,128]{1,0:T(8,128)(2,1)} %get-tuple-element.13) | copy-start | bytes 393220
  180.0 21.8 %all-to-all-start.2 = ((bf16[32,64,128]{2,1,0:T(8,128)(2,1)}), bf16[32,64,128]{2,1,0:T(8,128)(2,1)S(1)}, u32[]{:S(2)}, u32[]{:S(2)}) async-start(bf16[32,64,128]{2,1,0:T(8,128)(2,1)} %get-tuple-element.14), calls=%async_computation.2 | async-start | bytes 1048576 | tf_op jit(solution)/shard_map/all_to_all | solution.py:368
  185.6 4.5 %collective-permute-start.7 = (bf16[256,256]{1,0:T(8,128)(2,1)S(1)}, bf16[256,256]{1,0:T(8,128)(2,1)S(1)}, u32[]{:S(2)}, u32[]{:S(2)}) collective-permute-start(bf16[256,256]{1,0:T(8,128)(2,1)S(1)} %constant_dynamic-slice_fusion.1), channel_id=1, source_target_pairs={{0,8},{8,0},{16,24},{24,16},{32,40},{40,32},{48,56},{56,48},{64,72... | collective-permute-start | bytes 393224 | tf_op jit(solution)/shard_map/ppermute | solution.py:24
  203.1 16.1 %all-to-all-start.3 = ((bf16[8,32,128]{2,1,0:T(8,128)(2,1)}), bf16[8,32,128]{2,1,0:T(8,128)(2,1)S(1)}, u32[]{:S(2)}, u32[]{:S(2)}) async-start(bf16[8,32,128]{2,1,0:T(8,128)(2,1)} %broadcast_in_dim.33), calls=%async_computation.3 | async-start | bytes 131072 | tf_op jit(solution)/shard_map/all_to_all | solution.py:376
  (1 other events, 0.7 us)
Sparse Core Ops, SparseCore 0:
  29.8 40.9 all-gather.4
  72.8 59.1 all-gather.2
